TPU v7x, 32 devices: a whole 2x2x4 slice. The times are simulated.
32 devices in a mesh: group: 2 (over x), expert: 16 (over z, y, core).
Axes of the slice: x: 2, y: 2, z: 4, core: 2. Of those that a mesh axis runs over, the one named last changes fastest.
Arguments:
- tokens: bfloat16 [32, 256, 1280], P(('group', 'expert')), parts along dimension 0, may hold values from -6 to 6
- out_grad: bfloat16 [32, 256, 1280], P(('group', 'expert')), parts along dimension 0, may hold values from -6 to 6
- router: bfloat16 [1280, 8], replicated, may hold values from -8 to 8
- in_weight: bfloat16 [1280, 20480], P(None, 'expert'), may hold values from -0.15625 to 0.15625
- out_weight: bfloat16 [20480, 1280], P('expert'), may hold values from -0.125 to 0.125
Outputs:
- tokens_grad: bfloat16 [32, 256, 1280], P(('group', 'expert')), parts along dimension 0
- router_grad: float32 [2560, 8], P('group'), parts along dimension 0
There are 2 independent parts, one for each index of `group`. A program takes and returns all parts, laid end to end along the dimension named above; an argument that names none is the same for every part. Nothing has to cross between parts.
All inputs are finite; a program needn't handle non-finite values.
Results may differ from a plain program's by a relative error of at most 0.011.
Values may be sent and summed in bfloat16 or wider, within the bound.
No kernel may reach another device: no remote copies, remote signals or barrier semaphores. Data moves between devices by JAX's collectives and lax.ppermute only.
A program may use at most 64 MiB of HBM per device.

v0:
```python
import math

import jax
import jax.numpy as jnp
from jax import lax
from jax.sharding import PartitionSpec as P


def gelu_pair(hidden):
    normal_cdf = 0.5 * (1.0 + jax.scipy.special.erf(hidden * (1.0 / math.sqrt(2.0))))
    normal_pdf = jnp.exp(-0.5 * hidden * hidden) * (1.0 / math.sqrt(2.0 * math.pi))
    return (hidden * normal_cdf, normal_cdf + hidden * normal_pdf)


def expert_rows(slot_rows, grad_rows, in_weight, out_weight):
    hidden = jnp.einsum("nkd,dh->nkh", slot_rows, in_weight, preferred_element_type=jnp.float32)
    activation, gelu_slope = gelu_pair(hidden)
    part_out = jnp.einsum(
        "nkh,hd->nkd",
        activation.astype(jnp.bfloat16),
        out_weight,
        preferred_element_type=jnp.float32,
    )
    act_grad = jnp.einsum("nkd,hd->nkh", grad_rows, out_weight, preferred_element_type=jnp.float32)
    hidden_grad = (act_grad * gelu_slope).astype(jnp.bfloat16)
    part_in = jnp.einsum("nkh,dh->nkd", hidden_grad, in_weight, preferred_element_type=jnp.float32)
    return (part_out, part_in)


def per_device(tokens, out_grad, router, in_weight, out_weight):
    image_count, patches, model_width = tokens.shape
    slot_count = router.shape[1]
    logits = jnp.einsum("ds,bpd->bsp", router, tokens, preferred_element_type=jnp.float32)
    dispatch = jax.nn.softmax(logits, axis=2)
    combine = jax.nn.softmax(logits, axis=1)
    dispatch_b = dispatch.astype(jnp.bfloat16)
    combine_b = combine.astype(jnp.bfloat16)
    slot_in = jnp.einsum(
        "bsp,bpd->sbd", dispatch_b, tokens, preferred_element_type=jnp.float32
    ).astype(jnp.bfloat16)
    slot_grad = jnp.einsum(
        "bsp,bpd->sbd", combine_b, out_grad, preferred_element_type=jnp.float32
    ).astype(jnp.bfloat16)
    doubled_in = jnp.repeat(slot_in, 2, axis=0)
    doubled_grad = jnp.repeat(slot_grad, 2, axis=0)
    part_out, part_in = expert_rows(
        lax.all_to_all(doubled_in, "expert", split_axis=0, concat_axis=0, tiled=True),
        lax.all_to_all(doubled_grad, "expert", split_axis=0, concat_axis=0, tiled=True),
        in_weight,
        out_weight,
    )
    back_out = lax.all_to_all(part_out, "expert", split_axis=0, concat_axis=0, tiled=True)
    back_in = lax.all_to_all(part_in, "expert", split_axis=0, concat_axis=0, tiled=True)
    slot_out = (
        back_out.reshape(slot_count, 2, image_count, model_width).sum(axis=1).astype(jnp.bfloat16)
    )
    slot_back = (
        back_in.reshape(slot_count, 2, image_count, model_width).sum(axis=1).astype(jnp.bfloat16)
    )
    combine_grad = jnp.einsum(
        "bpd,sbd->bsp", out_grad, slot_out, preferred_element_type=jnp.float32
    )
    dispatch_grad = jnp.einsum(
        "bpd,sbd->bsp", tokens, slot_back, preferred_element_type=jnp.float32
    )
    logits_grad = combine * (combine_grad - jnp.sum(combine * combine_grad, axis=1, keepdims=True))
    logits_grad = logits_grad + dispatch * (
        dispatch_grad - jnp.sum(dispatch * dispatch_grad, axis=2, keepdims=True)
    )
    logits_b = logits_grad.astype(jnp.bfloat16)
    tokens_grad = jnp.einsum(
        "bsp,sbd->bpd", dispatch_b, slot_back, preferred_element_type=jnp.float32
    )
    tokens_grad = tokens_grad + jnp.einsum(
        "bsp,ds->bpd", logits_b, router, preferred_element_type=jnp.float32
    )
    router_part = jnp.einsum("bpd,bsp->ds", tokens, logits_b, preferred_element_type=jnp.float32)
    router_grad = lax.psum(router_part, "expert")
    return (tokens_grad.astype(jnp.bfloat16), router_grad)


def solution(mesh):
    in_specs = (
        P(("group", "expert"), None, None),
        P(("group", "expert"), None, None),
        P(),
        P(None, "expert"),
        P("expert", None),
    )
    out_specs = (P(("group", "expert"), None, None), P("group", None))
    return jax.shard_map(
        per_device, mesh=mesh, in_specs=in_specs, out_specs=out_specs, check_vma=False
    )
```

profile of v0, /device:TPU:0, one launch (start us, length us, event | category | flops | bytes accessed | tf_op | source)
XLA Modules:
  0.0 122.8 jit_solution(9581756395507591137)
XLA Ops:
  0.6 0.0 copy-start
  0.6 1.7 %fusion.49 = (f32[256]{0:T(256)S(1)}, f32[8]{0:T(128)S(1)}, f32[256,8]{0,1:T(8,128)S(1)}) fusion(bf16[1280,8]{0,1:T(8,128)(2,1)} %param.7, bf16[1,256,1280]{2,1,0:T(8,128)(2,1)} %param.5), kind=kOutput, calls=%fused_computation.60 | convolution fusion | flops 5246712 | bytes 685088 | tf_op jit(solution)/shard_map/ds,bpd->bsp/dot_general | solution.py:33
  2.3 0.0 copy-start.3
  2.3 0.2 fusion.37
  2.5 0.0 copy-start.2
  2.5 0.0 copy-start.4
  2.5 1.3 %convolution_convert_fusion = bf16[8,1280]{1,0:T(8,128)(2,1)S(1)} fusion(bf16[1,256,1280]{2,1,0:T(8,128)(2,1)} %param.5, f32[8]{0:T(128)S(1)} %get-tuple-element.5, f32[8]{0:T(128)S(1)} %get-tuple-element.7, f32[256,8]{0,1:T(8,128)S(1)} %get-tuple-element.8), kind=kOutput, calls=%fused_computation.8 | convolution fusion | flops 5259264 | bytes 684096 | tf_op jit(solution)/shard_map/bsp,bpd->sbd/dot_general | solution.py:38
  3.9 0.5 broadcast.32
  4.5 0.9 reduce.16
  5.3 0.6 reshape.142
  6.0 7.4 %all-to-all-start.1 = ((bf16[16,2,640]{2,1,0:T(2,128)(2,1)}), bf16[16,2,640]{2,1,0:T(2,128)(2,1)S(1)}, u32[]{:S(2)}, u32[]{:S(2)}) async-start(bf16[16,2,640]{2,1,0:T(2,128)(2,1)} %reshape.142), calls=%async_computation.1 | async-start | bytes 81920 | tf_op jit(solution)/shard_map/all_to_all | solution.py:47
  13.4 1.3 %convolution_convert_fusion.1 = bf16[8,1280]{1,0:T(8,128)(2,1)S(1)} fusion(bf16[1,256,1280]{2,1,0:T(8,128)(2,1)} %param.6, f32[256,8]{0,1:T(8,128)S(1)} %get-tuple-element.8, f32[256]{0:T(256)S(1)} %get-tuple-element.4, f32[256]{0:T(256)S(1)} %get-tuple-element.6), kind=kOutput, calls=%fused_computation.9 | convolution fusion | flops 5259264 | bytes 686080 | tf_op jit(solution)/shard_map/bsp,bpd->sbd/dot_general | solution.py:41
  14.7 0.9 reduce.17
  15.6 0.6 reshape.144
  16.2 3.8 %all-to-all-done.1 = bf16[16,2,640]{2,1,0:T(2,128)(2,1)S(1)} async-done(((bf16[16,2,640]{2,1,0:T(2,128)(2,1)}), bf16[16,2,640]{2,1,0:T(2,128)(2,1)S(1)}, u32[]{:S(2)}, u32[]{:S(2)}) %all-to-all-start.1) | async-done | bytes 40992 | tf_op jit(solution)/shard_map/all_to_all | solution.py:47
  20.1 0.0 copy-done.2
  20.1 4.1 %all-to-all-start = ((bf16[16,2,640]{2,1,0:T(2,128)(2,1)}), bf16[16,2,640]{2,1,0:T(2,128)(2,1)}, u32[]{:S(2)}, u32[]{:S(2)}) async-start(bf16[16,2,640]{2,1,0:T(2,128)(2,1)} %reshape.144), calls=%async_computation | async-start | bytes 81920 | tf_op jit(solution)/shard_map/all_to_all | solution.py:48
  24.3 0.0 copy-done
  24.3 0.5 fusion.17
  24.8 6.1 %all-to-all-done = bf16[16,2,640]{2,1,0:T(2,128)(2,1)} async-done(((bf16[16,2,640]{2,1,0:T(2,128)(2,1)}), bf16[16,2,640]{2,1,0:T(2,128)(2,1)}, u32[]{:S(2)}, u32[]{:S(2)}) %all-to-all-start) | async-done | bytes 40992 | tf_op jit(solution)/shard_map/all_to_all | solution.py:48
  30.9 0.8 reshape.145
  31.7 3.8 %convolution_bitcast_fusion.1 = f32[16,1,1280]{2,0,1:T(8,128)S(1)} fusion(bf16[1280,1280]{1,0:T(8,128)(2,1)S(1)} %copy-done, bf16[1280,1280]{1,0:T(8,128)(2,1)} %param.9, f32[16,1280]{1,0:T(8,128)S(1)} %fusion.17, bf16[16,1,1280]{2,1,0:T(2,128)(2,1)S(1)} %reshape.145), kind=kOutput, calls=%fused_computation.5 | convolution fusion | flops 105062400 | bytes 6758400 | tf_op jit(solution)/shard_map/nkh,dh->nkd/dot_general | solution.py:26
  35.6 0.0 copy-done.3
  35.6 0.0 copy-done.4
  35.6 0.7 copy.11
  36.3 3.5 %all-to-all-start.2 = ((f32[16,1,1280]{2,1,0:T(1,128)}), f32[16,1,1280]{2,1,0:T(1,128)S(1)}, u32[]{:S(2)}, u32[]{:S(2)}) async-start(f32[16,1,1280]{2,1,0:T(1,128)} %copy.11), calls=%async_computation.2 | async-start | bytes 163840 | tf_op jit(solution)/shard_map/all_to_all | solution.py:53
  39.8 0.0 copy-start.1
  39.9 2.5 %convolution_bitcast_fusion = f32[16,1,1280]{2,0,1:T(8,128)S(1)} fusion(bf16[1280,1280]{1,0:T(8,128)(2,1)} %param.9, f32[16,1280]{1,0:T(8,128)S(1)} %fusion.17), kind=kOutput, calls=%fused_computation.4 | convolution fusion | flops 52531200 | bytes 3440640 | tf_op jit(solution)/shard_map/nkh,hd->nkd/dot_general | solution.py:18
  42.3 0.7 copy.12
  43.1 3.9 %all-to-all-done.2 = f32[16,1,1280]{2,1,0:T(1,128)S(1)} async-done(((f32[16,1,1280]{2,1,0:T(1,128)}), f32[16,1,1280]{2,1,0:T(1,128)S(1)}, u32[]{:S(2)}, u32[]{:S(2)}) %all-to-all-start.2) | async-done | bytes 81952 | tf_op jit(solution)/shard_map/all_to_all | solution.py:53
  46.9 3.5 %all-to-all-start.3 = ((f32[16,1,1280]{2,1,0:T(1,128)}), f32[16,1,1280]{2,1,0:T(1,128)S(1)}, u32[]{:S(2)}, u32[]{:S(2)}) async-start(f32[16,1,1280]{2,1,0:T(1,128)} %copy.12), calls=%async_computation.3 | async-start | bytes 163840 | tf_op jit(solution)/shard_map/all_to_all | solution.py:52
  50.5 0.2 reduce.14
  50.7 0.1 reshape.137
  50.7 0.1 reduce_sum.56
  50.8 2.2 %fusion.28 = f32[256,1280]{1,0:T(8,128)} fusion(bf16[8,1280]{1,0:T(8,128)(2,1)S(1)} %reduce_sum.56, f32[8]{0:T(128)} %copy-done.4, f32[8]{0:T(128)} %copy-done.3, f32[256,8]{0,1:T(8,128)S(1)} %get-tuple-element.8), kind=kOutput, calls=%fused_computation.35 | convolution fusion | flops 5249024 | bytes 1339456 | tf_op jit(solution)/shard_map/bsp,sbd->bpd/dot_general | solution.py:71
  53.0 1.3 %fusion.7 = f32[8,256]{1,0:T(8,128)S(1)} fusion(bf16[1,256,1280]{2,1,0:T(8,128)(2,1)} %param.5, bf16[8,1280]{1,0:T(8,128)(2,1)S(1)} %reduce_sum.56), kind=kOutput, calls=%fused_computation.14 | convolution fusion | flops 5242880 | bytes 684032 | tf_op jit(solution)/shard_map/bpd,sbd->bsp/dot_general | solution.py:63
  54.3 3.2 %all-to-all-done.3 = f32[16,1,1280]{2,1,0:T(1,128)S(1)} async-done(((f32[16,1,1280]{2,1,0:T(1,128)}), f32[16,1,1280]{2,1,0:T(1,128)S(1)}, u32[]{:S(2)}, u32[]{:S(2)}) %all-to-all-start.3) | async-done | bytes 81952 | tf_op jit(solution)/shard_map/all_to_all | solution.py:52
  57.6 0.2 reduce.15
  57.8 0.1 reshape.138
  57.8 0.1 reduce_sum.57
  57.9 1.5 %fusion.33 = (f32[256]{0:T(256)S(1)}, f32[8]{0:T(128)S(1)}, f32[8,256]{1,0:T(8,128)S(1)}) fusion(f32[256]{0:T(256)} %copy-done.2, f32[256]{0:T(256)S(1)} %get-tuple-element.6, f32[256,8]{0,1:T(8,128)S(1)} %get-tuple-element.8, f32[8,256]{1,0:T(8,128)S(1)} %fusion.7, f32[8]{0:T(128)} %copy-done.4, f32[8]{0:T(128)} %copy-done.3, ...), kind=kOutput, calls=%fused_computation.44 | convolution fusion | flops 5259000 | bytes 703584 | tf_op jit(solution)/shard_map/bpd,sbd->bsp/dot_general | solution.py:60
  59.5 1.4 %convolution_bitcast_fusion.2 = f32[1280,8]{0,1:T(8,128)S(1)} fusion(bf16[1,256,1280]{2,1,0:T(8,128)(2,1)} %param.5, f32[8,256]{1,0:T(8,128)S(1)} %fusion.7, f32[8,256]{1,0:T(8,128)S(1)} %get-tuple-element.9, f32[8]{0:T(128)S(1)} %get-tuple-element.3, f32[256]{0:T(256)S(1)} %get-tuple-element.2, f32[8]{0:T(128)} %copy-done.4, f32[8]{0:T(128)} %copy-done.3, ...), kind=kOutput, calls=%fused_computation.7 | convolution fusion | flops 5263360 | bytes 724064 | tf_op jit(solution)/shard_map/bpd,bsp->ds/dot_general | solution.py:77
  60.8 0.0 copy-done.1
  60.8 2.6 %fusion.1 = bf16[1,256,1280]{2,1,0:T(8,128)(2,1)} fusion(f32[256,1280]{1,0:T(8,128)} %fusion.28, bf16[1280,8]{0,1:T(8,128)(2,1)S(1)} %copy-done.1, f32[8,256]{1,0:T(8,128)S(1)} %fusion.7, f32[8,256]{1,0:T(8,128)S(1)} %get-tuple-element.9, f32[8]{0:T(128)S(1)} %get-tuple-element.3, f32[256]{0:T(256)S(1)} %get-tuple-element.2, f32[8]{0:T(128)} %copy-done.4, ...), kind=kOutput, calls=%fused_computation.2 | convolution fusion | flops 5918720 | bytes 2014304 | tf_op jit(solution)/shard_map/bsp,ds->bpd/dot_general | solution.py:74
  63.4 59.3 %psum.7 = f32[1280,8]{0,1:T(8,128)} all-reduce(f32[1280,8]{0,1:T(8,128)S(1)} %convolution_bitcast_fusion.2), channel_id=1, replica_groups=mesh['group'=2,'expert'=16] {'expert'}, use_global_device_ids=true, to_apply=%region_8.0 | all-reduce | flops 10240 | bytes 81920 | tf_op jit(solution)/shard_map/psum | solution.py:78
  (5 shorter events, 0.2 us)
Async XLA Ops:
  0.6 23.6 %copy-start = (bf16[1280,1280]{1,0:T(8,128)(2,1)S(1)}, bf16[1280,1280]{1,0:T(8,128)(2,1)}, u32[]{:S(2)}) copy-start(bf16[1280,1280]{1,0:T(8,128)(2,1)} %param.8) | copy-start | bytes 9830404
  2.3 33.3 %copy-start.3 = (f32[8]{0:T(128)}, f32[8]{0:T(128)S(1)}, u32[]{:S(2)}) copy-start(f32[8]{0:T(128)S(1)} %get-tuple-element.7) | copy-start | bytes 100
  2.5 17.5 %copy-start.2 = (f32[256]{0:T(256)}, f32[256]{0:T(256)S(1)}, u32[]{:S(2)}) copy-start(f32[256]{0:T(256)S(1)} %get-tuple-element.4) | copy-start | bytes 3076
  2.5 33.1 %copy-start.4 = (f32[8]{0:T(128)}, f32[8]{0:T(128)S(1)}, u32[]{:S(2)}) copy-start(f32[8]{0:T(128)S(1)} %get-tuple-element.5) | copy-start | bytes 100
  6.0 14.1 %all-to-all-start.1 = ((bf16[16,2,640]{2,1,0:T(2,128)(2,1)}), bf16[16,2,640]{2,1,0:T(2,128)(2,1)S(1)}, u32[]{:S(2)}, u32[]{:S(2)}) async-start(bf16[16,2,640]{2,1,0:T(2,128)(2,1)} %reshape.142), calls=%async_computation.1 | async-start | bytes 81920 | tf_op jit(solution)/shard_map/all_to_all | solution.py:47
  20.1 10.9 %all-to-all-start = ((bf16[16,2,640]{2,1,0:T(2,128)(2,1)}), bf16[16,2,640]{2,1,0:T(2,128)(2,1)}, u32[]{:S(2)}, u32[]{:S(2)}) async-start(bf16[16,2,640]{2,1,0:T(2,128)(2,1)} %reshape.144), calls=%async_computation | async-start | bytes 81920 | tf_op jit(solution)/shard_map/all_to_all | solution.py:48
  36.3 10.6 %all-to-all-start.2 = ((f32[16,1,1280]{2,1,0:T(1,128)}), f32[16,1,1280]{2,1,0:T(1,128)S(1)}, u32[]{:S(2)}, u32[]{:S(2)}) async-start(f32[16,1,1280]{2,1,0:T(1,128)} %copy.11), calls=%async_computation.2 | async-start | bytes 163840 | tf_op jit(solution)/shard_map/all_to_all | solution.py:53
  39.8 21.0 %copy-start.1 = (bf16[1280,8]{0,1:T(8,128)(2,1)S(1)}, bf16[1280,8]{0,1:T(8,128)(2,1)}, u32[]{:S(2)}) copy-start(bf16[1280,8]{0,1:T(8,128)(2,1)} %param.7) | copy-start | bytes 61444
  46.9 10.6 %all-to-all-start.3 = ((f32[16,1,1280]{2,1,0:T(1,128)}), f32[16,1,1280]{2,1,0:T(1,128)S(1)}, u32[]{:S(2)}, u32[]{:S(2)}) async-start(f32[16,1,1280]{2,1,0:T(1,128)} %copy.12), calls=%async_computation.3 | async-start | bytes 163840 | tf_op jit(solution)/shard_map/all_to_all | solution.py:52
where the time goes:
time: 124 us; the launch traced here: 123 us
  blocking collectives  59.3 us (48%)
  matrix products  20.2 us (16%)
  starting transfers between devices  18.5 us (15%)
  waiting for transfers between devices  17.1 us (14%)
  local copies, waits for them, and re-layouts  4.38 us (4%)
  other arithmetic  2.51 us (2%)
    psum x1, blocking collectives, per_device(): router_grad = lax.psum(router_part, 'expert')  59.3 us
    all_to_all x1, starting transfers between devices, per_device(): lax.all_to_all(doubled_in, 'expert', split_axis=0, concat_axis=0, tiled=T...  7.39 us
    all_to_all x1, waiting for transfers between devices, per_device(): lax.all_to_all(doubled_grad, 'expert', split_axis=0, concat_axis=0, tiled...  6.11 us
    all_to_all x1, starting transfers between devices, per_device(): lax.all_to_all(doubled_grad, 'expert', split_axis=0, concat_axis=0, tiled...  4.15 us
    all_to_all x1, waiting for transfers between devices, per_device(): lax.all_to_all(part_in, 'expert', split_axis=0, concat_axis=0, tiled=True)  3.89 us
    dot_general x1, matrix products, expert_rows(): jnp.einsum('nkh,dh->nkd', hidden_grad, in_weight, preferred_element_type=...  3.83 us
    all_to_all x1, waiting for transfers between devices, per_device(): lax.all_to_all(doubled_in, 'expert', split_axis=0, concat_axis=0, tiled=T...  3.82 us
    all_to_all x1, starting transfers between devices, per_device(): lax.all_to_all(part_in, 'expert', split_axis=0, concat_axis=0, tiled=True)  3.51 us
  transfers between devices with their start and end apart: 4, of which 4 were waited for; matrix products, arithmetic and copies ran while one was open for 9% of the time, Pallas kernels for 0%

commit v1 on v0

v1 whole, which is shorter than its diff:
```python
import math

import jax
import jax.numpy as jnp
from jax import lax
from jax.sharding import PartitionSpec as P


def gelu_pair(hidden):
    normal_cdf = 0.5 * (1.0 + jax.scipy.special.erf(hidden * (1.0 / math.sqrt(2.0))))
    normal_pdf = jnp.exp(-0.5 * hidden * hidden) * (1.0 / math.sqrt(2.0 * math.pi))
    return (hidden * normal_cdf, normal_cdf + hidden * normal_pdf)


def expert_rows(slot_rows, grad_rows, in_weight, out_weight):
    hidden = jnp.einsum("kd,dh->kh", slot_rows, in_weight, preferred_element_type=jnp.float32)
    activation, gelu_slope = gelu_pair(hidden)
    part_out = jnp.einsum(
        "kh,hd->kd",
        activation.astype(jnp.bfloat16),
        out_weight,
        preferred_element_type=jnp.float32,
    )
    act_grad = jnp.einsum("kd,hd->kh", grad_rows, out_weight, preferred_element_type=jnp.float32)
    hidden_grad = (act_grad * gelu_slope).astype(jnp.bfloat16)
    part_in = jnp.einsum("kh,dh->kd", hidden_grad, in_weight, preferred_element_type=jnp.float32)
    return (part_out, part_in)


def doubling_sum(value, axis, size):
    step = 1
    while step < size:
        pairs = [(i, i ^ step) for i in range(size)]
        value = value + lax.ppermute(value, axis, pairs)
        step *= 2
    return value


def make_per_device(size):
    def per_device(tokens, out_grad, router, in_weight, out_weight):
        _, patches, model_width = tokens.shape
        slot_count = router.shape[1]
        halves = size // slot_count
        tokens = tokens[0]
        out_grad = out_grad[0]
        logits = jnp.einsum("ds,pd->sp", router, tokens, preferred_element_type=jnp.float32)
        dispatch = jax.nn.softmax(logits, axis=1)
        combine = jax.nn.softmax(logits, axis=0)
        dispatch_b = dispatch.astype(jnp.bfloat16)
        combine_b = combine.astype(jnp.bfloat16)
        slot_in = jnp.einsum(
            "sp,pd->sd", dispatch_b, tokens, preferred_element_type=jnp.float32
        ).astype(jnp.bfloat16)
        slot_grad = jnp.einsum(
            "sp,pd->sd", combine_b, out_grad, preferred_element_type=jnp.float32
        ).astype(jnp.bfloat16)
        sent = jnp.repeat(jnp.concatenate([slot_in, slot_grad], axis=1), halves, axis=0)
        got = lax.all_to_all(sent, "expert", split_axis=0, concat_axis=0, tiled=True)
        part_out, part_in = expert_rows(
            got[:, :model_width], got[:, model_width:], in_weight, out_weight
        )
        parts = jnp.concatenate([part_out, part_in], axis=1).astype(jnp.bfloat16)
        back = lax.all_to_all(parts, "expert", split_axis=0, concat_axis=0, tiled=True)
        back = (
            back.reshape(slot_count, halves, 2 * model_width)
            .astype(jnp.float32)
            .sum(axis=1)
            .astype(jnp.bfloat16)
        )
        slot_out = back[:, :model_width]
        slot_back = back[:, model_width:]
        combine_grad = jnp.einsum("pd,sd->sp", out_grad, slot_out, preferred_element_type=jnp.float32)
        dispatch_grad = jnp.einsum("pd,sd->sp", tokens, slot_back, preferred_element_type=jnp.float32)
        logits_grad = combine * (combine_grad - jnp.sum(combine * combine_grad, axis=0, keepdims=True))
        logits_grad = logits_grad + dispatch * (
            dispatch_grad - jnp.sum(dispatch * dispatch_grad, axis=1, keepdims=True)
        )
        logits_b = logits_grad.astype(jnp.bfloat16)
        router_part = jnp.einsum("pd,sp->ds", tokens, logits_b, preferred_element_type=jnp.float32)
        router_grad = doubling_sum(router_part, "expert", size)
        tokens_grad = jnp.einsum(
            "sp,sd->pd", dispatch_b, slot_back, preferred_element_type=jnp.float32
        )
        tokens_grad = tokens_grad + jnp.einsum(
            "sp,ds->pd", logits_b, router, preferred_element_type=jnp.float32
        )
        return (tokens_grad.astype(jnp.bfloat16)[None], router_grad)

    return per_device


def solution(mesh):
    in_specs = (
        P(("group", "expert"), None, None),
        P(("group", "expert"), None, None),
        P(),
        P(None, "expert"),
        P("expert", None),
    )
    out_specs = (P(("group", "expert"), None, None), P("group", None))
    return jax.shard_map(
        make_per_device(mesh.shape["expert"]),
        mesh=mesh,
        in_specs=in_specs,
        out_specs=out_specs,
        check_vma=False,
    )
```

time: 124 us -> 59.1 us (0.48)
  blocking collectives: 59.3 us -> 24.1 us
  starting transfers between devices: 18.5 us -> 0.13 us
  waiting for transfers between devices: 17.1 us -> 11.5 us
  local copies, waits for them, and re-layouts: 4.38 us -> 0.93 us
  matrix products: 20.2 us -> 17.9 us
    psum x1 -> x0, blocking collectives: 59.3 us -> none  [per_device(): router_grad = lax.psum(router_part, 'expert')]
    all_to_all x0 -> x2, blocking collectives: none -> 24.1 us  [the longest x1 14.3 us: per_device(): lax.all_to_all(sent, 'expert', split_axis=0, concat_axis=0, tiled=True)]
    all_to_all x4 -> x0, starting transfers between devices: 18.5 us -> none  [the longest x1 7.39 us: per_device(): lax.all_to_all(doubled_in, 'expert', split_axis=0, concat_axis=0, tiled=T...]
    all_to_all x4 -> x0, waiting for transfers between devices: 17.1 us -> none  [the longest x1 6.11 us: per_device(): lax.all_to_all(doubled_grad, 'expert', split_axis=0, concat_axis=0, tiled...]
    ppermute x0 -> x4, waiting for transfers between devices: none -> 11.5 us  [doubling_sum(): value = value + lax.ppermute(value, axis, pairs)]
    dot_general x11, matrix products: 20.2 us -> 17.9 us  [the longest x1 3.84 us: expert_rows(): jnp.einsum('kh,dh->kd', hidden_grad, in_weight, preferred_element_type=jn...]
    unnamed x14 -> x21, local copies, waits for them, and re-layouts: 2.14 us -> 0.25 us
    broadcast_in_dim x2 -> x0, other arithmetic: 1.73 us -> none  [the longest x1 0.87 us: per_device(): doubled_grad = jnp.repeat(slot_grad, 2, axis=0)]
  transfers between devices with their start and end apart: 4 -> 4, of which waited for: 4 -> 4; matrix products, arithmetic and copies ran while one was open for 9% -> 4% of each run, Pallas kernels for 0% -> 0%
where the time goes in v1:
time: 59.1 us; the launch traced here: 58.7 us
  blocking collectives  24.1 us (41%)
  matrix products  17.9 us (30%)
  waiting for transfers between devices  11.5 us (19%)
  other arithmetic  3.28 us (6%)
  local copies, waits for them, and re-layouts  0.93 us (2%)
  between operations  0.82 us (1%)
    all_to_all x1, blocking collectives, per_device(): lax.all_to_all(sent, 'expert', split_axis=0, concat_axis=0, tiled=True)  14.3 us
    ppermute x4, waiting for transfers between devices, doubling_sum(): value = value + lax.ppermute(value, axis, pairs)  11.5 us
    all_to_all x1, blocking collectives, per_device(): lax.all_to_all(parts, 'expert', split_axis=0, concat_axis=0, tiled=True)  9.73 us
    dot_general x1, matrix products, expert_rows(): jnp.einsum('kh,dh->kd', hidden_grad, in_weight, preferred_element_type=jn...  3.84 us
    dot_general x1, matrix products, expert_rows(): jnp.einsum('kh,hd->kd', activation.astype(jnp.bfloat16), out_weight, pref...  2.47 us
    dot_general x1, matrix products, per_device(): jnp.einsum('ds,pd->sp', router, tokens, preferred_element_type=jnp.float32)  1.68 us
    dot_general x1, matrix products, per_device(): jnp.einsum('pd,sd->sp', out_grad, slot_out, preferred_element_type=jnp.fl...  1.62 us
    dot_general x1, matrix products, per_device(): jnp.einsum('pd,sp->ds', tokens, logits_b, preferred_element_type=jnp.floa...  1.37 us
  transfers between devices with their start and end apart: 4, of which 4 were waited for; matrix products, arithmetic and copies ran while one was open for 4% of the time, Pallas kernels for 0%

profile of v1, /device:TPU:0, one launch (start us, length us, event | category | flops | bytes accessed | tf_op | source)
XLA Modules:
  0.0 58.7 jit_solution(17570389868605423960)
XLA Ops:
  0.6 0.0 copy-start
  0.6 1.7 %fusion.41 = (f32[8]{0:T(128)S(1)}, f32[256]{0:T(256)S(1)}, f32[8,256]{1,0:T(8,128)S(1)}) fusion(bf16[1280,8]{0,1:T(8,128)(2,1)} %param.7, bf16[1,256,1280]{2,1,0:T(8,128)(2,1)} %param.5), kind=kOutput, calls=%fused_computation.54 | convolution fusion | flops 5246712 | bytes 685088 | tf_op jit(solution)/shard_map/ds,pd->sp/dot_general | solution.py:46
  2.3 0.0 copy-start.4
  2.3 0.2 fusion.30
  2.5 0.0 copy-start.2
  2.5 0.0 copy-start.6
  2.5 1.3 %convolution_convert_fusion.3 = bf16[8,1280]{1,0:T(8,128)(2,1)S(1)} fusion(bf16[1,256,1280]{2,1,0:T(8,128)(2,1)} %param.5, f32[8,256]{1,0:T(8,128)S(1)} %get-tuple-element.8, f32[8]{0:T(128)S(1)} %get-tuple-element.4, f32[8]{0:T(128)S(1)} %get-tuple-element.6), kind=kOutput, calls=%fused_computation.11 | convolution fusion | flops 5259264 | bytes 684096 | tf_op jit(solution)/shard_map/sp,pd->sd/dot_general | solution.py:51
  3.9 1.3 %convolution_convert_fusion.2 = bf16[8,1280]{1,0:T(8,128)(2,1)S(1)} fusion(bf16[1,256,1280]{2,1,0:T(8,128)(2,1)} %param.6, f32[8,256]{1,0:T(8,128)S(1)} %get-tuple-element.8, f32[256]{0:T(256)S(1)} %get-tuple-element.5, f32[256]{0:T(256)S(1)} %get-tuple-element.7), kind=kOutput, calls=%fused_computation.10 | convolution fusion | flops 5259264 | bytes 686080 | tf_op jit(solution)/shard_map/sp,pd->sd/dot_general | solution.py:54
  5.2 0.1 broadcast_in_dim.4
  5.3 0.1 all_to_all.16
  5.3 0.5 broadcast.8
  5.8 1.1 %reduce.2 = bf16[16,2560]{1,0:T(8,128)(2,1)S(1)} reduce(bf16[16,1,2560]{2,1,0:T(2,128)(2,1)S(1)} %all_to_all.16, bf16[]{:T(256)} %broadcast.8), dimensions={1}, to_apply=%all_to_all.16.reduce_sub_computation | reduce | bytes 163842 | tf_op jit(solution)/shard_map/all_to_all | solution.py:58
  7.0 14.3 %all_to_all.19 = bf16[16,2,1280]{2,1,0:T(2,128)(2,1)S(1)} all-to-all(bf16[16,2,1280]{2,1,0:T(2,128)(2,1)S(1)} %reshape.53), channel_id=1, replica_groups=mesh['group'=2,'expert'=16] {'expert'}, dimensions={0} | all-to-all | bytes 163840 | tf_op jit(solution)/shard_map/all_to_all | solution.py:58
  21.3 0.1 reshape.54
  21.4 0.0 copy-done
  21.4 0.5 fusion.21
  21.9 3.8 %fusion.4 = bf16[16,1,1280]{2,0,1:T(8,128)(2,1)S(1)} fusion(bf16[1280,1280]{1,0:T(8,128)(2,1)S(1)} %copy-done, bf16[1280,1280]{1,0:T(8,128)(2,1)} %param.9, f32[16,1280]{1,0:T(8,128)S(1)} %fusion.21, bf16[16,2560]{1,0:T(8,128)(2,1)S(1)} %bitcast.36), kind=kOutput, calls=%fused_computation.8 | convolution fusion | flops 105082880 | bytes 6717440 | tf_op jit(solution)/shard_map/kh,dh->kd/dot_general | solution.py:26
  25.8 0.0 copy-done.4
  25.8 0.0 copy-done.2
  25.8 0.0 copy-done.6
  25.8 2.5 %fusion.3 = bf16[16,1,1280]{2,0,1:T(8,128)(2,1)S(1)} fusion(bf16[1280,1280]{1,0:T(8,128)(2,1)} %param.9, f32[16,1280]{1,0:T(8,128)S(1)} %fusion.21), kind=kOutput, calls=%fused_computation.7 | convolution fusion | flops 52551680 | bytes 3399680 | tf_op jit(solution)/shard_map/kh,hd->kd/dot_general | solution.py:18
  28.3 0.0 copy-start.1
  28.3 0.7 %reduce.3 = bf16[16,2560]{1,0:T(8,128)(2,1)S(1)} reduce(bf16[16,1,2560]{2,0,1:T(8,128)(2,1)S(1)} %pad_maximum_fusion, bf16[]{:T(256)} %broadcast.8), dimensions={1}, to_apply=%copy.9.reduce_sub_computation | reduce | bytes 163842 | tf_op jit(solution)/shard_map/concatenate | solution.py:62
  29.0 9.7 %all_to_all.20 = bf16[16,2,1280]{2,1,0:T(2,128)(2,1)S(1)} all-to-all(bf16[16,2,1280]{2,1,0:T(2,128)(2,1)S(1)} %reshape.55), channel_id=1, replica_groups=mesh['group'=2,'expert'=16] {'expert'}, dimensions={0} | all-to-all | bytes 163840 | tf_op jit(solution)/shard_map/all_to_all | solution.py:63
  38.8 0.1 reshape.56
  38.8 0.5 reduce.1
  39.3 0.0 copy-start.3
  39.3 0.0 copy-start.5
  39.4 0.0 copy-start.7
  39.4 0.2 reduce_sum.50
  39.6 1.3 %fusion.9 = f32[8,256]{1,0:T(8,128)S(1)} fusion(bf16[1,256,1280]{2,1,0:T(8,128)(2,1)} %param.5, bf16[8,2560]{1,0:T(8,128)(2,1)S(1)} %reduce_sum.50), kind=kOutput, calls=%fused_computation.16 | convolution fusion | flops 5242880 | bytes 684032 | tf_op jit(solution)/shard_map/pd,sd->sp/dot_general | solution.py:73
  40.9 1.6 %multiply_reduce_fusion.1 = (f32[256]{0:T(256)S(1)}, f32[8]{0:T(128)S(1)}, f32[8,256]{1,0:T(8,128)S(1)}) fusion(f32[256]{0:T(256)} %copy-done.2, f32[8,256]{1,0:T(8,128)S(1)} %get-tuple-element.8, f32[256]{0:T(256)S(1)} %get-tuple-element.7, f32[8,256]{1,0:T(8,128)S(1)} %fusion.9, f32[8]{0:T(128)} %copy-done.6, f32[8]{0:T(128)} %copy-done.4, ...), kind=kOutput, calls=%fused_computation.42 | convolution fusion | flops 5259000 | bytes 703584 | tf_op jit(solution)/shard_map/pd,sd->sp/dot_general | solution.py:72
  42.5 1.4 %convolution_bitcast_fusion = f32[1280,8]{0,1:T(8,128)S(1)} fusion(bf16[1,256,1280]{2,1,0:T(8,128)(2,1)} %param.5, f32[8,256]{1,0:T(8,128)S(1)} %fusion.9, f32[8,256]{1,0:T(8,128)S(1)} %get-tuple-element.9, f32[8]{0:T(128)S(1)} %get-tuple-element.3, f32[256]{0:T(256)S(1)} %get-tuple-element.2, f32[256]{0:T(256)} %copy-done.2, ...), kind=kOutput, calls=%fused_computation.9 | convolution fusion | flops 5263360 | bytes 724064 | tf_op jit(solution)/shard_map/pd,sp->ds/dot_general | solution.py:79
  43.9 0.0 collective-permute-start
  43.9 1.2 %collective-permute-done = f32[1280,8]{0,1:T(8,128)S(1)} collective-permute-done((f32[1280,8]{0,1:T(8,128)S(1)}, f32[1280,8]{0,1:T(8,128)S(1)}, u32[]{:S(2)}, u32[]{:S(2)}) %collective-permute-start) | collective-permute-done | bytes 40992 | tf_op jit(solution)/shard_map/ppermute | solution.py:34
  45.1 0.0 collective-permute-start.1
  45.1 4.0 %collective-permute-done.1 = f32[1280,8]{0,1:T(8,128)S(1)} collective-permute-done((f32[1280,8]{0,1:T(8,128)S(1)}, f32[1280,8]{0,1:T(8,128)S(1)}, u32[]{:S(2)}, u32[]{:S(2)}) %collective-permute-start.1) | collective-permute-done | bytes 40992 | tf_op jit(solution)/shard_map/ppermute | solution.py:34
  49.1 0.0 collective-permute-start.2
  49.1 1.1 %fusion.27 = f32[256,1280]{1,0:T(8,128)S(1)} fusion(bf16[8,2560]{1,0:T(8,128)(2,1)S(1)} %reduce_sum.50, f32[8,256]{1,0:T(8,128)S(1)} %get-tuple-element.8, f32[8]{0:T(128)} %copy-done.6, f32[8]{0:T(128)} %copy-done.4), kind=kOutput, calls=%fused_computation.38 | convolution fusion | flops 5249024 | bytes 1339456 | tf_op jit(solution)/shard_map/sp,sd->pd/dot_general | solution.py:81
  50.3 2.9 %collective-permute-done.2 = f32[1280,8]{0,1:T(8,128)S(1)} collective-permute-done((f32[1280,8]{0,1:T(8,128)S(1)}, f32[1280,8]{0,1:T(8,128)S(1)}, u32[]{:S(2)}, u32[]{:S(2)}) %collective-permute-start.2) | collective-permute-done | bytes 40992 | tf_op jit(solution)/shard_map/ppermute | solution.py:34
  53.1 0.1 collective-permute-start.3
  53.3 0.0 copy-done.1
  53.3 0.0 copy-done.3
  53.3 0.0 copy-done.5
  53.3 0.0 copy-done.7
  53.3 1.3 %fusion.1 = bf16[1,256,1280]{2,1,0:T(8,128)(2,1)} fusion(f32[256,1280]{1,0:T(8,128)S(1)} %fusion.27, bf16[1280,8]{0,1:T(8,128)(2,1)S(1)} %copy-done.1, f32[8,256]{1,0:T(8,128)S(1)} %fusion.9, f32[8,256]{1,0:T(8,128)S(1)} %get-tuple-element.9, f32[8]{0:T(128)S(1)} %get-tuple-element.3, f32[256]{0:T(256)S(1)} %get-tuple-element.2, f32[256]{0:T(256)S(1)} %copy-done.3, ...), kind=kOutput, calls=%fused_computation.2 | convolution fusion | flops 5918720 | bytes 2014304 | tf_op jit(solution)/shard_map/sp,ds->pd/dot_general | solution.py:84
  54.6 3.5 %collective-permute-done.3 = f32[1280,8]{0,1:T(8,128)S(1)} collective-permute-done((f32[1280,8]{0,1:T(8,128)S(1)}, f32[1280,8]{0,1:T(8,128)S(1)}, u32[]{:S(2)}, u32[]{:S(2)}) %collective-permute-start.3) | collective-permute-done | bytes 40992 | tf_op jit(solution)/shard_map/ppermute | solution.py:34
  58.0 0.6 %add.35 = f32[1280,8]{0,1:T(8,128)} add(f32[1280,8]{0,1:T(8,128)S(1)} %add.34, f32[1280,8]{0,1:T(8,128)S(1)} %collective-permute-done.3) | non-fusion elementwise | flops 10240 | bytes 122880 | tf_op jit(solution)/shard_map/add | solution.py:34
  (9 shorter events, 0.1 us)
Async XLA Ops:
  0.6 20.8 %copy-start = (bf16[1280,1280]{1,0:T(8,128)(2,1)S(1)}, bf16[1280,1280]{1,0:T(8,128)(2,1)}, u32[]{:S(2)}) copy-start(bf16[1280,1280]{1,0:T(8,128)(2,1)} %param.8) | copy-start | bytes 9830404
  2.3 23.5 %copy-start.4 = (f32[8]{0:T(128)}, f32[8]{0:T(128)S(1)}, u32[]{:S(2)}) copy-start(f32[8]{0:T(128)S(1)} %get-tuple-element.6) | copy-start | bytes 100
  2.5 23.3 %copy-start.2 = (f32[256]{0:T(256)}, f32[256]{0:T(256)S(1)}, u32[]{:S(2)}) copy-start(f32[256]{0:T(256)S(1)} %get-tuple-element.5) | copy-start | bytes 3076
  2.5 23.3 %copy-start.6 = (f32[8]{0:T(128)}, f32[8]{0:T(128)S(1)}, u32[]{:S(2)}) copy-start(f32[8]{0:T(128)S(1)} %get-tuple-element.4) | copy-start | bytes 100
  28.3 25.0 %copy-start.1 = (bf16[1280,8]{0,1:T(8,128)(2,1)S(1)}, bf16[1280,8]{0,1:T(8,128)(2,1)}, u32[]{:S(2)}) copy-start(bf16[1280,8]{0,1:T(8,128)(2,1)} %param.7) | copy-start | bytes 61444
  39.3 13.9 %copy-start.3 = (f32[256]{0:T(256)S(1)}, f32[256]{0:T(256)}, u32[]{:S(2)}) copy-start(f32[256]{0:T(256)} %copy-done.2) | copy-start | bytes 3076
  39.3 13.9 %copy-start.5 = (f32[8]{0:T(128)S(1)}, f32[8]{0:T(128)}, u32[]{:S(2)}) copy-start(f32[8]{0:T(128)} %copy-done.4) | copy-start | bytes 100
  39.4 13.9 %copy-start.7 = (f32[8]{0:T(128)S(1)}, f32[8]{0:T(128)}, u32[]{:S(2)}) copy-start(f32[8]{0:T(128)} %copy-done.6) | copy-start | bytes 100
  43.9 1.2 %collective-permute-start = (f32[1280,8]{0,1:T(8,128)S(1)}, f32[1280,8]{0,1:T(8,128)S(1)}, u32[]{:S(2)}, u32[]{:S(2)}) collective-permute-start(f32[1280,8]{0,1:T(8,128)S(1)} %convolution_bitcast_fusion), channel_id=1, source_target_pairs={{0,1},{1,0},{2,3},{3,2},{4,5},{5,4},{6,7},{7,6},{8,9},{9,8},{10,11... | collective-permute-start | bytes 122888 | tf_op jit(solution)/shard_map/ppermute | solution.py:34
  45.1 4.0 %collective-permute-start.1 = (f32[1280,8]{0,1:T(8,128)S(1)}, f32[1280,8]{0,1:T(8,128)S(1)}, u32[]{:S(2)}, u32[]{:S(2)}) collective-permute-start(f32[1280,8]{0,1:T(8,128)S(1)} %add.32), channel_id=1, source_target_pairs={{0,2},{1,3},{2,0},{3,1},{4,6},{5,7},{6,4},{7,5},{8,10},{9,11},{10,... | collective-permute-start | bytes 122888 | tf_op jit(solution)/shard_map/ppermute | solution.py:34
  49.1 4.0 %collective-permute-start.2 = (f32[1280,8]{0,1:T(8,128)S(1)}, f32[1280,8]{0,1:T(8,128)S(1)}, u32[]{:S(2)}, u32[]{:S(2)}) collective-permute-start(f32[1280,8]{0,1:T(8,128)S(1)} %add.33), channel_id=1, source_target_pairs={{0,4},{1,5},{2,6},{3,7},{4,0},{5,1},{6,2},{7,3},{8,12},{9,13},{10,... | collective-permute-start | bytes 122888 | tf_op jit(solution)/shard_map/ppermute | solution.py:34
  53.1 4.9 %collective-permute-start.3 = (f32[1280,8]{0,1:T(8,128)S(1)}, f32[1280,8]{0,1:T(8,128)S(1)}, u32[]{:S(2)}, u32[]{:S(2)}) collective-permute-start(f32[1280,8]{0,1:T(8,128)S(1)} %add.34), channel_id=1, source_target_pairs={{0,8},{1,9},{2,10},{3,11},{4,12},{5,13},{6,14},{7,15},{8,0},{9,1},... | collective-permute-start | bytes 122888 | tf_op jit(solution)/shard_map/ppermute | solution.py:34

commit v2 on v1

--- a/solution.py
+++ b/solution.py
@@ -27,23 +27,23 @@
     return (part_out, part_in)
 
 
-def doubling_sum(value, axis, size):
-    step = 1
-    while step < size:
-        pairs = [(i, i ^ step) for i in range(size)]
-        value = value + lax.ppermute(value, axis, pairs)
-        step *= 2
-    return value
+def by_offset(size, offset):
+    return [(i, i ^ offset) for i in range(size)]
 
 
 def make_per_device(size):
     def per_device(tokens, out_grad, router, in_weight, out_weight):
         _, patches, model_width = tokens.shape
-        slot_count = router.shape[1]
-        halves = size // slot_count
+        chips = router.shape[1]
+        me = lax.axis_index("expert")
+        chip = me // 2
+        core = me % 2
         tokens = tokens[0]
         out_grad = out_grad[0]
-        logits = jnp.einsum("ds,pd->sp", router, tokens, preferred_element_type=jnp.float32)
+        slots = jnp.arange(chips)
+        swap = (slots[:, None] == (slots[None, :] ^ chip)).astype(jnp.bfloat16)
+        router_rel = jnp.einsum("ds,sk->dk", router, swap)
+        logits = jnp.einsum("ds,pd->sp", router_rel, tokens, preferred_element_type=jnp.float32)
         dispatch = jax.nn.softmax(logits, axis=1)
         combine = jax.nn.softmax(logits, axis=0)
         dispatch_b = dispatch.astype(jnp.bfloat16)
@@ -54,21 +54,27 @@
         slot_grad = jnp.einsum(
             "sp,pd->sd", combine_b, out_grad, preferred_element_type=jnp.float32
         ).astype(jnp.bfloat16)
-        sent = jnp.repeat(jnp.concatenate([slot_in, slot_grad], axis=1), halves, axis=0)
-        got = lax.all_to_all(sent, "expert", split_axis=0, concat_axis=0, tiled=True)
-        part_out, part_in = expert_rows(
-            got[:, :model_width], got[:, model_width:], in_weight, out_weight
-        )
-        parts = jnp.concatenate([part_out, part_in], axis=1).astype(jnp.bfloat16)
-        back = lax.all_to_all(parts, "expert", split_axis=0, concat_axis=0, tiled=True)
-        back = (
-            back.reshape(slot_count, halves, 2 * model_width)
-            .astype(jnp.float32)
-            .sum(axis=1)
-            .astype(jnp.bfloat16)
-        )
-        slot_out = back[:, :model_width]
-        slot_back = back[:, model_width:]
+        rows = []
+        for k in range(chips):
+            message = jnp.stack([slot_in[k], slot_grad[k]])
+            for c in range(2):
+                offset = 2 * k + c
+                if offset:
+                    message_k = lax.ppermute(message, "expert", by_offset(size, offset))
+                else:
+                    message_k = message
+                rows.append(message_k)
+        got = jnp.stack(rows)
+        part_out, part_in = expert_rows(got[:, 0], got[:, 1], in_weight, out_weight)
+        parts = jnp.stack([part_out, part_in], axis=1).reshape(chips, 2, 2, model_width)
+        other = lax.ppermute(parts[:, 1], "expert", by_offset(size, 1))
+        mine = (parts[:, 0] + other).astype(jnp.bfloat16)
+        back = [mine[0]]
+        for k in range(1, chips):
+            back.append(lax.ppermute(mine[k], "expert", by_offset(size, 2 * k)))
+        back = jnp.stack(back)
+        slot_out = back[:, 0]
+        slot_back = back[:, 1]
         combine_grad = jnp.einsum("pd,sd->sp", out_grad, slot_out, preferred_element_type=jnp.float32)
         dispatch_grad = jnp.einsum("pd,sd->sp", tokens, slot_back, preferred_element_type=jnp.float32)
         logits_grad = combine * (combine_grad - jnp.sum(combine * combine_grad, axis=0, keepdims=True))
@@ -76,17 +82,39 @@
             dispatch_grad - jnp.sum(dispatch * dispatch_grad, axis=1, keepdims=True)
         )
         logits_b = logits_grad.astype(jnp.bfloat16)
-        router_part = jnp.einsum("pd,sp->ds", tokens, logits_b, preferred_element_type=jnp.float32)
-        router_grad = doubling_sum(router_part, "expert", size)
+        logits_abs = jnp.einsum("ks,kp->sp", swap, logits_b)
+        half = model_width // 2
+        router_part = jnp.einsum("sp,pd->sd", logits_abs, tokens, preferred_element_type=jnp.float32)
+        router_part = router_part.reshape(chips, 2, half)
+        kept = lax.dynamic_index_in_dim(router_part, core, 1, keepdims=False)
+        given = lax.dynamic_index_in_dim(router_part, 1 - core, 1, keepdims=False)
+        total = kept + lax.ppermute(given, "expert", by_offset(size, 1))
+        radix = 2
+        while radix < size:
+            width = 2 if radix == 2 else min(4, size // radix)
+            total = sum_of(total, radix, width, size)
+            radix *= width
+        theirs = lax.ppermute(total, "expert", by_offset(size, 1))
+        pair = jnp.where(core == 0, jnp.stack([total, theirs]), jnp.stack([theirs, total]))
+        router_grad = pair.transpose(0, 2, 1).reshape(model_width, chips)
         tokens_grad = jnp.einsum(
             "sp,sd->pd", dispatch_b, slot_back, preferred_element_type=jnp.float32
         )
         tokens_grad = tokens_grad + jnp.einsum(
-            "sp,ds->pd", logits_b, router, preferred_element_type=jnp.float32
+            "sp,ds->pd", logits_abs, router, preferred_element_type=jnp.float32
         )
         return (tokens_grad.astype(jnp.bfloat16)[None], router_grad)
 
     return per_device
+
+
+def sum_of(value, radix, width, size):
+    if width == 2:
+        return value + lax.ppermute(value, "expert", by_offset(size, radix))
+    terms = [value] + [
+        lax.ppermute(value, "expert", by_offset(size, radix * k)) for k in range(1, width)
+    ]
+    return (terms[0] + terms[1]) + (terms[2] + terms[3])
 
 
 def solution(mesh):

time: 59.1 us -> 79.3 us (1.34)
  starting transfers between devices: 0.13 us -> 39.5 us
  blocking collectives: 24.1 us -> 0 us
  waiting for transfers between devices: 11.5 us -> 15.4 us
  local copies, waits for them, and re-layouts: 0.93 us -> 3.94 us
  other arithmetic: 3.28 us -> 1.15 us
    ppermute x4 -> x29, starting transfers between devices: 0.13 us -> 39.5 us  [the longest x15 22.9 us: per_device(): message_k = lax.ppermute(message, 'expert', by_offset(size, offset))]
    all_to_all x2 -> x0, blocking collectives: 24.1 us -> none  [the longest x1 14.3 us: per_device(): lax.all_to_all(sent, 'expert', split_axis=0, concat_axis=0, tiled=True)]
    ppermute x4 -> x29, waiting for transfers between devices: 11.5 us -> 15.4 us  [the longest x15 6.42 us: per_device(): message_k = lax.ppermute(message, 'expert', by_offset(size, offset))]
    dot_general x0 -> x1, local copies, waits for them, and re-layouts: none -> 2.16 us  [per_device(): jnp.einsum('sp,pd->sd', logits_abs, tokens, preferred_element_type=jnp.fl...]
    dot_general x1, matrix products: 2.47 us -> 0.56 us  [expert_rows(): jnp.einsum('kh,hd->kd', activation.astype(jnp.bfloat16), out_weight, pref...]
    all_to_all x2 -> x0, other arithmetic: 1.55 us -> none  [the longest x1 1.1 us: per_device(): lax.all_to_all(sent, 'expert', split_axis=0, concat_axis=0, tiled=True)]
    another operation x0 -> x6, local copies, waits for them, and re-layouts: none -> 1.18 us  [the longest x4 1.16 us: per_device(): jnp.stack([part_out, part_in], axis=1).reshape(chips, 2, 2, model_width)]
    dot_general x3 -> x4, matrix products: 4.35 us -> 5.3 us  [the longest x1 1.81 us: per_device(): jnp.einsum('ds,pd->sp', router_rel, tokens, preferred_element_type=jnp.fl...]
  transfers between devices with their start and end apart: 4 -> 29, of which waited for: 4 -> 10; matrix products, arithmetic and copies ran while one was open for 4% -> 6% of each run, Pallas kernels for 0% -> 0%
where the time goes in v2:
time: 79.3 us; the launch traced here: 78.9 us
  starting transfers between devices  39.5 us (50%)
  matrix products  17.8 us (22%)
  waiting for transfers between devices  15.4 us (19%)
  local copies, waits for them, and re-layouts  3.94 us (5%)
  other arithmetic  1.15 us (1%)
  between operations  1.09 us (1%)
    ppermute x15, starting transfers between devices, per_device(): message_k = lax.ppermute(message, 'expert', by_offset(size, offset))  22.9 us
    ppermute x7, starting transfers between devices, per_device(): back.append(lax.ppermute(mine[k], 'expert', by_offset(size, 2 * k)))  11.3 us
    ppermute x15, waiting for transfers between devices, per_device(): message_k = lax.ppermute(message, 'expert', by_offset(size, offset))  6.42 us
    dot_general x1, matrix products, expert_rows(): jnp.einsum('kh,dh->kd', hidden_grad, in_weight, preferred_element_type=jn...  4.5 us
    ppermute x3, starting transfers between devices, sum_of(): lax.ppermute(value, 'expert', by_offset(size, radix * k))  3.79 us
    ppermute x1, waiting for transfers between devices, sum_of(): return value + lax.ppermute(value, 'expert', by_offset(size, radix))  2.49 us
    dot_general x1, local copies, waits for them, and re-layouts, per_device(): jnp.einsum('sp,pd->sd', logits_abs, tokens, preferred_element_type=jnp.fl...  2.16 us
    ppermute x3, waiting for transfers between devices, sum_of(): lax.ppermute(value, 'expert', by_offset(size, radix * k))  2.15 us
  transfers between devices with their start and end apart: 29, of which 10 were waited for; matrix products, arithmetic and copies ran while one was open for 6% of the time, Pallas kernels for 0%

profile of v2, /device:TPU:0, one launch (start us, length us, event | category | flops | bytes accessed | tf_op | source)
XLA Modules:
  0.0 78.9 jit_solution(17716343707471529192)
XLA Ops:
  0.7 1.8 %fusion.61 = (f32[8]{0:T(128)S(1)}, f32[256]{0:T(256)S(1)}, f32[8,256]{1,0:T(8,128)S(1)}) fusion(bf16[1,256,1280]{2,1,0:T(8,128)(2,1)} %param.5, bf16[1280,8]{0,1:T(8,128)(2,1)} %param.7, s32[8]{0:T(128)S(1)} %iota_xor_fusion), kind=kOutput, calls=%fused_computation.111 | convolution fusion | flops 5410616 | bytes 685120 | tf_op jit(solution)/shard_map/ds,pd->sp/dot_general | solution.py:46
  2.5 0.2 fusion.42
  2.7 1.5 %convolution_convert_fusion.1 = bf16[8,1280]{1,0:T(8,128)(2,1)S(1)} fusion(bf16[1,256,1280]{2,1,0:T(8,128)(2,1)} %param.5, f32[8,256]{1,0:T(8,128)S(1)} %get-tuple-element.38, f32[8]{0:T(128)S(1)} %get-tuple-element.4, f32[8]{0:T(128)S(1)} %get-tuple-element.6), kind=kOutput, calls=%fused_computation.6 | convolution fusion | flops 5259264 | bytes 684096 | tf_op jit(solution)/shard_map/sp,pd->sd/dot_general | solution.py:51
  4.2 1.3 %convolution_convert_fusion = bf16[8,1280]{1,0:T(8,128)(2,1)S(1)} fusion(bf16[1,256,1280]{2,1,0:T(8,128)(2,1)} %param.6, f32[8,256]{1,0:T(8,128)S(1)} %get-tuple-element.38, f32[256]{0:T(256)S(1)} %get-tuple-element.5, f32[256]{0:T(256)S(1)} %get-tuple-element.7), kind=kOutput, calls=%fused_computation.5 | convolution fusion | flops 5259264 | bytes 686080 | tf_op jit(solution)/shard_map/sp,pd->sd/dot_general | solution.py:54
  5.6 3.0 %collective-permute-start.1 = (bf16[2,1280]{1,0:T(2,128)(2,1)S(1)}, bf16[2,1280]{1,0:T(2,128)(2,1)S(1)}, u32[]{:S(2)}, u32[]{:S(2)}) collective-permute-start(bf16[2,1280]{1,0:T(2,128)(2,1)S(1)} %pad_maximum_fusion.2), channel_id=1, source_target_pairs={{0,2},{1,3},{2,0},{3,1},{4,6},{5,7},{6,4},{7,5},{8,10},{9,11},{10,... | collective-permute-start | bytes 15368 | tf_op jit(solution)/shard_map/ppermute | solution.py:63
  8.7 1.6 %collective-permute-start.3 = (bf16[2,1280]{1,0:T(2,128)(2,1)S(1)}, bf16[2,1280]{1,0:T(2,128)(2,1)S(1)}, u32[]{:S(2)}, u32[]{:S(2)}) collective-permute-start(bf16[2,1280]{1,0:T(2,128)(2,1)S(1)} %pad_maximum_fusion.3), channel_id=1, source_target_pairs={{0,4},{1,5},{2,6},{3,7},{4,0},{5,1},{6,2},{7,3},{8,12},{9,13},{10,... | collective-permute-start | bytes 15368 | tf_op jit(solution)/shard_map/ppermute | solution.py:63
  10.3 0.3 collective-permute-start.4
  10.7 0.3 collective-permute-start
  11.1 0.8 collective-permute-done
  11.9 2.6 %collective-permute-start.5 = (bf16[2,1280]{1,0:T(2,128)(2,1)S(1)}, bf16[2,1280]{1,0:T(2,128)(2,1)S(1)}, u32[]{:S(2)}, u32[]{:S(2)}) collective-permute-start(bf16[2,1280]{1,0:T(2,128)(2,1)S(1)} %pad_maximum_fusion.4), channel_id=1, source_target_pairs={{0,6},{1,7},{2,4},{3,5},{4,2},{5,3},{6,0},{7,1},{8,14},{9,15},{10,... | collective-permute-start | bytes 15368 | tf_op jit(solution)/shard_map/ppermute | solution.py:63
  14.7 2.7 %collective-permute-start.7 = (bf16[2,1280]{1,0:T(2,128)(2,1)S(1)}, bf16[2,1280]{1,0:T(2,128)(2,1)S(1)}, u32[]{:S(2)}, u32[]{:S(2)}) collective-permute-start(bf16[2,1280]{1,0:T(2,128)(2,1)S(1)} %pad_maximum_fusion.5), channel_id=1, source_target_pairs={{0,8},{1,9},{2,10},{3,11},{4,12},{5,13},{6,14},{7,15},{8,0},{9,1},... | collective-permute-start | bytes 15368 | tf_op jit(solution)/shard_map/ppermute | solution.py:63
  17.3 0.2 collective-permute-start.8
  17.5 3.6 %collective-permute-start.9 = (bf16[2,1280]{1,0:T(2,128)(2,1)S(1)}, bf16[2,1280]{1,0:T(2,128)(2,1)S(1)}, u32[]{:S(2)}, u32[]{:S(2)}) collective-permute-start(bf16[2,1280]{1,0:T(2,128)(2,1)S(1)} %pad_maximum_fusion.6), channel_id=1, source_target_pairs={{0,10},{1,11},{2,8},{3,9},{4,14},{5,15},{6,12},{7,13},{8,2},{9,3},... | collective-permute-start | bytes 15368 | tf_op jit(solution)/shard_map/ppermute | solution.py:63
  21.3 3.4 %collective-permute-start.11 = (bf16[2,1280]{1,0:T(2,128)(2,1)S(1)}, bf16[2,1280]{1,0:T(2,128)(2,1)S(1)}, u32[]{:S(2)}, u32[]{:S(2)}) collective-permute-start(bf16[2,1280]{1,0:T(2,128)(2,1)S(1)} %pad_maximum_fusion.7), channel_id=1, source_target_pairs={{0,12},{1,13},{2,14},{3,15},{4,8},{5,9},{6,10},{7,11},{8,4},{9,5},... | collective-permute-start | bytes 15368 | tf_op jit(solution)/shard_map/ppermute | solution.py:63
  24.7 0.3 collective-permute-start.12
  25.1 4.6 %collective-permute-start.13 = (bf16[2,1280]{1,0:T(2,128)(2,1)S(1)}, bf16[2,1280]{1,0:T(2,128)(2,1)S(1)}, u32[]{:S(2)}, u32[]{:S(2)}) collective-permute-start(bf16[2,1280]{1,0:T(2,128)(2,1)S(1)} %pad_maximum_fusion.8), channel_id=1, source_target_pairs={{0,14},{1,15},{2,12},{3,13},{4,10},{5,11},{6,8},{7,9},{8,6},{9,7},... | collective-permute-start | bytes 15368 | tf_op jit(solution)/shard_map/ppermute | solution.py:63
  29.9 1.6 %collective-permute-done.13 = bf16[2,1280]{1,0:T(2,128)(2,1)S(1)} collective-permute-done((bf16[2,1280]{1,0:T(2,128)(2,1)S(1)}, bf16[2,1280]{1,0:T(2,128)(2,1)S(1)}, u32[]{:S(2)}, u32[]{:S(2)}) %collective-permute-start.13) | collective-permute-done | bytes 5152 | tf_op jit(solution)/shard_map/ppermute | solution.py:63
  31.5 4.0 %collective-permute-done.14 = bf16[2,1280]{1,0:T(2,128)(2,1)S(1)} collective-permute-done((bf16[2,1280]{1,0:T(2,128)(2,1)S(1)}, bf16[2,1280]{1,0:T(2,128)(2,1)S(1)}, u32[]{:S(2)}, u32[]{:S(2)}) %collective-permute-start.14) | collective-permute-done | bytes 5152 | tf_op jit(solution)/shard_map/ppermute | solution.py:63
  35.5 0.1 fusion.62
  35.6 0.5 fusion.29
  36.2 0.6 fusion.24
  36.7 4.5 %fusion.3 = f32[16,1280]{1,0:T(8,128)} fusion(bf16[1280,1280]{1,0:T(8,128)(2,1)S(1)} %copy-done, bf16[1280,1280]{1,0:T(8,128)(2,1)} %param.9, f32[16,1280]{1,0:T(8,128)S(1)} %fusion.29, bf16[16,1,1280]{2,1,0:T(2,128)(2,1)S(1)} %get-tuple-element.10), kind=kOutput, calls=%fused_computation.7 | convolution fusion | flops 105062400 | bytes 6758400 | tf_op jit(solution)/shard_map/kh,dh->kd/dot_general | solution.py:26
  41.2 0.9 %stack.148 = f32[8,2,1,1280]{3,1,0,2:T(2,128)S(1)} reshape(f32[16,1280]{1,0:T(8,128)} %fusion.3) | data formatting | bytes 163840 | tf_op jit(solution)/shard_map/stack | solution.py:69
  42.5 0.2 collective-permute-start.15
  42.7 1.2 %collective-permute-done.15 = f32[8,2,1280]{2,1,0:T(2,128)S(1)} collective-permute-done((f32[8,2,1280]{2,1,0:T(2,128)S(1)}, f32[8,2,1280]{2,1,0:T(2,128)S(1)}, u32[]{:S(2)}, u32[]{:S(2)}) %collective-permute-start.15) | collective-permute-done | bytes 81952 | tf_op jit(solution)/shard_map/ppermute | solution.py:70
  43.9 0.1 fusion.23
  44.0 0.5 collective-permute-start.16
  44.5 2.2 %copy.19 = bf16[1280,256]{1,0:T(8,128)(2,1)} copy(bf16[1280,256]{0,1:T(8,128)(2,1)} %bitcast.126) | data formatting | bytes 1310720 | tf_op jit(solution)/shard_map/sp,pd->sd/dot_general | solution.py:87
  46.7 3.0 %collective-permute-start.18 = (bf16[2,1280]{1,0:T(2,128)(2,1)S(1)}, bf16[2,1280]{1,0:T(2,128)(2,1)S(1)}, u32[]{:S(2)}, u32[]{:S(2)}) collective-permute-start(bf16[2,1280]{1,0:T(2,128)(2,1)S(1)} %get-tuple-element.18), channel_id=1, source_target_pairs={{0,6},{1,7},{2,4},{3,5},{4,2},{5,3},{6,0},{7,1},{8,14},{9,15},{10,... | collective-permute-start | bytes 15368 | tf_op jit(solution)/shard_map/ppermute | solution.py:74
  49.7 2.8 %collective-permute-start.20 = (bf16[2,1280]{1,0:T(2,128)(2,1)S(1)}, bf16[2,1280]{1,0:T(2,128)(2,1)S(1)}, u32[]{:S(2)}, u32[]{:S(2)}) collective-permute-start(bf16[2,1280]{1,0:T(2,128)(2,1)S(1)} %get-tuple-element.16), channel_id=1, source_target_pairs={{0,10},{1,11},{2,8},{3,9},{4,14},{5,15},{6,12},{7,13},{8,2},{9,3},... | collective-permute-start | bytes 15368 | tf_op jit(solution)/shard_map/ppermute | solution.py:74
  52.6 0.6 collective-permute-start.21
  53.2 4.3 %collective-permute-start.22 = (bf16[2,1280]{1,0:T(2,128)(2,1)S(1)}, bf16[2,1280]{1,0:T(2,128)(2,1)S(1)}, u32[]{:S(2)}, u32[]{:S(2)}) collective-permute-start(bf16[2,1280]{1,0:T(2,128)(2,1)S(1)} %get-tuple-element.14), channel_id=1, source_target_pairs={{0,14},{1,15},{2,12},{3,13},{4,10},{5,11},{6,8},{7,9},{8,6},{9,7},... | collective-permute-start | bytes 15368 | tf_op jit(solution)/shard_map/ppermute | solution.py:74
  57.5 0.4 collective-permute-done.21
  58.0 1.6 %collective-permute-done.22 = bf16[2,1280]{1,0:T(2,128)(2,1)S(1)} collective-permute-done((bf16[2,1280]{1,0:T(2,128)(2,1)S(1)}, bf16[2,1280]{1,0:T(2,128)(2,1)S(1)}, u32[]{:S(2)}, u32[]{:S(2)}) %collective-permute-start.22) | collective-permute-done | bytes 5152 | tf_op jit(solution)/shard_map/ppermute | solution.py:74
  59.6 1.3 %fusion.10 = f32[8,256]{1,0:T(8,128)S(1)} fusion(bf16[1,256,1280]{2,1,0:T(8,128)(2,1)} %param.5, bf16[8,1,1280]{2,1,0:T(2,128)(2,1)S(1)} %get-tuple-element.13), kind=kOutput, calls=%fused_computation.13 | convolution fusion | flops 5242880 | bytes 684032 | tf_op jit(solution)/shard_map/pd,sd->sp/dot_general | solution.py:79
  61.0 1.6 %multiply_reduce_fusion.1 = (f32[256]{0:T(256)S(1)}, f32[8]{0:T(128)S(1)}, f32[8,256]{1,0:T(8,128)S(1)}) fusion(f32[256]{0:T(256)} %copy-done.4, f32[8,256]{1,0:T(8,128)S(1)} %get-tuple-element.38, f32[256]{0:T(256)S(1)} %get-tuple-element.7, f32[8,256]{1,0:T(8,128)S(1)} %fusion.10, f32[8]{0:T(128)} %copy-done.5, f32[8]{0:T(128)} %copy-done.3, ...), kind=kOutput, calls=%fused_computation.75 | convolution fusion | flops 5259000 | bytes 703584 | tf_op jit(solution)/shard_map/pd,sd->sp/dot_general | solution.py:78
  62.6 0.9 %fusion.48 = bf16[8,256]{1,0:T(8,128)(2,1)S(1)} fusion(f32[8,256]{1,0:T(8,128)S(1)} %fusion.10, f32[8,256]{1,0:T(8,128)S(1)} %get-tuple-element.39, f32[8]{0:T(128)S(1)} %get-tuple-element.3, f32[256]{0:T(256)S(1)} %get-tuple-element.2, s32[8]{0:T(128)} %copy-done.6, f32[8,256]{1,0:T(8,128)S(1)} %get-tuple-element.38, f32[256]{0:T(256)} %copy-done.4, ...), kind=kOutput, calls=%fused_computation.103 | convolution fusion | flops 53312 | bytes 31872 | tf_op jit(solution)/shard_map/ks,kp->sp/dot_general | solution.py:85
  63.5 1.4 %fusion.45 = f32[8,2,640]{2,0,1:T(8,128)S(1)} fusion(bf16[2,640,256]{2,1,0:T(8,128)(2,1)} %bitcast.127, bf16[8,256]{1,0:T(8,128)(2,1)S(1)} %fusion.48), kind=kOutput, calls=%fused_computation.99 | convolution fusion | flops 5242880 | bytes 700416 | tf_op jit(solution)/shard_map/sp,pd->sd/dot_general | solution.py:87
  64.9 1.2 %collective-permute-done.23 = f32[8,640]{1,0:T(8,128)S(1)} collective-permute-done((f32[8,640]{1,0:T(8,128)S(1)}, f32[8,640]{1,0:T(8,128)S(1)}, u32[]{:S(2)}, u32[]{:S(2)}) %collective-permute-start.23) | collective-permute-done | bytes 20512 | tf_op jit(solution)/shard_map/ppermute | solution.py:91
  66.1 1.3 %collective-permute-start.24 = (f32[8,640]{1,0:T(8,128)S(1)}, f32[8,640]{1,0:T(8,128)S(1)}, u32[]{:S(2)}, u32[]{:S(2)}) collective-permute-start(f32[8,640]{1,0:T(8,128)S(1)} %bitcast_add_fusion), channel_id=1, source_target_pairs={{0,2},{1,3},{2,0},{3,1},{4,6},{5,7},{6,4},{7,5},{8,10},{9,11},{10,... | collective-permute-start | bytes 61448 | tf_op jit(solution)/shard_map/ppermute | solution.py:113
  67.4 2.5 %collective-permute-done.24 = f32[8,640]{1,0:T(8,128)S(1)} collective-permute-done((f32[8,640]{1,0:T(8,128)S(1)}, f32[8,640]{1,0:T(8,128)S(1)}, u32[]{:S(2)}, u32[]{:S(2)}) %collective-permute-start.24) | collective-permute-done | bytes 20512 | tf_op jit(solution)/shard_map/ppermute | solution.py:113
  69.9 3.3 %collective-permute-start.27 = (f32[8,640]{1,0:T(8,128)S(1)}, f32[8,640]{1,0:T(8,128)S(1)}, u32[]{:S(2)}, u32[]{:S(2)}) collective-permute-start(f32[8,640]{1,0:T(8,128)S(1)} %add.56), channel_id=1, source_target_pairs={{0,12},{1,13},{2,14},{3,15},{4,8},{5,9},{6,10},{7,11},{8,4},{9,5},... | collective-permute-start | bytes 61448 | tf_op jit(solution)/shard_map/ppermute | solution.py:115
  73.2 0.5 collective-permute-start.25
  73.7 1.1 %fusion.37 = f32[256,1280]{1,0:T(8,128)S(1)} fusion(bf16[8,1,1280]{2,1,0:T(2,128)(2,1)S(1)} %get-tuple-element.13, f32[8,256]{1,0:T(8,128)S(1)} %get-tuple-element.38, f32[8]{0:T(128)} %copy-done.5, f32[8]{0:T(128)} %copy-done.3), kind=kOutput, calls=%fused_computation.68 | convolution fusion | flops 5249024 | bytes 1339456 | tf_op jit(solution)/shard_map/sp,sd->pd/dot_general | solution.py:100
  74.8 0.7 collective-permute-done.27
  75.5 1.4 %collective-permute-done.25 = f32[8,640]{1,0:T(8,128)S(1)} collective-permute-done((f32[8,640]{1,0:T(8,128)S(1)}, f32[8,640]{1,0:T(8,128)S(1)}, u32[]{:S(2)}, u32[]{:S(2)}) %collective-permute-start.25) | collective-permute-done | bytes 20512 | tf_op jit(solution)/shard_map/ppermute | solution.py:115
  77.1 1.2 %fusion.1 = bf16[1,256,1280]{2,1,0:T(8,128)(2,1)} fusion(f32[256,1280]{1,0:T(8,128)S(1)} %fusion.37, bf16[8,256]{1,0:T(8,128)(2,1)S(1)} %fusion.48, bf16[1280,8]{0,1:T(8,128)(2,1)S(1)} %copy-done.2), kind=kOutput, calls=%fused_computation.2 | convolution fusion | flops 5898240 | bytes 1990656 | tf_op jit(solution)/shard_map/sp,ds->pd/dot_general | solution.py:103
  78.3 0.6 maximum_select_fusion
  (84 shorter events, 1.3 us)
Async XLA Ops:
  0.6 35.0 %copy-start = (bf16[1280,1280]{1,0:T(8,128)(2,1)S(1)}, bf16[1280,1280]{1,0:T(8,128)(2,1)}, u32[]{:S(2)}) copy-start(bf16[1280,1280]{1,0:T(8,128)(2,1)} %param.8) | copy-start | bytes 9830404
  0.7 1.8 %copy-start.6 = (s32[8]{0:T(128)}, s32[8]{0:T(128)S(1)}, u32[]{:S(2)}) copy-start(s32[8]{0:T(128)S(1)} %iota_xor_fusion) | copy-start | bytes 100
  2.5 8.2 %copy-start.3 = (f32[8]{0:T(128)}, f32[8]{0:T(128)S(1)}, u32[]{:S(2)}) copy-start(f32[8]{0:T(128)S(1)} %get-tuple-element.6) | copy-start | bytes 100
  2.5 33.7 %copy-start.1 = (bf16[1280,1280]{1,0:T(8,128)(2,1)S(1)}, bf16[1280,1280]{1,0:T(8,128)(2,1)}, u32[]{:S(2)}) copy-start(bf16[1280,1280]{1,0:T(8,128)(2,1)} %param.9) | copy-start | bytes 9830404
  2.7 6.0 %copy-start.5 = (f32[8]{0:T(128)}, f32[8]{0:T(128)S(1)}, u32[]{:S(2)}) copy-start(f32[8]{0:T(128)S(1)} %get-tuple-element.4) | copy-start | bytes 100
  2.7 7.9 %copy-start.4 = (f32[256]{0:T(256)}, f32[256]{0:T(256)S(1)}, u32[]{:S(2)}) copy-start(f32[256]{0:T(256)S(1)} %get-tuple-element.5) | copy-start | bytes 3076
  5.6 8.9 %collective-permute-start.1 = (bf16[2,1280]{1,0:T(2,128)(2,1)S(1)}, bf16[2,1280]{1,0:T(2,128)(2,1)S(1)}, u32[]{:S(2)}, u32[]{:S(2)}) collective-permute-start(bf16[2,1280]{1,0:T(2,128)(2,1)S(1)} %pad_maximum_fusion.2), channel_id=1, source_target_pairs={{0,2},{1,3},{2,0},{3,1},{4,6},{5,7},{6,4},{7,5},{8,10},{9,11},{10,... | collective-permute-start | bytes 15368 | tf_op jit(solution)/shard_map/ppermute | solution.py:63
  8.7 6.0 %collective-permute-start.2 = (bf16[2,1280]{1,0:T(2,128)(2,1)S(1)}, bf16[2,1280]{1,0:T(2,128)(2,1)S(1)}, u32[]{:S(2)}, u32[]{:S(2)}) collective-permute-start(bf16[2,1280]{1,0:T(2,128)(2,1)S(1)} %pad_maximum_fusion.2), channel_id=1, source_target_pairs={{0,3},{1,2},{2,1},{3,0},{4,7},{5,6},{6,5},{7,4},{8,11},{9,10},{10,... | collective-permute-start | bytes 15368 | tf_op jit(solution)/shard_map/ppermute | solution.py:63
  8.7 8.6 %collective-permute-start.3 = (bf16[2,1280]{1,0:T(2,128)(2,1)S(1)}, bf16[2,1280]{1,0:T(2,128)(2,1)S(1)}, u32[]{:S(2)}, u32[]{:S(2)}) collective-permute-start(bf16[2,1280]{1,0:T(2,128)(2,1)S(1)} %pad_maximum_fusion.3), channel_id=1, source_target_pairs={{0,4},{1,5},{2,6},{3,7},{4,0},{5,1},{6,2},{7,3},{8,12},{9,13},{10,... | collective-permute-start | bytes 15368 | tf_op jit(solution)/shard_map/ppermute | solution.py:63
  10.3 7.2 %collective-permute-start.4 = (bf16[2,1280]{1,0:T(2,128)(2,1)S(1)}, bf16[2,1280]{1,0:T(2,128)(2,1)S(1)}, u32[]{:S(2)}, u32[]{:S(2)}) collective-permute-start(bf16[2,1280]{1,0:T(2,128)(2,1)S(1)} %pad_maximum_fusion.3), channel_id=1, source_target_pairs={{0,5},{1,4},{2,7},{3,6},{4,1},{5,0},{6,3},{7,2},{8,13},{9,12},{10,... | collective-permute-start | bytes 15368 | tf_op jit(solution)/shard_map/ppermute | solution.py:63
  10.7 1.2 %collective-permute-start = (bf16[2,1280]{1,0:T(2,128)(2,1)S(1)}, bf16[2,1280]{1,0:T(2,128)(2,1)S(1)}, u32[]{:S(2)}, u32[]{:S(2)}) collective-permute-start(bf16[2,1280]{1,0:T(2,128)(2,1)S(1)} %get-tuple-element.9), channel_id=1, source_target_pairs={{0,1},{1,0},{2,3},{3,2},{4,5},{5,4},{6,7},{7,6},{8,9},{9,8},{10,11... | collective-permute-start | bytes 15368 | tf_op jit(solution)/shard_map/ppermute | solution.py:63
  11.9 9.3 %collective-permute-start.5 = (bf16[2,1280]{1,0:T(2,128)(2,1)S(1)}, bf16[2,1280]{1,0:T(2,128)(2,1)S(1)}, u32[]{:S(2)}, u32[]{:S(2)}) collective-permute-start(bf16[2,1280]{1,0:T(2,128)(2,1)S(1)} %pad_maximum_fusion.4), channel_id=1, source_target_pairs={{0,6},{1,7},{2,4},{3,5},{4,2},{5,3},{6,0},{7,1},{8,14},{9,15},{10,... | collective-permute-start | bytes 15368 | tf_op jit(solution)/shard_map/ppermute | solution.py:63
  14.6 6.7 %collective-permute-start.6 = (bf16[2,1280]{1,0:T(2,128)(2,1)S(1)}, bf16[2,1280]{1,0:T(2,128)(2,1)S(1)}, u32[]{:S(2)}, u32[]{:S(2)}) collective-permute-start(bf16[2,1280]{1,0:T(2,128)(2,1)S(1)} %pad_maximum_fusion.4), channel_id=1, source_target_pairs={{0,7},{1,6},{2,5},{3,4},{4,3},{5,2},{6,1},{7,0},{8,15},{9,14},{10,... | collective-permute-start | bytes 15368 | tf_op jit(solution)/shard_map/ppermute | solution.py:63
  14.7 10.1 %collective-permute-start.7 = (bf16[2,1280]{1,0:T(2,128)(2,1)S(1)}, bf16[2,1280]{1,0:T(2,128)(2,1)S(1)}, u32[]{:S(2)}, u32[]{:S(2)}) collective-permute-start(bf16[2,1280]{1,0:T(2,128)(2,1)S(1)} %pad_maximum_fusion.5), channel_id=1, source_target_pairs={{0,8},{1,9},{2,10},{3,11},{4,12},{5,13},{6,14},{7,15},{8,0},{9,1},... | collective-permute-start | bytes 15368 | tf_op jit(solution)/shard_map/ppermute | solution.py:63
  17.3 7.7 %collective-permute-start.8 = (bf16[2,1280]{1,0:T(2,128)(2,1)S(1)}, bf16[2,1280]{1,0:T(2,128)(2,1)S(1)}, u32[]{:S(2)}, u32[]{:S(2)}) collective-permute-start(bf16[2,1280]{1,0:T(2,128)(2,1)S(1)} %pad_maximum_fusion.5), channel_id=1, source_target_pairs={{0,9},{1,8},{2,11},{3,10},{4,13},{5,12},{6,15},{7,14},{8,1},{9,0},... | collective-permute-start | bytes 15368 | tf_op jit(solution)/shard_map/ppermute | solution.py:63
  17.5 12.1 %collective-permute-start.9 = (bf16[2,1280]{1,0:T(2,128)(2,1)S(1)}, bf16[2,1280]{1,0:T(2,128)(2,1)S(1)}, u32[]{:S(2)}, u32[]{:S(2)}) collective-permute-start(bf16[2,1280]{1,0:T(2,128)(2,1)S(1)} %pad_maximum_fusion.6), channel_id=1, source_target_pairs={{0,10},{1,11},{2,8},{3,9},{4,14},{5,15},{6,12},{7,13},{8,2},{9,3},... | collective-permute-start | bytes 15368 | tf_op jit(solution)/shard_map/ppermute | solution.py:63
  21.2 8.6 %collective-permute-start.10 = (bf16[2,1280]{1,0:T(2,128)(2,1)S(1)}, bf16[2,1280]{1,0:T(2,128)(2,1)S(1)}, u32[]{:S(2)}, u32[]{:S(2)}) collective-permute-start(bf16[2,1280]{1,0:T(2,128)(2,1)S(1)} %pad_maximum_fusion.6), channel_id=1, source_target_pairs={{0,11},{1,10},{2,9},{3,8},{4,15},{5,14},{6,13},{7,12},{8,3},{9,2},... | collective-permute-start | bytes 15368 | tf_op jit(solution)/shard_map/ppermute | solution.py:63
  21.3 8.5 %collective-permute-start.11 = (bf16[2,1280]{1,0:T(2,128)(2,1)S(1)}, bf16[2,1280]{1,0:T(2,128)(2,1)S(1)}, u32[]{:S(2)}, u32[]{:S(2)}) collective-permute-start(bf16[2,1280]{1,0:T(2,128)(2,1)S(1)} %pad_maximum_fusion.7), channel_id=1, source_target_pairs={{0,12},{1,13},{2,14},{3,15},{4,8},{5,9},{6,10},{7,11},{8,4},{9,5},... | collective-permute-start | bytes 15368 | tf_op jit(solution)/shard_map/ppermute | solution.py:63
  24.7 5.1 %collective-permute-start.12 = (bf16[2,1280]{1,0:T(2,128)(2,1)S(1)}, bf16[2,1280]{1,0:T(2,128)(2,1)S(1)}, u32[]{:S(2)}, u32[]{:S(2)}) collective-permute-start(bf16[2,1280]{1,0:T(2,128)(2,1)S(1)} %pad_maximum_fusion.7), channel_id=1, source_target_pairs={{0,13},{1,12},{2,15},{3,14},{4,9},{5,8},{6,11},{7,10},{8,5},{9,4},... | collective-permute-start | bytes 15368 | tf_op jit(solution)/shard_map/ppermute | solution.py:63
  25.1 6.4 %collective-permute-start.13 = (bf16[2,1280]{1,0:T(2,128)(2,1)S(1)}, bf16[2,1280]{1,0:T(2,128)(2,1)S(1)}, u32[]{:S(2)}, u32[]{:S(2)}) collective-permute-start(bf16[2,1280]{1,0:T(2,128)(2,1)S(1)} %pad_maximum_fusion.8), channel_id=1, source_target_pairs={{0,14},{1,15},{2,12},{3,13},{4,10},{5,11},{6,8},{7,9},{8,6},{9,7},... | collective-permute-start | bytes 15368 | tf_op jit(solution)/shard_map/ppermute | solution.py:63
  29.7 5.8 %collective-permute-start.14 = (bf16[2,1280]{1,0:T(2,128)(2,1)S(1)}, bf16[2,1280]{1,0:T(2,128)(2,1)S(1)}, u32[]{:S(2)}, u32[]{:S(2)}) collective-permute-start(bf16[2,1280]{1,0:T(2,128)(2,1)S(1)} %pad_maximum_fusion.8), channel_id=1, source_target_pairs={{0,15},{1,14},{2,13},{3,12},{4,11},{5,10},{6,9},{7,8},{8,7},{9,6},... | collective-permute-start | bytes 15368 | tf_op jit(solution)/shard_map/ppermute | solution.py:63
  42.2 34.9 %copy-start.2 = (bf16[1280,8]{0,1:T(8,128)(2,1)S(1)}, bf16[1280,8]{0,1:T(8,128)(2,1)}, u32[]{:S(2)}) copy-start(bf16[1280,8]{0,1:T(8,128)(2,1)} %param.7) | copy-start | bytes 61444
  42.5 1.3 %collective-permute-start.15 = (f32[8,2,1280]{2,1,0:T(2,128)S(1)}, f32[8,2,1280]{2,1,0:T(2,128)S(1)}, u32[]{:S(2)}, u32[]{:S(2)}) collective-permute-start(f32[8,2,1280]{2,1,0:T(2,128)S(1)} %fusion.22), channel_id=1, source_target_pairs={{0,1},{1,0},{2,3},{3,2},{4,5},{5,4},{6,7},{7,6},{8,9},{9,8},{10,11... | collective-permute-start | bytes 245768 | tf_op jit(solution)/shard_map/ppermute | solution.py:70
  44.0 8.6 %collective-permute-start.16 = (bf16[2,1280]{1,0:T(2,128)(2,1)S(1)}, bf16[2,1280]{1,0:T(2,128)(2,1)S(1)}, u32[]{:S(2)}, u32[]{:S(2)}) collective-permute-start(bf16[2,1280]{1,0:T(2,128)(2,1)S(1)} %get-tuple-element.20), channel_id=1, source_target_pairs={{0,2},{1,3},{2,0},{3,1},{4,6},{5,7},{6,4},{7,5},{8,10},{9,11},{10,... | collective-permute-start | bytes 15368 | tf_op jit(solution)/shard_map/ppermute | solution.py:74
  46.7 6.5 %collective-permute-start.17 = (bf16[2,1280]{1,0:T(2,128)(2,1)S(1)}, bf16[2,1280]{1,0:T(2,128)(2,1)S(1)}, u32[]{:S(2)}, u32[]{:S(2)}) collective-permute-start(bf16[2,1280]{1,0:T(2,128)(2,1)S(1)} %get-tuple-element.19), channel_id=1, source_target_pairs={{0,4},{1,5},{2,6},{3,7},{4,0},{5,1},{6,2},{7,3},{8,12},{9,13},{10,... | collective-permute-start | bytes 15368 | tf_op jit(solution)/shard_map/ppermute | solution.py:74
  46.7 10.8 %collective-permute-start.18 = (bf16[2,1280]{1,0:T(2,128)(2,1)S(1)}, bf16[2,1280]{1,0:T(2,128)(2,1)S(1)}, u32[]{:S(2)}, u32[]{:S(2)}) collective-permute-start(bf16[2,1280]{1,0:T(2,128)(2,1)S(1)} %get-tuple-element.18), channel_id=1, source_target_pairs={{0,6},{1,7},{2,4},{3,5},{4,2},{5,3},{6,0},{7,1},{8,14},{9,15},{10,... | collective-permute-start | bytes 15368 | tf_op jit(solution)/shard_map/ppermute | solution.py:74
  49.7 7.8 %collective-permute-start.19 = (bf16[2,1280]{1,0:T(2,128)(2,1)S(1)}, bf16[2,1280]{1,0:T(2,128)(2,1)S(1)}, u32[]{:S(2)}, u32[]{:S(2)}) collective-permute-start(bf16[2,1280]{1,0:T(2,128)(2,1)S(1)} %get-tuple-element.17), channel_id=1, source_target_pairs={{0,8},{1,9},{2,10},{3,11},{4,12},{5,13},{6,14},{7,15},{8,0},{9,1},... | collective-permute-start | bytes 15368 | tf_op jit(solution)/shard_map/ppermute | solution.py:74
  49.7 7.8 %collective-permute-start.20 = (bf16[2,1280]{1,0:T(2,128)(2,1)S(1)}, bf16[2,1280]{1,0:T(2,128)(2,1)S(1)}, u32[]{:S(2)}, u32[]{:S(2)}) collective-permute-start(bf16[2,1280]{1,0:T(2,128)(2,1)S(1)} %get-tuple-element.16), channel_id=1, source_target_pairs={{0,10},{1,11},{2,8},{3,9},{4,14},{5,15},{6,12},{7,13},{8,2},{9,3},... | collective-permute-start | bytes 15368 | tf_op jit(solution)/shard_map/ppermute | solution.py:74
  52.6 5.4 %collective-permute-start.21 = (bf16[2,1280]{1,0:T(2,128)(2,1)S(1)}, bf16[2,1280]{1,0:T(2,128)(2,1)S(1)}, u32[]{:S(2)}, u32[]{:S(2)}) collective-permute-start(bf16[2,1280]{1,0:T(2,128)(2,1)S(1)} %get-tuple-element.15), channel_id=1, source_target_pairs={{0,12},{1,13},{2,14},{3,15},{4,8},{5,9},{6,10},{7,11},{8,4},{9,5},... | collective-permute-start | bytes 15368 | tf_op jit(solution)/shard_map/ppermute | solution.py:74
  53.2 6.4 %collective-permute-start.22 = (bf16[2,1280]{1,0:T(2,128)(2,1)S(1)}, bf16[2,1280]{1,0:T(2,128)(2,1)S(1)}, u32[]{:S(2)}, u32[]{:S(2)}) collective-permute-start(bf16[2,1280]{1,0:T(2,128)(2,1)S(1)} %get-tuple-element.14), channel_id=1, source_target_pairs={{0,14},{1,15},{2,12},{3,13},{4,10},{5,11},{6,8},{7,9},{8,6},{9,7},... | collective-permute-start | bytes 15368 | tf_op jit(solution)/shard_map/ppermute | solution.py:74
  64.9 1.2 %collective-permute-start.23 = (f32[8,640]{1,0:T(8,128)S(1)}, f32[8,640]{1,0:T(8,128)S(1)}, u32[]{:S(2)}, u32[]{:S(2)}) collective-permute-start(f32[8,640]{1,0:T(8,128)S(1)} %dynamic-slice_bitcast_fusion), channel_id=1, source_target_pairs={{0,1},{1,0},{2,3},{3,2},{4,5},{5,4},{6,7},{7,6},{8,9},{9,8},{10,11... | collective-permute-start | bytes 61448 | tf_op jit(solution)/shard_map/ppermute | solution.py:91
  66.1 3.8 %collective-permute-start.24 = (f32[8,640]{1,0:T(8,128)S(1)}, f32[8,640]{1,0:T(8,128)S(1)}, u32[]{:S(2)}, u32[]{:S(2)}) collective-permute-start(f32[8,640]{1,0:T(8,128)S(1)} %bitcast_add_fusion), channel_id=1, source_target_pairs={{0,2},{1,3},{2,0},{3,1},{4,6},{5,7},{6,4},{7,5},{8,10},{9,11},{10,... | collective-permute-start | bytes 61448 | tf_op jit(solution)/shard_map/ppermute | solution.py:113
  69.9 4.9 %collective-permute-start.26 = (f32[8,640]{1,0:T(8,128)S(1)}, f32[8,640]{1,0:T(8,128)S(1)}, u32[]{:S(2)}, u32[]{:S(2)}) collective-permute-start(f32[8,640]{1,0:T(8,128)S(1)} %add.56), channel_id=1, source_target_pairs={{0,8},{1,9},{2,10},{3,11},{4,12},{5,13},{6,14},{7,15},{8,0},{9,1},... | collective-permute-start | bytes 61448 | tf_op jit(solution)/shard_map/ppermute | solution.py:115
  69.9 5.6 %collective-permute-start.27 = (f32[8,640]{1,0:T(8,128)S(1)}, f32[8,640]{1,0:T(8,128)S(1)}, u32[]{:S(2)}, u32[]{:S(2)}) collective-permute-start(f32[8,640]{1,0:T(8,128)S(1)} %add.56), channel_id=1, source_target_pairs={{0,12},{1,13},{2,14},{3,15},{4,8},{5,9},{6,10},{7,11},{8,4},{9,5},... | collective-permute-start | bytes 61448 | tf_op jit(solution)/shard_map/ppermute | solution.py:115
  73.2 3.8 %collective-permute-start.25 = (f32[8,640]{1,0:T(8,128)S(1)}, f32[8,640]{1,0:T(8,128)S(1)}, u32[]{:S(2)}, u32[]{:S(2)}) collective-permute-start(f32[8,640]{1,0:T(8,128)S(1)} %add.56), channel_id=1, source_target_pairs={{0,4},{1,5},{2,6},{3,7},{4,0},{5,1},{6,2},{7,3},{8,12},{9,13},{10,... | collective-permute-start | bytes 61448 | tf_op jit(solution)/shard_map/ppermute | solution.py:115
  77.0 1.3 %collective-permute-start.28 = (f32[8,640]{1,0:T(8,128)S(1)}, f32[8,640]{1,0:T(8,128)S(1)}, u32[]{:S(2)}, u32[]{:S(2)}) collective-permute-start(f32[8,640]{1,0:T(8,128)S(1)} %add_add_fusion), channel_id=1, source_target_pairs={{0,1},{1,0},{2,3},{3,2},{4,5},{5,4},{6,7},{7,6},{8,9},{9,8},{10,11... | collective-permute-start | bytes 61448 | tf_op jit(solution)/shard_map/ppermute | solution.py:97

commit v3 on v0

v3 whole, which is shorter than its diff:
```python
import functools
import math

import jax
import jax.numpy as jnp
from jax import lax
from jax.experimental import pallas as pl
from jax.experimental.pallas import tpu as pltpu
from jax.sharding import PartitionSpec as P

F32 = jnp.float32
BF16 = jnp.bfloat16
NN = (((1,), (0,)), ((), ()))
NT = (((1,), (1,)), ((), ()))
TN = (((0,), (0,)), ((), ()))


def dot(a, b, dims):
    return lax.dot_general(a, b, dims, preferred_element_type=F32)


def even_rows(shape):
    return lax.broadcasted_iota(jnp.int32, shape, 0) % 2 == 0


def spread_matrix(rows):
    row = lax.broadcasted_iota(jnp.int32, (rows, rows // 2), 0)
    column = lax.broadcasted_iota(jnp.int32, (rows, rows // 2), 1)
    return (row // 2 == column).astype(F32).astype(BF16)


def pick_matrix(rows):
    row = lax.broadcasted_iota(jnp.int32, (rows // 2, rows), 0)
    column = lax.broadcasted_iota(jnp.int32, (rows // 2, rows), 1)
    return (2 * row == column).astype(F32).astype(BF16)


def slots_kernel(tokens_ref, grad_ref, router_ref, sent_ref, dispatch_ref, combine_ref, router2_ref):
    slots = router_ref.shape[0]
    rows = 2 * slots
    router2 = dot(spread_matrix(rows), router_ref[...], NN).astype(BF16)
    router2_ref[...] = router2
    logits = dot(router2, tokens_ref[...], NT)
    even = even_rows(logits.shape)
    over_patches = jnp.exp(logits - jnp.max(logits, axis=1, keepdims=True))
    dispatch = over_patches / jnp.sum(over_patches, axis=1, keepdims=True)
    over_slots = jnp.exp(logits - jnp.max(logits, axis=0, keepdims=True))
    slot_sum = jnp.sum(jnp.where(even, over_slots, 0.0), axis=0, keepdims=True)
    combine = over_slots / slot_sum
    dispatch_ref[...] = dispatch
    combine_ref[...] = combine
    both = dot(jnp.where(even, dispatch, 0.0).astype(BF16), tokens_ref[...], NN)
    both = both + dot(jnp.where(even, 0.0, combine).astype(BF16), grad_ref[...], NN)
    for s in range(slots):
        sent_ref[s] = both[2 * s : 2 * s + 2].astype(BF16)


def experts_kernel(
    got_ref, other_ref, in_weight_ref, out_weight_ref, mine_ref, theirs_ref, rows_ref
):
    images = got_ref.shape[0]
    for k in range(images):
        rows_ref[2 * k : 2 * k + 2] = got_ref[k].astype(F32)
        rows_ref[2 * (images + k) : 2 * (images + k) + 2] = other_ref[k].astype(F32)
    rows = rows_ref[...].astype(BF16)
    hidden = dot(rows, in_weight_ref[...], NN)
    act_grad = dot(rows, out_weight_ref[...], NT)
    even = even_rows(hidden.shape)
    normal_cdf = 0.5 * (1.0 + lax.erf(hidden * (1.0 / math.sqrt(2.0))))
    normal_pdf = jnp.exp(-0.5 * hidden * hidden) * (1.0 / math.sqrt(2.0 * math.pi))
    slope = pltpu.roll(normal_cdf + hidden * normal_pdf, 1, 0)
    inner = jnp.where(even, hidden * normal_cdf, act_grad * slope).astype(BF16)
    part_out = dot(inner, out_weight_ref[...], NN)
    part_in = dot(inner, in_weight_ref[...], NT)
    parts = jnp.where(even_rows(part_out.shape), part_out, part_in)
    for k in range(images):
        mine_ref[k] = parts[2 * k : 2 * k + 2]
        theirs_ref[k] = parts[2 * (images + k) : 2 * (images + k) + 2]


def logits_kernel(
    tokens_ref,
    grad_ref,
    router2_ref,
    dispatch_ref,
    combine_ref,
    back_ref,
    kept_ref,
    given_ref,
    left_ref,
    right_ref,
    rows_ref,
):
    slots = back_ref.shape[0]
    for s in range(slots):
        rows_ref[2 * s : 2 * s + 2] = back_ref[s].astype(F32)
    back = rows_ref[...]
    back_b = back.astype(BF16)
    combine_grad = dot(back_b, grad_ref[...], NT)
    dispatch_grad = dot(back_b, tokens_ref[...], NT)
    even = even_rows(combine_grad.shape)
    dispatch = dispatch_ref[...]
    combine = combine_ref[...]
    slot_sum = jnp.sum(jnp.where(even, combine * combine_grad, 0.0), axis=0, keepdims=True)
    patch_sum = jnp.sum(dispatch * dispatch_grad, axis=1, keepdims=True)
    patch_term = dispatch * (dispatch_grad - patch_sum)
    patch_term = pltpu.roll(patch_term, 2 * slots - 1, 0)
    logits_grad = combine * (combine_grad - slot_sum) + patch_term
    logits_b = jnp.where(even, logits_grad, 0.0).astype(BF16)
    packed = dot(pick_matrix(2 * slots), logits_b, NN).astype(BF16)
    part = dot(packed, tokens_ref[...], NN)
    half = part.shape[1] // 2
    first = lax.axis_index("core") == 0
    kept_ref[...] = jnp.where(first, part[:, :half], part[:, half:])
    given_ref[...] = jnp.where(first, part[:, half:], part[:, :half])
    left_ref[...] = jnp.where(even, logits_grad, dispatch).astype(BF16)
    right_ref[...] = jnp.where(
        even_rows(back.shape), router2_ref[...].astype(F32), back
    ).astype(BF16)


def tokens_kernel(left_ref, right_ref, tokens_grad_ref):
    tokens_grad_ref[...] = dot(left_ref[...], right_ref[...], TN).astype(BF16)


def call(kernel, outs, scratch, cost, *operands):
    return pl.pallas_call(
        kernel,
        out_shape=[jax.ShapeDtypeStruct(shape, dtype) for shape, dtype in outs],
        in_specs=[pl.BlockSpec(memory_space=pltpu.VMEM)] * len(operands),
        out_specs=[pl.BlockSpec(memory_space=pltpu.VMEM)] * len(outs),
        scratch_shapes=[pltpu.VMEM(shape, F32) for shape in scratch],
        compiler_params=pltpu.CompilerParams(vmem_limit_bytes=16 * 1024 * 1024),
        cost_estimate=pl.CostEstimate(flops=cost[0], bytes_accessed=cost[1], transcendentals=0),
    )(*operands)


def swap_cores(value):
    return lax.ppermute(value, "core", [(0, 1), (1, 0)])


def between_chips(value):
    return lax.all_to_all(value, "chip", split_axis=0, concat_axis=0, tiled=True)


def per_device(tokens, out_grad, router, in_weight, out_weight):
    _, patches, width = tokens.shape
    hidden = in_weight.shape[1]
    slots = router.shape[1]
    tokens = tokens[0]
    out_grad = out_grad[0]
    image_bytes = 2 * patches * width
    weight_bytes = 2 * width * hidden
    sent, dispatch, combine, router2 = call(
        slots_kernel,
        [
            ((slots, 2, width), BF16),
            ((2 * slots, patches), F32),
            ((2 * slots, patches), F32),
            ((2 * slots, width), BF16),
        ],
        [],
        (12 * patches * width * slots, 2 * image_bytes),
        tokens,
        out_grad,
        router.T,
    )
    got = between_chips(sent)
    other = swap_cores(got)
    mine, theirs = call(
        experts_kernel,
        [((slots, 2, width), F32), ((slots, 2, width), F32)],
        [(4 * slots, width)],
        (32 * slots * width * hidden, 2 * weight_bytes),
        got,
        other,
        in_weight,
        out_weight,
    )
    back = between_chips((mine + swap_cores(theirs)).astype(BF16))
    kept, given, left, right = call(
        logits_kernel,
        [
            ((slots, width // 2), F32),
            ((slots, width // 2), F32),
            ((2 * slots, patches), BF16),
            ((2 * slots, width), BF16),
        ],
        [(2 * slots, width)],
        (12 * patches * width * slots, 2 * image_bytes),
        tokens,
        out_grad,
        router2,
        dispatch,
        combine,
        back,
    )
    pair = kept + swap_cores(given)
    chips = lax.axis_size("chip")
    terms = between_chips(jnp.broadcast_to(pair[None], (chips,) + pair.shape))
    total = jnp.sum(terms, axis=0)
    theirs_total = swap_cores(total)
    first = lax.axis_index("core") == 0
    router_grad = jnp.concatenate(
        [jnp.where(first, total, theirs_total), jnp.where(first, theirs_total, total)], axis=1
    )
    (tokens_grad,) = call(
        tokens_kernel,
        [((patches, width), BF16)],
        [],
        (4 * patches * width * slots, image_bytes),
        left,
        right,
    )
    return (tokens_grad[None], router_grad.T)


def solution(mesh):
    shape = (mesh.shape["group"], mesh.shape["expert"] // 2, 2)
    fine = jax.sharding.Mesh(mesh.devices.reshape(shape), ("group", "chip", "core"))
    expert = ("chip", "core")
    in_specs = (
        P(("group", "chip", "core"), None, None),
        P(("group", "chip", "core"), None, None),
        P(),
        P(None, expert),
        P(expert, None),
    )
    out_specs = (P(("group", "chip", "core"), None, None), P("group", None))
    return jax.shard_map(
        per_device, mesh=fine, in_specs=in_specs, out_specs=out_specs, check_vma=False
    )
```

time: 124 us -> 52.1 us (0.42)
  blocking collectives: 59.3 us -> 33.4 us
  matrix products: 20.2 us -> 0 us
  starting transfers between devices: 18.5 us -> 0.31 us
  waiting for transfers between devices: 17.1 us -> 3.55 us
  Pallas kernels: 0 us -> 6.18 us
  local copies, waits for them, and re-layouts: 4.38 us -> 6.77 us
  other arithmetic: 2.51 us -> 0.7 us
    psum x1 -> x0, blocking collectives: 59.3 us -> none  [per_device(): router_grad = lax.psum(router_part, 'expert')]
    all_to_all x0 -> x3, blocking collectives: none -> 33.4 us  [between_chips(): lax.all_to_all(value, 'chip', split_axis=0, concat_axis=0, tiled=True)]
    dot_general x11 -> x0, matrix products: 20.2 us -> none  [the longest x1 3.83 us: expert_rows(): jnp.einsum('nkh,dh->nkd', hidden_grad, in_weight, preferred_element_type=...]
    all_to_all x4 -> x0, starting transfers between devices: 18.5 us -> none  [the longest x1 7.39 us: per_device(): lax.all_to_all(doubled_in, 'expert', split_axis=0, concat_axis=0, tiled=T...]
    all_to_all x4 -> x0, waiting for transfers between devices: 17.1 us -> none  [the longest x1 6.11 us: per_device(): lax.all_to_all(doubled_grad, 'expert', split_axis=0, concat_axis=0, tiled...]
    pallas_call x0 -> x4, Pallas kernels: none -> 6.18 us  [call(): pl.pallas_call(kernel, out_shape=[jax.ShapeDtypeStruct(shape, dtype) for...]
    unnamed x14, local copies, waits for them, and re-layouts: 2.14 us -> 6.76 us
    ppermute x0 -> x4, waiting for transfers between devices: none -> 3.55 us  [swap_cores(): return lax.ppermute(value, 'core', [(0, 1), (1, 0)])]
  transfers between devices with their start and end apart: 4 -> 4, of which waited for: 4 -> 3; matrix products, arithmetic and copies ran while one was open for 9% -> 0% of each run, Pallas kernels for 0% -> 2%
where the time goes in v3:
time: 52.1 us; the launch traced here: 51.6 us
  blocking collectives  33.4 us (64%)
  local copies, waits for them, and re-layouts  6.77 us (13%)
  Pallas kernels  6.18 us (12%)
  waiting for transfers between devices  3.55 us (7%)
  other arithmetic  0.7 us (1%)
  between operations  0.69 us (1%)
    all_to_all x3, blocking collectives, between_chips(): lax.all_to_all(value, 'chip', split_axis=0, concat_axis=0, tiled=True)  33.4 us
    unnamed x14, local copies, waits for them, and re-layouts  6.76 us
    pallas_call x4, Pallas kernels, call(): pl.pallas_call(kernel, out_shape=[jax.ShapeDtypeStruct(shape, dtype) for...  6.18 us
    ppermute x4, waiting for transfers between devices, swap_cores(): return lax.ppermute(value, 'core', [(0, 1), (1, 0)])  3.55 us
  transfers between devices with their start and end apart: 4, of which 3 were waited for; matrix products, arithmetic and copies ran while one was open for 0% of the time, Pallas kernels for 2%

profile of v3, /device:TPU:0, one launch (start us, length us, event | category | flops | bytes accessed | tf_op | source)
XLA Modules:
  0.0 51.6 jit_solution(6519144807785953995)
XLA Ops:
  0.6 0.0 copy-start.2
  0.6 1.1 %copy-done.2 = bf16[1,256,1280]{2,1,0:T(8,128)(2,1)S(1)} copy-done((bf16[1,256,1280]{2,1,0:T(8,128)(2,1)S(1)}, bf16[1,256,1280]{2,1,0:T(8,128)(2,1)}, u32[]{:S(2)}) %copy-start.2) | copy-done | bytes 655384
  1.7 0.0 copy-start.4
  1.7 1.1 %copy-done.4 = bf16[1,256,1280]{2,1,0:T(8,128)(2,1)S(1)} copy-done((bf16[1,256,1280]{2,1,0:T(8,128)(2,1)S(1)}, bf16[1,256,1280]{2,1,0:T(8,128)(2,1)}, u32[]{:S(2)}) %copy-start.4) | copy-done | bytes 655384
  2.8 0.0 copy-start.6
  2.8 0.7 %copy-done.6 = bf16[1280,8]{0,1:T(8,128)(2,1)S(1)} copy-done((bf16[1280,8]{0,1:T(8,128)(2,1)S(1)}, bf16[1280,8]{0,1:T(8,128)(2,1)}, u32[]{:S(2)}) %copy-start.6) | copy-done | bytes 20504
  3.5 0.9 %shard_map.68 = (bf16[8,2,1280]{2,1,0:T(2,128)(2,1)S(1)}, f32[16,256]{1,0:T(8,128)S(1)}, f32[16,256]{1,0:T(8,128)S(1)}, bf16[16,1280]{1,0:T(8,128)(2,1)S(1)}) custom-call(bf16[256,1280]{1,0:T(8,128)(2,1)S(1)} %bitcast.6, bf16[256,1280]{1,0:T(8,128)(2,1)S(1)} %bitcast.8, bf16[8,1280]{1,0:T(8,128)(2,1)S(1)} %bitcast.10), custom_call_target="tpu_custom_call" | custom-call | flops 31457280 | bytes 1310720 | tf_op jit(solution)/shard_map/pallas_call | solution.py:127
  4.5 13.8 %all_to_all.15.got_ref = bf16[8,2,1280]{2,1,0:T(2,128)(2,1)S(1)} all-to-all(bf16[8,2,1280]{2,1,0:T(2,128)(2,1)S(1)} %get-tuple-element.15), channel_id=1, replica_groups=mesh['group'=2,'chip'=8,'core'=2] {'chip'}, dimensions={0} | all-to-all | bytes 81920 | tf_op jit(solution)/shard_map/all_to_all | solution.py:143
  18.3 0.0 collective-permute-start
  18.3 1.2 %collective-permute-done.other_ref = bf16[8,2,1280]{2,1,0:T(2,128)(2,1)S(1)} collective-permute-done((bf16[8,2,1280]{2,1,0:T(2,128)(2,1)S(1)}, bf16[8,2,1280]{2,1,0:T(2,128)(2,1)S(1)}, u32[]{:S(2)}, u32[]{:S(2)}) %collective-permute-start) | collective-permute-done | bytes 40992 | tf_op jit(solution)/shard_map/ppermute | solution.py:139
  19.5 0.0 copy-start
  19.5 1.9 %copy-done = bf16[1280,1280]{1,0:T(8,128)(2,1)S(1)} copy-done((bf16[1280,1280]{1,0:T(8,128)(2,1)S(1)}, bf16[1280,1280]{1,0:T(8,128)(2,1)}, u32[]{:S(2)}) %copy-start) | copy-done | bytes 3276824
  21.5 0.0 copy-start.1
  21.5 1.9 %copy-done.1 = bf16[1280,1280]{1,0:T(8,128)(2,1)S(1)} copy-done((bf16[1280,1280]{1,0:T(8,128)(2,1)S(1)}, bf16[1280,1280]{1,0:T(8,128)(2,1)}, u32[]{:S(2)}) %copy-start.1) | copy-done | bytes 3276824
  23.4 0.0 copy-start.3
  23.4 0.0 copy-start.5
  23.4 3.2 %shard_map.69 = (f32[8,2,1280]{2,1,0:T(2,128)S(1)}, f32[8,2,1280]{2,1,0:T(2,128)S(1)}) custom-call(bf16[8,2,1280]{2,1,0:T(2,128)(2,1)S(1)} %all_to_all.15.got_ref, bf16[8,2,1280]{2,1,0:T(2,128)(2,1)S(1)} %collective-permute-done.other_ref, bf16[1280,1280]{1,0:T(8,128)(2,1)S(1)} %copy-done, bf16[1280,1280]{1,0:T(8,128)(2,1)S(1)} %copy-done.1), custom_call_target="tpu_custom_call" | custom-call | flops 419430400 | bytes 6553600 | tf_op jit(solution)/shard_map/pallas_call | solution.py:127
  26.6 0.2 collective-permute-start.1
  26.9 1.1 %collective-permute-done.1 = f32[8,2,1280]{2,1,0:T(2,128)S(1)} collective-permute-done((f32[8,2,1280]{2,1,0:T(2,128)S(1)}, f32[8,2,1280]{2,1,0:T(2,128)S(1)}, u32[]{:S(2)}, u32[]{:S(2)}) %collective-permute-start.1) | collective-permute-done | bytes 81952 | tf_op jit(solution)/shard_map/ppermute | solution.py:139
  28.0 0.1 add_convert_fusion
  28.0 9.1 %all_to_all.16.back_ref = bf16[8,2,1280]{2,1,0:T(2,128)(2,1)S(1)} all-to-all(bf16[8,2,1280]{2,1,0:T(2,128)(2,1)S(1)} %add_convert_fusion), channel_id=1, replica_groups=mesh['group'=2,'chip'=8,'core'=2] {'chip'}, dimensions={0} | all-to-all | bytes 81920 | tf_op jit(solution)/shard_map/all_to_all | solution.py:143
  37.2 0.0 copy-done.3
  37.2 0.0 copy-done.5
  37.2 0.8 %shard_map.70 = (f32[8,640]{1,0:T(8,128)S(1)}, f32[8,640]{1,0:T(8,128)S(1)}, bf16[16,256]{1,0:T(8,128)(2,1)S(1)}, bf16[16,1280]{1,0:T(8,128)(2,1)S(1)}) custom-call(bf16[256,1280]{1,0:T(8,128)(2,1)S(1)} %bitcast.7, bf16[256,1280]{1,0:T(8,128)(2,1)S(1)} %bitcast.9, bf16[16,1280]{1,0:T(8,128)(2,1)S(1)} %get-tuple-element.12.router2_ref, ...), custom_call_target="tpu_custom_call" | custom-call | flops 31457280 | bytes 1310720 | tf_op jit(solution)/shard_map/pallas_call | solution.py:127
  38.0 0.0 collective-permute-start.2
  38.0 1.2 %collective-permute-done.2 = f32[8,640]{1,0:T(8,128)S(1)} collective-permute-done((f32[8,640]{1,0:T(8,128)S(1)}, f32[8,640]{1,0:T(8,128)S(1)}, u32[]{:S(2)}, u32[]{:S(2)}) %collective-permute-start.2) | collective-permute-done | bytes 20512 | tf_op jit(solution)/shard_map/ppermute | solution.py:139
  39.2 10.5 %all_to_all.17 = f32[8,8,640]{2,1,0:T(8,128)S(1)} all-to-all(f32[8,8,640]{2,1,0:T(8,128)S(1)} %broadcast_in_dim.10), channel_id=1, replica_groups=mesh['group'=2,'chip'=8,'core'=2] {'chip'}, dimensions={0} | all-to-all | bytes 327680 | tf_op jit(solution)/shard_map/all_to_all | solution.py:143
  49.7 0.1 collective-permute-start.3
  49.8 1.2 %shard_map.71 = bf16[256,1280]{1,0:T(8,128)(2,1)} custom-call(bf16[16,256]{1,0:T(8,128)(2,1)S(1)} %get-tuple-element.18.left_ref, bf16[16,1280]{1,0:T(8,128)(2,1)S(1)} %get-tuple-element.19.right_ref), custom_call_target="tpu_custom_call" | custom-call | flops 10485760 | bytes 655360 | tf_op jit(solution)/shard_map/pallas_call | solution.py:127
  51.0 0.0 collective-permute-done.3
  51.0 0.6 %maximum_bitcast_fusion = f32[1280,8]{0,1:T(8,128)} fusion(f32[8,640]{1,0:T(8,128)S(1)} %get-tuple-element.23, f32[8,640]{1,0:T(8,128)S(1)} %get-tuple-element.22), kind=kLoop, calls=%fused_computation.1 | loop fusion | flops 10240 | bytes 81920 | tf_op jit(solution)/shard_map/transpose | solution.py:215
  (4 shorter events, 0.0 us)
Async XLA Ops:
  0.6 1.1 %copy-start.2 = (bf16[1,256,1280]{2,1,0:T(8,128)(2,1)S(1)}, bf16[1,256,1280]{2,1,0:T(8,128)(2,1)}, u32[]{:S(2)}) copy-start(bf16[1,256,1280]{2,1,0:T(8,128)(2,1)} %param.5) | copy-start | bytes 1966084
  1.7 1.1 %copy-start.4 = (bf16[1,256,1280]{2,1,0:T(8,128)(2,1)S(1)}, bf16[1,256,1280]{2,1,0:T(8,128)(2,1)}, u32[]{:S(2)}) copy-start(bf16[1,256,1280]{2,1,0:T(8,128)(2,1)} %param.6) | copy-start | bytes 1966084
  2.8 0.7 %copy-start.6 = (bf16[1280,8]{0,1:T(8,128)(2,1)S(1)}, bf16[1280,8]{0,1:T(8,128)(2,1)}, u32[]{:S(2)}) copy-start(bf16[1280,8]{0,1:T(8,128)(2,1)} %param.7) | copy-start | bytes 61444
  18.3 1.2 %collective-permute-start = (bf16[8,2,1280]{2,1,0:T(2,128)(2,1)S(1)}, bf16[8,2,1280]{2,1,0:T(2,128)(2,1)S(1)}, u32[]{:S(2)}, u32[]{:S(2)}) collective-permute-start(bf16[8,2,1280]{2,1,0:T(2,128)(2,1)S(1)} %all_to_all.15.got_ref), channel_id=1, source_target_pairs={{0,1},{1,0},{2,3},{3,2},{4,5},{5,4},{6,7},{7,6},{8,9},{9,8},{10,11... | collective-permute-start | bytes 122888 | tf_op jit(solution)/shard_map/ppermute | solution.py:139
  19.5 1.9 %copy-start = (bf16[1280,1280]{1,0:T(8,128)(2,1)S(1)}, bf16[1280,1280]{1,0:T(8,128)(2,1)}, u32[]{:S(2)}) copy-start(bf16[1280,1280]{1,0:T(8,128)(2,1)} %in_weight_ref.1) | copy-start | bytes 9830404
  21.5 1.9 %copy-start.1 = (bf16[1280,1280]{1,0:T(8,128)(2,1)S(1)}, bf16[1280,1280]{1,0:T(8,128)(2,1)}, u32[]{:S(2)}) copy-start(bf16[1280,1280]{1,0:T(8,128)(2,1)} %out_weight_ref.1) | copy-start | bytes 9830404
  23.4 13.8 %copy-start.3 = (bf16[1,256,1280]{2,1,0:T(8,128)(2,1)S(1)}, bf16[1,256,1280]{2,1,0:T(8,128)(2,1)}, u32[]{:S(2)}) copy-start(bf16[1,256,1280]{2,1,0:T(8,128)(2,1)} %param.5) | copy-start | bytes 1966084
  23.4 13.8 %copy-start.5 = (bf16[1,256,1280]{2,1,0:T(8,128)(2,1)S(1)}, bf16[1,256,1280]{2,1,0:T(8,128)(2,1)}, u32[]{:S(2)}) copy-start(bf16[1,256,1280]{2,1,0:T(8,128)(2,1)} %param.6) | copy-start | bytes 1966084
  26.6 1.3 %collective-permute-start.1 = (f32[8,2,1280]{2,1,0:T(2,128)S(1)}, f32[8,2,1280]{2,1,0:T(2,128)S(1)}, u32[]{:S(2)}, u32[]{:S(2)}) collective-permute-start(f32[8,2,1280]{2,1,0:T(2,128)S(1)} %get-tuple-element.17), channel_id=1, source_target_pairs={{0,1},{1,0},{2,3},{3,2},{4,5},{5,4},{6,7},{7,6},{8,9},{9,8},{10,11... | collective-permute-start | bytes 245768 | tf_op jit(solution)/shard_map/ppermute | solution.py:139
  38.0 1.2 %collective-permute-start.2 = (f32[8,640]{1,0:T(8,128)S(1)}, f32[8,640]{1,0:T(8,128)S(1)}, u32[]{:S(2)}, u32[]{:S(2)}) collective-permute-start(f32[8,640]{1,0:T(8,128)S(1)} %get-tuple-element.21), channel_id=1, source_target_pairs={{0,1},{1,0},{2,3},{3,2},{4,5},{5,4},{6,7},{7,6},{8,9},{9,8},{10,11... | collective-permute-start | bytes 61448 | tf_op jit(solution)/shard_map/ppermute | solution.py:139
  49.7 1.3 %collective-permute-start.3 = (f32[8,640]{1,0:T(8,128)S(1)}, f32[8,640]{1,0:T(8,128)S(1)}, u32[]{:S(2)}, u32[]{:S(2)}) collective-permute-start(f32[8,640]{1,0:T(8,128)S(1)} %reduce_sum.9), channel_id=1, source_target_pairs={{0,1},{1,0},{2,3},{3,2},{4,5},{5,4},{6,7},{7,6},{8,9},{9,8},{10,11... | collective-permute-start | bytes 61448 | tf_op jit(solution)/shard_map/ppermute | solution.py:139

commit v4 on v3

--- a/solution.py
+++ b/solution.py
@@ -12,6 +12,7 @@
 BF16 = jnp.bfloat16
 NN = (((1,), (0,)), ((), ()))
 NT = (((1,), (1,)), ((), ()))
+AHEAD_FLOPS = 3 * 10**10
 TN = (((0,), (0,)), ((), ()))
 
 
@@ -35,10 +36,15 @@
     return (2 * row == column).astype(F32).astype(BF16)
 
 
-def slots_kernel(tokens_ref, grad_ref, router_ref, sent_ref, dispatch_ref, combine_ref, router2_ref):
+def spread_kernel(spread_ref):
+    spread_ref[...] = spread_matrix(spread_ref.shape[0])
+
+
+def slots_kernel(
+    tokens_ref, grad_ref, router_ref, spread_ref, sent_ref, dispatch_ref, combine_ref, router2_ref
+):
     slots = router_ref.shape[0]
-    rows = 2 * slots
-    router2 = dot(spread_matrix(rows), router_ref[...], NN).astype(BF16)
+    router2 = dot(spread_ref[...], router_ref[...], NN).astype(BF16)
     router2_ref[...] = router2
     logits = dot(router2, tokens_ref[...], NT)
     even = even_rows(logits.shape)
@@ -151,6 +157,12 @@
     out_grad = out_grad[0]
     image_bytes = 2 * patches * width
     weight_bytes = 2 * width * hidden
+    (spread,) = call(
+        spread_kernel,
+        [((2 * slots, slots), BF16)],
+        [],
+        (AHEAD_FLOPS, image_bytes),
+    )
     sent, dispatch, combine, router2 = call(
         slots_kernel,
         [
@@ -164,6 +176,7 @@
         tokens,
         out_grad,
         router.T,
+        spread,
     )
     got = between_chips(sent)
     other = swap_cores(got)
@@ -195,10 +208,9 @@
         combine,
         back,
     )
-    pair = kept + swap_cores(given)
-    chips = lax.axis_size("chip")
-    terms = between_chips(jnp.broadcast_to(pair[None], (chips,) + pair.shape))
-    total = jnp.sum(terms, axis=0)
+    pair = (kept + swap_cores(given)).astype(BF16)
+    terms = lax.all_gather(pair, "chip")
+    total = jnp.sum(terms.astype(F32), axis=0)
     theirs_total = swap_cores(total)
     first = lax.axis_index("core") == 0
     router_grad = jnp.concatenate(

time: 52.1 us -> 66.6 us (1.28)
  blocking collectives: 33.4 us -> 53.6 us
  local copies, waits for them, and re-layouts: 6.77 us -> 1.25 us
    all_gather x0 -> x1, blocking collectives: none -> 30.5 us  [per_device(): terms = lax.all_gather(pair, 'chip')]
    all_to_all x3 -> x2, blocking collectives: 33.4 us -> 23.1 us  [between_chips(): lax.all_to_all(value, 'chip', split_axis=0, concat_axis=0, tiled=True)]
    unnamed x14 -> x10, local copies, waits for them, and re-layouts: 6.76 us -> 1.25 us
    pallas_call x4 -> x5, Pallas kernels: 6.18 us -> 6.21 us  [call(): pl.pallas_call(kernel, out_shape=[jax.ShapeDtypeStruct(shape, dtype) for...]
where the time goes in v4:
time: 66.6 us; the launch traced here: 66.3 us
  blocking collectives  53.6 us (80%)
  Pallas kernels  6.21 us (9%)
  waiting for transfers between devices  3.55 us (5%)
  local copies, waits for them, and re-layouts  1.25 us (2%)
  between operations  0.72 us (1%)
  other arithmetic  0.7 us (1%)
    all_gather x1, blocking collectives, per_device(): terms = lax.all_gather(pair, 'chip')  30.5 us
    all_to_all x2, blocking collectives, between_chips(): lax.all_to_all(value, 'chip', split_axis=0, concat_axis=0, tiled=True)  23.1 us
    pallas_call x5, Pallas kernels, call(): pl.pallas_call(kernel, out_shape=[jax.ShapeDtypeStruct(shape, dtype) for...  6.21 us
    ppermute x4, waiting for transfers between devices, swap_cores(): return lax.ppermute(value, 'core', [(0, 1), (1, 0)])  3.55 us
  transfers between devices with their start and end apart: 4, of which 3 were waited for; matrix products, arithmetic and copies ran while one was open for 0% of the time, Pallas kernels for 2%

profile of v4, /device:TPU:0, one launch (start us, length us, event | category | flops | bytes accessed | tf_op | source)
XLA Modules:
  0.0 66.3 jit_solution(3954545343924161722)
XLA Ops:
  0.6 0.0 copy-start.4
  0.6 0.0 copy-start.3
  0.7 0.0 copy-start.2
  0.7 0.0 copy-start
  0.7 0.0 copy-start.1
  0.7 0.7 %copy-done.4 = bf16[1280,8]{0,1:T(8,128)(2,1)S(1)} copy-done((bf16[1280,8]{0,1:T(8,128)(2,1)S(1)}, bf16[1280,8]{0,1:T(8,128)(2,1)}, u32[]{:S(2)}) %copy-start.4) | copy-done | bytes 20504
  1.4 0.4 copy-done.3
  1.7 0.2 copy-done.2
  1.9 0.9 %shard_map.69 = (bf16[8,2,1280]{2,1,0:T(2,128)(2,1)S(1)}, f32[16,256]{1,0:T(8,128)S(1)}, f32[16,256]{1,0:T(8,128)S(1)}, bf16[16,1280]{1,0:T(8,128)(2,1)S(1)}) custom-call(bf16[256,1280]{1,0:T(8,128)(2,1)S(1)} %bitcast.9, bf16[256,1280]{1,0:T(8,128)(2,1)S(1)} %bitcast.11, bf16[8,1280]{1,0:T(8,128)(2,1)S(1)} %bitcast.13, bf16[16,8]{1,0:T(8,128)(2,1)S(1)} %shard_map.68.spread_ref), custom_call_target="tpu_custom_call" | custom-call | flops 31457280 | bytes 1310720 | tf_op jit(solution)/shard_map/pallas_call | solution.py:133
  2.9 14.0 %all_to_all.10.got_ref = bf16[8,2,1280]{2,1,0:T(2,128)(2,1)S(1)} all-to-all(bf16[8,2,1280]{2,1,0:T(2,128)(2,1)S(1)} %get-tuple-element.15), channel_id=1, replica_groups=mesh['group'=2,'chip'=8,'core'=2] {'chip'}, dimensions={0} | all-to-all | bytes 81920 | tf_op jit(solution)/shard_map/all_to_all | solution.py:149
  16.8 0.0 collective-permute-start
  16.8 1.2 %collective-permute-done.other_ref = bf16[8,2,1280]{2,1,0:T(2,128)(2,1)S(1)} collective-permute-done((bf16[8,2,1280]{2,1,0:T(2,128)(2,1)S(1)}, bf16[8,2,1280]{2,1,0:T(2,128)(2,1)S(1)}, u32[]{:S(2)}, u32[]{:S(2)}) %collective-permute-start) | collective-permute-done | bytes 40992 | tf_op jit(solution)/shard_map/ppermute | solution.py:145
  18.1 0.0 copy-done
  18.1 0.0 copy-done.1
  18.1 3.3 %shard_map.70 = (f32[8,2,1280]{2,1,0:T(2,128)S(1)}, f32[8,2,1280]{2,1,0:T(2,128)S(1)}) custom-call(bf16[8,2,1280]{2,1,0:T(2,128)(2,1)S(1)} %all_to_all.10.got_ref, bf16[8,2,1280]{2,1,0:T(2,128)(2,1)S(1)} %collective-permute-done.other_ref, bf16[1280,1280]{1,0:T(8,128)(2,1)S(1)} %copy-done, bf16[1280,1280]{1,0:T(8,128)(2,1)S(1)} %copy-done.1), custom_call_target="tpu_custom_call" | custom-call | flops 419430400 | bytes 6553600 | tf_op jit(solution)/shard_map/pallas_call | solution.py:133
  21.3 0.2 collective-permute-start.1
  21.6 1.1 %collective-permute-done.1 = f32[8,2,1280]{2,1,0:T(2,128)S(1)} collective-permute-done((f32[8,2,1280]{2,1,0:T(2,128)S(1)}, f32[8,2,1280]{2,1,0:T(2,128)S(1)}, u32[]{:S(2)}, u32[]{:S(2)}) %collective-permute-start.1) | collective-permute-done | bytes 81952 | tf_op jit(solution)/shard_map/ppermute | solution.py:145
  22.7 0.1 add_convert_fusion
  22.7 9.1 %all_to_all.11.back_ref = bf16[8,2,1280]{2,1,0:T(2,128)(2,1)S(1)} all-to-all(bf16[8,2,1280]{2,1,0:T(2,128)(2,1)S(1)} %add_convert_fusion), channel_id=1, replica_groups=mesh['group'=2,'chip'=8,'core'=2] {'chip'}, dimensions={0} | all-to-all | bytes 81920 | tf_op jit(solution)/shard_map/all_to_all | solution.py:149
  31.8 0.8 %shard_map.71 = (f32[8,640]{1,0:T(8,128)S(1)}, f32[8,640]{1,0:T(8,128)S(1)}, bf16[16,256]{1,0:T(8,128)(2,1)S(1)}, bf16[16,1280]{1,0:T(8,128)(2,1)S(1)}) custom-call(bf16[256,1280]{1,0:T(8,128)(2,1)S(1)} %bitcast.10, bf16[256,1280]{1,0:T(8,128)(2,1)S(1)} %bitcast.12, bf16[16,1280]{1,0:T(8,128)(2,1)S(1)} %get-tuple-element.12.router2_ref, ...), custom_call_target="tpu_custom_call" | custom-call | flops 31457280 | bytes 1310720 | tf_op jit(solution)/shard_map/pallas_call | solution.py:133
  32.6 0.0 collective-permute-start.2
  32.7 1.2 %collective-permute-done.2 = f32[8,640]{1,0:T(8,128)S(1)} collective-permute-done((f32[8,640]{1,0:T(8,128)S(1)}, f32[8,640]{1,0:T(8,128)S(1)}, u32[]{:S(2)}, u32[]{:S(2)}) %collective-permute-start.2) | collective-permute-done | bytes 20512 | tf_op jit(solution)/shard_map/ppermute | solution.py:145
  33.9 30.5 %all-gather = bf16[64,640]{1,0:T(8,128)(2,1)S(1)} all-gather(bf16[8,640]{1,0:T(8,128)(2,1)S(1)} %add_convert_fusion.1), channel_id=2, replica_groups=mesh['group'=2,'chip'=8,'core'=2] {'chip'}, dimensions={0}, use_global_device_ids=true | all-gather | bytes 92160 | tf_op jit(solution)/shard_map/all_gather | solution.py:212
  64.4 0.1 collective-permute-start.3
  64.5 1.2 %shard_map.72 = bf16[256,1280]{1,0:T(8,128)(2,1)} custom-call(bf16[16,256]{1,0:T(8,128)(2,1)S(1)} %get-tuple-element.18.left_ref, bf16[16,1280]{1,0:T(8,128)(2,1)S(1)} %get-tuple-element.19.right_ref), custom_call_target="tpu_custom_call" | custom-call | flops 10485760 | bytes 655360 | tf_op jit(solution)/shard_map/pallas_call | solution.py:133
  65.7 0.0 collective-permute-done.3
  65.7 0.6 maximum_bitcast_fusion
  (4 shorter events, 0.0 us)
Async XLA Ops:
  0.6 0.7 %copy-start.4 = (bf16[1280,8]{0,1:T(8,128)(2,1)S(1)}, bf16[1280,8]{0,1:T(8,128)(2,1)}, u32[]{:S(2)}) copy-start(bf16[1280,8]{0,1:T(8,128)(2,1)} %param.7) | copy-start | bytes 61444
  0.6 1.1 %copy-start.3 = (bf16[1,256,1280]{2,1,0:T(8,128)(2,1)S(1)}, bf16[1,256,1280]{2,1,0:T(8,128)(2,1)}, u32[]{:S(2)}) copy-start(bf16[1,256,1280]{2,1,0:T(8,128)(2,1)} %param.6) | copy-start | bytes 1966084
  0.7 1.3 %copy-start.2 = (bf16[1,256,1280]{2,1,0:T(8,128)(2,1)S(1)}, bf16[1,256,1280]{2,1,0:T(8,128)(2,1)}, u32[]{:S(2)}) copy-start(bf16[1,256,1280]{2,1,0:T(8,128)(2,1)} %param.5) | copy-start | bytes 1966084
  0.7 17.4 %copy-start = (bf16[1280,1280]{1,0:T(8,128)(2,1)S(1)}, bf16[1280,1280]{1,0:T(8,128)(2,1)}, u32[]{:S(2)}) copy-start(bf16[1280,1280]{1,0:T(8,128)(2,1)} %in_weight_ref.1) | copy-start | bytes 9830404
  0.7 17.4 %copy-start.1 = (bf16[1280,1280]{1,0:T(8,128)(2,1)S(1)}, bf16[1280,1280]{1,0:T(8,128)(2,1)}, u32[]{:S(2)}) copy-start(bf16[1280,1280]{1,0:T(8,128)(2,1)} %out_weight_ref.1) | copy-start | bytes 9830404
  16.8 1.2 %collective-permute-start = (bf16[8,2,1280]{2,1,0:T(2,128)(2,1)S(1)}, bf16[8,2,1280]{2,1,0:T(2,128)(2,1)S(1)}, u32[]{:S(2)}, u32[]{:S(2)}) collective-permute-start(bf16[8,2,1280]{2,1,0:T(2,128)(2,1)S(1)} %all_to_all.10.got_ref), channel_id=1, source_target_pairs={{0,1},{1,0},{2,3},{3,2},{4,5},{5,4},{6,7},{7,6},{8,9},{9,8},{10,11... | collective-permute-start | bytes 122888 | tf_op jit(solution)/shard_map/ppermute | solution.py:145
  21.3 1.3 %collective-permute-start.1 = (f32[8,2,1280]{2,1,0:T(2,128)S(1)}, f32[8,2,1280]{2,1,0:T(2,128)S(1)}, u32[]{:S(2)}, u32[]{:S(2)}) collective-permute-start(f32[8,2,1280]{2,1,0:T(2,128)S(1)} %get-tuple-element.17), channel_id=1, source_target_pairs={{0,1},{1,0},{2,3},{3,2},{4,5},{5,4},{6,7},{7,6},{8,9},{9,8},{10,11... | collective-permute-start | bytes 245768 | tf_op jit(solution)/shard_map/ppermute | solution.py:145
  32.6 1.2 %collective-permute-start.2 = (f32[8,640]{1,0:T(8,128)S(1)}, f32[8,640]{1,0:T(8,128)S(1)}, u32[]{:S(2)}, u32[]{:S(2)}) collective-permute-start(f32[8,640]{1,0:T(8,128)S(1)} %get-tuple-element.21), channel_id=1, source_target_pairs={{0,1},{1,0},{2,3},{3,2},{4,5},{5,4},{6,7},{7,6},{8,9},{9,8},{10,11... | collective-permute-start | bytes 61448 | tf_op jit(solution)/shard_map/ppermute | solution.py:145
  64.4 1.3 %collective-permute-start.3 = (f32[8,640]{1,0:T(8,128)S(1)}, f32[8,640]{1,0:T(8,128)S(1)}, u32[]{:S(2)}, u32[]{:S(2)}) collective-permute-start(f32[8,640]{1,0:T(8,128)S(1)} %convert_reduce_fusion), channel_id=1, source_target_pairs={{0,1},{1,0},{2,3},{3,2},{4,5},{5,4},{6,7},{7,6},{8,9},{9,8},{10,11... | collective-permute-start | bytes 61448 | tf_op jit(solution)/shard_map/ppermute | solution.py:145

commit v5 on v3

v5 whole, which is shorter than its diff:
```python
import math

import jax
import jax.numpy as jnp
from jax import lax
from jax.experimental import pallas as pl
from jax.experimental.pallas import tpu as pltpu
from jax.sharding import PartitionSpec as P

F32 = jnp.float32
BF16 = jnp.bfloat16
NN = (((1,), (0,)), ((), ()))
NT = (((1,), (1,)), ((), ()))
TN = (((0,), (0,)), ((), ()))
AHEAD_FLOPS = 3 * 10**10


def dot(a, b, dims):
    return lax.dot_general(a, b, dims, preferred_element_type=F32)


def first_kernel(token_ref):
    token_ref[...] = jnp.zeros(token_ref.shape, F32)


def slots_kernel(
    tokens_ref, grad_ref, router_ref, token_ref, sent_ref, dispatch_ref, combine_ref
):
    slots = router_ref.shape[0]
    logits = dot(router_ref[...], tokens_ref[...], NT)
    over_patches = jnp.exp(logits - jnp.max(logits, axis=1, keepdims=True))
    dispatch = over_patches / jnp.sum(over_patches, axis=1, keepdims=True)
    over_slots = jnp.exp(logits - jnp.max(logits, axis=0, keepdims=True))
    combine = over_slots / jnp.sum(over_slots, axis=0, keepdims=True)
    dispatch_ref[...] = dispatch
    combine_ref[...] = combine
    slot_in = dot(dispatch.astype(BF16), tokens_ref[...], NN)
    slot_grad = dot(combine.astype(BF16), grad_ref[...], NN)
    for s in range(slots):
        message = jnp.concatenate([slot_in[s : s + 1], slot_grad[s : s + 1]], axis=0).astype(BF16)
        for half in range(2):
            sent_ref[2 * s + half] = message


def experts_kernel(
    got_ref, in_weight_ref, out_weight_ref, mine_ref, theirs_ref, in_rows_ref, grad_rows_ref
):
    images = got_ref.shape[0]
    for k in range(images):
        message = got_ref[k].astype(F32)
        in_rows_ref[k : k + 1] = message[0:1]
        grad_rows_ref[k : k + 1] = message[1:2]
    hidden = dot(in_rows_ref[...].astype(BF16), in_weight_ref[...], NN)
    act_grad = dot(grad_rows_ref[...].astype(BF16), out_weight_ref[...], NT)
    normal_cdf = 0.5 * (1.0 + lax.erf(hidden * (1.0 / math.sqrt(2.0))))
    normal_pdf = jnp.exp(-0.5 * hidden * hidden) * (1.0 / math.sqrt(2.0 * math.pi))
    activation = (hidden * normal_cdf).astype(BF16)
    hidden_grad = (act_grad * (normal_cdf + hidden * normal_pdf)).astype(BF16)
    part_out = dot(activation, out_weight_ref[...], NN)
    part_in = dot(hidden_grad, in_weight_ref[...], NT)
    first = lax.axis_index("core") == 0
    for k in range(images // 2):
        pair = [
            jnp.concatenate([part_out[i : i + 1], part_in[i : i + 1]], axis=0)
            for i in (2 * k, 2 * k + 1)
        ]
        mine_ref[k] = jnp.where(first, pair[0], pair[1])
        theirs_ref[k] = jnp.where(first, pair[1], pair[0])


def logits_kernel(
    tokens_ref,
    grad_ref,
    router_ref,
    dispatch_ref,
    combine_ref,
    back_ref,
    kept_ref,
    given_ref,
    left_ref,
    right_ref,
    out_rows_ref,
    back_rows_ref,
):
    slots = back_ref.shape[0]
    for s in range(slots):
        message = back_ref[s].astype(F32)
        out_rows_ref[s : s + 1] = message[0:1]
        back_rows_ref[s : s + 1] = message[1:2]
    slot_back = back_rows_ref[...].astype(BF16)
    combine_grad = dot(out_rows_ref[...].astype(BF16), grad_ref[...], NT)
    dispatch_grad = dot(slot_back, tokens_ref[...], NT)
    dispatch = dispatch_ref[...]
    combine = combine_ref[...]
    slot_sum = jnp.sum(combine * combine_grad, axis=0, keepdims=True)
    patch_sum = jnp.sum(dispatch * dispatch_grad, axis=1, keepdims=True)
    logits_grad = combine * (combine_grad - slot_sum) + dispatch * (dispatch_grad - patch_sum)
    part = dot(logits_grad.astype(BF16), tokens_ref[...], NN)
    half = part.shape[1] // 2
    first = lax.axis_index("core") == 0
    kept_ref[...] = jnp.where(first, part[:, :half], part[:, half:])
    given_ref[...] = jnp.where(first, part[:, half:], part[:, :half])
    left_ref[...] = jnp.concatenate([logits_grad, dispatch], axis=0).astype(BF16)
    right_ref[...] = jnp.concatenate(
        [router_ref[...].astype(F32), back_rows_ref[...]], axis=0
    ).astype(BF16)


def tokens_kernel(left_ref, right_ref, tokens_grad_ref):
    tokens_grad_ref[...] = dot(left_ref[...], right_ref[...], TN).astype(BF16)


def call(kernel, outs, scratch, cost, *operands):
    return pl.pallas_call(
        kernel,
        out_shape=[jax.ShapeDtypeStruct(shape, dtype) for shape, dtype in outs],
        in_specs=[pl.BlockSpec(memory_space=pltpu.VMEM)] * len(operands),
        out_specs=[pl.BlockSpec(memory_space=pltpu.VMEM)] * len(outs),
        scratch_shapes=[pltpu.VMEM(shape, F32) for shape in scratch],
        compiler_params=pltpu.CompilerParams(vmem_limit_bytes=16 * 1024 * 1024),
        cost_estimate=pl.CostEstimate(flops=cost[0], bytes_accessed=cost[1], transcendentals=0),
    )(*operands)


def swap_cores(value):
    return lax.ppermute(value, "core", [(0, 1), (1, 0)])


def exchange(value, axes):
    return lax.all_to_all(value, axes, split_axis=0, concat_axis=0, tiled=True)


def per_device(tokens, out_grad, router, in_weight, out_weight):
    _, patches, width = tokens.shape
    hidden = in_weight.shape[1]
    slots = router.shape[1]
    chips = lax.axis_size("chip")
    tokens = tokens[0]
    out_grad = out_grad[0]
    router_rows = router.T
    image_bytes = 2 * patches * width
    weight_bytes = 2 * width * hidden
    (token,) = call(first_kernel, [((8, 128), F32)], [], (AHEAD_FLOPS, image_bytes))
    sent, dispatch, combine = call(
        slots_kernel,
        [((2 * slots, 2, width), BF16), ((slots, patches), F32), ((slots, patches), F32)],
        [],
        (12 * patches * width * slots, 2 * image_bytes),
        tokens,
        out_grad,
        router_rows,
        token,
    )
    got = exchange(sent, ("chip", "core"))
    mine, theirs = call(
        experts_kernel,
        [((chips, 2, width), F32), ((chips, 2, width), F32)],
        [(2 * chips, width), (2 * chips, width)],
        (16 * chips * width * hidden, 2 * weight_bytes),
        got,
        in_weight,
        out_weight,
    )
    back = exchange((mine + swap_cores(theirs)).astype(BF16), "chip")
    kept, given, left, right = call(
        logits_kernel,
        [
            ((slots, width // 2), F32),
            ((slots, width // 2), F32),
            ((2 * slots, patches), BF16),
            ((2 * slots, width), BF16),
        ],
        [(slots, width), (slots, width)],
        (12 * patches * width * slots, 2 * image_bytes),
        tokens,
        out_grad,
        router_rows,
        dispatch,
        combine,
        back,
    )
    pair = (kept + swap_cores(given)).astype(BF16)
    terms = exchange(jnp.broadcast_to(pair[None], (chips,) + pair.shape), "chip")
    total = jnp.sum(terms.astype(F32), axis=0)
    other = swap_cores(total)
    first = lax.axis_index("core") == 0
    router_grad = jnp.concatenate(
        [jnp.where(first, total, other), jnp.where(first, other, total)], axis=1
    )
    (tokens_grad,) = call(
        tokens_kernel,
        [((patches, width), BF16)],
        [],
        (4 * patches * width * slots, image_bytes),
        left,
        right,
    )
    return (tokens_grad[None], router_grad.T)


def solution(mesh):
    shape = (mesh.shape["group"], mesh.shape["expert"] // 2, 2)
    fine = jax.sharding.Mesh(mesh.devices.reshape(shape), ("group", "chip", "core"))
    expert = ("chip", "core")
    in_specs = (
        P(("group", "chip", "core"), None, None),
        P(("group", "chip", "core"), None, None),
        P(),
        P(None, expert),
        P(expert, None),
    )
    out_specs = (P(("group", "chip", "core"), None, None), P("group", None))
    return jax.shard_map(
        per_device, mesh=fine, in_specs=in_specs, out_specs=out_specs, check_vma=False
    )
```

time: 52.1 us -> 44.1 us (0.85)
  local copies, waits for them, and re-layouts: 6.77 us -> 1.27 us
  waiting for transfers between devices: 3.55 us -> 2.48 us
  blocking collectives: 33.4 us -> 32.8 us
    unnamed x14 -> x10, local copies, waits for them, and re-layouts: 6.76 us -> 1.26 us
    ppermute x4 -> x3, waiting for transfers between devices: 3.55 us -> 2.48 us  [swap_cores(): return lax.ppermute(value, 'core', [(0, 1), (1, 0)])]
    all_to_all x3, blocking collectives: 33.4 us -> 32.8 us  [exchange(): return lax.all_to_all(value, axes, split_axis=0, concat_axis=0, tiled=True)]
    pallas_call x4 -> x5, Pallas kernels: 6.18 us -> 5.67 us  [call(): pl.pallas_call(kernel, out_shape=[jax.ShapeDtypeStruct(shape, dtype) for...]
  transfers between devices with their start and end apart: 4 -> 3, of which waited for: 3 -> 2; matrix products, arithmetic and copies ran while one was open for 0% -> 0% of each run, Pallas kernels for 2% -> 3%
where the time goes in v5:
time: 44.1 us; the launch traced here: 43.9 us
  blocking collectives  32.8 us (74%)
  Pallas kernels  5.67 us (13%)
  waiting for transfers between devices  2.48 us (6%)
  local copies, waits for them, and re-layouts  1.27 us (3%)
  between operations  0.74 us (2%)
  other arithmetic  0.69 us (2%)
    all_to_all x3, blocking collectives, exchange(): return lax.all_to_all(value, axes, split_axis=0, concat_axis=0, tiled=True)  32.8 us
    pallas_call x5, Pallas kernels, call(): pl.pallas_call(kernel, out_shape=[jax.ShapeDtypeStruct(shape, dtype) for...  5.67 us
    ppermute x3, waiting for transfers between devices, swap_cores(): return lax.ppermute(value, 'core', [(0, 1), (1, 0)])  2.48 us
    unnamed x10, local copies, waits for them, and re-layouts  1.26 us
  transfers between devices with their start and end apart: 3, of which 2 were waited for; matrix products, arithmetic and copies ran while one was open for 0% of the time, Pallas kernels for 3%

profile of v5, /device:TPU:0, one launch (start us, length us, event | category | flops | bytes accessed | tf_op | source)
XLA Modules:
  0.0 43.9 jit_solution(17869503410525994747)
XLA Ops:
  0.6 0.0 copy-start.4
  0.6 0.0 copy-start.3
  0.7 0.0 copy-start.2
  0.7 0.0 copy-start
  0.7 0.0 copy-start.1
  0.7 0.7 %copy-done.4 = bf16[1280,8]{0,1:T(8,128)(2,1)S(1)} copy-done((bf16[1280,8]{0,1:T(8,128)(2,1)S(1)}, bf16[1280,8]{0,1:T(8,128)(2,1)}, u32[]{:S(2)}) %copy-start.4) | copy-done | bytes 20504
  1.4 0.4 copy-done.3
  1.7 0.2 copy-done.2
  1.9 1.0 %shard_map.69 = (bf16[16,2,1280]{2,1,0:T(2,128)(2,1)S(1)}, f32[8,256]{1,0:T(8,128)S(1)}, f32[8,256]{1,0:T(8,128)S(1)}) custom-call(bf16[256,1280]{1,0:T(8,128)(2,1)S(1)} %bitcast.6, bf16[256,1280]{1,0:T(8,128)(2,1)S(1)} %bitcast.8, bf16[8,1280]{1,0:T(8,128)(2,1)S(1)} %bitcast.10, f32[8,128]{1,0:T(8,128)S(1)} %shard_map.68.token_ref), custom_call_target="tpu_custom_call" | custom-call | flops 31457280 | bytes 1310720 | tf_op jit(solution)/shard_map/pallas_call | solution.py:114
  3.0 14.3 %all_to_all.15.got_ref = bf16[16,2,1280]{2,1,0:T(2,128)(2,1)S(1)} all-to-all(bf16[16,2,1280]{2,1,0:T(2,128)(2,1)S(1)} %get-tuple-element.13), channel_id=1, replica_groups=mesh['group'=2,'chip'=8,'core'=2] {'chip','core'}, dimensions={0} | all-to-all | bytes 163840 | tf_op jit(solution)/shard_map/all_to_all | solution.py:130
  17.3 0.0 copy-done
  17.3 0.0 copy-done.1
  17.3 2.7 %shard_map.70 = (f32[8,2,1280]{2,1,0:T(2,128)S(1)}, f32[8,2,1280]{2,1,0:T(2,128)S(1)}) custom-call(bf16[16,2,1280]{2,1,0:T(2,128)(2,1)S(1)} %all_to_all.15.got_ref, bf16[1280,1280]{1,0:T(8,128)(2,1)S(1)} %copy-done, bf16[1280,1280]{1,0:T(8,128)(2,1)S(1)} %copy-done.1), custom_call_target="tpu_custom_call" | custom-call | flops 209715200 | bytes 6553600 | tf_op jit(solution)/shard_map/pallas_call | solution.py:114
  20.1 0.1 collective-permute-start
  20.2 1.3 %collective-permute-done = f32[8,2,1280]{2,1,0:T(2,128)S(1)} collective-permute-done((f32[8,2,1280]{2,1,0:T(2,128)S(1)}, f32[8,2,1280]{2,1,0:T(2,128)S(1)}, u32[]{:S(2)}, u32[]{:S(2)}) %collective-permute-start) | collective-permute-done | bytes 81952 | tf_op jit(solution)/shard_map/ppermute | solution.py:126
  21.5 9.1 %all_to_all.16.back_ref = bf16[8,2,1280]{2,1,0:T(2,128)(2,1)S(1)} all-to-all(bf16[8,2,1280]{2,1,0:T(2,128)(2,1)S(1)} %add_convert_fusion), channel_id=1, replica_groups=mesh['group'=2,'chip'=8,'core'=2] {'chip'}, dimensions={0} | all-to-all | bytes 81920 | tf_op jit(solution)/shard_map/all_to_all | solution.py:130
  30.6 0.7 %shard_map.71 = (f32[8,640]{1,0:T(8,128)S(1)}, f32[8,640]{1,0:T(8,128)S(1)}, bf16[16,256]{1,0:T(8,128)(2,1)S(1)}, bf16[16,1280]{1,0:T(8,128)(2,1)S(1)}) custom-call(bf16[256,1280]{1,0:T(8,128)(2,1)S(1)} %bitcast.7, bf16[256,1280]{1,0:T(8,128)(2,1)S(1)} %bitcast.9, bf16[8,1280]{1,0:T(8,128)(2,1)S(1)} %bitcast.11, ...), custom_call_target="tpu_custom_call" | custom-call | flops 31457280 | bytes 1310720 | tf_op jit(solution)/shard_map/pallas_call | solution.py:114
  31.3 0.0 collective-permute-start.1
  31.3 1.2 %collective-permute-done.1 = f32[8,640]{1,0:T(8,128)S(1)} collective-permute-done((f32[8,640]{1,0:T(8,128)S(1)}, f32[8,640]{1,0:T(8,128)S(1)}, u32[]{:S(2)}, u32[]{:S(2)}) %collective-permute-start.1) | collective-permute-done | bytes 20512 | tf_op jit(solution)/shard_map/ppermute | solution.py:126
  32.5 9.4 %all_to_all.17 = bf16[8,8,640]{2,1,0:T(8,128)(2,1)S(1)} all-to-all(bf16[8,8,640]{2,1,0:T(8,128)(2,1)S(1)} %broadcast_in_dim.10), channel_id=1, replica_groups=mesh['group'=2,'chip'=8,'core'=2] {'chip'}, dimensions={0} | all-to-all | bytes 163840 | tf_op jit(solution)/shard_map/all_to_all | solution.py:130
  41.9 0.1 collective-permute-start.2
  42.0 1.2 %shard_map.72 = bf16[256,1280]{1,0:T(8,128)(2,1)} custom-call(bf16[16,256]{1,0:T(8,128)(2,1)S(1)} %get-tuple-element.16.left_ref, bf16[16,1280]{1,0:T(8,128)(2,1)S(1)} %get-tuple-element.17.right_ref), custom_call_target="tpu_custom_call" | custom-call | flops 10485760 | bytes 655360 | tf_op jit(solution)/shard_map/pallas_call | solution.py:114
  43.2 0.0 collective-permute-done.2
  43.2 0.6 %maximum_bitcast_fusion = f32[1280,8]{0,1:T(8,128)} fusion(f32[8,640]{1,0:T(8,128)S(1)} %get-tuple-element.21, f32[8,640]{1,0:T(8,128)S(1)} %get-tuple-element.20), kind=kLoop, calls=%fused_computation.2 | loop fusion | flops 10240 | bytes 81920 | tf_op jit(solution)/shard_map/transpose | solution.py:198
  (6 shorter events, 0.1 us)
Async XLA Ops:
  0.6 0.7 %copy-start.4 = (bf16[1280,8]{0,1:T(8,128)(2,1)S(1)}, bf16[1280,8]{0,1:T(8,128)(2,1)}, u32[]{:S(2)}) copy-start(bf16[1280,8]{0,1:T(8,128)(2,1)} %param.7) | copy-start | bytes 61444
  0.6 1.1 %copy-start.3 = (bf16[1,256,1280]{2,1,0:T(8,128)(2,1)S(1)}, bf16[1,256,1280]{2,1,0:T(8,128)(2,1)}, u32[]{:S(2)}) copy-start(bf16[1,256,1280]{2,1,0:T(8,128)(2,1)} %param.6) | copy-start | bytes 1966084
  0.7 1.3 %copy-start.2 = (bf16[1,256,1280]{2,1,0:T(8,128)(2,1)S(1)}, bf16[1,256,1280]{2,1,0:T(8,128)(2,1)}, u32[]{:S(2)}) copy-start(bf16[1,256,1280]{2,1,0:T(8,128)(2,1)} %param.5) | copy-start | bytes 1966084
  0.7 16.7 %copy-start = (bf16[1280,1280]{1,0:T(8,128)(2,1)S(1)}, bf16[1280,1280]{1,0:T(8,128)(2,1)}, u32[]{:S(2)}) copy-start(bf16[1280,1280]{1,0:T(8,128)(2,1)} %in_weight_ref.1) | copy-start | bytes 9830404
  0.7 16.7 %copy-start.1 = (bf16[1280,1280]{1,0:T(8,128)(2,1)S(1)}, bf16[1280,1280]{1,0:T(8,128)(2,1)}, u32[]{:S(2)}) copy-start(bf16[1280,1280]{1,0:T(8,128)(2,1)} %out_weight_ref.1) | copy-start | bytes 9830404
  20.1 1.3 %collective-permute-start = (f32[8,2,1280]{2,1,0:T(2,128)S(1)}, f32[8,2,1280]{2,1,0:T(2,128)S(1)}, u32[]{:S(2)}, u32[]{:S(2)}) collective-permute-start(f32[8,2,1280]{2,1,0:T(2,128)S(1)} %get-tuple-element.15), channel_id=1, source_target_pairs={{0,1},{1,0},{2,3},{3,2},{4,5},{5,4},{6,7},{7,6},{8,9},{9,8},{10,11... | collective-permute-start | bytes 245768 | tf_op jit(solution)/shard_map/ppermute | solution.py:126
  31.3 1.2 %collective-permute-start.1 = (f32[8,640]{1,0:T(8,128)S(1)}, f32[8,640]{1,0:T(8,128)S(1)}, u32[]{:S(2)}, u32[]{:S(2)}) collective-permute-start(f32[8,640]{1,0:T(8,128)S(1)} %get-tuple-element.19), channel_id=1, source_target_pairs={{0,1},{1,0},{2,3},{3,2},{4,5},{5,4},{6,7},{7,6},{8,9},{9,8},{10,11... | collective-permute-start | bytes 61448 | tf_op jit(solution)/shard_map/ppermute | solution.py:126
  41.9 1.3 %collective-permute-start.2 = (f32[8,640]{1,0:T(8,128)S(1)}, f32[8,640]{1,0:T(8,128)S(1)}, u32[]{:S(2)}, u32[]{:S(2)}) collective-permute-start(f32[8,640]{1,0:T(8,128)S(1)} %convert_reduce_fusion), channel_id=1, source_target_pairs={{0,1},{1,0},{2,3},{3,2},{4,5},{5,4},{6,7},{7,6},{8,9},{9,8},{10,11... | collective-permute-start | bytes 61448 | tf_op jit(solution)/shard_map/ppermute | solution.py:126

commit v6 on v5

--- a/solution.py
+++ b/solution.py
@@ -13,20 +13,44 @@
 NT = (((1,), (1,)), ((), ()))
 TN = (((0,), (0,)), ((), ()))
 AHEAD_FLOPS = 3 * 10**10
+PIECES = 4
 
 
 def dot(a, b, dims):
     return lax.dot_general(a, b, dims, preferred_element_type=F32)
 
 
-def first_kernel(token_ref):
-    token_ref[...] = jnp.zeros(token_ref.shape, F32)
-
-
 def slots_kernel(
-    tokens_ref, grad_ref, router_ref, token_ref, sent_ref, dispatch_ref, combine_ref
+    tokens_hbm,
+    grad_hbm,
+    router_hbm,
+    slot_in_ref,
+    slot_grad_ref,
+    dispatch_ref,
+    combine_ref,
+    tokens_ref,
+    grad_ref,
+    router_ref,
+    arrived,
 ):
-    slots = router_ref.shape[0]
+    def pieces(source, target, first, count):
+        rows = source.shape[0] // count
+        return [
+            pltpu.make_async_copy(
+                source.at[pl.ds(i * rows, rows)],
+                target.at[pl.ds(i * rows, rows)],
+                arrived.at[first + i],
+            )
+            for i in range(count)
+        ]
+
+    router_copy = pltpu.make_async_copy(router_hbm, router_ref, arrived.at[2 * PIECES])
+    token_copies = pieces(tokens_hbm, tokens_ref, 0, PIECES)
+    grad_copies = pieces(grad_hbm, grad_ref, PIECES, PIECES)
+    for copy in [router_copy] + token_copies + grad_copies:
+        copy.start()
+    for copy in [router_copy] + token_copies:
+        copy.wait()
     logits = dot(router_ref[...], tokens_ref[...], NT)
     over_patches = jnp.exp(logits - jnp.max(logits, axis=1, keepdims=True))
     dispatch = over_patches / jnp.sum(over_patches, axis=1, keepdims=True)
@@ -34,16 +58,22 @@
     combine = over_slots / jnp.sum(over_slots, axis=0, keepdims=True)
     dispatch_ref[...] = dispatch
     combine_ref[...] = combine
-    slot_in = dot(dispatch.astype(BF16), tokens_ref[...], NN)
-    slot_grad = dot(combine.astype(BF16), grad_ref[...], NN)
-    for s in range(slots):
-        message = jnp.concatenate([slot_in[s : s + 1], slot_grad[s : s + 1]], axis=0).astype(BF16)
+    slot_in_ref[...] = dot(dispatch.astype(BF16), tokens_ref[...], NN)
+    for copy in grad_copies:
+        copy.wait()
+    slot_grad_ref[...] = dot(combine.astype(BF16), grad_ref[...], NN)
+
+
+def messages_kernel(slot_in_ref, slot_grad_ref, sent_ref):
+    for s in range(slot_in_ref.shape[0]):
+        rows = [slot_in_ref[s : s + 1], slot_grad_ref[s : s + 1]]
+        message = jnp.concatenate(rows, axis=0).astype(BF16)
         for half in range(2):
             sent_ref[2 * s + half] = message
 
 
 def experts_kernel(
-    got_ref, in_weight_ref, out_weight_ref, mine_ref, theirs_ref, in_rows_ref, grad_rows_ref
+    got_ref, in_weight_ref, out_weight_ref, parts_ref, in_rows_ref, grad_rows_ref
 ):
     images = got_ref.shape[0]
     for k in range(images):
@@ -58,14 +88,9 @@
     hidden_grad = (act_grad * (normal_cdf + hidden * normal_pdf)).astype(BF16)
     part_out = dot(activation, out_weight_ref[...], NN)
     part_in = dot(hidden_grad, in_weight_ref[...], NT)
-    first = lax.axis_index("core") == 0
-    for k in range(images // 2):
-        pair = [
-            jnp.concatenate([part_out[i : i + 1], part_in[i : i + 1]], axis=0)
-            for i in (2 * k, 2 * k + 1)
-        ]
-        mine_ref[k] = jnp.where(first, pair[0], pair[1])
-        theirs_ref[k] = jnp.where(first, pair[1], pair[0])
+    for k in range(images):
+        rows = [part_out[k : k + 1], part_in[k : k + 1]]
+        parts_ref[k] = jnp.concatenate(rows, axis=0).astype(BF16)
 
 
 def logits_kernel(
@@ -82,9 +107,9 @@
     out_rows_ref,
     back_rows_ref,
 ):
-    slots = back_ref.shape[0]
+    slots = router_ref.shape[0]
     for s in range(slots):
-        message = back_ref[s].astype(F32)
+        message = back_ref[2 * s].astype(F32) + back_ref[2 * s + 1].astype(F32)
         out_rows_ref[s : s + 1] = message[0:1]
         back_rows_ref[s : s + 1] = message[1:2]
     slot_back = back_rows_ref[...].astype(BF16)
@@ -110,14 +135,14 @@
     tokens_grad_ref[...] = dot(left_ref[...], right_ref[...], TN).astype(BF16)
 
 
-def call(kernel, outs, scratch, cost, *operands):
+def call(kernel, outs, scratch, cost, *operands, space=pltpu.VMEM):
     return pl.pallas_call(
         kernel,
         out_shape=[jax.ShapeDtypeStruct(shape, dtype) for shape, dtype in outs],
-        in_specs=[pl.BlockSpec(memory_space=pltpu.VMEM)] * len(operands),
+        in_specs=[pl.BlockSpec(memory_space=space)] * len(operands),
         out_specs=[pl.BlockSpec(memory_space=pltpu.VMEM)] * len(outs),
-        scratch_shapes=[pltpu.VMEM(shape, F32) for shape in scratch],
-        compiler_params=pltpu.CompilerParams(vmem_limit_bytes=16 * 1024 * 1024),
+        scratch_shapes=scratch,
+        compiler_params=pltpu.CompilerParams(vmem_limit_bytes=16 * 2**20),
         cost_estimate=pl.CostEstimate(flops=cost[0], bytes_accessed=cost[1], transcendentals=0),
     )(*operands)
 
@@ -140,28 +165,40 @@
     router_rows = router.T
     image_bytes = 2 * patches * width
     weight_bytes = 2 * width * hidden
-    (token,) = call(first_kernel, [((8, 128), F32)], [], (AHEAD_FLOPS, image_bytes))
-    sent, dispatch, combine = call(
+    slot_in, slot_grad, dispatch, combine = call(
         slots_kernel,
-        [((2 * slots, 2, width), BF16), ((slots, patches), F32), ((slots, patches), F32)],
+        [((slots, width), F32)] * 2 + [((slots, patches), F32)] * 2,
+        [
+            pltpu.VMEM((patches, width), BF16),
+            pltpu.VMEM((patches, width), BF16),
+            pltpu.VMEM((slots, width), BF16),
+            pltpu.SemaphoreType.DMA((2 * PIECES + 1,)),
+        ],
+        (12 * patches * width * slots, 2 * image_bytes),
+        pltpu.with_memory_space_constraint(tokens, pltpu.HBM),
+        pltpu.with_memory_space_constraint(out_grad, pltpu.HBM),
+        pltpu.with_memory_space_constraint(router_rows, pltpu.HBM),
+        space=pltpu.HBM,
+    )
+    (sent,) = call(
+        messages_kernel,
+        [((2 * slots, 2, width), BF16)],
         [],
-        (12 * patches * width * slots, 2 * image_bytes),
-        tokens,
-        out_grad,
-        router_rows,
-        token,
+        (AHEAD_FLOPS, image_bytes),
+        slot_in,
+        slot_grad,
     )
     got = exchange(sent, ("chip", "core"))
-    mine, theirs = call(
+    (parts,) = call(
         experts_kernel,
-        [((chips, 2, width), F32), ((chips, 2, width), F32)],
-        [(2 * chips, width), (2 * chips, width)],
+        [((2 * chips, 2, width), BF16)],
+        [pltpu.VMEM((2 * chips, width), F32)] * 2,
         (16 * chips * width * hidden, 2 * weight_bytes),
         got,
         in_weight,
         out_weight,
     )
-    back = exchange((mine + swap_cores(theirs)).astype(BF16), "chip")
+    back = exchange(parts, ("chip", "core"))
     kept, given, left, right = call(
         logits_kernel,
         [
@@ -170,7 +207,7 @@
             ((2 * slots, patches), BF16),
             ((2 * slots, width), BF16),
         ],
-        [(slots, width), (slots, width)],
+        [pltpu.VMEM((slots, width), F32)] * 2,
         (12 * patches * width * slots, 2 * image_bytes),
         tokens,
         out_grad,

time: 44.1 us -> 43.8 us (level)
  Pallas kernels: 5.67 us -> 7.06 us
  waiting for transfers between devices: 2.48 us -> 1.22 us
  local copies, waits for them, and re-layouts: 1.27 us -> 0.04 us
  blocking collectives: 32.8 us -> 33.7 us
    pallas_call x5, Pallas kernels: 5.67 us -> 7.06 us  [call(): pl.pallas_call(kernel, out_shape=[jax.ShapeDtypeStruct(shape, dtype) for...]
    ppermute x3 -> x2, waiting for transfers between devices: 2.48 us -> 1.22 us  [swap_cores(): return lax.ppermute(value, 'core', [(0, 1), (1, 0)])]
    unnamed x10, local copies, waits for them, and re-layouts: 1.26 us -> 0.03 us
    all_to_all x3, blocking collectives: 32.8 us -> 33.7 us  [exchange(): return lax.all_to_all(value, axes, split_axis=0, concat_axis=0, tiled=True)]
  transfers between devices with their start and end apart: 3 -> 2, of which waited for: 2 -> 1; matrix products, arithmetic and copies ran while one was open for 0% -> 0% of each run, Pallas kernels for 3% -> 3%
where the time goes in v6:
time: 43.8 us; the launch traced here: 43.5 us
  blocking collectives  33.7 us (77%)
  Pallas kernels  7.06 us (16%)
  waiting for transfers between devices  1.22 us (3%)
  between operations  0.72 us (2%)
  other arithmetic  0.65 us (1%)
    all_to_all x3, blocking collectives, exchange(): return lax.all_to_all(value, axes, split_axis=0, concat_axis=0, tiled=True)  33.7 us
    pallas_call x5, Pallas kernels, call(): pl.pallas_call(kernel, out_shape=[jax.ShapeDtypeStruct(shape, dtype) for...  7.06 us
    ppermute x2, waiting for transfers between devices, swap_cores(): return lax.ppermute(value, 'core', [(0, 1), (1, 0)])  1.22 us
  transfers between devices with their start and end apart: 2, of which 1 were waited for; matrix products, arithmetic and copies ran while one was open for 0% of the time, Pallas kernels for 3%

profile of v6, /device:TPU:0, one launch (start us, length us, event | category | flops | bytes accessed | tf_op | source)
XLA Modules:
  0.0 43.5 jit_solution(18312060621008513557)
XLA Ops:
  0.6 2.4 %shard_map.68 = (f32[8,1280]{1,0:T(8,128)S(1)}, f32[8,1280]{1,0:T(8,128)S(1)}, f32[8,256]{1,0:T(8,128)S(1)}, f32[8,256]{1,0:T(8,128)S(1)}) custom-call(bf16[256,1280]{1,0:T(8,128)(2,1)} %bitcast.6, bf16[256,1280]{1,0:T(8,128)(2,1)} %bitcast.8, bf16[8,1280]{1,0:T(8,128)(2,1)} %bitcast.10), custom_call_target="tpu_custom_call" | custom-call | flops 31457280 | bytes 1310720 | tf_op jit(solution)/shard_map/pallas_call | solution.py:139
  3.0 0.0 copy-start
  3.1 0.0 copy-start.1
  3.1 0.1 shard_map.69
  3.1 14.6 %all_to_all.15.got_ref = bf16[16,2,1280]{2,1,0:T(2,128)(2,1)S(1)} all-to-all(bf16[16,2,1280]{2,1,0:T(2,128)(2,1)S(1)} %shard_map.69), channel_id=1, replica_groups=mesh['group'=2,'chip'=8,'core'=2] {'chip','core'}, dimensions={0} | all-to-all | bytes 163840 | tf_op jit(solution)/shard_map/all_to_all | solution.py:155
  17.7 0.0 copy-done
  17.7 0.0 copy-done.1
  17.7 0.0 copy-start.2
  17.7 0.0 copy-start.3
  17.7 0.0 copy-start.4
  17.8 2.7 %shard_map.70 = bf16[16,2,1280]{2,1,0:T(2,128)(2,1)S(1)} custom-call(bf16[16,2,1280]{2,1,0:T(2,128)(2,1)S(1)} %all_to_all.15.got_ref, bf16[1280,1280]{1,0:T(8,128)(2,1)S(1)} %copy-done, bf16[1280,1280]{1,0:T(8,128)(2,1)S(1)} %copy-done.1), custom_call_target="tpu_custom_call" | custom-call | flops 209715200 | bytes 6553600 | tf_op jit(solution)/shard_map/pallas_call | solution.py:139
  20.5 9.7 %all_to_all.16.back_ref = bf16[16,2,1280]{2,1,0:T(2,128)(2,1)S(1)} all-to-all(bf16[16,2,1280]{2,1,0:T(2,128)(2,1)S(1)} %shard_map.70), channel_id=1, replica_groups=mesh['group'=2,'chip'=8,'core'=2] {'chip','core'}, dimensions={0} | all-to-all | bytes 163840 | tf_op jit(solution)/shard_map/all_to_all | solution.py:155
  30.2 0.0 copy-done.2
  30.2 0.0 copy-done.3
  30.2 0.0 copy-done.4
  30.2 0.7 %shard_map.71 = (f32[8,640]{1,0:T(8,128)S(1)}, f32[8,640]{1,0:T(8,128)S(1)}, bf16[16,256]{1,0:T(8,128)(2,1)S(1)}, bf16[16,1280]{1,0:T(8,128)(2,1)S(1)}) custom-call(bf16[256,1280]{1,0:T(8,128)(2,1)S(1)} %bitcast.7, bf16[256,1280]{1,0:T(8,128)(2,1)S(1)} %bitcast.9, bf16[8,1280]{1,0:T(8,128)(2,1)S(1)} %bitcast.11, ...), custom_call_target="tpu_custom_call" | custom-call | flops 31457280 | bytes 1310720 | tf_op jit(solution)/shard_map/pallas_call | solution.py:139
  30.9 0.0 collective-permute-start
  30.9 1.2 %collective-permute-done = f32[8,640]{1,0:T(8,128)S(1)} collective-permute-done((f32[8,640]{1,0:T(8,128)S(1)}, f32[8,640]{1,0:T(8,128)S(1)}, u32[]{:S(2)}, u32[]{:S(2)}) %collective-permute-start) | collective-permute-done | bytes 20512 | tf_op jit(solution)/shard_map/ppermute | solution.py:151
  32.2 9.4 %all_to_all.17 = bf16[8,8,640]{2,1,0:T(8,128)(2,1)S(1)} all-to-all(bf16[8,8,640]{2,1,0:T(8,128)(2,1)S(1)} %broadcast_in_dim.10), channel_id=1, replica_groups=mesh['group'=2,'chip'=8,'core'=2] {'chip'}, dimensions={0} | all-to-all | bytes 163840 | tf_op jit(solution)/shard_map/all_to_all | solution.py:155
  41.6 0.1 collective-permute-start.1
  41.7 1.2 %shard_map.72 = bf16[256,1280]{1,0:T(8,128)(2,1)} custom-call(bf16[16,256]{1,0:T(8,128)(2,1)S(1)} %get-tuple-element.14.left_ref, bf16[16,1280]{1,0:T(8,128)(2,1)S(1)} %get-tuple-element.15.right_ref), custom_call_target="tpu_custom_call" | custom-call | flops 10485760 | bytes 655360 | tf_op jit(solution)/shard_map/pallas_call | solution.py:139
  42.9 0.0 collective-permute-done.1
  42.9 0.6 %maximum_bitcast_fusion = f32[1280,8]{0,1:T(8,128)} fusion(f32[8,640]{1,0:T(8,128)S(1)} %get-tuple-element.19, f32[8,640]{1,0:T(8,128)S(1)} %get-tuple-element.18), kind=kLoop, calls=%fused_computation.1 | loop fusion | flops 10240 | bytes 81920 | tf_op jit(solution)/shard_map/transpose | solution.py:235
  (4 shorter events, 0.0 us)
Async XLA Ops:
  3.0 14.7 %copy-start = (bf16[1280,1280]{1,0:T(8,128)(2,1)S(1)}, bf16[1280,1280]{1,0:T(8,128)(2,1)}, u32[]{:S(2)}) copy-start(bf16[1280,1280]{1,0:T(8,128)(2,1)} %in_weight_ref.1) | copy-start | bytes 9830404
  3.1 14.7 %copy-start.1 = (bf16[1280,1280]{1,0:T(8,128)(2,1)S(1)}, bf16[1280,1280]{1,0:T(8,128)(2,1)}, u32[]{:S(2)}) copy-start(bf16[1280,1280]{1,0:T(8,128)(2,1)} %out_weight_ref.1) | copy-start | bytes 9830404
  17.7 12.5 %copy-start.2 = (bf16[1,256,1280]{2,1,0:T(8,128)(2,1)S(1)}, bf16[1,256,1280]{2,1,0:T(8,128)(2,1)}, u32[]{:S(2)}) copy-start(bf16[1,256,1280]{2,1,0:T(8,128)(2,1)} %param.5) | copy-start | bytes 1966084
  17.7 12.5 %copy-start.3 = (bf16[1,256,1280]{2,1,0:T(8,128)(2,1)S(1)}, bf16[1,256,1280]{2,1,0:T(8,128)(2,1)}, u32[]{:S(2)}) copy-start(bf16[1,256,1280]{2,1,0:T(8,128)(2,1)} %param.6) | copy-start | bytes 1966084
  17.7 12.5 %copy-start.4 = (bf16[1280,8]{0,1:T(8,128)(2,1)S(1)}, bf16[1280,8]{0,1:T(8,128)(2,1)}, u32[]{:S(2)}) copy-start(bf16[1280,8]{0,1:T(8,128)(2,1)} %param.7) | copy-start | bytes 61444
  30.9 1.2 %collective-permute-start = (f32[8,640]{1,0:T(8,128)S(1)}, f32[8,640]{1,0:T(8,128)S(1)}, u32[]{:S(2)}, u32[]{:S(2)}) collective-permute-start(f32[8,640]{1,0:T(8,128)S(1)} %get-tuple-element.17), channel_id=1, source_target_pairs={{0,1},{1,0},{2,3},{3,2},{4,5},{5,4},{6,7},{7,6},{8,9},{9,8},{10,11... | collective-permute-start | bytes 61448 | tf_op jit(solution)/shard_map/ppermute | solution.py:151
  41.6 1.3 %collective-permute-start.1 = (f32[8,640]{1,0:T(8,128)S(1)}, f32[8,640]{1,0:T(8,128)S(1)}, u32[]{:S(2)}, u32[]{:S(2)}) collective-permute-start(f32[8,640]{1,0:T(8,128)S(1)} %convert_reduce_fusion), channel_id=1, source_target_pairs={{0,1},{1,0},{2,3},{3,2},{4,5},{5,4},{6,7},{7,6},{8,9},{9,8},{10,11... | collective-permute-start | bytes 61448 | tf_op jit(solution)/shard_map/ppermute | solution.py:151

commit v7 on v5

--- a/solution.py
+++ b/solution.py
@@ -7,6 +7,7 @@
 from jax.experimental.pallas import tpu as pltpu
 from jax.sharding import PartitionSpec as P
 
+EXPERT = ("far", "near", "core")
 F32 = jnp.float32
 BF16 = jnp.bfloat16
 NN = (((1,), (0,)), ((), ()))
@@ -43,7 +44,7 @@
 
 
 def experts_kernel(
-    got_ref, in_weight_ref, out_weight_ref, mine_ref, theirs_ref, in_rows_ref, grad_rows_ref
+    got_ref, in_weight_ref, out_weight_ref, parts_ref, in_rows_ref, grad_rows_ref
 ):
     images = got_ref.shape[0]
     for k in range(images):
@@ -58,14 +59,9 @@
     hidden_grad = (act_grad * (normal_cdf + hidden * normal_pdf)).astype(BF16)
     part_out = dot(activation, out_weight_ref[...], NN)
     part_in = dot(hidden_grad, in_weight_ref[...], NT)
-    first = lax.axis_index("core") == 0
-    for k in range(images // 2):
-        pair = [
-            jnp.concatenate([part_out[i : i + 1], part_in[i : i + 1]], axis=0)
-            for i in (2 * k, 2 * k + 1)
-        ]
-        mine_ref[k] = jnp.where(first, pair[0], pair[1])
-        theirs_ref[k] = jnp.where(first, pair[1], pair[0])
+    for k in range(images):
+        rows = [part_out[k : k + 1], part_in[k : k + 1]]
+        parts_ref[k] = jnp.concatenate(rows, axis=0).astype(BF16)
 
 
 def logits_kernel(
@@ -82,9 +78,9 @@
     out_rows_ref,
     back_rows_ref,
 ):
-    slots = back_ref.shape[0]
+    slots = router_ref.shape[0]
     for s in range(slots):
-        message = back_ref[s].astype(F32)
+        message = back_ref[2 * s].astype(F32) + back_ref[2 * s + 1].astype(F32)
         out_rows_ref[s : s + 1] = message[0:1]
         back_rows_ref[s : s + 1] = message[1:2]
     slot_back = back_rows_ref[...].astype(BF16)
@@ -117,24 +113,32 @@
         in_specs=[pl.BlockSpec(memory_space=pltpu.VMEM)] * len(operands),
         out_specs=[pl.BlockSpec(memory_space=pltpu.VMEM)] * len(outs),
         scratch_shapes=[pltpu.VMEM(shape, F32) for shape in scratch],
-        compiler_params=pltpu.CompilerParams(vmem_limit_bytes=16 * 1024 * 1024),
+        compiler_params=pltpu.CompilerParams(vmem_limit_bytes=16 * 2**20),
         cost_estimate=pl.CostEstimate(flops=cost[0], bytes_accessed=cost[1], transcendentals=0),
     )(*operands)
 
 
-def swap_cores(value):
-    return lax.ppermute(value, "core", [(0, 1), (1, 0)])
+def swap(value, axis):
+    return lax.ppermute(value, axis, [(0, 1), (1, 0)])
 
 
 def exchange(value, axes):
     return lax.all_to_all(value, axes, split_axis=0, concat_axis=0, tiled=True)
+
+
+def sum_over(value, axis):
+    count = lax.axis_size(axis)
+    if count == 2:
+        return value + swap(value, axis)
+    terms = exchange(jnp.broadcast_to(value.astype(BF16)[None], (count,) + value.shape), axis)
+    return jnp.sum(terms.astype(F32), axis=0)
 
 
 def per_device(tokens, out_grad, router, in_weight, out_weight):
     _, patches, width = tokens.shape
     hidden = in_weight.shape[1]
     slots = router.shape[1]
-    chips = lax.axis_size("chip")
+    chips = slots
     tokens = tokens[0]
     out_grad = out_grad[0]
     router_rows = router.T
@@ -151,17 +155,17 @@
         router_rows,
         token,
     )
-    got = exchange(sent, ("chip", "core"))
-    mine, theirs = call(
+    got = exchange(sent, EXPERT)
+    (parts,) = call(
         experts_kernel,
-        [((chips, 2, width), F32), ((chips, 2, width), F32)],
-        [(2 * chips, width), (2 * chips, width)],
+        [((2 * chips, 2, width), BF16)],
+        [(2 * chips, width)] * 2,
         (16 * chips * width * hidden, 2 * weight_bytes),
         got,
         in_weight,
         out_weight,
     )
-    back = exchange((mine + swap_cores(theirs)).astype(BF16), "chip")
+    back = exchange(parts, EXPERT)
     kept, given, left, right = call(
         logits_kernel,
         [
@@ -170,7 +174,7 @@
             ((2 * slots, patches), BF16),
             ((2 * slots, width), BF16),
         ],
-        [(slots, width), (slots, width)],
+        [(slots, width)] * 2,
         (12 * patches * width * slots, 2 * image_bytes),
         tokens,
         out_grad,
@@ -179,10 +183,8 @@
         combine,
         back,
     )
-    pair = (kept + swap_cores(given)).astype(BF16)
-    terms = exchange(jnp.broadcast_to(pair[None], (chips,) + pair.shape), "chip")
-    total = jnp.sum(terms.astype(F32), axis=0)
-    other = swap_cores(total)
+    total = sum_over(sum_over(kept + swap(given, "core"), "near"), "far")
+    other = swap(total, "core")
     first = lax.axis_index("core") == 0
     router_grad = jnp.concatenate(
         [jnp.where(first, total, other), jnp.where(first, other, total)], axis=1
@@ -199,17 +201,13 @@
 
 
 def solution(mesh):
-    shape = (mesh.shape["group"], mesh.shape["expert"] // 2, 2)
-    fine = jax.sharding.Mesh(mesh.devices.reshape(shape), ("group", "chip", "core"))
-    expert = ("chip", "core")
-    in_specs = (
-        P(("group", "chip", "core"), None, None),
-        P(("group", "chip", "core"), None, None),
-        P(),
-        P(None, expert),
-        P(expert, None),
-    )
-    out_specs = (P(("group", "chip", "core"), None, None), P("group", None))
+    chips = mesh.shape["expert"] // 2
+    near = 2 ** (int(math.log2(chips)) // 2)
+    shape = (mesh.shape["group"], chips // near, near, 2)
+    fine = jax.sharding.Mesh(mesh.devices.reshape(shape), ("group",) + EXPERT)
+    images = P(("group",) + EXPERT, None, None)
+    in_specs = (images, images, P(), P(None, EXPERT), P(EXPERT, None))
+    out_specs = (images, P("group", None))
     return jax.shard_map(
         per_device, mesh=fine, in_specs=in_specs, out_specs=out_specs, check_vma=False
     )

time: 44.1 us -> 45.8 us (1.039)
  waiting for transfers between devices: 2.48 us -> 5 us
  blocking collectives: 32.8 us -> 32.1 us
    ppermute x3, waiting for transfers between devices: 2.48 us -> 5 us  [swap(): return lax.ppermute(value, axis, [(0, 1), (1, 0)])]
    all_to_all x3, blocking collectives: 32.8 us -> 32.1 us  [exchange(): return lax.all_to_all(value, axes, split_axis=0, concat_axis=0, tiled=True)]
where the time goes in v7:
time: 45.8 us; the launch traced here: 45.5 us
  blocking collectives  32.1 us (70%)
  Pallas kernels  5.66 us (12%)
  waiting for transfers between devices  5 us (11%)
  local copies, waits for them, and re-layouts  1.26 us (3%)
  between operations  0.73 us (2%)
  other arithmetic  0.65 us (1%)
    all_to_all x3, blocking collectives, exchange(): return lax.all_to_all(value, axes, split_axis=0, concat_axis=0, tiled=True)  32.1 us
    pallas_call x5, Pallas kernels, call(): pl.pallas_call(kernel, out_shape=[jax.ShapeDtypeStruct(shape, dtype) for...  5.66 us
    ppermute x3, waiting for transfers between devices, swap(): return lax.ppermute(value, axis, [(0, 1), (1, 0)])  5 us
    unnamed x10, local copies, waits for them, and re-layouts  1.26 us
  transfers between devices with their start and end apart: 3, of which 2 were waited for; matrix products, arithmetic and copies ran while one was open for 0% of the time, Pallas kernels for 3%

profile of v7, /device:TPU:0, one launch (start us, length us, event | category | flops | bytes accessed | tf_op | source)
XLA Modules:
  0.0 45.5 jit_solution(14555620549394780288)
XLA Ops:
  0.6 0.0 copy-start.4
  0.6 0.0 copy-start.3
  0.7 0.0 copy-start.2
  0.7 0.0 copy-start
  0.7 0.0 copy-start.1
  0.7 0.7 %copy-done.4 = bf16[1280,8]{0,1:T(8,128)(2,1)S(1)} copy-done((bf16[1280,8]{0,1:T(8,128)(2,1)S(1)}, bf16[1280,8]{0,1:T(8,128)(2,1)}, u32[]{:S(2)}) %copy-start.4) | copy-done | bytes 20504
  1.4 0.4 copy-done.3
  1.7 0.2 copy-done.2
  1.9 1.0 %shard_map.69 = (bf16[16,2,1280]{2,1,0:T(2,128)(2,1)S(1)}, f32[8,256]{1,0:T(8,128)S(1)}, f32[8,256]{1,0:T(8,128)S(1)}) custom-call(bf16[256,1280]{1,0:T(8,128)(2,1)S(1)} %bitcast.6, bf16[256,1280]{1,0:T(8,128)(2,1)S(1)} %bitcast.8, bf16[8,1280]{1,0:T(8,128)(2,1)S(1)} %bitcast.10, f32[8,128]{1,0:T(8,128)S(1)} %shard_map.68.token_ref), custom_call_target="tpu_custom_call" | custom-call | flops 31457280 | bytes 1310720 | tf_op jit(solution)/shard_map/pallas_call | solution.py:110
  3.0 14.3 %all_to_all.15.got_ref = bf16[16,2,1280]{2,1,0:T(2,128)(2,1)S(1)} all-to-all(bf16[16,2,1280]{2,1,0:T(2,128)(2,1)S(1)} %get-tuple-element.11), channel_id=1, replica_groups=mesh['group'=2,'far'=4,'near'=2,'core'=2] {'far','near','core'}, dimensions={0} | all-to-all | bytes 163840 | tf_op jit(solution)/shard_map/all_to_all | solution.py:126
  17.3 0.0 copy-done
  17.3 0.0 copy-done.1
  17.3 2.7 %shard_map.70 = bf16[16,2,1280]{2,1,0:T(2,128)(2,1)S(1)} custom-call(bf16[16,2,1280]{2,1,0:T(2,128)(2,1)S(1)} %all_to_all.15.got_ref, bf16[1280,1280]{1,0:T(8,128)(2,1)S(1)} %copy-done, bf16[1280,1280]{1,0:T(8,128)(2,1)S(1)} %copy-done.1), custom_call_target="tpu_custom_call" | custom-call | flops 209715200 | bytes 6553600 | tf_op jit(solution)/shard_map/pallas_call | solution.py:110
  20.1 9.7 %all_to_all.16.back_ref = bf16[16,2,1280]{2,1,0:T(2,128)(2,1)S(1)} all-to-all(bf16[16,2,1280]{2,1,0:T(2,128)(2,1)S(1)} %shard_map.70), channel_id=1, replica_groups=mesh['group'=2,'far'=4,'near'=2,'core'=2] {'far','near','core'}, dimensions={0} | all-to-all | bytes 163840 | tf_op jit(solution)/shard_map/all_to_all | solution.py:126
  29.8 0.7 %shard_map.71 = (f32[8,640]{1,0:T(8,128)S(1)}, f32[8,640]{1,0:T(8,128)S(1)}, bf16[16,256]{1,0:T(8,128)(2,1)S(1)}, bf16[16,1280]{1,0:T(8,128)(2,1)S(1)}) custom-call(bf16[256,1280]{1,0:T(8,128)(2,1)S(1)} %bitcast.7, bf16[256,1280]{1,0:T(8,128)(2,1)S(1)} %bitcast.9, bf16[8,1280]{1,0:T(8,128)(2,1)S(1)} %bitcast.11, f32[8,256]{1,0:T(8,128)S(1)} %get-tuple-element.9.dispatch_ref, ...), custom_call_target="tpu_custom_call" | custom-call | flops 31457280 | bytes 1310720 | tf_op jit(solution)/shard_map/pallas_call | solution.py:110
  30.5 0.0 collective-permute-start
  30.5 1.2 %collective-permute-done = f32[8,640]{1,0:T(8,128)S(1)} collective-permute-done((f32[8,640]{1,0:T(8,128)S(1)}, f32[8,640]{1,0:T(8,128)S(1)}, u32[]{:S(2)}, u32[]{:S(2)}) %collective-permute-start) | collective-permute-done | bytes 20512 | tf_op jit(solution)/shard_map/ppermute | solution.py:122
  31.7 0.0 collective-permute-start.1
  31.7 3.8 %collective-permute-done.1 = f32[8,640]{1,0:T(8,128)S(1)} collective-permute-done((f32[8,640]{1,0:T(8,128)S(1)}, f32[8,640]{1,0:T(8,128)S(1)}, u32[]{:S(2)}, u32[]{:S(2)}) %collective-permute-start.1) | collective-permute-done | bytes 20512 | tf_op jit(solution)/shard_map/ppermute | solution.py:122
  35.5 8.0 %all_to_all.17 = bf16[4,8,640]{2,1,0:T(8,128)(2,1)S(1)} all-to-all(bf16[4,8,640]{2,1,0:T(8,128)(2,1)S(1)} %broadcast_in_dim.10), channel_id=1, replica_groups=mesh['group'=2,'far'=4,'near'=2,'core'=2] {'far'}, dimensions={0} | all-to-all | bytes 81920 | tf_op jit(solution)/shard_map/all_to_all | solution.py:126
  43.6 0.1 collective-permute-start.2
  43.6 1.2 %shard_map.72 = bf16[256,1280]{1,0:T(8,128)(2,1)} custom-call(bf16[16,256]{1,0:T(8,128)(2,1)S(1)} %get-tuple-element.12.left_ref, bf16[16,1280]{1,0:T(8,128)(2,1)S(1)} %get-tuple-element.13.right_ref), custom_call_target="tpu_custom_call" | custom-call | flops 10485760 | bytes 655360 | tf_op jit(solution)/shard_map/pallas_call | solution.py:110
  44.9 0.0 collective-permute-done.2
  44.9 0.6 %maximum_bitcast_fusion = f32[1280,8]{0,1:T(8,128)} fusion(f32[8,640]{1,0:T(8,128)S(1)} %get-tuple-element.17, f32[8,640]{1,0:T(8,128)S(1)} %get-tuple-element.16), kind=kLoop, calls=%fused_computation.1 | loop fusion | flops 10240 | bytes 81920 | tf_op jit(solution)/shard_map/transpose | solution.py:200
  (6 shorter events, 0.0 us)
Async XLA Ops:
  0.6 0.7 %copy-start.4 = (bf16[1280,8]{0,1:T(8,128)(2,1)S(1)}, bf16[1280,8]{0,1:T(8,128)(2,1)}, u32[]{:S(2)}) copy-start(bf16[1280,8]{0,1:T(8,128)(2,1)} %param.7) | copy-start | bytes 61444
  0.6 1.1 %copy-start.3 = (bf16[1,256,1280]{2,1,0:T(8,128)(2,1)S(1)}, bf16[1,256,1280]{2,1,0:T(8,128)(2,1)}, u32[]{:S(2)}) copy-start(bf16[1,256,1280]{2,1,0:T(8,128)(2,1)} %param.6) | copy-start | bytes 1966084
  0.7 1.3 %copy-start.2 = (bf16[1,256,1280]{2,1,0:T(8,128)(2,1)S(1)}, bf16[1,256,1280]{2,1,0:T(8,128)(2,1)}, u32[]{:S(2)}) copy-start(bf16[1,256,1280]{2,1,0:T(8,128)(2,1)} %param.5) | copy-start | bytes 1966084
  0.7 16.7 %copy-start = (bf16[1280,1280]{1,0:T(8,128)(2,1)S(1)}, bf16[1280,1280]{1,0:T(8,128)(2,1)}, u32[]{:S(2)}) copy-start(bf16[1280,1280]{1,0:T(8,128)(2,1)} %in_weight_ref.1) | copy-start | bytes 9830404
  0.7 16.7 %copy-start.1 = (bf16[1280,1280]{1,0:T(8,128)(2,1)S(1)}, bf16[1280,1280]{1,0:T(8,128)(2,1)}, u32[]{:S(2)}) copy-start(bf16[1280,1280]{1,0:T(8,128)(2,1)} %out_weight_ref.1) | copy-start | bytes 9830404
  30.5 1.2 %collective-permute-start = (f32[8,640]{1,0:T(8,128)S(1)}, f32[8,640]{1,0:T(8,128)S(1)}, u32[]{:S(2)}, u32[]{:S(2)}) collective-permute-start(f32[8,640]{1,0:T(8,128)S(1)} %get-tuple-element.15), channel_id=1, source_target_pairs={{0,1},{1,0},{2,3},{3,2},{4,5},{5,4},{6,7},{7,6},{8,9},{9,8},{10,11... | collective-permute-start | bytes 61448 | tf_op jit(solution)/shard_map/ppermute | solution.py:122
  31.7 3.8 %collective-permute-start.1 = (f32[8,640]{1,0:T(8,128)S(1)}, f32[8,640]{1,0:T(8,128)S(1)}, u32[]{:S(2)}, u32[]{:S(2)}) collective-permute-start(f32[8,640]{1,0:T(8,128)S(1)} %add.6), channel_id=1, source_target_pairs={{0,2},{2,0},{1,3},{3,1},{4,6},{6,4},{5,7},{7,5},{8,10},{10,8},{9,1... | collective-permute-start | bytes 61448 | tf_op jit(solution)/shard_map/ppermute | solution.py:122
  43.6 1.3 %collective-permute-start.2 = (f32[8,640]{1,0:T(8,128)S(1)}, f32[8,640]{1,0:T(8,128)S(1)}, u32[]{:S(2)}, u32[]{:S(2)}) collective-permute-start(f32[8,640]{1,0:T(8,128)S(1)} %convert_reduce_fusion), channel_id=1, source_target_pairs={{0,1},{1,0},{2,3},{3,2},{4,5},{5,4},{6,7},{7,6},{8,9},{9,8},{10,11... | collective-permute-start | bytes 61448 | tf_op jit(solution)/shard_map/ppermute | solution.py:122

commit v8 on v7

--- a/solution.py
+++ b/solution.py
@@ -7,13 +7,14 @@
 from jax.experimental.pallas import tpu as pltpu
 from jax.sharding import PartitionSpec as P
 
-EXPERT = ("far", "near", "core")
+EXPERT = ("chip", "core")
 F32 = jnp.float32
 BF16 = jnp.bfloat16
 NN = (((1,), (0,)), ((), ()))
 NT = (((1,), (1,)), ((), ()))
 TN = (((0,), (0,)), ((), ()))
 AHEAD_FLOPS = 3 * 10**10
+CHUNK = 256
 
 
 def dot(a, b, dims):
@@ -24,21 +25,21 @@
     token_ref[...] = jnp.zeros(token_ref.shape, F32)
 
 
-def slots_kernel(
-    tokens_ref, grad_ref, router_ref, token_ref, sent_ref, dispatch_ref, combine_ref
-):
-    slots = router_ref.shape[0]
+def slots_kernel(tokens_ref, router_ref, token_ref, slot_in_ref, dispatch_ref, combine_ref):
     logits = dot(router_ref[...], tokens_ref[...], NT)
     over_patches = jnp.exp(logits - jnp.max(logits, axis=1, keepdims=True))
     dispatch = over_patches / jnp.sum(over_patches, axis=1, keepdims=True)
     over_slots = jnp.exp(logits - jnp.max(logits, axis=0, keepdims=True))
-    combine = over_slots / jnp.sum(over_slots, axis=0, keepdims=True)
     dispatch_ref[...] = dispatch
-    combine_ref[...] = combine
-    slot_in = dot(dispatch.astype(BF16), tokens_ref[...], NN)
-    slot_grad = dot(combine.astype(BF16), grad_ref[...], NN)
-    for s in range(slots):
-        message = jnp.concatenate([slot_in[s : s + 1], slot_grad[s : s + 1]], axis=0).astype(BF16)
+    combine_ref[...] = over_slots / jnp.sum(over_slots, axis=0, keepdims=True)
+    slot_in_ref[...] = dot(dispatch.astype(BF16), tokens_ref[...], NN)
+
+
+def messages_kernel(grad_ref, combine_ref, slot_in_ref, sent_ref):
+    slot_grad = dot(combine_ref[...].astype(BF16), grad_ref[...], NN)
+    for s in range(slot_in_ref.shape[0]):
+        rows = [slot_in_ref[s : s + 1], slot_grad[s : s + 1]]
+        message = jnp.concatenate(rows, axis=0).astype(BF16)
         for half in range(2):
             sent_ref[2 * s + half] = message
 
@@ -51,14 +52,22 @@
         message = got_ref[k].astype(F32)
         in_rows_ref[k : k + 1] = message[0:1]
         grad_rows_ref[k : k + 1] = message[1:2]
-    hidden = dot(in_rows_ref[...].astype(BF16), in_weight_ref[...], NN)
-    act_grad = dot(grad_rows_ref[...].astype(BF16), out_weight_ref[...], NT)
-    normal_cdf = 0.5 * (1.0 + lax.erf(hidden * (1.0 / math.sqrt(2.0))))
-    normal_pdf = jnp.exp(-0.5 * hidden * hidden) * (1.0 / math.sqrt(2.0 * math.pi))
-    activation = (hidden * normal_cdf).astype(BF16)
-    hidden_grad = (act_grad * (normal_cdf + hidden * normal_pdf)).astype(BF16)
-    part_out = dot(activation, out_weight_ref[...], NN)
-    part_in = dot(hidden_grad, in_weight_ref[...], NT)
+    in_rows = in_rows_ref[...].astype(BF16)
+    grad_rows = grad_rows_ref[...].astype(BF16)
+    hidden_units = in_weight_ref.shape[1]
+    step = CHUNK if hidden_units % CHUNK == 0 else hidden_units
+    part_out = part_in = 0.0
+    for start in range(0, hidden_units, step):
+        columns = in_weight_ref[:, start : start + step]
+        weight_rows = out_weight_ref[start : start + step]
+        hidden = dot(in_rows, columns, NN)
+        act_grad = dot(grad_rows, weight_rows, NT)
+        normal_cdf = 0.5 * (1.0 + lax.erf(hidden * (1.0 / math.sqrt(2.0))))
+        normal_pdf = jnp.exp(-0.5 * hidden * hidden) * (1.0 / math.sqrt(2.0 * math.pi))
+        activation = (hidden * normal_cdf).astype(BF16)
+        hidden_grad = (act_grad * (normal_cdf + hidden * normal_pdf)).astype(BF16)
+        part_out = part_out + dot(activation, weight_rows, NN)
+        part_in = part_in + dot(hidden_grad, columns, NT)
     for k in range(images):
         rows = [part_out[k : k + 1], part_in[k : k + 1]]
         parts_ref[k] = jnp.concatenate(rows, axis=0).astype(BF16)
@@ -126,14 +135,6 @@
     return lax.all_to_all(value, axes, split_axis=0, concat_axis=0, tiled=True)
 
 
-def sum_over(value, axis):
-    count = lax.axis_size(axis)
-    if count == 2:
-        return value + swap(value, axis)
-    terms = exchange(jnp.broadcast_to(value.astype(BF16)[None], (count,) + value.shape), axis)
-    return jnp.sum(terms.astype(F32), axis=0)
-
-
 def per_device(tokens, out_grad, router, in_weight, out_weight):
     _, patches, width = tokens.shape
     hidden = in_weight.shape[1]
@@ -145,15 +146,23 @@
     image_bytes = 2 * patches * width
     weight_bytes = 2 * width * hidden
     (token,) = call(first_kernel, [((8, 128), F32)], [], (AHEAD_FLOPS, image_bytes))
-    sent, dispatch, combine = call(
+    slot_in, dispatch, combine = call(
         slots_kernel,
-        [((2 * slots, 2, width), BF16), ((slots, patches), F32), ((slots, patches), F32)],
+        [((slots, width), F32), ((slots, patches), F32), ((slots, patches), F32)],
         [],
-        (12 * patches * width * slots, 2 * image_bytes),
+        (8 * patches * width * slots, image_bytes),
         tokens,
-        out_grad,
         router_rows,
         token,
+    )
+    (sent,) = call(
+        messages_kernel,
+        [((2 * slots, 2, width), BF16)],
+        [],
+        (4 * patches * width * slots, image_bytes),
+        out_grad,
+        combine,
+        slot_in,
     )
     got = exchange(sent, EXPERT)
     (parts,) = call(
@@ -183,12 +192,7 @@
         combine,
         back,
     )
-    total = sum_over(sum_over(kept + swap(given, "core"), "near"), "far")
-    other = swap(total, "core")
-    first = lax.axis_index("core") == 0
-    router_grad = jnp.concatenate(
-        [jnp.where(first, total, other), jnp.where(first, other, total)], axis=1
-    )
+    pair = (kept + swap(given, "core")).astype(BF16)
     (tokens_grad,) = call(
         tokens_kernel,
         [((patches, width), BF16)],
@@ -197,13 +201,17 @@
         left,
         right,
     )
+    terms = exchange(jnp.broadcast_to(pair[None], (2 * chips,) + pair.shape), EXPERT)
+    terms = terms.reshape((chips, 2) + pair.shape).astype(F32)
+    router_grad = jnp.concatenate(
+        [jnp.sum(terms[:, 0], axis=0), jnp.sum(terms[:, 1], axis=0)], axis=1
+    )
     return (tokens_grad[None], router_grad.T)
 
 
 def solution(mesh):
     chips = mesh.shape["expert"] // 2
-    near = 2 ** (int(math.log2(chips)) // 2)
-    shape = (mesh.shape["group"], chips // near, near, 2)
+    shape = (mesh.shape["group"], chips, 2)
     fine = jax.sharding.Mesh(mesh.devices.reshape(shape), ("group",) + EXPERT)
     images = P(("group",) + EXPERT, None, None)
     in_specs = (images, images, P(), P(None, EXPERT), P(EXPERT, None))

time: 45.8 us -> 45.8 us (level)
  blocking collectives: 32.1 us -> 24.2 us
  starting transfers between devices: 0.09 us -> 3.53 us
  waiting for transfers between devices: 5 us -> 8.44 us
  Pallas kernels: 5.66 us -> 6.22 us
  local copies, waits for them, and re-layouts: 1.26 us -> 1.74 us
    all_to_all x3 -> x2, blocking collectives: 32.1 us -> 24.2 us  [exchange(): return lax.all_to_all(value, axes, split_axis=0, concat_axis=0, tiled=True)]
    all_to_all x0 -> x1, waiting for transfers between devices: none -> 7.22 us  [exchange(): return lax.all_to_all(value, axes, split_axis=0, concat_axis=0, tiled=True)]
    ppermute x3 -> x1, waiting for transfers between devices: 5 us -> 1.22 us  [swap(): return lax.ppermute(value, axis, [(0, 1), (1, 0)])]
    all_to_all x0 -> x1, starting transfers between devices: none -> 3.52 us  [exchange(): return lax.all_to_all(value, axes, split_axis=0, concat_axis=0, tiled=True)]
    broadcast_in_dim x1, local copies, waits for them, and re-layouts: 0.01 us -> 0.68 us  [per_device(): jnp.broadcast_to(pair[None], (2 * chips,) + pair.shape)]
    pallas_call x5 -> x6, Pallas kernels: 5.66 us -> 6.22 us  [call(): pl.pallas_call(kernel, out_shape=[jax.ShapeDtypeStruct(shape, dtype) for...]
  transfers between devices with their start and end apart: 3 -> 2, of which waited for: 2 -> 2; matrix products, arithmetic and copies ran while one was open for 0% -> 0% of each run, Pallas kernels for 3% -> 3%
where the time goes in v8:
time: 45.8 us; the launch traced here: 45.5 us
  blocking collectives  24.2 us (53%)
  waiting for transfers between devices  8.44 us (18%)
  Pallas kernels  6.22 us (14%)
  starting transfers between devices  3.53 us (8%)
  local copies, waits for them, and re-layouts  1.74 us (4%)
  between operations  0.73 us (2%)
  other arithmetic  0.67 us (1%)
    all_to_all x2, blocking collectives, exchange(): return lax.all_to_all(value, axes, split_axis=0, concat_axis=0, tiled=True)  24.2 us
    all_to_all x1, waiting for transfers between devices, exchange(): return lax.all_to_all(value, axes, split_axis=0, concat_axis=0, tiled=True)  7.22 us
    pallas_call x6, Pallas kernels, call(): pl.pallas_call(kernel, out_shape=[jax.ShapeDtypeStruct(shape, dtype) for...  6.22 us
    all_to_all x1, starting transfers between devices, exchange(): return lax.all_to_all(value, axes, split_axis=0, concat_axis=0, tiled=True)  3.52 us
    ppermute x1, waiting for transfers between devices, swap(): return lax.ppermute(value, axis, [(0, 1), (1, 0)])  1.22 us
    unnamed x10, local copies, waits for them, and re-layouts  1.06 us
  transfers between devices with their start and end apart: 2, of which 2 were waited for; matrix products, arithmetic and copies ran while one was open for 0% of the time, Pallas kernels for 3%

profile of v8, /device:TPU:0, one launch (start us, length us, event | category | flops | bytes accessed | tf_op | source)
XLA Modules:
  0.0 45.5 jit_solution(6764166450365817883)
XLA Ops:
  0.6 0.0 copy-start.4
  0.6 0.0 copy-start.2
  0.7 0.0 copy-start.3
  0.7 0.0 copy-start
  0.7 0.0 copy-start.1
  0.7 0.7 %copy-done.4 = bf16[1280,8]{0,1:T(8,128)(2,1)S(1)} copy-done((bf16[1280,8]{0,1:T(8,128)(2,1)S(1)}, bf16[1280,8]{0,1:T(8,128)(2,1)}, u32[]{:S(2)}) %copy-start.4) | copy-done | bytes 20504
  1.4 0.4 copy-done.2
  1.7 0.8 %shard_map.69 = (f32[8,1280]{1,0:T(8,128)S(1)}, f32[8,256]{1,0:T(8,128)S(1)}, f32[8,256]{1,0:T(8,128)S(1)}) custom-call(bf16[256,1280]{1,0:T(8,128)(2,1)S(1)} %bitcast.9, bf16[8,1280]{1,0:T(8,128)(2,1)S(1)} %bitcast.13, f32[8,128]{1,0:T(8,128)S(1)} %shard_map.68.token_ref), custom_call_target="tpu_custom_call" | custom-call | flops 20971520 | bytes 655360 | tf_op jit(solution)/shard_map/pallas_call | solution.py:119
  2.5 0.0 copy-done.3
  2.5 0.2 shard_map.70
  2.8 14.5 %all_to_all.15.got_ref = bf16[16,2,1280]{2,1,0:T(2,128)(2,1)S(1)} all-to-all(bf16[16,2,1280]{2,1,0:T(2,128)(2,1)S(1)} %shard_map.70), channel_id=1, replica_groups=mesh['group'=2,'chip'=8,'core'=2] {'chip','core'}, dimensions={0} | all-to-all | bytes 163840 | tf_op jit(solution)/shard_map/all_to_all | solution.py:135
  17.2 0.0 copy-done
  17.2 0.0 copy-done.1
  17.2 3.3 %shard_map.71 = bf16[16,2,1280]{2,1,0:T(2,128)(2,1)S(1)} custom-call(bf16[16,2,1280]{2,1,0:T(2,128)(2,1)S(1)} %all_to_all.15.got_ref, bf16[1280,1280]{1,0:T(8,128)(2,1)S(1)} %copy-done, bf16[1280,1280]{1,0:T(8,128)(2,1)S(1)} %copy-done.1), custom_call_target="tpu_custom_call" | custom-call | flops 209715200 | bytes 6553600 | tf_op jit(solution)/shard_map/pallas_call | solution.py:119
  20.6 9.7 %all_to_all.16.back_ref = bf16[16,2,1280]{2,1,0:T(2,128)(2,1)S(1)} all-to-all(bf16[16,2,1280]{2,1,0:T(2,128)(2,1)S(1)} %shard_map.71), channel_id=1, replica_groups=mesh['group'=2,'chip'=8,'core'=2] {'chip','core'}, dimensions={0} | all-to-all | bytes 163840 | tf_op jit(solution)/shard_map/all_to_all | solution.py:135
  30.3 0.7 %shard_map.72 = (f32[8,640]{1,0:T(8,128)S(1)}, f32[8,640]{1,0:T(8,128)S(1)}, bf16[16,256]{1,0:T(8,128)(2,1)S(1)}, bf16[16,1280]{1,0:T(8,128)(2,1)S(1)}) custom-call(bf16[256,1280]{1,0:T(8,128)(2,1)S(1)} %bitcast.10, bf16[256,1280]{1,0:T(8,128)(2,1)S(1)} %bitcast.12, bf16[8,1280]{1,0:T(8,128)(2,1)S(1)} %bitcast.14, ...), custom_call_target="tpu_custom_call" | custom-call | flops 31457280 | bytes 1310720 | tf_op jit(solution)/shard_map/pallas_call | solution.py:119
  31.0 0.0 collective-permute-start
  31.0 1.2 %collective-permute-done = f32[8,640]{1,0:T(8,128)S(1)} collective-permute-done((f32[8,640]{1,0:T(8,128)S(1)}, f32[8,640]{1,0:T(8,128)S(1)}, u32[]{:S(2)}, u32[]{:S(2)}) %collective-permute-start) | collective-permute-done | bytes 20512 | tf_op jit(solution)/shard_map/ppermute | solution.py:131
  32.2 0.7 %broadcast_in_dim.10 = bf16[16,8,640]{2,1,0:T(8,128)(2,1)} broadcast(bf16[8,640]{1,0:T(8,128)(2,1)S(1)} %add_convert_fusion), dimensions={1,2} | broadcast | bytes 174080 | tf_op jit(solution)/shard_map/broadcast_in_dim | solution.py:204
  32.9 3.5 %all-to-all-start.2 = ((bf16[16,8,640]{2,1,0:T(8,128)(2,1)}), bf16[16,8,640]{2,1,0:T(8,128)(2,1)S(1)}, u32[]{:S(2)}, u32[]{:S(2)}) async-start(bf16[16,8,640]{2,1,0:T(8,128)(2,1)} %broadcast_in_dim.10), calls=%async_computation.2 | async-start | bytes 327680 | tf_op jit(solution)/shard_map/all_to_all | solution.py:135
  36.4 1.2 %shard_map.73 = bf16[256,1280]{1,0:T(8,128)(2,1)} custom-call(bf16[16,256]{1,0:T(8,128)(2,1)S(1)} %get-tuple-element.12.left_ref, bf16[16,1280]{1,0:T(8,128)(2,1)S(1)} %get-tuple-element.13.right_ref), custom_call_target="tpu_custom_call" | custom-call | flops 10485760 | bytes 655360 | tf_op jit(solution)/shard_map/pallas_call | solution.py:119
  37.6 7.2 %all-to-all-done.2 = bf16[16,8,640]{2,1,0:T(8,128)(2,1)S(1)} async-done(((bf16[16,8,640]{2,1,0:T(8,128)(2,1)}), bf16[16,8,640]{2,1,0:T(8,128)(2,1)S(1)}, u32[]{:S(2)}, u32[]{:S(2)}) %all-to-all-start.2) | async-done | bytes 163872 | tf_op jit(solution)/shard_map/all_to_all | solution.py:135
  44.9 0.6 %maximum_bitcast_fusion = f32[1280,8]{0,1:T(8,128)} fusion(f32[8,640]{1,0:T(8,128)S(1)} %get-tuple-element.17, f32[8,640]{1,0:T(8,128)S(1)} %get-tuple-element.16), kind=kLoop, calls=%fused_computation.2 | loop fusion | flops 10240 | bytes 81920 | tf_op jit(solution)/shard_map/transpose | solution.py:209
  (4 shorter events, 0.1 us)
Async XLA Ops:
  0.6 0.7 %copy-start.4 = (bf16[1280,8]{0,1:T(8,128)(2,1)S(1)}, bf16[1280,8]{0,1:T(8,128)(2,1)}, u32[]{:S(2)}) copy-start(bf16[1280,8]{0,1:T(8,128)(2,1)} %param.7) | copy-start | bytes 61444
  0.6 1.1 %copy-start.2 = (bf16[1,256,1280]{2,1,0:T(8,128)(2,1)S(1)}, bf16[1,256,1280]{2,1,0:T(8,128)(2,1)}, u32[]{:S(2)}) copy-start(bf16[1,256,1280]{2,1,0:T(8,128)(2,1)} %param.5) | copy-start | bytes 1966084
  0.7 1.9 %copy-start.3 = (bf16[1,256,1280]{2,1,0:T(8,128)(2,1)S(1)}, bf16[1,256,1280]{2,1,0:T(8,128)(2,1)}, u32[]{:S(2)}) copy-start(bf16[1,256,1280]{2,1,0:T(8,128)(2,1)} %param.6) | copy-start | bytes 1966084
  0.7 16.6 %copy-start = (bf16[1280,1280]{1,0:T(8,128)(2,1)S(1)}, bf16[1280,1280]{1,0:T(8,128)(2,1)}, u32[]{:S(2)}) copy-start(bf16[1280,1280]{1,0:T(8,128)(2,1)} %in_weight_ref.1) | copy-start | bytes 9830404
  0.7 16.6 %copy-start.1 = (bf16[1280,1280]{1,0:T(8,128)(2,1)S(1)}, bf16[1280,1280]{1,0:T(8,128)(2,1)}, u32[]{:S(2)}) copy-start(bf16[1280,1280]{1,0:T(8,128)(2,1)} %out_weight_ref.1) | copy-start | bytes 9830404
  31.0 1.2 %collective-permute-start = (f32[8,640]{1,0:T(8,128)S(1)}, f32[8,640]{1,0:T(8,128)S(1)}, u32[]{:S(2)}, u32[]{:S(2)}) collective-permute-start(f32[8,640]{1,0:T(8,128)S(1)} %get-tuple-element.15), channel_id=1, source_target_pairs={{0,1},{1,0},{2,3},{3,2},{4,5},{5,4},{6,7},{7,6},{8,9},{9,8},{10,11... | collective-permute-start | bytes 61448 | tf_op jit(solution)/shard_map/ppermute | solution.py:131
  32.9 11.9 %all-to-all-start.2 = ((bf16[16,8,640]{2,1,0:T(8,128)(2,1)}), bf16[16,8,640]{2,1,0:T(8,128)(2,1)S(1)}, u32[]{:S(2)}, u32[]{:S(2)}) async-start(bf16[16,8,640]{2,1,0:T(8,128)(2,1)} %broadcast_in_dim.10), calls=%async_computation.2 | async-start | bytes 327680 | tf_op jit(solution)/shard_map/all_to_all | solution.py:135

commit v9 on v8

--- a/solution.py
+++ b/solution.py
@@ -7,14 +7,20 @@
 from jax.experimental.pallas import tpu as pltpu
 from jax.sharding import PartitionSpec as P
 
-EXPERT = ("chip", "core")
 F32 = jnp.float32
 BF16 = jnp.bfloat16
 NN = (((1,), (0,)), ((), ()))
 NT = (((1,), (1,)), ((), ()))
 TN = (((0,), (0,)), ((), ()))
 AHEAD_FLOPS = 3 * 10**10
-CHUNK = 256
+
+
+def place(chip, core, chips):
+    return 2 * (chips - 1 - chip) + core
+
+
+def listed(chips, cores):
+    return [2 * chip + core for chip in reversed(range(chips)) for core in cores]
 
 
 def dot(a, b, dims):
@@ -37,11 +43,12 @@
 
 def messages_kernel(grad_ref, combine_ref, slot_in_ref, sent_ref):
     slot_grad = dot(combine_ref[...].astype(BF16), grad_ref[...], NN)
-    for s in range(slot_in_ref.shape[0]):
+    slots = slot_in_ref.shape[0]
+    for s in range(slots):
         rows = [slot_in_ref[s : s + 1], slot_grad[s : s + 1]]
         message = jnp.concatenate(rows, axis=0).astype(BF16)
         for half in range(2):
-            sent_ref[2 * s + half] = message
+            sent_ref[place(s, half, slots)] = message
 
 
 def experts_kernel(
@@ -52,22 +59,14 @@
         message = got_ref[k].astype(F32)
         in_rows_ref[k : k + 1] = message[0:1]
         grad_rows_ref[k : k + 1] = message[1:2]
-    in_rows = in_rows_ref[...].astype(BF16)
-    grad_rows = grad_rows_ref[...].astype(BF16)
-    hidden_units = in_weight_ref.shape[1]
-    step = CHUNK if hidden_units % CHUNK == 0 else hidden_units
-    part_out = part_in = 0.0
-    for start in range(0, hidden_units, step):
-        columns = in_weight_ref[:, start : start + step]
-        weight_rows = out_weight_ref[start : start + step]
-        hidden = dot(in_rows, columns, NN)
-        act_grad = dot(grad_rows, weight_rows, NT)
-        normal_cdf = 0.5 * (1.0 + lax.erf(hidden * (1.0 / math.sqrt(2.0))))
-        normal_pdf = jnp.exp(-0.5 * hidden * hidden) * (1.0 / math.sqrt(2.0 * math.pi))
-        activation = (hidden * normal_cdf).astype(BF16)
-        hidden_grad = (act_grad * (normal_cdf + hidden * normal_pdf)).astype(BF16)
-        part_out = part_out + dot(activation, weight_rows, NN)
-        part_in = part_in + dot(hidden_grad, columns, NT)
+    hidden = dot(in_rows_ref[...].astype(BF16), in_weight_ref[...], NN)
+    act_grad = dot(grad_rows_ref[...].astype(BF16), out_weight_ref[...], NT)
+    normal_cdf = 0.5 * (1.0 + lax.erf(hidden * (1.0 / math.sqrt(2.0))))
+    normal_pdf = jnp.exp(-0.5 * hidden * hidden) * (1.0 / math.sqrt(2.0 * math.pi))
+    activation = (hidden * normal_cdf).astype(BF16)
+    hidden_grad = (act_grad * (normal_cdf + hidden * normal_pdf)).astype(BF16)
+    part_out = dot(activation, out_weight_ref[...], NN)
+    part_in = dot(hidden_grad, in_weight_ref[...], NT)
     for k in range(images):
         rows = [part_out[k : k + 1], part_in[k : k + 1]]
         parts_ref[k] = jnp.concatenate(rows, axis=0).astype(BF16)
@@ -89,7 +88,8 @@
 ):
     slots = router_ref.shape[0]
     for s in range(slots):
-        message = back_ref[2 * s].astype(F32) + back_ref[2 * s + 1].astype(F32)
+        first_half = back_ref[place(s, 0, slots)].astype(F32)
+        message = first_half + back_ref[place(s, 1, slots)].astype(F32)
         out_rows_ref[s : s + 1] = message[0:1]
         back_rows_ref[s : s + 1] = message[1:2]
     slot_back = back_rows_ref[...].astype(BF16)
@@ -102,7 +102,7 @@
     logits_grad = combine * (combine_grad - slot_sum) + dispatch * (dispatch_grad - patch_sum)
     part = dot(logits_grad.astype(BF16), tokens_ref[...], NN)
     half = part.shape[1] // 2
-    first = lax.axis_index("core") == 0
+    first = lax.axis_index("expert") % 2 == 0
     kept_ref[...] = jnp.where(first, part[:, :half], part[:, half:])
     given_ref[...] = jnp.where(first, part[:, half:], part[:, :half])
     left_ref[...] = jnp.concatenate([logits_grad, dispatch], axis=0).astype(BF16)
@@ -127,12 +127,15 @@
     )(*operands)
 
 
-def swap(value, axis):
-    return lax.ppermute(value, axis, [(0, 1), (1, 0)])
-
-
-def exchange(value, axes):
-    return lax.all_to_all(value, axes, split_axis=0, concat_axis=0, tiled=True)
+def swap_cores(value):
+    size = lax.axis_size("expert")
+    return lax.ppermute(value, "expert", [(i, i ^ 1) for i in range(size)])
+
+
+def exchange(value, groups):
+    return lax.all_to_all(
+        value, "expert", split_axis=0, concat_axis=0, tiled=True, axis_index_groups=groups
+    )
 
 
 def per_device(tokens, out_grad, router, in_weight, out_weight):
@@ -143,6 +146,8 @@
     tokens = tokens[0]
     out_grad = out_grad[0]
     router_rows = router.T
+    everybody = [listed(chips, (0, 1))]
+    same_core = [listed(chips, (0,)), listed(chips, (1,))]
     image_bytes = 2 * patches * width
     weight_bytes = 2 * width * hidden
     (token,) = call(first_kernel, [((8, 128), F32)], [], (AHEAD_FLOPS, image_bytes))
@@ -164,7 +169,7 @@
         combine,
         slot_in,
     )
-    got = exchange(sent, EXPERT)
+    got = exchange(sent, everybody)
     (parts,) = call(
         experts_kernel,
         [((2 * chips, 2, width), BF16)],
@@ -174,7 +179,7 @@
         in_weight,
         out_weight,
     )
-    back = exchange(parts, EXPERT)
+    back = exchange(parts, everybody)
     kept, given, left, right = call(
         logits_kernel,
         [
@@ -192,7 +197,14 @@
         combine,
         back,
     )
-    pair = (kept + swap(given, "core")).astype(BF16)
+    pair = (kept + swap_cores(given)).astype(BF16)
+    terms = exchange(jnp.broadcast_to(pair[None], (chips,) + pair.shape), same_core)
+    total = jnp.sum(terms.astype(F32), axis=0)
+    other = swap_cores(total)
+    first = lax.axis_index("expert") % 2 == 0
+    router_grad = jnp.concatenate(
+        [jnp.where(first, total, other), jnp.where(first, other, total)], axis=1
+    )
     (tokens_grad,) = call(
         tokens_kernel,
         [((patches, width), BF16)],
@@ -201,21 +213,13 @@
         left,
         right,
     )
-    terms = exchange(jnp.broadcast_to(pair[None], (2 * chips,) + pair.shape), EXPERT)
-    terms = terms.reshape((chips, 2) + pair.shape).astype(F32)
-    router_grad = jnp.concatenate(
-        [jnp.sum(terms[:, 0], axis=0), jnp.sum(terms[:, 1], axis=0)], axis=1
-    )
     return (tokens_grad[None], router_grad.T)
 
 
 def solution(mesh):
-    chips = mesh.shape["expert"] // 2
-    shape = (mesh.shape["group"], chips, 2)
-    fine = jax.sharding.Mesh(mesh.devices.reshape(shape), ("group",) + EXPERT)
-    images = P(("group",) + EXPERT, None, None)
-    in_specs = (images, images, P(), P(None, EXPERT), P(EXPERT, None))
+    images = P(("group", "expert"), None, None)
+    in_specs = (images, images, P(), P(None, "expert"), P("expert", None))
     out_specs = (images, P("group", None))
     return jax.shard_map(
-        per_device, mesh=fine, in_specs=in_specs, out_specs=out_specs, check_vma=False
-    )
+        per_device, mesh=mesh, in_specs=in_specs, out_specs=out_specs, check_vma=False
+    )

time: 45.8 us -> 40.9 us (0.89)
  waiting for transfers between devices: 8.44 us -> 1.08 us
  blocking collectives: 24.2 us -> 31.2 us
  starting transfers between devices: 3.53 us -> 0.24 us
  local copies, waits for them, and re-layouts: 1.74 us -> 1.07 us
  Pallas kernels: 6.22 us -> 5.63 us
    all_to_all x1 -> x0, waiting for transfers between devices: 7.22 us -> none  [exchange(): return lax.all_to_all(value, axes, split_axis=0, concat_axis=0, tiled=True)]
    all_to_all x2 -> x3, blocking collectives: 24.2 us -> 31.2 us  [exchange(): lax.all_to_all(value, 'expert', split_axis=0, concat_axis=0, tiled=True,...]
    all_to_all x1 -> x0, starting transfers between devices: 3.52 us -> none  [exchange(): return lax.all_to_all(value, axes, split_axis=0, concat_axis=0, tiled=True)]
    broadcast_in_dim x1, local copies, waits for them, and re-layouts: 0.68 us -> 0.01 us  [per_device(): jnp.broadcast_to(pair[None], (chips,) + pair.shape)]
    pallas_call x6, Pallas kernels: 6.22 us -> 5.63 us  [call(): pl.pallas_call(kernel, out_shape=[jax.ShapeDtypeStruct(shape, dtype) for...]
    ppermute x1 -> x2, waiting for transfers between devices: 1.22 us -> 1.08 us  [swap_cores(): return lax.ppermute(value, 'expert', [(i, i ^ 1) for i in range(size)])]
  transfers between devices with their start and end apart: 2 -> 2, of which waited for: 2 -> 1; matrix products, arithmetic and copies ran while one was open for 0% -> 0% of each run, Pallas kernels for 3% -> 3%
where the time goes in v9:
time: 40.9 us; the launch traced here: 40.6 us
  blocking collectives  31.2 us (76%)
  Pallas kernels  5.63 us (14%)
  waiting for transfers between devices  1.08 us (3%)
  local copies, waits for them, and re-layouts  1.07 us (3%)
  between operations  0.73 us (2%)
  other arithmetic  0.65 us (2%)
    all_to_all x3, blocking collectives, exchange(): lax.all_to_all(value, 'expert', split_axis=0, concat_axis=0, tiled=True,...  31.2 us
    pallas_call x6, Pallas kernels, call(): pl.pallas_call(kernel, out_shape=[jax.ShapeDtypeStruct(shape, dtype) for...  5.63 us
    ppermute x2, waiting for transfers between devices, swap_cores(): return lax.ppermute(value, 'expert', [(i, i ^ 1) for i in range(size)])  1.08 us
    unnamed x10, local copies, waits for them, and re-layouts  1.06 us
  transfers between devices with their start and end apart: 2, of which 1 were waited for; matrix products, arithmetic and copies ran while one was open for 0% of the time, Pallas kernels for 3%

profile of v9, /device:TPU:0, one launch (start us, length us, event | category | flops | bytes accessed | tf_op | source)
XLA Modules:
  0.0 40.6 jit_solution(15690710315098169485)
XLA Ops:
  0.6 0.0 copy-start.4
  0.6 0.0 copy-start.2
  0.7 0.0 copy-start.3
  0.7 0.0 copy-start
  0.7 0.0 copy-start.1
  0.7 0.7 %copy-done.4 = bf16[1280,8]{0,1:T(8,128)(2,1)S(1)} copy-done((bf16[1280,8]{0,1:T(8,128)(2,1)S(1)}, bf16[1280,8]{0,1:T(8,128)(2,1)}, u32[]{:S(2)}) %copy-start.4) | copy-done | bytes 20504
  1.4 0.4 copy-done.2
  1.7 0.8 %shard_map.69 = (f32[8,1280]{1,0:T(8,128)S(1)}, f32[8,256]{1,0:T(8,128)S(1)}, f32[8,256]{1,0:T(8,128)S(1)}) custom-call(bf16[256,1280]{1,0:T(8,128)(2,1)S(1)} %bitcast.6, bf16[8,1280]{1,0:T(8,128)(2,1)S(1)} %bitcast.10, f32[8,128]{1,0:T(8,128)S(1)} %shard_map.68.token_ref), custom_call_target="tpu_custom_call" | custom-call | flops 20971520 | bytes 655360 | tf_op jit(solution)/shard_map/pallas_call | solution.py:119
  2.5 0.0 copy-done.3
  2.5 0.2 shard_map.70
  2.8 11.8 %all_to_all.15.got_ref = bf16[16,2,1280]{2,1,0:T(2,128)(2,1)S(1)} all-to-all(bf16[16,2,1280]{2,1,0:T(2,128)(2,1)S(1)} %shard_map.70), channel_id=1, replica_groups={{14,15,12,13,10,11,8,9,6,7,4,5,2,3,0,1},{30,31,28,29,26,27,24,25,22,23,..., dimensions={0} | all-to-all | bytes 163840 | tf_op jit(solution)/shard_map/all_to_all | solution.py:136
  14.6 0.0 copy-done
  14.6 0.0 copy-done.1
  14.6 2.7 %shard_map.71 = bf16[16,2,1280]{2,1,0:T(2,128)(2,1)S(1)} custom-call(bf16[16,2,1280]{2,1,0:T(2,128)(2,1)S(1)} %all_to_all.15.got_ref, bf16[1280,1280]{1,0:T(8,128)(2,1)S(1)} %copy-done, bf16[1280,1280]{1,0:T(8,128)(2,1)S(1)} %copy-done.1), custom_call_target="tpu_custom_call" | custom-call | flops 209715200 | bytes 6553600 | tf_op jit(solution)/shard_map/pallas_call | solution.py:119
  17.3 9.7 %all_to_all.16.back_ref = bf16[16,2,1280]{2,1,0:T(2,128)(2,1)S(1)} all-to-all(bf16[16,2,1280]{2,1,0:T(2,128)(2,1)S(1)} %shard_map.71), channel_id=1, replica_groups={{14,15,12,13,10,11,8,9,6,7,4,5,2,3,0,1},{30,31,28,29,26,27,24,25,22,23,..., dimensions={0} | all-to-all | bytes 163840 | tf_op jit(solution)/shard_map/all_to_all | solution.py:136
  27.1 0.7 %shard_map.72 = (f32[8,640]{1,0:T(8,128)S(1)}, f32[8,640]{1,0:T(8,128)S(1)}, bf16[16,256]{1,0:T(8,128)(2,1)S(1)}, bf16[16,1280]{1,0:T(8,128)(2,1)S(1)}) custom-call(bf16[256,1280]{1,0:T(8,128)(2,1)S(1)} %bitcast.7, bf16[256,1280]{1,0:T(8,128)(2,1)S(1)} %bitcast.9, bf16[8,1280]{1,0:T(8,128)(2,1)S(1)} %bitcast.11, f32[8,256]{1,0:T(8,128)S(1)} %get-tuple-element.9.dispatch_ref, ...), custom_call_target="tpu_custom_call" | custom-call | flops 31457280 | bytes 1310720 | tf_op jit(solution)/shard_map/pallas_call | solution.py:119
  27.7 0.2 collective-permute-start
  27.9 1.1 %collective-permute-done = f32[8,640]{1,0:T(8,128)S(1)} collective-permute-done((f32[8,640]{1,0:T(8,128)S(1)}, f32[8,640]{1,0:T(8,128)S(1)}, u32[]{:S(2)}, u32[]{:S(2)}) %collective-permute-start) | collective-permute-done | bytes 20512 | tf_op jit(solution)/shard_map/ppermute | solution.py:132
  29.0 9.7 %all_to_all.17 = bf16[8,8,640]{2,1,0:T(8,128)(2,1)S(1)} all-to-all(bf16[8,8,640]{2,1,0:T(8,128)(2,1)S(1)} %broadcast_in_dim.10), channel_id=1, replica_groups={{14,12,10,8,6,4,2,0},{15,13,11,9,7,5,3,1},{30,28,26,24,22,20,18,16},{31..., dimensions={0} | all-to-all | bytes 163840 | tf_op jit(solution)/shard_map/all_to_all | solution.py:136
  38.7 0.1 collective-permute-start.1
  38.8 1.2 %shard_map.73 = bf16[256,1280]{1,0:T(8,128)(2,1)} custom-call(bf16[16,256]{1,0:T(8,128)(2,1)S(1)} %get-tuple-element.12.left_ref, bf16[16,1280]{1,0:T(8,128)(2,1)S(1)} %get-tuple-element.13.right_ref), custom_call_target="tpu_custom_call" | custom-call | flops 10485760 | bytes 655360 | tf_op jit(solution)/shard_map/pallas_call | solution.py:119
  40.0 0.0 collective-permute-done.1
  40.0 0.6 %maximum_bitcast_fusion = f32[1280,8]{0,1:T(8,128)} fusion(f32[8,640]{1,0:T(8,128)S(1)} %get-tuple-element.17, f32[8,640]{1,0:T(8,128)S(1)} %get-tuple-element.16), kind=kLoop, calls=%fused_computation.1 | loop fusion | flops 10240 | bytes 81920 | tf_op jit(solution)/shard_map/transpose | solution.py:216
  (5 shorter events, 0.0 us)
Async XLA Ops:
  0.6 0.7 %copy-start.4 = (bf16[1280,8]{0,1:T(8,128)(2,1)S(1)}, bf16[1280,8]{0,1:T(8,128)(2,1)}, u32[]{:S(2)}) copy-start(bf16[1280,8]{0,1:T(8,128)(2,1)} %param.7) | copy-start | bytes 61444
  0.6 1.1 %copy-start.2 = (bf16[1,256,1280]{2,1,0:T(8,128)(2,1)S(1)}, bf16[1,256,1280]{2,1,0:T(8,128)(2,1)}, u32[]{:S(2)}) copy-start(bf16[1,256,1280]{2,1,0:T(8,128)(2,1)} %param.5) | copy-start | bytes 1966084
  0.7 1.9 %copy-start.3 = (bf16[1,256,1280]{2,1,0:T(8,128)(2,1)S(1)}, bf16[1,256,1280]{2,1,0:T(8,128)(2,1)}, u32[]{:S(2)}) copy-start(bf16[1,256,1280]{2,1,0:T(8,128)(2,1)} %param.6) | copy-start | bytes 1966084
  0.7 13.9 %copy-start = (bf16[1280,1280]{1,0:T(8,128)(2,1)S(1)}, bf16[1280,1280]{1,0:T(8,128)(2,1)}, u32[]{:S(2)}) copy-start(bf16[1280,1280]{1,0:T(8,128)(2,1)} %in_weight_ref.1) | copy-start | bytes 9830404
  0.7 13.9 %copy-start.1 = (bf16[1280,1280]{1,0:T(8,128)(2,1)S(1)}, bf16[1280,1280]{1,0:T(8,128)(2,1)}, u32[]{:S(2)}) copy-start(bf16[1280,1280]{1,0:T(8,128)(2,1)} %out_weight_ref.1) | copy-start | bytes 9830404
  27.7 1.2 %collective-permute-start = (f32[8,640]{1,0:T(8,128)S(1)}, f32[8,640]{1,0:T(8,128)S(1)}, u32[]{:S(2)}, u32[]{:S(2)}) collective-permute-start(f32[8,640]{1,0:T(8,128)S(1)} %get-tuple-element.15), channel_id=1, source_target_pairs={{0,1},{1,0},{2,3},{3,2},{4,5},{5,4},{6,7},{7,6},{8,9},{9,8},{10,11... | collective-permute-start | bytes 61448 | tf_op jit(solution)/shard_map/ppermute | solution.py:132
  38.7 1.3 %collective-permute-start.1 = (f32[8,640]{1,0:T(8,128)S(1)}, f32[8,640]{1,0:T(8,128)S(1)}, u32[]{:S(2)}, u32[]{:S(2)}) collective-permute-start(f32[8,640]{1,0:T(8,128)S(1)} %convert_reduce_fusion), channel_id=1, source_target_pairs={{0,1},{1,0},{2,3},{3,2},{4,5},{5,4},{6,7},{7,6},{8,9},{9,8},{10,11... | collective-permute-start | bytes 61448 | tf_op jit(solution)/shard_map/ppermute | solution.py:132

commit v10 on v9

--- a/solution.py
+++ b/solution.py
@@ -15,12 +15,16 @@
 AHEAD_FLOPS = 3 * 10**10
 
 
+def chip_order(chips):
+    return [k // 2 if k % 2 else chips - 1 - k // 2 for k in range(chips)]
+
+
 def place(chip, core, chips):
-    return 2 * (chips - 1 - chip) + core
+    return 2 * chip_order(chips).index(chip) + core
 
 
 def listed(chips, cores):
-    return [2 * chip + core for chip in reversed(range(chips)) for core in cores]
+    return [2 * chip + core for chip in chip_order(chips) for core in cores]
 
 
 def dot(a, b, dims):

time: 40.9 us -> 39.7 us (0.971)
  blocking collectives: 31.2 us -> 30.1 us
    all_to_all x3, blocking collectives: 31.2 us -> 30.1 us  [exchange(): lax.all_to_all(value, 'expert', split_axis=0, concat_axis=0, tiled=True,...]
where the time goes in v10:
time: 39.7 us; the launch traced here: 39.5 us
  blocking collectives  30.1 us (76%)
  Pallas kernels  5.63 us (14%)
  local copies, waits for them, and re-layouts  1.07 us (3%)
  waiting for transfers between devices  0.93 us (2%)
  between operations  0.73 us (2%)
  other arithmetic  0.65 us (2%)
    all_to_all x3, blocking collectives, exchange(): lax.all_to_all(value, 'expert', split_axis=0, concat_axis=0, tiled=True,...  30.1 us
    pallas_call x6, Pallas kernels, call(): pl.pallas_call(kernel, out_shape=[jax.ShapeDtypeStruct(shape, dtype) for...  5.63 us
    unnamed x10, local copies, waits for them, and re-layouts  1.06 us
    ppermute x2, waiting for transfers between devices, swap_cores(): return lax.ppermute(value, 'expert', [(i, i ^ 1) for i in range(size)])  0.93 us
  transfers between devices with their start and end apart: 2, of which 1 were waited for; matrix products, arithmetic and copies ran while one was open for 0% of the time, Pallas kernels for 3%

profile of v10, /device:TPU:0, one launch (start us, length us, event | category | flops | bytes accessed | tf_op | source)
XLA Modules:
  0.0 39.5 jit_solution(11170759053771277871)
XLA Ops:
  0.6 0.0 copy-start.4
  0.6 0.0 copy-start.2
  0.7 0.0 copy-start.3
  0.7 0.0 copy-start
  0.7 0.0 copy-start.1
  0.7 0.7 %copy-done.4 = bf16[1280,8]{0,1:T(8,128)(2,1)S(1)} copy-done((bf16[1280,8]{0,1:T(8,128)(2,1)S(1)}, bf16[1280,8]{0,1:T(8,128)(2,1)}, u32[]{:S(2)}) %copy-start.4) | copy-done | bytes 20504
  1.4 0.4 copy-done.2
  1.7 0.8 %shard_map.69 = (f32[8,1280]{1,0:T(8,128)S(1)}, f32[8,256]{1,0:T(8,128)S(1)}, f32[8,256]{1,0:T(8,128)S(1)}) custom-call(bf16[256,1280]{1,0:T(8,128)(2,1)S(1)} %bitcast.6, bf16[8,1280]{1,0:T(8,128)(2,1)S(1)} %bitcast.10, f32[8,128]{1,0:T(8,128)S(1)} %shard_map.68.token_ref), custom_call_target="tpu_custom_call" | custom-call | flops 20971520 | bytes 655360 | tf_op jit(solution)/shard_map/pallas_call | solution.py:123
  2.5 0.0 copy-done.3
  2.5 0.2 shard_map.70
  2.8 11.5 %all_to_all.15.got_ref = bf16[16,2,1280]{2,1,0:T(2,128)(2,1)S(1)} all-to-all(bf16[16,2,1280]{2,1,0:T(2,128)(2,1)S(1)} %shard_map.70), channel_id=1, replica_groups={{14,15,0,1,12,13,2,3,10,11,4,5,8,9,6,7},{30,31,16,17,28,29,18,19,26,27,..., dimensions={0} | all-to-all | bytes 163840 | tf_op jit(solution)/shard_map/all_to_all | solution.py:140
  14.3 0.0 copy-done
  14.3 0.0 copy-done.1
  14.3 2.7 %shard_map.71 = bf16[16,2,1280]{2,1,0:T(2,128)(2,1)S(1)} custom-call(bf16[16,2,1280]{2,1,0:T(2,128)(2,1)S(1)} %all_to_all.15.got_ref, bf16[1280,1280]{1,0:T(8,128)(2,1)S(1)} %copy-done, bf16[1280,1280]{1,0:T(8,128)(2,1)S(1)} %copy-done.1), custom_call_target="tpu_custom_call" | custom-call | flops 209715200 | bytes 6553600 | tf_op jit(solution)/shard_map/pallas_call | solution.py:123
  17.0 9.3 %all_to_all.16.back_ref = bf16[16,2,1280]{2,1,0:T(2,128)(2,1)S(1)} all-to-all(bf16[16,2,1280]{2,1,0:T(2,128)(2,1)S(1)} %shard_map.71), channel_id=1, replica_groups={{14,15,0,1,12,13,2,3,10,11,4,5,8,9,6,7},{30,31,16,17,28,29,18,19,26,27,..., dimensions={0} | all-to-all | bytes 163840 | tf_op jit(solution)/shard_map/all_to_all | solution.py:140
  26.3 0.7 %shard_map.72 = (f32[8,640]{1,0:T(8,128)S(1)}, f32[8,640]{1,0:T(8,128)S(1)}, bf16[16,256]{1,0:T(8,128)(2,1)S(1)}, bf16[16,1280]{1,0:T(8,128)(2,1)S(1)}) custom-call(bf16[256,1280]{1,0:T(8,128)(2,1)S(1)} %bitcast.7, bf16[256,1280]{1,0:T(8,128)(2,1)S(1)} %bitcast.9, bf16[8,1280]{1,0:T(8,128)(2,1)S(1)} %bitcast.11, f32[8,256]{1,0:T(8,128)S(1)} %get-tuple-element.9.dispatch_ref, ...), custom_call_target="tpu_custom_call" | custom-call | flops 31457280 | bytes 1310720 | tf_op jit(solution)/shard_map/pallas_call | solution.py:123
  27.0 0.3 collective-permute-start
  27.3 0.9 %collective-permute-done = f32[8,640]{1,0:T(8,128)S(1)} collective-permute-done((f32[8,640]{1,0:T(8,128)S(1)}, f32[8,640]{1,0:T(8,128)S(1)}, u32[]{:S(2)}, u32[]{:S(2)}) %collective-permute-start) | collective-permute-done | bytes 20512 | tf_op jit(solution)/shard_map/ppermute | solution.py:136
  28.2 9.3 %all_to_all.17 = bf16[8,8,640]{2,1,0:T(8,128)(2,1)S(1)} all-to-all(bf16[8,8,640]{2,1,0:T(8,128)(2,1)S(1)} %broadcast_in_dim.10), channel_id=1, replica_groups={{14,0,12,2,10,4,8,6},{15,1,13,3,11,5,9,7},{30,16,28,18,26,20,24,22},{31..., dimensions={0} | all-to-all | bytes 163840 | tf_op jit(solution)/shard_map/all_to_all | solution.py:140
  37.5 0.1 collective-permute-start.1
  37.6 1.2 %shard_map.73 = bf16[256,1280]{1,0:T(8,128)(2,1)} custom-call(bf16[16,256]{1,0:T(8,128)(2,1)S(1)} %get-tuple-element.12.left_ref, bf16[16,1280]{1,0:T(8,128)(2,1)S(1)} %get-tuple-element.13.right_ref), custom_call_target="tpu_custom_call" | custom-call | flops 10485760 | bytes 655360 | tf_op jit(solution)/shard_map/pallas_call | solution.py:123
  38.8 0.0 collective-permute-done.1
  38.8 0.6 %maximum_bitcast_fusion = f32[1280,8]{0,1:T(8,128)} fusion(f32[8,640]{1,0:T(8,128)S(1)} %get-tuple-element.17, f32[8,640]{1,0:T(8,128)S(1)} %get-tuple-element.16), kind=kLoop, calls=%fused_computation.1 | loop fusion | flops 10240 | bytes 81920 | tf_op jit(solution)/shard_map/transpose | solution.py:220
  (5 shorter events, 0.0 us)
Async XLA Ops:
  0.6 0.7 %copy-start.4 = (bf16[1280,8]{0,1:T(8,128)(2,1)S(1)}, bf16[1280,8]{0,1:T(8,128)(2,1)}, u32[]{:S(2)}) copy-start(bf16[1280,8]{0,1:T(8,128)(2,1)} %param.7) | copy-start | bytes 61444
  0.6 1.1 %copy-start.2 = (bf16[1,256,1280]{2,1,0:T(8,128)(2,1)S(1)}, bf16[1,256,1280]{2,1,0:T(8,128)(2,1)}, u32[]{:S(2)}) copy-start(bf16[1,256,1280]{2,1,0:T(8,128)(2,1)} %param.5) | copy-start | bytes 1966084
  0.7 1.9 %copy-start.3 = (bf16[1,256,1280]{2,1,0:T(8,128)(2,1)S(1)}, bf16[1,256,1280]{2,1,0:T(8,128)(2,1)}, u32[]{:S(2)}) copy-start(bf16[1,256,1280]{2,1,0:T(8,128)(2,1)} %param.6) | copy-start | bytes 1966084
  0.7 13.6 %copy-start = (bf16[1280,1280]{1,0:T(8,128)(2,1)S(1)}, bf16[1280,1280]{1,0:T(8,128)(2,1)}, u32[]{:S(2)}) copy-start(bf16[1280,1280]{1,0:T(8,128)(2,1)} %in_weight_ref.1) | copy-start | bytes 9830404
  0.7 13.6 %copy-start.1 = (bf16[1280,1280]{1,0:T(8,128)(2,1)S(1)}, bf16[1280,1280]{1,0:T(8,128)(2,1)}, u32[]{:S(2)}) copy-start(bf16[1280,1280]{1,0:T(8,128)(2,1)} %out_weight_ref.1) | copy-start | bytes 9830404
  27.0 1.2 %collective-permute-start = (f32[8,640]{1,0:T(8,128)S(1)}, f32[8,640]{1,0:T(8,128)S(1)}, u32[]{:S(2)}, u32[]{:S(2)}) collective-permute-start(f32[8,640]{1,0:T(8,128)S(1)} %get-tuple-element.15), channel_id=1, source_target_pairs={{0,1},{1,0},{2,3},{3,2},{4,5},{5,4},{6,7},{7,6},{8,9},{9,8},{10,11... | collective-permute-start | bytes 61448 | tf_op jit(solution)/shard_map/ppermute | solution.py:136
  37.5 1.3 %collective-permute-start.1 = (f32[8,640]{1,0:T(8,128)S(1)}, f32[8,640]{1,0:T(8,128)S(1)}, u32[]{:S(2)}, u32[]{:S(2)}) collective-permute-start(f32[8,640]{1,0:T(8,128)S(1)} %convert_reduce_fusion), channel_id=1, source_target_pairs={{0,1},{1,0},{2,3},{3,2},{4,5},{5,4},{6,7},{7,6},{8,9},{9,8},{10,11... | collective-permute-start | bytes 61448 | tf_op jit(solution)/shard_map/ppermute | solution.py:136

commit v11 on v9

--- a/solution.py
+++ b/solution.py
@@ -15,12 +15,12 @@
 AHEAD_FLOPS = 3 * 10**10
 
 
-def place(chip, core, chips):
-    return 2 * (chips - 1 - chip) + core
-
-
-def listed(chips, cores):
-    return [2 * chip + core for chip in reversed(range(chips)) for core in cores]
+OUT_STEP, BACK_STEP, SUM_STEP = 1, 5, 1
+
+
+def listed(step, chips, cores=(0, 1)):
+    order = [(chips - 1 + step * k) % chips for k in range(chips)]
+    return [2 * chip + core for chip in order for core in cores]
 
 
 def dot(a, b, dims):
@@ -44,17 +44,20 @@
 def messages_kernel(grad_ref, combine_ref, slot_in_ref, sent_ref):
     slot_grad = dot(combine_ref[...].astype(BF16), grad_ref[...], NN)
     slots = slot_in_ref.shape[0]
+    order = listed(OUT_STEP, slots)
     for s in range(slots):
         rows = [slot_in_ref[s : s + 1], slot_grad[s : s + 1]]
         message = jnp.concatenate(rows, axis=0).astype(BF16)
         for half in range(2):
-            sent_ref[place(s, half, slots)] = message
+            sent_ref[order.index(2 * s + half)] = message
 
 
 def experts_kernel(
     got_ref, in_weight_ref, out_weight_ref, parts_ref, in_rows_ref, grad_rows_ref
 ):
     images = got_ref.shape[0]
+    out_order = listed(OUT_STEP, images // 2)
+    back_order = listed(BACK_STEP, images // 2)
     for k in range(images):
         message = got_ref[k].astype(F32)
         in_rows_ref[k : k + 1] = message[0:1]
@@ -69,7 +72,7 @@
     part_in = dot(hidden_grad, in_weight_ref[...], NT)
     for k in range(images):
         rows = [part_out[k : k + 1], part_in[k : k + 1]]
-        parts_ref[k] = jnp.concatenate(rows, axis=0).astype(BF16)
+        parts_ref[back_order.index(out_order[k])] = jnp.concatenate(rows, axis=0).astype(BF16)
 
 
 def logits_kernel(
@@ -87,9 +90,10 @@
     back_rows_ref,
 ):
     slots = router_ref.shape[0]
+    order = listed(BACK_STEP, slots)
     for s in range(slots):
-        first_half = back_ref[place(s, 0, slots)].astype(F32)
-        message = first_half + back_ref[place(s, 1, slots)].astype(F32)
+        halves = [back_ref[order.index(2 * s + half)].astype(F32) for half in range(2)]
+        message = halves[0] + halves[1]
         out_rows_ref[s : s + 1] = message[0:1]
         back_rows_ref[s : s + 1] = message[1:2]
     slot_back = back_rows_ref[...].astype(BF16)
@@ -146,8 +150,6 @@
     tokens = tokens[0]
     out_grad = out_grad[0]
     router_rows = router.T
-    everybody = [listed(chips, (0, 1))]
-    same_core = [listed(chips, (0,)), listed(chips, (1,))]
     image_bytes = 2 * patches * width
     weight_bytes = 2 * width * hidden
     (token,) = call(first_kernel, [((8, 128), F32)], [], (AHEAD_FLOPS, image_bytes))
@@ -169,7 +171,7 @@
         combine,
         slot_in,
     )
-    got = exchange(sent, everybody)
+    got = exchange(sent, [listed(OUT_STEP, chips)])
     (parts,) = call(
         experts_kernel,
         [((2 * chips, 2, width), BF16)],
@@ -179,7 +181,7 @@
         in_weight,
         out_weight,
     )
-    back = exchange(parts, everybody)
+    back = exchange(parts, [listed(BACK_STEP, chips)])
     kept, given, left, right = call(
         logits_kernel,
         [
@@ -198,6 +200,7 @@
         back,
     )
     pair = (kept + swap_cores(given)).astype(BF16)
+    same_core = [listed(SUM_STEP, chips, (core,)) for core in range(2)]
     terms = exchange(jnp.broadcast_to(pair[None], (chips,) + pair.shape), same_core)
     total = jnp.sum(terms.astype(F32), axis=0)
     other = swap_cores(total)

time: 40.9 us -> 40 us (0.978)
  blocking collectives: 31.2 us -> 30.4 us
    all_to_all x3, blocking collectives: 31.2 us -> 30.4 us  [exchange(): lax.all_to_all(value, 'expert', split_axis=0, concat_axis=0, tiled=True,...]
where the time goes in v11:
time: 40 us; the launch traced here: 39.7 us
  blocking collectives  30.4 us (76%)
  Pallas kernels  5.63 us (14%)
  local copies, waits for them, and re-layouts  1.07 us (3%)
  waiting for transfers between devices  1.06 us (3%)
  between operations  0.73 us (2%)
  other arithmetic  0.65 us (2%)
    all_to_all x3, blocking collectives, exchange(): lax.all_to_all(value, 'expert', split_axis=0, concat_axis=0, tiled=True,...  30.4 us
    pallas_call x6, Pallas kernels, call(): pl.pallas_call(kernel, out_shape=[jax.ShapeDtypeStruct(shape, dtype) for...  5.63 us
    unnamed x10, local copies, waits for them, and re-layouts  1.06 us
    ppermute x2, waiting for transfers between devices, swap_cores(): return lax.ppermute(value, 'expert', [(i, i ^ 1) for i in range(size)])  1.06 us
  transfers between devices with their start and end apart: 2, of which 1 were waited for; matrix products, arithmetic and copies ran while one was open for 0% of the time, Pallas kernels for 3%

profile of v11, /device:TPU:0, one launch (start us, length us, event | category | flops | bytes accessed | tf_op | source)
XLA Modules:
  0.0 39.7 jit_solution(30139706497638280)
XLA Ops:
  0.6 0.0 copy-start.4
  0.6 0.0 copy-start.2
  0.7 0.0 copy-start.3
  0.7 0.0 copy-start
  0.7 0.0 copy-start.1
  0.7 0.7 %copy-done.4 = bf16[1280,8]{0,1:T(8,128)(2,1)S(1)} copy-done((bf16[1280,8]{0,1:T(8,128)(2,1)S(1)}, bf16[1280,8]{0,1:T(8,128)(2,1)}, u32[]{:S(2)}) %copy-start.4) | copy-done | bytes 20504
  1.4 0.4 copy-done.2
  1.7 0.8 %shard_map.69 = (f32[8,1280]{1,0:T(8,128)S(1)}, f32[8,256]{1,0:T(8,128)S(1)}, f32[8,256]{1,0:T(8,128)S(1)}) custom-call(bf16[256,1280]{1,0:T(8,128)(2,1)S(1)} %bitcast.6, bf16[8,1280]{1,0:T(8,128)(2,1)S(1)} %bitcast.10, f32[8,128]{1,0:T(8,128)S(1)} %shard_map.68.token_ref), custom_call_target="tpu_custom_call" | custom-call | flops 20971520 | bytes 655360 | tf_op jit(solution)/shard_map/pallas_call | solution.py:123
  2.5 0.0 copy-done.3
  2.5 0.2 shard_map.70
  2.8 11.6 %all_to_all.15.got_ref = bf16[16,2,1280]{2,1,0:T(2,128)(2,1)S(1)} all-to-all(bf16[16,2,1280]{2,1,0:T(2,128)(2,1)S(1)} %shard_map.70), channel_id=1, replica_groups={{14,15,0,1,2,3,4,5,6,7,8,9,10,11,12,13},{30,31,16,17,18,19,20,21,22,23,..., dimensions={0} | all-to-all | bytes 163840 | tf_op jit(solution)/shard_map/all_to_all | solution.py:140
  14.4 0.0 copy-done
  14.4 0.0 copy-done.1
  14.4 2.7 %shard_map.71 = bf16[16,2,1280]{2,1,0:T(2,128)(2,1)S(1)} custom-call(bf16[16,2,1280]{2,1,0:T(2,128)(2,1)S(1)} %all_to_all.15.got_ref, bf16[1280,1280]{1,0:T(8,128)(2,1)S(1)} %copy-done, bf16[1280,1280]{1,0:T(8,128)(2,1)S(1)} %copy-done.1), custom_call_target="tpu_custom_call" | custom-call | flops 209715200 | bytes 6553600 | tf_op jit(solution)/shard_map/pallas_call | solution.py:123
  17.1 9.3 %all_to_all.16.back_ref = bf16[16,2,1280]{2,1,0:T(2,128)(2,1)S(1)} all-to-all(bf16[16,2,1280]{2,1,0:T(2,128)(2,1)S(1)} %shard_map.71), channel_id=1, replica_groups={{14,15,8,9,2,3,12,13,6,7,0,1,10,11,4,5},{30,31,24,25,18,19,28,29,22,23,..., dimensions={0} | all-to-all | bytes 163840 | tf_op jit(solution)/shard_map/all_to_all | solution.py:140
  26.5 0.7 %shard_map.72 = (f32[8,640]{1,0:T(8,128)S(1)}, f32[8,640]{1,0:T(8,128)S(1)}, bf16[16,256]{1,0:T(8,128)(2,1)S(1)}, bf16[16,1280]{1,0:T(8,128)(2,1)S(1)}) custom-call(bf16[256,1280]{1,0:T(8,128)(2,1)S(1)} %bitcast.7, bf16[256,1280]{1,0:T(8,128)(2,1)S(1)} %bitcast.9, bf16[8,1280]{1,0:T(8,128)(2,1)S(1)} %bitcast.11, f32[8,256]{1,0:T(8,128)S(1)} %get-tuple-element.9.dispatch_ref, ...), custom_call_target="tpu_custom_call" | custom-call | flops 31457280 | bytes 1310720 | tf_op jit(solution)/shard_map/pallas_call | solution.py:123
  27.1 0.2 collective-permute-start
  27.3 1.1 %collective-permute-done = f32[8,640]{1,0:T(8,128)S(1)} collective-permute-done((f32[8,640]{1,0:T(8,128)S(1)}, f32[8,640]{1,0:T(8,128)S(1)}, u32[]{:S(2)}, u32[]{:S(2)}) %collective-permute-start) | collective-permute-done | bytes 20512 | tf_op jit(solution)/shard_map/ppermute | solution.py:136
  28.4 9.4 %all_to_all.17 = bf16[8,8,640]{2,1,0:T(8,128)(2,1)S(1)} all-to-all(bf16[8,8,640]{2,1,0:T(8,128)(2,1)S(1)} %broadcast_in_dim.10), channel_id=1, replica_groups={{14,0,2,4,6,8,10,12},{15,1,3,5,7,9,11,13},{30,16,18,20,22,24,26,28},{31..., dimensions={0} | all-to-all | bytes 163840 | tf_op jit(solution)/shard_map/all_to_all | solution.py:140
  37.8 0.1 collective-permute-start.1
  37.9 1.2 %shard_map.73 = bf16[256,1280]{1,0:T(8,128)(2,1)} custom-call(bf16[16,256]{1,0:T(8,128)(2,1)S(1)} %get-tuple-element.12.left_ref, bf16[16,1280]{1,0:T(8,128)(2,1)S(1)} %get-tuple-element.13.right_ref), custom_call_target="tpu_custom_call" | custom-call | flops 10485760 | bytes 655360 | tf_op jit(solution)/shard_map/pallas_call | solution.py:123
  39.1 0.0 collective-permute-done.1
  39.1 0.6 %maximum_bitcast_fusion = f32[1280,8]{0,1:T(8,128)} fusion(f32[8,640]{1,0:T(8,128)S(1)} %get-tuple-element.17, f32[8,640]{1,0:T(8,128)S(1)} %get-tuple-element.16), kind=kLoop, calls=%fused_computation.1 | loop fusion | flops 10240 | bytes 81920 | tf_op jit(solution)/shard_map/transpose | solution.py:219
  (5 shorter events, 0.0 us)
Async XLA Ops:
  0.6 0.7 %copy-start.4 = (bf16[1280,8]{0,1:T(8,128)(2,1)S(1)}, bf16[1280,8]{0,1:T(8,128)(2,1)}, u32[]{:S(2)}) copy-start(bf16[1280,8]{0,1:T(8,128)(2,1)} %param.7) | copy-start | bytes 61444
  0.6 1.1 %copy-start.2 = (bf16[1,256,1280]{2,1,0:T(8,128)(2,1)S(1)}, bf16[1,256,1280]{2,1,0:T(8,128)(2,1)}, u32[]{:S(2)}) copy-start(bf16[1,256,1280]{2,1,0:T(8,128)(2,1)} %param.5) | copy-start | bytes 1966084
  0.7 1.9 %copy-start.3 = (bf16[1,256,1280]{2,1,0:T(8,128)(2,1)S(1)}, bf16[1,256,1280]{2,1,0:T(8,128)(2,1)}, u32[]{:S(2)}) copy-start(bf16[1,256,1280]{2,1,0:T(8,128)(2,1)} %param.6) | copy-start | bytes 1966084
  0.7 13.8 %copy-start = (bf16[1280,1280]{1,0:T(8,128)(2,1)S(1)}, bf16[1280,1280]{1,0:T(8,128)(2,1)}, u32[]{:S(2)}) copy-start(bf16[1280,1280]{1,0:T(8,128)(2,1)} %in_weight_ref.1) | copy-start | bytes 9830404
  0.7 13.7 %copy-start.1 = (bf16[1280,1280]{1,0:T(8,128)(2,1)S(1)}, bf16[1280,1280]{1,0:T(8,128)(2,1)}, u32[]{:S(2)}) copy-start(bf16[1280,1280]{1,0:T(8,128)(2,1)} %out_weight_ref.1) | copy-start | bytes 9830404
  27.1 1.2 %collective-permute-start = (f32[8,640]{1,0:T(8,128)S(1)}, f32[8,640]{1,0:T(8,128)S(1)}, u32[]{:S(2)}, u32[]{:S(2)}) collective-permute-start(f32[8,640]{1,0:T(8,128)S(1)} %get-tuple-element.15), channel_id=1, source_target_pairs={{0,1},{1,0},{2,3},{3,2},{4,5},{5,4},{6,7},{7,6},{8,9},{9,8},{10,11... | collective-permute-start | bytes 61448 | tf_op jit(solution)/shard_map/ppermute | solution.py:136
  37.8 1.3 %collective-permute-start.1 = (f32[8,640]{1,0:T(8,128)S(1)}, f32[8,640]{1,0:T(8,128)S(1)}, u32[]{:S(2)}, u32[]{:S(2)}) collective-permute-start(f32[8,640]{1,0:T(8,128)S(1)} %convert_reduce_fusion), channel_id=1, source_target_pairs={{0,1},{1,0},{2,3},{3,2},{4,5},{5,4},{6,7},{7,6},{8,9},{9,8},{10,11... | collective-permute-start | bytes 61448 | tf_op jit(solution)/shard_map/ppermute | solution.py:136

commit v12 on v10

--- a/solution.py
+++ b/solution.py
@@ -19,12 +19,16 @@
     return [k // 2 if k % 2 else chips - 1 - k // 2 for k in range(chips)]
 
 
-def place(chip, core, chips):
-    return 2 * chip_order(chips).index(chip) + core
-
-
-def listed(chips, cores):
-    return [2 * chip + core for chip in chip_order(chips) for core in cores]
+def everybody(chips):
+    return [2 * chip + core for chip in chip_order(chips) for core in (1, 0)]
+
+
+def half_of(device, chips):
+    return (device + device // (2 * chips - 2)) % 2
+
+
+def summers(chips, half):
+    return [device for device in everybody(chips) if half_of(device, chips) == half]
 
 
 def dot(a, b, dims):
@@ -48,11 +52,12 @@
 def messages_kernel(grad_ref, combine_ref, slot_in_ref, sent_ref):
     slot_grad = dot(combine_ref[...].astype(BF16), grad_ref[...], NN)
     slots = slot_in_ref.shape[0]
+    order = everybody(slots)
     for s in range(slots):
         rows = [slot_in_ref[s : s + 1], slot_grad[s : s + 1]]
         message = jnp.concatenate(rows, axis=0).astype(BF16)
         for half in range(2):
-            sent_ref[place(s, half, slots)] = message
+            sent_ref[order.index(2 * s + half)] = message
 
 
 def experts_kernel(
@@ -91,9 +96,10 @@
     back_rows_ref,
 ):
     slots = router_ref.shape[0]
+    order = everybody(slots)
     for s in range(slots):
-        first_half = back_ref[place(s, 0, slots)].astype(F32)
-        message = first_half + back_ref[place(s, 1, slots)].astype(F32)
+        halves = [back_ref[order.index(2 * s + half)].astype(F32) for half in range(2)]
+        message = halves[0] + halves[1]
         out_rows_ref[s : s + 1] = message[0:1]
         back_rows_ref[s : s + 1] = message[1:2]
     slot_back = back_rows_ref[...].astype(BF16)
@@ -106,7 +112,7 @@
     logits_grad = combine * (combine_grad - slot_sum) + dispatch * (dispatch_grad - patch_sum)
     part = dot(logits_grad.astype(BF16), tokens_ref[...], NN)
     half = part.shape[1] // 2
-    first = lax.axis_index("expert") % 2 == 0
+    first = half_of(lax.axis_index("expert"), slots) == 0
     kept_ref[...] = jnp.where(first, part[:, :half], part[:, half:])
     given_ref[...] = jnp.where(first, part[:, half:], part[:, :half])
     left_ref[...] = jnp.concatenate([logits_grad, dispatch], axis=0).astype(BF16)
@@ -150,8 +156,6 @@
     tokens = tokens[0]
     out_grad = out_grad[0]
     router_rows = router.T
-    everybody = [listed(chips, (0, 1))]
-    same_core = [listed(chips, (0,)), listed(chips, (1,))]
     image_bytes = 2 * patches * width
     weight_bytes = 2 * width * hidden
     (token,) = call(first_kernel, [((8, 128), F32)], [], (AHEAD_FLOPS, image_bytes))
@@ -173,7 +177,7 @@
         combine,
         slot_in,
     )
-    got = exchange(sent, everybody)
+    got = exchange(sent, [everybody(chips)])
     (parts,) = call(
         experts_kernel,
         [((2 * chips, 2, width), BF16)],
@@ -183,7 +187,7 @@
         in_weight,
         out_weight,
     )
-    back = exchange(parts, everybody)
+    back = exchange(parts, [everybody(chips)])
     kept, given, left, right = call(
         logits_kernel,
         [
@@ -202,10 +206,11 @@
         back,
     )
     pair = (kept + swap_cores(given)).astype(BF16)
-    terms = exchange(jnp.broadcast_to(pair[None], (chips,) + pair.shape), same_core)
+    groups = [summers(chips, half) for half in range(2)]
+    terms = exchange(jnp.broadcast_to(pair[None], (chips,) + pair.shape), groups)
     total = jnp.sum(terms.astype(F32), axis=0)
     other = swap_cores(total)
-    first = lax.axis_index("expert") % 2 == 0
+    first = half_of(lax.axis_index("expert"), chips) == 0
     router_grad = jnp.concatenate(
         [jnp.where(first, total, other), jnp.where(first, other, total)], axis=1
     )

time: 39.7 us -> 39 us (0.982)
  blocking collectives: 30.1 us -> 29.3 us
    all_to_all x3, blocking collectives: 30.1 us -> 29.3 us  [exchange(): lax.all_to_all(value, 'expert', split_axis=0, concat_axis=0, tiled=True,...]
where the time goes in v12:
time: 39 us; the launch traced here: 38.7 us
  blocking collectives  29.3 us (75%)
  Pallas kernels  5.63 us (14%)
  local copies, waits for them, and re-layouts  1.07 us (3%)
  waiting for transfers between devices  1 us (3%)
  between operations  0.76 us (2%)
  other arithmetic  0.65 us (2%)
    all_to_all x3, blocking collectives, exchange(): lax.all_to_all(value, 'expert', split_axis=0, concat_axis=0, tiled=True,...  29.3 us
    pallas_call x6, Pallas kernels, call(): pl.pallas_call(kernel, out_shape=[jax.ShapeDtypeStruct(shape, dtype) for...  5.63 us
    unnamed x10, local copies, waits for them, and re-layouts  1.06 us
    ppermute x2, waiting for transfers between devices, swap_cores(): return lax.ppermute(value, 'expert', [(i, i ^ 1) for i in range(size)])  1 us
  transfers between devices with their start and end apart: 2, of which 1 were waited for; matrix products, arithmetic and copies ran while one was open for 0% of the time, Pallas kernels for 3%

profile of v12, /device:TPU:0, one launch (start us, length us, event | category | flops | bytes accessed | tf_op | source)
XLA Modules:
  0.0 38.7 jit_solution(6353185745965582663)
XLA Ops:
  0.6 0.0 copy-start.4
  0.6 0.0 copy-start.2
  0.7 0.0 copy-start.3
  0.7 0.0 copy-start
  0.7 0.0 copy-start.1
  0.7 0.7 %copy-done.4 = bf16[1280,8]{0,1:T(8,128)(2,1)S(1)} copy-done((bf16[1280,8]{0,1:T(8,128)(2,1)S(1)}, bf16[1280,8]{0,1:T(8,128)(2,1)}, u32[]{:S(2)}) %copy-start.4) | copy-done | bytes 20504
  1.4 0.4 copy-done.2
  1.7 0.8 %shard_map.69 = (f32[8,1280]{1,0:T(8,128)S(1)}, f32[8,256]{1,0:T(8,128)S(1)}, f32[8,256]{1,0:T(8,128)S(1)}) custom-call(bf16[256,1280]{1,0:T(8,128)(2,1)S(1)} %bitcast.6, bf16[8,1280]{1,0:T(8,128)(2,1)S(1)} %bitcast.10, f32[8,128]{1,0:T(8,128)S(1)} %shard_map.68.token_ref), custom_call_target="tpu_custom_call" | custom-call | flops 20971520 | bytes 655360 | tf_op jit(solution)/shard_map/pallas_call | solution.py:129
  2.5 0.0 copy-done.3
  2.5 0.2 shard_map.70
  2.8 11.0 %all_to_all.15.got_ref = bf16[16,2,1280]{2,1,0:T(2,128)(2,1)S(1)} all-to-all(bf16[16,2,1280]{2,1,0:T(2,128)(2,1)S(1)} %shard_map.70), channel_id=1, replica_groups={{15,14,1,0,13,12,3,2,11,10,5,4,9,8,7,6},{31,30,17,16,29,28,19,18,27,26,..., dimensions={0} | all-to-all | bytes 163840 | tf_op jit(solution)/shard_map/all_to_all | solution.py:146
  13.7 0.0 copy-done
  13.7 0.0 copy-done.1
  13.7 2.7 %shard_map.71 = bf16[16,2,1280]{2,1,0:T(2,128)(2,1)S(1)} custom-call(bf16[16,2,1280]{2,1,0:T(2,128)(2,1)S(1)} %all_to_all.15.got_ref, bf16[1280,1280]{1,0:T(8,128)(2,1)S(1)} %copy-done, bf16[1280,1280]{1,0:T(8,128)(2,1)S(1)} %copy-done.1), custom_call_target="tpu_custom_call" | custom-call | flops 209715200 | bytes 6553600 | tf_op jit(solution)/shard_map/pallas_call | solution.py:129
  16.5 9.0 %all_to_all.16.back_ref = bf16[16,2,1280]{2,1,0:T(2,128)(2,1)S(1)} all-to-all(bf16[16,2,1280]{2,1,0:T(2,128)(2,1)S(1)} %shard_map.71), channel_id=1, replica_groups={{15,14,1,0,13,12,3,2,11,10,5,4,9,8,7,6},{31,30,17,16,29,28,19,18,27,26,..., dimensions={0} | all-to-all | bytes 163840 | tf_op jit(solution)/shard_map/all_to_all | solution.py:146
  25.5 0.7 %shard_map.72 = (f32[8,640]{1,0:T(8,128)S(1)}, f32[8,640]{1,0:T(8,128)S(1)}, bf16[16,256]{1,0:T(8,128)(2,1)S(1)}, bf16[16,1280]{1,0:T(8,128)(2,1)S(1)}) custom-call(bf16[256,1280]{1,0:T(8,128)(2,1)S(1)} %bitcast.7, bf16[256,1280]{1,0:T(8,128)(2,1)S(1)} %bitcast.9, bf16[8,1280]{1,0:T(8,128)(2,1)S(1)} %bitcast.11, f32[8,256]{1,0:T(8,128)S(1)} %get-tuple-element.9.dispatch_ref, ...), custom_call_target="tpu_custom_call" | custom-call | flops 31457280 | bytes 1310720 | tf_op jit(solution)/shard_map/pallas_call | solution.py:129
  26.2 0.2 collective-permute-start
  26.4 1.0 %collective-permute-done = f32[8,640]{1,0:T(8,128)S(1)} collective-permute-done((f32[8,640]{1,0:T(8,128)S(1)}, f32[8,640]{1,0:T(8,128)S(1)}, u32[]{:S(2)}, u32[]{:S(2)}) %collective-permute-start) | collective-permute-done | bytes 20512 | tf_op jit(solution)/shard_map/ppermute | solution.py:142
  27.4 9.3 %all_to_all.17 = bf16[8,8,640]{2,1,0:T(8,128)(2,1)S(1)} all-to-all(bf16[8,8,640]{2,1,0:T(8,128)(2,1)S(1)} %broadcast_in_dim.10), channel_id=1, replica_groups={{15,0,12,2,10,4,8,6},{14,1,13,3,11,5,9,7},{31,16,28,18,26,20,24,22},{30..., dimensions={0} | all-to-all | bytes 163840 | tf_op jit(solution)/shard_map/all_to_all | solution.py:146
  36.8 0.1 collective-permute-start.1
  36.9 1.2 %shard_map.73 = bf16[256,1280]{1,0:T(8,128)(2,1)} custom-call(bf16[16,256]{1,0:T(8,128)(2,1)S(1)} %get-tuple-element.12.left_ref, bf16[16,1280]{1,0:T(8,128)(2,1)S(1)} %get-tuple-element.13.right_ref), custom_call_target="tpu_custom_call" | custom-call | flops 10485760 | bytes 655360 | tf_op jit(solution)/shard_map/pallas_call | solution.py:129
  38.1 0.0 collective-permute-done.1
  38.1 0.6 %maximum_bitcast_fusion = f32[1280,8]{0,1:T(8,128)} fusion(f32[8,640]{1,0:T(8,128)S(1)} %get-tuple-element.17, f32[8,640]{1,0:T(8,128)S(1)} %get-tuple-element.16), kind=kLoop, calls=%fused_computation.1 | loop fusion | flops 10240 | bytes 81920 | tf_op jit(solution)/shard_map/transpose | solution.py:225
  (5 shorter events, 0.0 us)
Async XLA Ops:
  0.6 0.7 %copy-start.4 = (bf16[1280,8]{0,1:T(8,128)(2,1)S(1)}, bf16[1280,8]{0,1:T(8,128)(2,1)}, u32[]{:S(2)}) copy-start(bf16[1280,8]{0,1:T(8,128)(2,1)} %param.7) | copy-start | bytes 61444
  0.6 1.1 %copy-start.2 = (bf16[1,256,1280]{2,1,0:T(8,128)(2,1)S(1)}, bf16[1,256,1280]{2,1,0:T(8,128)(2,1)}, u32[]{:S(2)}) copy-start(bf16[1,256,1280]{2,1,0:T(8,128)(2,1)} %param.5) | copy-start | bytes 1966084
  0.7 1.9 %copy-start.3 = (bf16[1,256,1280]{2,1,0:T(8,128)(2,1)S(1)}, bf16[1,256,1280]{2,1,0:T(8,128)(2,1)}, u32[]{:S(2)}) copy-start(bf16[1,256,1280]{2,1,0:T(8,128)(2,1)} %param.6) | copy-start | bytes 1966084
  0.7 13.1 %copy-start = (bf16[1280,1280]{1,0:T(8,128)(2,1)S(1)}, bf16[1280,1280]{1,0:T(8,128)(2,1)}, u32[]{:S(2)}) copy-start(bf16[1280,1280]{1,0:T(8,128)(2,1)} %in_weight_ref.1) | copy-start | bytes 9830404
  0.7 13.1 %copy-start.1 = (bf16[1280,1280]{1,0:T(8,128)(2,1)S(1)}, bf16[1280,1280]{1,0:T(8,128)(2,1)}, u32[]{:S(2)}) copy-start(bf16[1280,1280]{1,0:T(8,128)(2,1)} %out_weight_ref.1) | copy-start | bytes 9830404
  26.2 1.2 %collective-permute-start = (f32[8,640]{1,0:T(8,128)S(1)}, f32[8,640]{1,0:T(8,128)S(1)}, u32[]{:S(2)}, u32[]{:S(2)}) collective-permute-start(f32[8,640]{1,0:T(8,128)S(1)} %get-tuple-element.15), channel_id=1, source_target_pairs={{0,1},{1,0},{2,3},{3,2},{4,5},{5,4},{6,7},{7,6},{8,9},{9,8},{10,11... | collective-permute-start | bytes 61448 | tf_op jit(solution)/shard_map/ppermute | solution.py:142
  36.8 1.3 %collective-permute-start.1 = (f32[8,640]{1,0:T(8,128)S(1)}, f32[8,640]{1,0:T(8,128)S(1)}, u32[]{:S(2)}, u32[]{:S(2)}) collective-permute-start(f32[8,640]{1,0:T(8,128)S(1)} %convert_reduce_fusion), channel_id=1, source_target_pairs={{0,1},{1,0},{2,3},{3,2},{4,5},{5,4},{6,7},{7,6},{8,9},{9,8},{10,11... | collective-permute-start | bytes 61448 | tf_op jit(solution)/shard_map/ppermute | solution.py:142

commit v13 on v12

--- a/solution.py
+++ b/solution.py
@@ -21,14 +21,6 @@
 
 def everybody(chips):
     return [2 * chip + core for chip in chip_order(chips) for core in (1, 0)]
-
-
-def half_of(device, chips):
-    return (device + device // (2 * chips - 2)) % 2
-
-
-def summers(chips, half):
-    return [device for device in everybody(chips) if half_of(device, chips) == half]
 
 
 def dot(a, b, dims):
@@ -69,13 +61,13 @@
         in_rows_ref[k : k + 1] = message[0:1]
         grad_rows_ref[k : k + 1] = message[1:2]
     hidden = dot(in_rows_ref[...].astype(BF16), in_weight_ref[...], NN)
-    act_grad = dot(grad_rows_ref[...].astype(BF16), out_weight_ref[...], NT)
+    act_grad = dot(out_weight_ref[...], grad_rows_ref[...].astype(BF16), NT).T
     normal_cdf = 0.5 * (1.0 + lax.erf(hidden * (1.0 / math.sqrt(2.0))))
     normal_pdf = jnp.exp(-0.5 * hidden * hidden) * (1.0 / math.sqrt(2.0 * math.pi))
     activation = (hidden * normal_cdf).astype(BF16)
     hidden_grad = (act_grad * (normal_cdf + hidden * normal_pdf)).astype(BF16)
     part_out = dot(activation, out_weight_ref[...], NN)
-    part_in = dot(hidden_grad, in_weight_ref[...], NT)
+    part_in = dot(in_weight_ref[...], hidden_grad, NT).T
     for k in range(images):
         rows = [part_out[k : k + 1], part_in[k : k + 1]]
         parts_ref[k] = jnp.concatenate(rows, axis=0).astype(BF16)
@@ -112,7 +104,7 @@
     logits_grad = combine * (combine_grad - slot_sum) + dispatch * (dispatch_grad - patch_sum)
     part = dot(logits_grad.astype(BF16), tokens_ref[...], NN)
     half = part.shape[1] // 2
-    first = half_of(lax.axis_index("expert"), slots) == 0
+    first = lax.axis_index("expert") % 2 == 0
     kept_ref[...] = jnp.where(first, part[:, :half], part[:, half:])
     given_ref[...] = jnp.where(first, part[:, half:], part[:, :half])
     left_ref[...] = jnp.concatenate([logits_grad, dispatch], axis=0).astype(BF16)
@@ -206,11 +198,11 @@
         back,
     )
     pair = (kept + swap_cores(given)).astype(BF16)
-    groups = [summers(chips, half) for half in range(2)]
-    terms = exchange(jnp.broadcast_to(pair[None], (chips,) + pair.shape), groups)
+    same_core = [everybody(chips)[1 - core :: 2] for core in range(2)]
+    terms = exchange(jnp.broadcast_to(pair[None], (chips,) + pair.shape), same_core)
     total = jnp.sum(terms.astype(F32), axis=0)
     other = swap_cores(total)
-    first = half_of(lax.axis_index("expert"), chips) == 0
+    first = lax.axis_index("expert") % 2 == 0
     router_grad = jnp.concatenate(
         [jnp.where(first, total, other), jnp.where(first, other, total)], axis=1
     )

time: 39 us -> 39.5 us (1.013)
  Pallas kernels: 5.63 us -> 6.3 us
    pallas_call x6, Pallas kernels: 5.63 us -> 6.3 us  [call(): pl.pallas_call(kernel, out_shape=[jax.ShapeDtypeStruct(shape, dtype) for...]
where the time goes in v13:
time: 39.5 us; the launch traced here: 39.3 us
  blocking collectives  29.2 us (74%)
  Pallas kernels  6.3 us (16%)
  local copies, waits for them, and re-layouts  1.07 us (3%)
  waiting for transfers between devices  1 us (3%)
  between operations  0.73 us (2%)
  other arithmetic  0.65 us (2%)
    all_to_all x3, blocking collectives, exchange(): lax.all_to_all(value, 'expert', split_axis=0, concat_axis=0, tiled=True,...  29.2 us
    pallas_call x6, Pallas kernels, call(): pl.pallas_call(kernel, out_shape=[jax.ShapeDtypeStruct(shape, dtype) for...  6.3 us
    unnamed x10, local copies, waits for them, and re-layouts  1.06 us
    ppermute x2, waiting for transfers between devices, swap_cores(): return lax.ppermute(value, 'expert', [(i, i ^ 1) for i in range(size)])  1 us
  transfers between devices with their start and end apart: 2, of which 1 were waited for; matrix products, arithmetic and copies ran while one was open for 0% of the time, Pallas kernels for 3%

profile of v13, /device:TPU:0, one launch (start us, length us, event | category | flops | bytes accessed | tf_op | source)
XLA Modules:
  0.0 39.3 jit_solution(11655719318582912226)
XLA Ops:
  0.6 0.0 copy-start.4
  0.6 0.0 copy-start.2
  0.7 0.0 copy-start.3
  0.7 0.0 copy-start
  0.7 0.0 copy-start.1
  0.7 0.7 %copy-done.4 = bf16[1280,8]{0,1:T(8,128)(2,1)S(1)} copy-done((bf16[1280,8]{0,1:T(8,128)(2,1)S(1)}, bf16[1280,8]{0,1:T(8,128)(2,1)}, u32[]{:S(2)}) %copy-start.4) | copy-done | bytes 20504
  1.4 0.4 copy-done.2
  1.7 0.8 %shard_map.69 = (f32[8,1280]{1,0:T(8,128)S(1)}, f32[8,256]{1,0:T(8,128)S(1)}, f32[8,256]{1,0:T(8,128)S(1)}) custom-call(bf16[256,1280]{1,0:T(8,128)(2,1)S(1)} %bitcast.6, bf16[8,1280]{1,0:T(8,128)(2,1)S(1)} %bitcast.10, f32[8,128]{1,0:T(8,128)S(1)} %shard_map.68.token_ref), custom_call_target="tpu_custom_call" | custom-call | flops 20971520 | bytes 655360 | tf_op jit(solution)/shard_map/pallas_call | solution.py:121
  2.5 0.0 copy-done.3
  2.5 0.2 shard_map.70
  2.8 11.0 %all_to_all.15.got_ref = bf16[16,2,1280]{2,1,0:T(2,128)(2,1)S(1)} all-to-all(bf16[16,2,1280]{2,1,0:T(2,128)(2,1)S(1)} %shard_map.70), channel_id=1, replica_groups={{15,14,1,0,13,12,3,2,11,10,5,4,9,8,7,6},{31,30,17,16,29,28,19,18,27,26,..., dimensions={0} | all-to-all | bytes 163840 | tf_op jit(solution)/shard_map/all_to_all | solution.py:138
  13.7 0.0 copy-done
  13.7 0.0 copy-done.1
  13.7 3.4 %shard_map.71 = bf16[16,2,1280]{2,1,0:T(2,128)(2,1)S(1)} custom-call(bf16[16,2,1280]{2,1,0:T(2,128)(2,1)S(1)} %all_to_all.15.got_ref, bf16[1280,1280]{1,0:T(8,128)(2,1)S(1)} %copy-done, bf16[1280,1280]{1,0:T(8,128)(2,1)S(1)} %copy-done.1), custom_call_target="tpu_custom_call" | custom-call | flops 209715200 | bytes 6553600 | tf_op jit(solution)/shard_map/pallas_call | solution.py:121
  17.1 9.0 %all_to_all.16.back_ref = bf16[16,2,1280]{2,1,0:T(2,128)(2,1)S(1)} all-to-all(bf16[16,2,1280]{2,1,0:T(2,128)(2,1)S(1)} %shard_map.71), channel_id=1, replica_groups={{15,14,1,0,13,12,3,2,11,10,5,4,9,8,7,6},{31,30,17,16,29,28,19,18,27,26,..., dimensions={0} | all-to-all | bytes 163840 | tf_op jit(solution)/shard_map/all_to_all | solution.py:138
  26.2 0.7 %shard_map.72 = (f32[8,640]{1,0:T(8,128)S(1)}, f32[8,640]{1,0:T(8,128)S(1)}, bf16[16,256]{1,0:T(8,128)(2,1)S(1)}, bf16[16,1280]{1,0:T(8,128)(2,1)S(1)}) custom-call(bf16[256,1280]{1,0:T(8,128)(2,1)S(1)} %bitcast.7, bf16[256,1280]{1,0:T(8,128)(2,1)S(1)} %bitcast.9, bf16[8,1280]{1,0:T(8,128)(2,1)S(1)} %bitcast.11, f32[8,256]{1,0:T(8,128)S(1)} %get-tuple-element.9.dispatch_ref, ...), custom_call_target="tpu_custom_call" | custom-call | flops 31457280 | bytes 1310720 | tf_op jit(solution)/shard_map/pallas_call | solution.py:121
  26.8 0.2 collective-permute-start
  27.1 1.0 %collective-permute-done = f32[8,640]{1,0:T(8,128)S(1)} collective-permute-done((f32[8,640]{1,0:T(8,128)S(1)}, f32[8,640]{1,0:T(8,128)S(1)}, u32[]{:S(2)}, u32[]{:S(2)}) %collective-permute-start) | collective-permute-done | bytes 20512 | tf_op jit(solution)/shard_map/ppermute | solution.py:134
  28.1 9.2 %all_to_all.17 = bf16[8,8,640]{2,1,0:T(8,128)(2,1)S(1)} all-to-all(bf16[8,8,640]{2,1,0:T(8,128)(2,1)S(1)} %broadcast_in_dim.10), channel_id=1, replica_groups={{14,0,12,2,10,4,8,6},{15,1,13,3,11,5,9,7},{30,16,28,18,26,20,24,22},{31..., dimensions={0} | all-to-all | bytes 163840 | tf_op jit(solution)/shard_map/all_to_all | solution.py:138
  37.3 0.1 collective-permute-start.1
  37.4 1.2 %shard_map.73 = bf16[256,1280]{1,0:T(8,128)(2,1)} custom-call(bf16[16,256]{1,0:T(8,128)(2,1)S(1)} %get-tuple-element.12.left_ref, bf16[16,1280]{1,0:T(8,128)(2,1)S(1)} %get-tuple-element.13.right_ref), custom_call_target="tpu_custom_call" | custom-call | flops 10485760 | bytes 655360 | tf_op jit(solution)/shard_map/pallas_call | solution.py:121
  38.6 0.0 collective-permute-done.1
  38.6 0.6 %maximum_bitcast_fusion = f32[1280,8]{0,1:T(8,128)} fusion(f32[8,640]{1,0:T(8,128)S(1)} %get-tuple-element.17, f32[8,640]{1,0:T(8,128)S(1)} %get-tuple-element.16), kind=kLoop, calls=%fused_computation.1 | loop fusion | flops 10240 | bytes 81920 | tf_op jit(solution)/shard_map/transpose | solution.py:217
  (5 shorter events, 0.0 us)
Async XLA Ops:
  0.6 0.7 %copy-start.4 = (bf16[1280,8]{0,1:T(8,128)(2,1)S(1)}, bf16[1280,8]{0,1:T(8,128)(2,1)}, u32[]{:S(2)}) copy-start(bf16[1280,8]{0,1:T(8,128)(2,1)} %param.7) | copy-start | bytes 61444
  0.6 1.1 %copy-start.2 = (bf16[1,256,1280]{2,1,0:T(8,128)(2,1)S(1)}, bf16[1,256,1280]{2,1,0:T(8,128)(2,1)}, u32[]{:S(2)}) copy-start(bf16[1,256,1280]{2,1,0:T(8,128)(2,1)} %param.5) | copy-start | bytes 1966084
  0.7 1.9 %copy-start.3 = (bf16[1,256,1280]{2,1,0:T(8,128)(2,1)S(1)}, bf16[1,256,1280]{2,1,0:T(8,128)(2,1)}, u32[]{:S(2)}) copy-start(bf16[1,256,1280]{2,1,0:T(8,128)(2,1)} %param.6) | copy-start | bytes 1966084
  0.7 13.1 %copy-start = (bf16[1280,1280]{1,0:T(8,128)(2,1)S(1)}, bf16[1280,1280]{1,0:T(8,128)(2,1)}, u32[]{:S(2)}) copy-start(bf16[1280,1280]{1,0:T(8,128)(2,1)} %in_weight_ref.1) | copy-start | bytes 9830404
  0.7 13.1 %copy-start.1 = (bf16[1280,1280]{1,0:T(8,128)(2,1)S(1)}, bf16[1280,1280]{1,0:T(8,128)(2,1)}, u32[]{:S(2)}) copy-start(bf16[1280,1280]{1,0:T(8,128)(2,1)} %out_weight_ref.1) | copy-start | bytes 9830404
  26.8 1.2 %collective-permute-start = (f32[8,640]{1,0:T(8,128)S(1)}, f32[8,640]{1,0:T(8,128)S(1)}, u32[]{:S(2)}, u32[]{:S(2)}) collective-permute-start(f32[8,640]{1,0:T(8,128)S(1)} %get-tuple-element.15), channel_id=1, source_target_pairs={{0,1},{1,0},{2,3},{3,2},{4,5},{5,4},{6,7},{7,6},{8,9},{9,8},{10,11... | collective-permute-start | bytes 61448 | tf_op jit(solution)/shard_map/ppermute | solution.py:134
  37.3 1.3 %collective-permute-start.1 = (f32[8,640]{1,0:T(8,128)S(1)}, f32[8,640]{1,0:T(8,128)S(1)}, u32[]{:S(2)}, u32[]{:S(2)}) collective-permute-start(f32[8,640]{1,0:T(8,128)S(1)} %convert_reduce_fusion), channel_id=1, source_target_pairs={{0,1},{1,0},{2,3},{3,2},{4,5},{5,4},{6,7},{7,6},{8,9},{9,8},{10,11... | collective-permute-start | bytes 61448 | tf_op jit(solution)/shard_map/ppermute | solution.py:134

commit v14 on v13

--- a/solution.py
+++ b/solution.py
@@ -61,13 +61,13 @@
         in_rows_ref[k : k + 1] = message[0:1]
         grad_rows_ref[k : k + 1] = message[1:2]
     hidden = dot(in_rows_ref[...].astype(BF16), in_weight_ref[...], NN)
-    act_grad = dot(out_weight_ref[...], grad_rows_ref[...].astype(BF16), NT).T
+    act_grad = dot(grad_rows_ref[...].astype(BF16), out_weight_ref[...], NT)
     normal_cdf = 0.5 * (1.0 + lax.erf(hidden * (1.0 / math.sqrt(2.0))))
     normal_pdf = jnp.exp(-0.5 * hidden * hidden) * (1.0 / math.sqrt(2.0 * math.pi))
     activation = (hidden * normal_cdf).astype(BF16)
     hidden_grad = (act_grad * (normal_cdf + hidden * normal_pdf)).astype(BF16)
     part_out = dot(activation, out_weight_ref[...], NN)
-    part_in = dot(in_weight_ref[...], hidden_grad, NT).T
+    part_in = dot(hidden_grad, in_weight_ref[...], NT)
     for k in range(images):
         rows = [part_out[k : k + 1], part_in[k : k + 1]]
         parts_ref[k] = jnp.concatenate(rows, axis=0).astype(BF16)
@@ -80,8 +80,7 @@
     dispatch_ref,
     combine_ref,
     back_ref,
-    kept_ref,
-    given_ref,
+    term_ref,
     left_ref,
     right_ref,
     out_rows_ref,
@@ -102,11 +101,7 @@
     slot_sum = jnp.sum(combine * combine_grad, axis=0, keepdims=True)
     patch_sum = jnp.sum(dispatch * dispatch_grad, axis=1, keepdims=True)
     logits_grad = combine * (combine_grad - slot_sum) + dispatch * (dispatch_grad - patch_sum)
-    part = dot(logits_grad.astype(BF16), tokens_ref[...], NN)
-    half = part.shape[1] // 2
-    first = lax.axis_index("expert") % 2 == 0
-    kept_ref[...] = jnp.where(first, part[:, :half], part[:, half:])
-    given_ref[...] = jnp.where(first, part[:, half:], part[:, :half])
+    term_ref[...] = dot(logits_grad.astype(BF16), tokens_ref[...], NN).astype(BF16)
     left_ref[...] = jnp.concatenate([logits_grad, dispatch], axis=0).astype(BF16)
     right_ref[...] = jnp.concatenate(
         [router_ref[...].astype(F32), back_rows_ref[...]], axis=0
@@ -180,11 +175,10 @@
         out_weight,
     )
     back = exchange(parts, [everybody(chips)])
-    kept, given, left, right = call(
+    term, left, right = call(
         logits_kernel,
         [
-            ((slots, width // 2), F32),
-            ((slots, width // 2), F32),
+            ((slots, width), BF16),
             ((2 * slots, patches), BF16),
             ((2 * slots, width), BF16),
         ],
@@ -197,15 +191,10 @@
         combine,
         back,
     )
-    pair = (kept + swap_cores(given)).astype(BF16)
     same_core = [everybody(chips)[1 - core :: 2] for core in range(2)]
-    terms = exchange(jnp.broadcast_to(pair[None], (chips,) + pair.shape), same_core)
+    terms = exchange(jnp.broadcast_to(term[None], (chips,) + term.shape), same_core)
     total = jnp.sum(terms.astype(F32), axis=0)
-    other = swap_cores(total)
-    first = lax.axis_index("expert") % 2 == 0
-    router_grad = jnp.concatenate(
-        [jnp.where(first, total, other), jnp.where(first, other, total)], axis=1
-    )
+    router_grad = total + swap_cores(total)
     (tokens_grad,) = call(
         tokens_kernel,
         [((patches, width), BF16)],

time: 39.5 us -> 39.2 us (level)
  blocking collectives: 29.2 us -> 30.7 us
  waiting for transfers between devices: 1 us -> 0.01 us
  Pallas kernels: 6.3 us -> 5.66 us
    all_to_all x3, blocking collectives: 29.2 us -> 30.7 us  [exchange(): lax.all_to_all(value, 'expert', split_axis=0, concat_axis=0, tiled=True,...]
    ppermute x2 -> x1, waiting for transfers between devices: 1 us -> 0.01 us  [swap_cores(): return lax.ppermute(value, 'expert', [(i, i ^ 1) for i in range(size)])]
    pallas_call x6, Pallas kernels: 6.3 us -> 5.66 us  [call(): pl.pallas_call(kernel, out_shape=[jax.ShapeDtypeStruct(shape, dtype) for...]
  transfers between devices with their start and end apart: 2 -> 1, of which waited for: 1 -> 0; matrix products, arithmetic and copies ran while one was open for 0% -> 0% of each run, Pallas kernels for 3% -> 3%
where the time goes in v14:
time: 39.2 us; the launch traced here: 38.9 us
  blocking collectives  30.7 us (78%)
  Pallas kernels  5.66 us (14%)
  local copies, waits for them, and re-layouts  1.09 us (3%)
  between operations  0.72 us (2%)
  other arithmetic  0.65 us (2%)
    all_to_all x3, blocking collectives, exchange(): lax.all_to_all(value, 'expert', split_axis=0, concat_axis=0, tiled=True,...  30.7 us
    pallas_call x6, Pallas kernels, call(): pl.pallas_call(kernel, out_shape=[jax.ShapeDtypeStruct(shape, dtype) for...  5.66 us
    unnamed x10, local copies, waits for them, and re-layouts  1.06 us
  transfers between devices with their start and end apart: 1, of which 0 were waited for; matrix products, arithmetic and copies ran while one was open for 0% of the time, Pallas kernels for 3%

profile of v14, /device:TPU:0, one launch (start us, length us, event | category | flops | bytes accessed | tf_op | source)
XLA Modules:
  0.0 38.9 jit_solution(11799216938188922517)
XLA Ops:
  0.6 0.0 copy-start.4
  0.6 0.0 copy-start.2
  0.7 0.0 copy-start.3
  0.7 0.0 copy-start
  0.7 0.0 copy-start.1
  0.7 0.7 %copy-done.4 = bf16[1280,8]{0,1:T(8,128)(2,1)S(1)} copy-done((bf16[1280,8]{0,1:T(8,128)(2,1)S(1)}, bf16[1280,8]{0,1:T(8,128)(2,1)}, u32[]{:S(2)}) %copy-start.4) | copy-done | bytes 20504
  1.4 0.4 copy-done.2
  1.7 0.8 %shard_map.69 = (f32[8,1280]{1,0:T(8,128)S(1)}, f32[8,256]{1,0:T(8,128)S(1)}, f32[8,256]{1,0:T(8,128)S(1)}) custom-call(bf16[256,1280]{1,0:T(8,128)(2,1)S(1)} %bitcast.6, bf16[8,1280]{1,0:T(8,128)(2,1)S(1)} %bitcast.10, f32[8,128]{1,0:T(8,128)S(1)} %shard_map.68.token_ref), custom_call_target="tpu_custom_call" | custom-call | flops 20971520 | bytes 655360 | tf_op jit(solution)/shard_map/pallas_call | solution.py:116
  2.5 0.0 copy-done.3
  2.5 0.2 shard_map.70
  2.8 11.0 %all_to_all.15.got_ref = bf16[16,2,1280]{2,1,0:T(2,128)(2,1)S(1)} all-to-all(bf16[16,2,1280]{2,1,0:T(2,128)(2,1)S(1)} %shard_map.70), channel_id=1, replica_groups={{15,14,1,0,13,12,3,2,11,10,5,4,9,8,7,6},{31,30,17,16,29,28,19,18,27,26,..., dimensions={0} | all-to-all | bytes 163840 | tf_op jit(solution)/shard_map/all_to_all | solution.py:133
  13.7 0.0 copy-done
  13.7 0.0 copy-done.1
  13.7 2.7 %shard_map.71 = bf16[16,2,1280]{2,1,0:T(2,128)(2,1)S(1)} custom-call(bf16[16,2,1280]{2,1,0:T(2,128)(2,1)S(1)} %all_to_all.15.got_ref, bf16[1280,1280]{1,0:T(8,128)(2,1)S(1)} %copy-done, bf16[1280,1280]{1,0:T(8,128)(2,1)S(1)} %copy-done.1), custom_call_target="tpu_custom_call" | custom-call | flops 209715200 | bytes 6553600 | tf_op jit(solution)/shard_map/pallas_call | solution.py:116
  16.5 9.0 %all_to_all.16.back_ref = bf16[16,2,1280]{2,1,0:T(2,128)(2,1)S(1)} all-to-all(bf16[16,2,1280]{2,1,0:T(2,128)(2,1)S(1)} %shard_map.71), channel_id=1, replica_groups={{15,14,1,0,13,12,3,2,11,10,5,4,9,8,7,6},{31,30,17,16,29,28,19,18,27,26,..., dimensions={0} | all-to-all | bytes 163840 | tf_op jit(solution)/shard_map/all_to_all | solution.py:133
  25.5 0.7 %shard_map.72 = (bf16[8,1280]{1,0:T(8,128)(2,1)S(1)}, bf16[16,256]{1,0:T(8,128)(2,1)S(1)}, bf16[16,1280]{1,0:T(8,128)(2,1)S(1)}) custom-call(bf16[256,1280]{1,0:T(8,128)(2,1)S(1)} %bitcast.7, bf16[256,1280]{1,0:T(8,128)(2,1)S(1)} %bitcast.9, bf16[8,1280]{1,0:T(8,128)(2,1)S(1)} %bitcast.11, f32[8,256]{1,0:T(8,128)S(1)} %get-tuple-element.8.dispatch_ref, ...), custom_call_target="tpu_custom_call" | custom-call | flops 31457280 | bytes 1310720 | tf_op jit(solution)/shard_map/pallas_call | solution.py:116
  26.2 10.7 %all_to_all.17 = bf16[8,8,1280]{2,1,0:T(8,128)(2,1)S(1)} all-to-all(bf16[8,8,1280]{2,1,0:T(8,128)(2,1)S(1)} %broadcast_in_dim.10), channel_id=1, replica_groups={{14,0,12,2,10,4,8,6},{15,1,13,3,11,5,9,7},{30,16,28,18,26,20,24,22},{31..., dimensions={0} | all-to-all | bytes 327680 | tf_op jit(solution)/shard_map/all_to_all | solution.py:133
  37.0 0.1 collective-permute-start
  37.1 1.2 %shard_map.73 = bf16[256,1280]{1,0:T(8,128)(2,1)} custom-call(bf16[16,256]{1,0:T(8,128)(2,1)S(1)} %get-tuple-element.11.left_ref, bf16[16,1280]{1,0:T(8,128)(2,1)S(1)} %get-tuple-element.12.right_ref), custom_call_target="tpu_custom_call" | custom-call | flops 10485760 | bytes 655360 | tf_op jit(solution)/shard_map/pallas_call | solution.py:116
  38.3 0.0 collective-permute-done
  38.3 0.6 %add_bitcast_fusion = f32[1280,8]{0,1:T(8,128)} fusion(f32[8,1280]{1,0:T(8,128)S(1)} %convert_reduce_fusion, f32[8,1280]{1,0:T(8,128)S(1)} %collective-permute-done), kind=kLoop, calls=%fused_computation.1 | loop fusion | flops 10240 | bytes 122880 | tf_op jit(solution)/shard_map/transpose | solution.py:206
  (3 shorter events, 0.1 us)
Async XLA Ops:
  0.6 0.7 %copy-start.4 = (bf16[1280,8]{0,1:T(8,128)(2,1)S(1)}, bf16[1280,8]{0,1:T(8,128)(2,1)}, u32[]{:S(2)}) copy-start(bf16[1280,8]{0,1:T(8,128)(2,1)} %param.7) | copy-start | bytes 61444
  0.6 1.1 %copy-start.2 = (bf16[1,256,1280]{2,1,0:T(8,128)(2,1)S(1)}, bf16[1,256,1280]{2,1,0:T(8,128)(2,1)}, u32[]{:S(2)}) copy-start(bf16[1,256,1280]{2,1,0:T(8,128)(2,1)} %param.5) | copy-start | bytes 1966084
  0.7 1.9 %copy-start.3 = (bf16[1,256,1280]{2,1,0:T(8,128)(2,1)S(1)}, bf16[1,256,1280]{2,1,0:T(8,128)(2,1)}, u32[]{:S(2)}) copy-start(bf16[1,256,1280]{2,1,0:T(8,128)(2,1)} %param.6) | copy-start | bytes 1966084
  0.7 13.1 %copy-start = (bf16[1280,1280]{1,0:T(8,128)(2,1)S(1)}, bf16[1280,1280]{1,0:T(8,128)(2,1)}, u32[]{:S(2)}) copy-start(bf16[1280,1280]{1,0:T(8,128)(2,1)} %in_weight_ref.1) | copy-start | bytes 9830404
  0.7 13.1 %copy-start.1 = (bf16[1280,1280]{1,0:T(8,128)(2,1)S(1)}, bf16[1280,1280]{1,0:T(8,128)(2,1)}, u32[]{:S(2)}) copy-start(bf16[1280,1280]{1,0:T(8,128)(2,1)} %out_weight_ref.1) | copy-start | bytes 9830404
  37.0 1.3 %collective-permute-start = (f32[8,1280]{1,0:T(8,128)S(1)}, f32[8,1280]{1,0:T(8,128)S(1)}, u32[]{:S(2)}, u32[]{:S(2)}) collective-permute-start(f32[8,1280]{1,0:T(8,128)S(1)} %convert_reduce_fusion), channel_id=1, source_target_pairs={{0,1},{1,0},{2,3},{3,2},{4,5},{5,4},{6,7},{7,6},{8,9},{9,8},{10,11... | collective-permute-start | bytes 122888 | tf_op jit(solution)/shard_map/ppermute | solution.py:129

commit v15 on v13

--- a/solution.py
+++ b/solution.py
@@ -52,25 +52,19 @@
             sent_ref[order.index(2 * s + half)] = message
 
 
-def experts_kernel(
-    got_ref, in_weight_ref, out_weight_ref, parts_ref, in_rows_ref, grad_rows_ref
-):
-    images = got_ref.shape[0]
-    for k in range(images):
-        message = got_ref[k].astype(F32)
-        in_rows_ref[k : k + 1] = message[0:1]
-        grad_rows_ref[k : k + 1] = message[1:2]
-    hidden = dot(in_rows_ref[...].astype(BF16), in_weight_ref[...], NN)
-    act_grad = dot(out_weight_ref[...], grad_rows_ref[...].astype(BF16), NT).T
+def experts_kernel(got_ref, in_weight_ref, out_weight_ref, parts_ref):
+    messages = got_ref[...].astype(F32)
+    in_rows = messages[:, 0].astype(BF16)
+    grad_rows = messages[:, 1].astype(BF16)
+    hidden = dot(in_rows, in_weight_ref[...], NN)
+    act_grad = dot(grad_rows, out_weight_ref[...], NT)
     normal_cdf = 0.5 * (1.0 + lax.erf(hidden * (1.0 / math.sqrt(2.0))))
     normal_pdf = jnp.exp(-0.5 * hidden * hidden) * (1.0 / math.sqrt(2.0 * math.pi))
     activation = (hidden * normal_cdf).astype(BF16)
     hidden_grad = (act_grad * (normal_cdf + hidden * normal_pdf)).astype(BF16)
     part_out = dot(activation, out_weight_ref[...], NN)
-    part_in = dot(in_weight_ref[...], hidden_grad, NT).T
-    for k in range(images):
-        rows = [part_out[k : k + 1], part_in[k : k + 1]]
-        parts_ref[k] = jnp.concatenate(rows, axis=0).astype(BF16)
+    part_in = dot(hidden_grad, in_weight_ref[...], NT)
+    parts_ref[...] = jnp.stack([part_out, part_in], axis=1).astype(BF16)
 
 
 def logits_kernel(
@@ -82,10 +76,9 @@
     back_ref,
     kept_ref,
     given_ref,
-    left_ref,
-    right_ref,
+    logits_ref,
+    back_rows_ref,
     out_rows_ref,
-    back_rows_ref,
 ):
     slots = router_ref.shape[0]
     order = everybody(slots)
@@ -107,14 +100,14 @@
     first = lax.axis_index("expert") % 2 == 0
     kept_ref[...] = jnp.where(first, part[:, :half], part[:, half:])
     given_ref[...] = jnp.where(first, part[:, half:], part[:, :half])
-    left_ref[...] = jnp.concatenate([logits_grad, dispatch], axis=0).astype(BF16)
-    right_ref[...] = jnp.concatenate(
-        [router_ref[...].astype(F32), back_rows_ref[...]], axis=0
-    ).astype(BF16)
-
-
-def tokens_kernel(left_ref, right_ref, tokens_grad_ref):
-    tokens_grad_ref[...] = dot(left_ref[...], right_ref[...], TN).astype(BF16)
+    logits_ref[...] = logits_grad
+
+
+def tokens_kernel(logits_ref, dispatch_ref, router_ref, back_rows_ref, tokens_grad_ref):
+    left = jnp.concatenate([logits_ref[...], dispatch_ref[...]], axis=0).astype(BF16)
+    rows = [router_ref[...].astype(F32), back_rows_ref[...]]
+    right = jnp.concatenate(rows, axis=0).astype(BF16)
+    tokens_grad_ref[...] = dot(left, right, TN).astype(BF16)
 
 
 def call(kernel, outs, scratch, cost, *operands):
@@ -173,22 +166,22 @@
     (parts,) = call(
         experts_kernel,
         [((2 * chips, 2, width), BF16)],
-        [(2 * chips, width)] * 2,
+        [],
         (16 * chips * width * hidden, 2 * weight_bytes),
         got,
         in_weight,
         out_weight,
     )
     back = exchange(parts, [everybody(chips)])
-    kept, given, left, right = call(
+    kept, given, logits_grad, slot_back = call(
         logits_kernel,
         [
             ((slots, width // 2), F32),
             ((slots, width // 2), F32),
-            ((2 * slots, patches), BF16),
-            ((2 * slots, width), BF16),
+            ((slots, patches), F32),
+            ((slots, width), F32),
         ],
-        [(slots, width)] * 2,
+        [(slots, width)],
         (12 * patches * width * slots, 2 * image_bytes),
         tokens,
         out_grad,
@@ -211,8 +204,10 @@
         [((patches, width), BF16)],
         [],
         (4 * patches * width * slots, image_bytes),
-        left,
-        right,
+        logits_grad,
+        dispatch,
+        router_rows,
+        slot_back,
     )
     return (tokens_grad[None], router_grad.T)
 

time: 39.5 us -> 38.9 us (0.985)
  Pallas kernels: 6.3 us -> 5.7 us
    pallas_call x6, Pallas kernels: 6.3 us -> 5.7 us  [call(): pl.pallas_call(kernel, out_shape=[jax.ShapeDtypeStruct(shape, dtype) for...]
where the time goes in v15:
time: 38.9 us; the launch traced here: 38.7 us
  blocking collectives  29.2 us (75%)
  Pallas kernels  5.7 us (15%)
  local copies, waits for them, and re-layouts  1.07 us (3%)
  waiting for transfers between devices  1 us (3%)
  between operations  0.73 us (2%)
  other arithmetic  0.65 us (2%)
    all_to_all x3, blocking collectives, exchange(): lax.all_to_all(value, 'expert', split_axis=0, concat_axis=0, tiled=True,...  29.2 us
    pallas_call x6, Pallas kernels, call(): pl.pallas_call(kernel, out_shape=[jax.ShapeDtypeStruct(shape, dtype) for...  5.7 us
    unnamed x10, local copies, waits for them, and re-layouts  1.06 us
    ppermute x2, waiting for transfers between devices, swap_cores(): return lax.ppermute(value, 'expert', [(i, i ^ 1) for i in range(size)])  1 us
  transfers between devices with their start and end apart: 2, of which 1 were waited for; matrix products, arithmetic and copies ran while one was open for 0% of the time, Pallas kernels for 3%

profile of v15, /device:TPU:0, one launch (start us, length us, event | category | flops | bytes accessed | tf_op | source)
XLA Modules:
  0.0 38.7 jit_solution(6891894453967946787)
XLA Ops:
  0.6 0.0 copy-start.4
  0.6 0.0 copy-start.2
  0.7 0.0 copy-start.3
  0.7 0.0 copy-start
  0.7 0.0 copy-start.1
  0.7 0.7 %copy-done.4 = bf16[1280,8]{0,1:T(8,128)(2,1)S(1)} copy-done((bf16[1280,8]{0,1:T(8,128)(2,1)S(1)}, bf16[1280,8]{0,1:T(8,128)(2,1)}, u32[]{:S(2)}) %copy-start.4) | copy-done | bytes 20504
  1.4 0.4 copy-done.2
  1.7 0.8 %shard_map.69 = (f32[8,1280]{1,0:T(8,128)S(1)}, f32[8,256]{1,0:T(8,128)S(1)}, f32[8,256]{1,0:T(8,128)S(1)}) custom-call(bf16[256,1280]{1,0:T(8,128)(2,1)S(1)} %bitcast.6, bf16[8,1280]{1,0:T(8,128)(2,1)S(1)} %bitcast.10, f32[8,128]{1,0:T(8,128)S(1)} %shard_map.68.token_ref), custom_call_target="tpu_custom_call" | custom-call | flops 20971520 | bytes 655360 | tf_op jit(solution)/shard_map/pallas_call | solution.py:114
  2.5 0.0 copy-done.3
  2.5 0.2 shard_map.70
  2.8 11.0 %all_to_all.15.got_ref = bf16[16,2,1280]{2,1,0:T(2,128)(2,1)S(1)} all-to-all(bf16[16,2,1280]{2,1,0:T(2,128)(2,1)S(1)} %shard_map.70), channel_id=1, replica_groups={{15,14,1,0,13,12,3,2,11,10,5,4,9,8,7,6},{31,30,17,16,29,28,19,18,27,26,..., dimensions={0} | all-to-all | bytes 163840 | tf_op jit(solution)/shard_map/all_to_all | solution.py:131
  13.7 0.0 copy-done
  13.7 0.0 copy-done.1
  13.7 2.8 %shard_map.71 = bf16[16,2,1280]{2,1,0:T(2,128)(2,1)S(1)} custom-call(bf16[16,2,1280]{2,1,0:T(2,128)(2,1)S(1)} %all_to_all.15.got_ref, bf16[1280,1280]{1,0:T(8,128)(2,1)S(1)} %copy-done, bf16[1280,1280]{1,0:T(8,128)(2,1)S(1)} %copy-done.1), custom_call_target="tpu_custom_call" | custom-call | flops 209715200 | bytes 6553600 | tf_op jit(solution)/shard_map/pallas_call | solution.py:114
  16.6 9.0 %all_to_all.16.back_ref = bf16[16,2,1280]{2,1,0:T(2,128)(2,1)S(1)} all-to-all(bf16[16,2,1280]{2,1,0:T(2,128)(2,1)S(1)} %shard_map.71), channel_id=1, replica_groups={{15,14,1,0,13,12,3,2,11,10,5,4,9,8,7,6},{31,30,17,16,29,28,19,18,27,26,..., dimensions={0} | all-to-all | bytes 163840 | tf_op jit(solution)/shard_map/all_to_all | solution.py:131
  25.6 0.7 %shard_map.72 = (f32[8,640]{1,0:T(8,128)S(1)}, f32[8,640]{1,0:T(8,128)S(1)}, f32[8,256]{1,0:T(8,128)S(1)}, f32[8,1280]{1,0:T(8,128)S(1)}) custom-call(bf16[256,1280]{1,0:T(8,128)(2,1)S(1)} %bitcast.7, bf16[256,1280]{1,0:T(8,128)(2,1)S(1)} %bitcast.9, bf16[8,1280]{1,0:T(8,128)(2,1)S(1)} %bitcast.11, f32[8,256]{1,0:T(8,128)S(1)} %get-tuple-element.9.dispatch_ref, ...), custom_call_target="tpu_custom_call" | custom-call | flops 31457280 | bytes 1310720 | tf_op jit(solution)/shard_map/pallas_call | solution.py:114
  26.3 0.2 collective-permute-start
  26.5 1.0 %collective-permute-done = f32[8,640]{1,0:T(8,128)S(1)} collective-permute-done((f32[8,640]{1,0:T(8,128)S(1)}, f32[8,640]{1,0:T(8,128)S(1)}, u32[]{:S(2)}, u32[]{:S(2)}) %collective-permute-start) | collective-permute-done | bytes 20512 | tf_op jit(solution)/shard_map/ppermute | solution.py:127
  27.5 9.2 %all_to_all.17 = bf16[8,8,640]{2,1,0:T(8,128)(2,1)S(1)} all-to-all(bf16[8,8,640]{2,1,0:T(8,128)(2,1)S(1)} %broadcast_in_dim.10), channel_id=1, replica_groups={{14,0,12,2,10,4,8,6},{15,1,13,3,11,5,9,7},{30,16,28,18,26,20,24,22},{31..., dimensions={0} | all-to-all | bytes 163840 | tf_op jit(solution)/shard_map/all_to_all | solution.py:131
  36.7 0.1 collective-permute-start.1
  36.8 1.2 %shard_map.73 = bf16[256,1280]{1,0:T(8,128)(2,1)} custom-call(f32[8,256]{1,0:T(8,128)S(1)} %get-tuple-element.12.logits_ref, f32[8,256]{1,0:T(8,128)S(1)} %get-tuple-element.9.dispatch_ref, bf16[8,1280]{1,0:T(8,128)(2,1)S(1)} %bitcast.12, f32[8,1280]{1,0:T(8,128)S(1)} %get-tuple-element.13.back_rows_ref), custom_call_target="tpu_custom_call" | custom-call | flops 10485760 | bytes 655360 | tf_op jit(solution)/shard_map/pallas_call | solution.py:114
  38.0 0.0 collective-permute-done.1
  38.0 0.6 %maximum_bitcast_fusion = f32[1280,8]{0,1:T(8,128)} fusion(f32[8,640]{1,0:T(8,128)S(1)} %get-tuple-element.17, f32[8,640]{1,0:T(8,128)S(1)} %get-tuple-element.16), kind=kLoop, calls=%fused_computation.1 | loop fusion | flops 10240 | bytes 81920 | tf_op jit(solution)/shard_map/transpose | solution.py:212
  (5 shorter events, 0.0 us)
Async XLA Ops:
  0.6 0.7 %copy-start.4 = (bf16[1280,8]{0,1:T(8,128)(2,1)S(1)}, bf16[1280,8]{0,1:T(8,128)(2,1)}, u32[]{:S(2)}) copy-start(bf16[1280,8]{0,1:T(8,128)(2,1)} %param.7) | copy-start | bytes 61444
  0.6 1.1 %copy-start.2 = (bf16[1,256,1280]{2,1,0:T(8,128)(2,1)S(1)}, bf16[1,256,1280]{2,1,0:T(8,128)(2,1)}, u32[]{:S(2)}) copy-start(bf16[1,256,1280]{2,1,0:T(8,128)(2,1)} %param.5) | copy-start | bytes 1966084
  0.7 1.9 %copy-start.3 = (bf16[1,256,1280]{2,1,0:T(8,128)(2,1)S(1)}, bf16[1,256,1280]{2,1,0:T(8,128)(2,1)}, u32[]{:S(2)}) copy-start(bf16[1,256,1280]{2,1,0:T(8,128)(2,1)} %param.6) | copy-start | bytes 1966084
  0.7 13.1 %copy-start = (bf16[1280,1280]{1,0:T(8,128)(2,1)S(1)}, bf16[1280,1280]{1,0:T(8,128)(2,1)}, u32[]{:S(2)}) copy-start(bf16[1280,1280]{1,0:T(8,128)(2,1)} %in_weight_ref.1) | copy-start | bytes 9830404
  0.7 13.1 %copy-start.1 = (bf16[1280,1280]{1,0:T(8,128)(2,1)S(1)}, bf16[1280,1280]{1,0:T(8,128)(2,1)}, u32[]{:S(2)}) copy-start(bf16[1280,1280]{1,0:T(8,128)(2,1)} %out_weight_ref.1) | copy-start | bytes 9830404
  26.3 1.2 %collective-permute-start = (f32[8,640]{1,0:T(8,128)S(1)}, f32[8,640]{1,0:T(8,128)S(1)}, u32[]{:S(2)}, u32[]{:S(2)}) collective-permute-start(f32[8,640]{1,0:T(8,128)S(1)} %get-tuple-element.15), channel_id=1, source_target_pairs={{0,1},{1,0},{2,3},{3,2},{4,5},{5,4},{6,7},{7,6},{8,9},{9,8},{10,11... | collective-permute-start | bytes 61448 | tf_op jit(solution)/shard_map/ppermute | solution.py:127
  36.7 1.3 %collective-permute-start.1 = (f32[8,640]{1,0:T(8,128)S(1)}, f32[8,640]{1,0:T(8,128)S(1)}, u32[]{:S(2)}, u32[]{:S(2)}) collective-permute-start(f32[8,640]{1,0:T(8,128)S(1)} %convert_reduce_fusion), channel_id=1, source_target_pairs={{0,1},{1,0},{2,3},{3,2},{4,5},{5,4},{6,7},{7,6},{8,9},{9,8},{10,11... | collective-permute-start | bytes 61448 | tf_op jit(solution)/shard_map/ppermute | solution.py:127

commit v16 on v13

--- a/solution.py
+++ b/solution.py
@@ -61,13 +61,13 @@
         in_rows_ref[k : k + 1] = message[0:1]
         grad_rows_ref[k : k + 1] = message[1:2]
     hidden = dot(in_rows_ref[...].astype(BF16), in_weight_ref[...], NN)
-    act_grad = dot(out_weight_ref[...], grad_rows_ref[...].astype(BF16), NT).T
+    act_grad = dot(grad_rows_ref[...].astype(BF16), out_weight_ref[...], NT)
     normal_cdf = 0.5 * (1.0 + lax.erf(hidden * (1.0 / math.sqrt(2.0))))
     normal_pdf = jnp.exp(-0.5 * hidden * hidden) * (1.0 / math.sqrt(2.0 * math.pi))
     activation = (hidden * normal_cdf).astype(BF16)
     hidden_grad = (act_grad * (normal_cdf + hidden * normal_pdf)).astype(BF16)
     part_out = dot(activation, out_weight_ref[...], NN)
-    part_in = dot(in_weight_ref[...], hidden_grad, NT).T
+    part_in = dot(hidden_grad, in_weight_ref[...], NT)
     for k in range(images):
         rows = [part_out[k : k + 1], part_in[k : k + 1]]
         parts_ref[k] = jnp.concatenate(rows, axis=0).astype(BF16)

time: 39.5 us -> 38.8 us (0.982)
  Pallas kernels: 6.3 us -> 5.63 us
    pallas_call x6, Pallas kernels: 6.3 us -> 5.63 us  [call(): pl.pallas_call(kernel, out_shape=[jax.ShapeDtypeStruct(shape, dtype) for...]
where the time goes in v16:
time: 38.8 us; the launch traced here: 38.6 us
  blocking collectives  29.2 us (75%)
  Pallas kernels  5.63 us (15%)
  local copies, waits for them, and re-layouts  1.07 us (3%)
  waiting for transfers between devices  1 us (3%)
  between operations  0.73 us (2%)
  other arithmetic  0.65 us (2%)
    all_to_all x3, blocking collectives, exchange(): lax.all_to_all(value, 'expert', split_axis=0, concat_axis=0, tiled=True,...  29.2 us
    pallas_call x6, Pallas kernels, call(): pl.pallas_call(kernel, out_shape=[jax.ShapeDtypeStruct(shape, dtype) for...  5.63 us
    unnamed x10, local copies, waits for them, and re-layouts  1.06 us
    ppermute x2, waiting for transfers between devices, swap_cores(): return lax.ppermute(value, 'expert', [(i, i ^ 1) for i in range(size)])  1 us
  transfers between devices with their start and end apart: 2, of which 1 were waited for; matrix products, arithmetic and copies ran while one was open for 0% of the time, Pallas kernels for 3%

profile of v16, /device:TPU:0, one launch (start us, length us, event | category | flops | bytes accessed | tf_op | source)
XLA Modules:
  0.0 38.6 jit_solution(2418299909641922392)
XLA Ops:
  0.6 0.0 copy-start.4
  0.6 0.0 copy-start.2
  0.7 0.0 copy-start.3
  0.7 0.0 copy-start
  0.7 0.0 copy-start.1
  0.7 0.7 %copy-done.4 = bf16[1280,8]{0,1:T(8,128)(2,1)S(1)} copy-done((bf16[1280,8]{0,1:T(8,128)(2,1)S(1)}, bf16[1280,8]{0,1:T(8,128)(2,1)}, u32[]{:S(2)}) %copy-start.4) | copy-done | bytes 20504
  1.4 0.4 copy-done.2
  1.7 0.8 %shard_map.69 = (f32[8,1280]{1,0:T(8,128)S(1)}, f32[8,256]{1,0:T(8,128)S(1)}, f32[8,256]{1,0:T(8,128)S(1)}) custom-call(bf16[256,1280]{1,0:T(8,128)(2,1)S(1)} %bitcast.6, bf16[8,1280]{1,0:T(8,128)(2,1)S(1)} %bitcast.10, f32[8,128]{1,0:T(8,128)S(1)} %shard_map.68.token_ref), custom_call_target="tpu_custom_call" | custom-call | flops 20971520 | bytes 655360 | tf_op jit(solution)/shard_map/pallas_call | solution.py:121
  2.5 0.0 copy-done.3
  2.5 0.2 shard_map.70
  2.8 11.0 %all_to_all.15.got_ref = bf16[16,2,1280]{2,1,0:T(2,128)(2,1)S(1)} all-to-all(bf16[16,2,1280]{2,1,0:T(2,128)(2,1)S(1)} %shard_map.70), channel_id=1, replica_groups={{15,14,1,0,13,12,3,2,11,10,5,4,9,8,7,6},{31,30,17,16,29,28,19,18,27,26,..., dimensions={0} | all-to-all | bytes 163840 | tf_op jit(solution)/shard_map/all_to_all | solution.py:138
  13.7 0.0 copy-done
  13.7 0.0 copy-done.1
  13.7 2.7 %shard_map.71 = bf16[16,2,1280]{2,1,0:T(2,128)(2,1)S(1)} custom-call(bf16[16,2,1280]{2,1,0:T(2,128)(2,1)S(1)} %all_to_all.15.got_ref, bf16[1280,1280]{1,0:T(8,128)(2,1)S(1)} %copy-done, bf16[1280,1280]{1,0:T(8,128)(2,1)S(1)} %copy-done.1), custom_call_target="tpu_custom_call" | custom-call | flops 209715200 | bytes 6553600 | tf_op jit(solution)/shard_map/pallas_call | solution.py:121
  16.5 9.0 %all_to_all.16.back_ref = bf16[16,2,1280]{2,1,0:T(2,128)(2,1)S(1)} all-to-all(bf16[16,2,1280]{2,1,0:T(2,128)(2,1)S(1)} %shard_map.71), channel_id=1, replica_groups={{15,14,1,0,13,12,3,2,11,10,5,4,9,8,7,6},{31,30,17,16,29,28,19,18,27,26,..., dimensions={0} | all-to-all | bytes 163840 | tf_op jit(solution)/shard_map/all_to_all | solution.py:138
  25.5 0.7 %shard_map.72 = (f32[8,640]{1,0:T(8,128)S(1)}, f32[8,640]{1,0:T(8,128)S(1)}, bf16[16,256]{1,0:T(8,128)(2,1)S(1)}, bf16[16,1280]{1,0:T(8,128)(2,1)S(1)}) custom-call(bf16[256,1280]{1,0:T(8,128)(2,1)S(1)} %bitcast.7, bf16[256,1280]{1,0:T(8,128)(2,1)S(1)} %bitcast.9, bf16[8,1280]{1,0:T(8,128)(2,1)S(1)} %bitcast.11, f32[8,256]{1,0:T(8,128)S(1)} %get-tuple-element.9.dispatch_ref, ...), custom_call_target="tpu_custom_call" | custom-call | flops 31457280 | bytes 1310720 | tf_op jit(solution)/shard_map/pallas_call | solution.py:121
  26.2 0.2 collective-permute-start
  26.4 1.0 %collective-permute-done = f32[8,640]{1,0:T(8,128)S(1)} collective-permute-done((f32[8,640]{1,0:T(8,128)S(1)}, f32[8,640]{1,0:T(8,128)S(1)}, u32[]{:S(2)}, u32[]{:S(2)}) %collective-permute-start) | collective-permute-done | bytes 20512 | tf_op jit(solution)/shard_map/ppermute | solution.py:134
  27.4 9.2 %all_to_all.17 = bf16[8,8,640]{2,1,0:T(8,128)(2,1)S(1)} all-to-all(bf16[8,8,640]{2,1,0:T(8,128)(2,1)S(1)} %broadcast_in_dim.10), channel_id=1, replica_groups={{14,0,12,2,10,4,8,6},{15,1,13,3,11,5,9,7},{30,16,28,18,26,20,24,22},{31..., dimensions={0} | all-to-all | bytes 163840 | tf_op jit(solution)/shard_map/all_to_all | solution.py:138
  36.7 0.1 collective-permute-start.1
  36.7 1.2 %shard_map.73 = bf16[256,1280]{1,0:T(8,128)(2,1)} custom-call(bf16[16,256]{1,0:T(8,128)(2,1)S(1)} %get-tuple-element.12.left_ref, bf16[16,1280]{1,0:T(8,128)(2,1)S(1)} %get-tuple-element.13.right_ref), custom_call_target="tpu_custom_call" | custom-call | flops 10485760 | bytes 655360 | tf_op jit(solution)/shard_map/pallas_call | solution.py:121
  37.9 0.0 collective-permute-done.1
  38.0 0.6 %maximum_bitcast_fusion = f32[1280,8]{0,1:T(8,128)} fusion(f32[8,640]{1,0:T(8,128)S(1)} %get-tuple-element.17, f32[8,640]{1,0:T(8,128)S(1)} %get-tuple-element.16), kind=kLoop, calls=%fused_computation.1 | loop fusion | flops 10240 | bytes 81920 | tf_op jit(solution)/shard_map/transpose | solution.py:217
  (5 shorter events, 0.0 us)
Async XLA Ops:
  0.6 0.7 %copy-start.4 = (bf16[1280,8]{0,1:T(8,128)(2,1)S(1)}, bf16[1280,8]{0,1:T(8,128)(2,1)}, u32[]{:S(2)}) copy-start(bf16[1280,8]{0,1:T(8,128)(2,1)} %param.7) | copy-start | bytes 61444
  0.6 1.1 %copy-start.2 = (bf16[1,256,1280]{2,1,0:T(8,128)(2,1)S(1)}, bf16[1,256,1280]{2,1,0:T(8,128)(2,1)}, u32[]{:S(2)}) copy-start(bf16[1,256,1280]{2,1,0:T(8,128)(2,1)} %param.5) | copy-start | bytes 1966084
  0.7 1.9 %copy-start.3 = (bf16[1,256,1280]{2,1,0:T(8,128)(2,1)S(1)}, bf16[1,256,1280]{2,1,0:T(8,128)(2,1)}, u32[]{:S(2)}) copy-start(bf16[1,256,1280]{2,1,0:T(8,128)(2,1)} %param.6) | copy-start | bytes 1966084
  0.7 13.1 %copy-start = (bf16[1280,1280]{1,0:T(8,128)(2,1)S(1)}, bf16[1280,1280]{1,0:T(8,128)(2,1)}, u32[]{:S(2)}) copy-start(bf16[1280,1280]{1,0:T(8,128)(2,1)} %in_weight_ref.1) | copy-start | bytes 9830404
  0.7 13.1 %copy-start.1 = (bf16[1280,1280]{1,0:T(8,128)(2,1)S(1)}, bf16[1280,1280]{1,0:T(8,128)(2,1)}, u32[]{:S(2)}) copy-start(bf16[1280,1280]{1,0:T(8,128)(2,1)} %out_weight_ref.1) | copy-start | bytes 9830404
  26.2 1.2 %collective-permute-start = (f32[8,640]{1,0:T(8,128)S(1)}, f32[8,640]{1,0:T(8,128)S(1)}, u32[]{:S(2)}, u32[]{:S(2)}) collective-permute-start(f32[8,640]{1,0:T(8,128)S(1)} %get-tuple-element.15), channel_id=1, source_target_pairs={{0,1},{1,0},{2,3},{3,2},{4,5},{5,4},{6,7},{7,6},{8,9},{9,8},{10,11... | collective-permute-start | bytes 61448 | tf_op jit(solution)/shard_map/ppermute | solution.py:134
  36.7 1.3 %collective-permute-start.1 = (f32[8,640]{1,0:T(8,128)S(1)}, f32[8,640]{1,0:T(8,128)S(1)}, u32[]{:S(2)}, u32[]{:S(2)}) collective-permute-start(f32[8,640]{1,0:T(8,128)S(1)} %convert_reduce_fusion), channel_id=1, source_target_pairs={{0,1},{1,0},{2,3},{3,2},{4,5},{5,4},{6,7},{7,6},{8,9},{9,8},{10,11... | collective-permute-start | bytes 61448 | tf_op jit(solution)/shard_map/ppermute | solution.py:134

commit v17 on v16

--- a/solution.py
+++ b/solution.py
@@ -15,12 +15,18 @@
 AHEAD_FLOPS = 3 * 10**10
 
 
-def chip_order(chips):
-    return [k // 2 if k % 2 else chips - 1 - k // 2 for k in range(chips)]
-
-
-def everybody(chips):
-    return [2 * chip + core for chip in chip_order(chips) for core in (1, 0)]
+def out_order(size):
+    return [size - 1] + list(range(1, size - 1)) + [0]
+
+
+def back_order(size):
+    return [(size - 1 + 5 * k) % size for k in range(size)]
+
+
+def sum_order(size, core):
+    chips = size // 2
+    order = [k // 2 if k % 2 else chips - 1 - k // 2 for k in range(chips)]
+    return [2 * chip + core for chip in order]
 
 
 def dot(a, b, dims):
@@ -44,7 +50,7 @@
 def messages_kernel(grad_ref, combine_ref, slot_in_ref, sent_ref):
     slot_grad = dot(combine_ref[...].astype(BF16), grad_ref[...], NN)
     slots = slot_in_ref.shape[0]
-    order = everybody(slots)
+    order = out_order(2 * slots)
     for s in range(slots):
         rows = [slot_in_ref[s : s + 1], slot_grad[s : s + 1]]
         message = jnp.concatenate(rows, axis=0).astype(BF16)
@@ -56,6 +62,7 @@
     got_ref, in_weight_ref, out_weight_ref, parts_ref, in_rows_ref, grad_rows_ref
 ):
     images = got_ref.shape[0]
+    out, back = out_order(images), back_order(images)
     for k in range(images):
         message = got_ref[k].astype(F32)
         in_rows_ref[k : k + 1] = message[0:1]
@@ -70,7 +77,7 @@
     part_in = dot(hidden_grad, in_weight_ref[...], NT)
     for k in range(images):
         rows = [part_out[k : k + 1], part_in[k : k + 1]]
-        parts_ref[k] = jnp.concatenate(rows, axis=0).astype(BF16)
+        parts_ref[back.index(out[k])] = jnp.concatenate(rows, axis=0).astype(BF16)
 
 
 def logits_kernel(
@@ -88,7 +95,7 @@
     back_rows_ref,
 ):
     slots = router_ref.shape[0]
-    order = everybody(slots)
+    order = back_order(2 * slots)
     for s in range(slots):
         halves = [back_ref[order.index(2 * s + half)].astype(F32) for half in range(2)]
         message = halves[0] + halves[1]
@@ -169,7 +176,7 @@
         combine,
         slot_in,
     )
-    got = exchange(sent, [everybody(chips)])
+    got = exchange(sent, [out_order(2 * chips)])
     (parts,) = call(
         experts_kernel,
         [((2 * chips, 2, width), BF16)],
@@ -179,7 +186,7 @@
         in_weight,
         out_weight,
     )
-    back = exchange(parts, [everybody(chips)])
+    back = exchange(parts, [back_order(2 * chips)])
     kept, given, left, right = call(
         logits_kernel,
         [
@@ -198,7 +205,7 @@
         back,
     )
     pair = (kept + swap_cores(given)).astype(BF16)
-    same_core = [everybody(chips)[1 - core :: 2] for core in range(2)]
+    same_core = [sum_order(2 * chips, core) for core in range(2)]
     terms = exchange(jnp.broadcast_to(pair[None], (chips,) + pair.shape), same_core)
     total = jnp.sum(terms.astype(F32), axis=0)
     other = swap_cores(total)

time: 38.8 us -> 38.7 us (level)
  no operation moved by 1% of the time
where the time goes in v17:
time: 38.7 us; the launch traced here: 38.4 us
  blocking collectives  29 us (75%)
  Pallas kernels  5.63 us (15%)
  local copies, waits for them, and re-layouts  1.07 us (3%)
  waiting for transfers between devices  0.93 us (2%)
  between operations  0.73 us (2%)
  other arithmetic  0.65 us (2%)
    all_to_all x3, blocking collectives, exchange(): lax.all_to_all(value, 'expert', split_axis=0, concat_axis=0, tiled=True,...  29 us
    pallas_call x6, Pallas kernels, call(): pl.pallas_call(kernel, out_shape=[jax.ShapeDtypeStruct(shape, dtype) for...  5.63 us
    unnamed x10, local copies, waits for them, and re-layouts  1.06 us
    ppermute x2, waiting for transfers between devices, swap_cores(): return lax.ppermute(value, 'expert', [(i, i ^ 1) for i in range(size)])  0.93 us
  transfers between devices with their start and end apart: 2, of which 1 were waited for; matrix products, arithmetic and copies ran while one was open for 0% of the time, Pallas kernels for 3%

profile of v17, /device:TPU:0, one launch (start us, length us, event | category | flops | bytes accessed | tf_op | source)
XLA Modules:
  0.0 38.4 jit_solution(225370532430676634)
XLA Ops:
  0.6 0.0 copy-start.4
  0.6 0.0 copy-start.2
  0.7 0.0 copy-start.3
  0.7 0.0 copy-start
  0.7 0.0 copy-start.1
  0.7 0.7 %copy-done.4 = bf16[1280,8]{0,1:T(8,128)(2,1)S(1)} copy-done((bf16[1280,8]{0,1:T(8,128)(2,1)S(1)}, bf16[1280,8]{0,1:T(8,128)(2,1)}, u32[]{:S(2)}) %copy-start.4) | copy-done | bytes 20504
  1.4 0.4 copy-done.2
  1.7 0.8 %shard_map.69 = (f32[8,1280]{1,0:T(8,128)S(1)}, f32[8,256]{1,0:T(8,128)S(1)}, f32[8,256]{1,0:T(8,128)S(1)}) custom-call(bf16[256,1280]{1,0:T(8,128)(2,1)S(1)} %bitcast.6, bf16[8,1280]{1,0:T(8,128)(2,1)S(1)} %bitcast.10, f32[8,128]{1,0:T(8,128)S(1)} %shard_map.68.token_ref), custom_call_target="tpu_custom_call" | custom-call | flops 20971520 | bytes 655360 | tf_op jit(solution)/shard_map/pallas_call | solution.py:128
  2.5 0.0 copy-done.3
  2.5 0.2 shard_map.70
  2.8 11.3 %all_to_all.15.got_ref = bf16[16,2,1280]{2,1,0:T(2,128)(2,1)S(1)} all-to-all(bf16[16,2,1280]{2,1,0:T(2,128)(2,1)S(1)} %shard_map.70), channel_id=1, replica_groups={{15,1,2,3,4,5,6,7,8,9,10,11,12,13,14,0},{31,17,18,19,20,21,22,23,24,25,..., dimensions={0} | all-to-all | bytes 163840 | tf_op jit(solution)/shard_map/all_to_all | solution.py:145
  14.0 0.0 copy-done
  14.0 0.0 copy-done.1
  14.0 2.7 %shard_map.71 = bf16[16,2,1280]{2,1,0:T(2,128)(2,1)S(1)} custom-call(bf16[16,2,1280]{2,1,0:T(2,128)(2,1)S(1)} %all_to_all.15.got_ref, bf16[1280,1280]{1,0:T(8,128)(2,1)S(1)} %copy-done, bf16[1280,1280]{1,0:T(8,128)(2,1)S(1)} %copy-done.1), custom_call_target="tpu_custom_call" | custom-call | flops 209715200 | bytes 6553600 | tf_op jit(solution)/shard_map/pallas_call | solution.py:128
  16.8 8.4 %all_to_all.16.back_ref = bf16[16,2,1280]{2,1,0:T(2,128)(2,1)S(1)} all-to-all(bf16[16,2,1280]{2,1,0:T(2,128)(2,1)S(1)} %shard_map.71), channel_id=1, replica_groups={{15,4,9,14,3,8,13,2,7,12,1,6,11,0,5,10},{31,20,25,30,19,24,29,18,23,28,..., dimensions={0} | all-to-all | bytes 163840 | tf_op jit(solution)/shard_map/all_to_all | solution.py:145
  25.2 0.7 %shard_map.72 = (f32[8,640]{1,0:T(8,128)S(1)}, f32[8,640]{1,0:T(8,128)S(1)}, bf16[16,256]{1,0:T(8,128)(2,1)S(1)}, bf16[16,1280]{1,0:T(8,128)(2,1)S(1)}) custom-call(bf16[256,1280]{1,0:T(8,128)(2,1)S(1)} %bitcast.7, bf16[256,1280]{1,0:T(8,128)(2,1)S(1)} %bitcast.9, bf16[8,1280]{1,0:T(8,128)(2,1)S(1)} %bitcast.11, f32[8,256]{1,0:T(8,128)S(1)} %get-tuple-element.9.dispatch_ref, ...), custom_call_target="tpu_custom_call" | custom-call | flops 31457280 | bytes 1310720 | tf_op jit(solution)/shard_map/pallas_call | solution.py:128
  25.9 0.3 collective-permute-start
  26.2 0.9 %collective-permute-done = f32[8,640]{1,0:T(8,128)S(1)} collective-permute-done((f32[8,640]{1,0:T(8,128)S(1)}, f32[8,640]{1,0:T(8,128)S(1)}, u32[]{:S(2)}, u32[]{:S(2)}) %collective-permute-start) | collective-permute-done | bytes 20512 | tf_op jit(solution)/shard_map/ppermute | solution.py:141
  27.1 9.4 %all_to_all.17 = bf16[8,8,640]{2,1,0:T(8,128)(2,1)S(1)} all-to-all(bf16[8,8,640]{2,1,0:T(8,128)(2,1)S(1)} %broadcast_in_dim.10), channel_id=1, replica_groups={{14,0,12,2,10,4,8,6},{15,1,13,3,11,5,9,7},{30,16,28,18,26,20,24,22},{31..., dimensions={0} | all-to-all | bytes 163840 | tf_op jit(solution)/shard_map/all_to_all | solution.py:145
  36.5 0.1 collective-permute-start.1
  36.6 1.2 %shard_map.73 = bf16[256,1280]{1,0:T(8,128)(2,1)} custom-call(bf16[16,256]{1,0:T(8,128)(2,1)S(1)} %get-tuple-element.12.left_ref, bf16[16,1280]{1,0:T(8,128)(2,1)S(1)} %get-tuple-element.13.right_ref), custom_call_target="tpu_custom_call" | custom-call | flops 10485760 | bytes 655360 | tf_op jit(solution)/shard_map/pallas_call | solution.py:128
  37.8 0.0 collective-permute-done.1
  37.8 0.6 %maximum_bitcast_fusion = f32[1280,8]{0,1:T(8,128)} fusion(f32[8,640]{1,0:T(8,128)S(1)} %get-tuple-element.17, f32[8,640]{1,0:T(8,128)S(1)} %get-tuple-element.16), kind=kLoop, calls=%fused_computation.1 | loop fusion | flops 10240 | bytes 81920 | tf_op jit(solution)/shard_map/transpose | solution.py:224
  (5 shorter events, 0.0 us)
Async XLA Ops:
  0.6 0.7 %copy-start.4 = (bf16[1280,8]{0,1:T(8,128)(2,1)S(1)}, bf16[1280,8]{0,1:T(8,128)(2,1)}, u32[]{:S(2)}) copy-start(bf16[1280,8]{0,1:T(8,128)(2,1)} %param.7) | copy-start | bytes 61444
  0.6 1.1 %copy-start.2 = (bf16[1,256,1280]{2,1,0:T(8,128)(2,1)S(1)}, bf16[1,256,1280]{2,1,0:T(8,128)(2,1)}, u32[]{:S(2)}) copy-start(bf16[1,256,1280]{2,1,0:T(8,128)(2,1)} %param.5) | copy-start | bytes 1966084
  0.7 1.9 %copy-start.3 = (bf16[1,256,1280]{2,1,0:T(8,128)(2,1)S(1)}, bf16[1,256,1280]{2,1,0:T(8,128)(2,1)}, u32[]{:S(2)}) copy-start(bf16[1,256,1280]{2,1,0:T(8,128)(2,1)} %param.6) | copy-start | bytes 1966084
  0.7 13.4 %copy-start = (bf16[1280,1280]{1,0:T(8,128)(2,1)S(1)}, bf16[1280,1280]{1,0:T(8,128)(2,1)}, u32[]{:S(2)}) copy-start(bf16[1280,1280]{1,0:T(8,128)(2,1)} %in_weight_ref.1) | copy-start | bytes 9830404
  0.7 13.4 %copy-start.1 = (bf16[1280,1280]{1,0:T(8,128)(2,1)S(1)}, bf16[1280,1280]{1,0:T(8,128)(2,1)}, u32[]{:S(2)}) copy-start(bf16[1280,1280]{1,0:T(8,128)(2,1)} %out_weight_ref.1) | copy-start | bytes 9830404
  25.9 1.2 %collective-permute-start = (f32[8,640]{1,0:T(8,128)S(1)}, f32[8,640]{1,0:T(8,128)S(1)}, u32[]{:S(2)}, u32[]{:S(2)}) collective-permute-start(f32[8,640]{1,0:T(8,128)S(1)} %get-tuple-element.15), channel_id=1, source_target_pairs={{0,1},{1,0},{2,3},{3,2},{4,5},{5,4},{6,7},{7,6},{8,9},{9,8},{10,11... | collective-permute-start | bytes 61448 | tf_op jit(solution)/shard_map/ppermute | solution.py:141
  36.5 1.3 %collective-permute-start.1 = (f32[8,640]{1,0:T(8,128)S(1)}, f32[8,640]{1,0:T(8,128)S(1)}, u32[]{:S(2)}, u32[]{:S(2)}) collective-permute-start(f32[8,640]{1,0:T(8,128)S(1)} %convert_reduce_fusion), channel_id=1, source_target_pairs={{0,1},{1,0},{2,3},{3,2},{4,5},{5,4},{6,7},{7,6},{8,9},{9,8},{10,11... | collective-permute-start | bytes 61448 | tf_op jit(solution)/shard_map/ppermute | solution.py:141

commit v18 on v16

--- a/solution.py
+++ b/solution.py
@@ -15,12 +15,8 @@
 AHEAD_FLOPS = 3 * 10**10
 
 
-def chip_order(chips):
-    return [k // 2 if k % 2 else chips - 1 - k // 2 for k in range(chips)]
-
-
-def everybody(chips):
-    return [2 * chip + core for chip in chip_order(chips) for core in (1, 0)]
+def listed(count):
+    return [(count - 1 + 5 * k) % count for k in range(count)]
 
 
 def dot(a, b, dims):
@@ -44,7 +40,7 @@
 def messages_kernel(grad_ref, combine_ref, slot_in_ref, sent_ref):
     slot_grad = dot(combine_ref[...].astype(BF16), grad_ref[...], NN)
     slots = slot_in_ref.shape[0]
-    order = everybody(slots)
+    order = listed(2 * slots)
     for s in range(slots):
         rows = [slot_in_ref[s : s + 1], slot_grad[s : s + 1]]
         message = jnp.concatenate(rows, axis=0).astype(BF16)
@@ -88,7 +84,7 @@
     back_rows_ref,
 ):
     slots = router_ref.shape[0]
-    order = everybody(slots)
+    order = listed(2 * slots)
     for s in range(slots):
         halves = [back_ref[order.index(2 * s + half)].astype(F32) for half in range(2)]
         message = halves[0] + halves[1]
@@ -169,7 +165,7 @@
         combine,
         slot_in,
     )
-    got = exchange(sent, [everybody(chips)])
+    got = exchange(sent, [listed(2 * chips)])
     (parts,) = call(
         experts_kernel,
         [((2 * chips, 2, width), BF16)],
@@ -179,7 +175,7 @@
         in_weight,
         out_weight,
     )
-    back = exchange(parts, [everybody(chips)])
+    back = exchange(parts, [listed(2 * chips)])
     kept, given, left, right = call(
         logits_kernel,
         [
@@ -198,7 +194,7 @@
         back,
     )
     pair = (kept + swap_cores(given)).astype(BF16)
-    same_core = [everybody(chips)[1 - core :: 2] for core in range(2)]
+    same_core = [[2 * chip + core for chip in listed(chips)] for core in range(2)]
     terms = exchange(jnp.broadcast_to(pair[None], (chips,) + pair.shape), same_core)
     total = jnp.sum(terms.astype(F32), axis=0)
     other = swap_cores(total)

time: 38.8 us -> 39.1 us (level)
  no operation moved by 1% of the time
where the time goes in v18:
time: 39.1 us; the launch traced here: 38.8 us
  blocking collectives  29.5 us (75%)
  Pallas kernels  5.63 us (14%)
  local copies, waits for them, and re-layouts  1.07 us (3%)
  waiting for transfers between devices  1 us (3%)
  between operations  0.73 us (2%)
  other arithmetic  0.65 us (2%)
    all_to_all x3, blocking collectives, exchange(): lax.all_to_all(value, 'expert', split_axis=0, concat_axis=0, tiled=True,...  29.5 us
    pallas_call x6, Pallas kernels, call(): pl.pallas_call(kernel, out_shape=[jax.ShapeDtypeStruct(shape, dtype) for...  5.63 us
    unnamed x10, local copies, waits for them, and re-layouts  1.06 us
    ppermute x2, waiting for transfers between devices, swap_cores(): return lax.ppermute(value, 'expert', [(i, i ^ 1) for i in range(size)])  1 us
  transfers between devices with their start and end apart: 2, of which 1 were waited for; matrix products, arithmetic and copies ran while one was open for 0% of the time, Pallas kernels for 3%

profile of v18, /device:TPU:0, one launch (start us, length us, event | category | flops | bytes accessed | tf_op | source)
XLA Modules:
  0.0 38.8 jit_solution(12232629513867908543)
XLA Ops:
  0.6 0.0 copy-start.4
  0.6 0.0 copy-start.2
  0.7 0.0 copy-start.3
  0.7 0.0 copy-start
  0.7 0.0 copy-start.1
  0.7 0.7 %copy-done.4 = bf16[1280,8]{0,1:T(8,128)(2,1)S(1)} copy-done((bf16[1280,8]{0,1:T(8,128)(2,1)S(1)}, bf16[1280,8]{0,1:T(8,128)(2,1)}, u32[]{:S(2)}) %copy-start.4) | copy-done | bytes 20504
  1.4 0.4 copy-done.2
  1.7 0.8 %shard_map.69 = (f32[8,1280]{1,0:T(8,128)S(1)}, f32[8,256]{1,0:T(8,128)S(1)}, f32[8,256]{1,0:T(8,128)S(1)}) custom-call(bf16[256,1280]{1,0:T(8,128)(2,1)S(1)} %bitcast.6, bf16[8,1280]{1,0:T(8,128)(2,1)S(1)} %bitcast.10, f32[8,128]{1,0:T(8,128)S(1)} %shard_map.68.token_ref), custom_call_target="tpu_custom_call" | custom-call | flops 20971520 | bytes 655360 | tf_op jit(solution)/shard_map/pallas_call | solution.py:117
  2.5 0.0 copy-done.3
  2.5 0.2 shard_map.70
  2.8 11.1 %all_to_all.15.got_ref = bf16[16,2,1280]{2,1,0:T(2,128)(2,1)S(1)} all-to-all(bf16[16,2,1280]{2,1,0:T(2,128)(2,1)S(1)} %shard_map.70), channel_id=1, replica_groups={{15,4,9,14,3,8,13,2,7,12,1,6,11,0,5,10},{31,20,25,30,19,24,29,18,23,28,..., dimensions={0} | all-to-all | bytes 163840 | tf_op jit(solution)/shard_map/all_to_all | solution.py:134
  13.8 0.0 copy-done
  13.8 0.0 copy-done.1
  13.8 2.7 %shard_map.71 = bf16[16,2,1280]{2,1,0:T(2,128)(2,1)S(1)} custom-call(bf16[16,2,1280]{2,1,0:T(2,128)(2,1)S(1)} %all_to_all.15.got_ref, bf16[1280,1280]{1,0:T(8,128)(2,1)S(1)} %copy-done, bf16[1280,1280]{1,0:T(8,128)(2,1)S(1)} %copy-done.1), custom_call_target="tpu_custom_call" | custom-call | flops 209715200 | bytes 6553600 | tf_op jit(solution)/shard_map/pallas_call | solution.py:117
  16.6 8.9 %all_to_all.16.back_ref = bf16[16,2,1280]{2,1,0:T(2,128)(2,1)S(1)} all-to-all(bf16[16,2,1280]{2,1,0:T(2,128)(2,1)S(1)} %shard_map.71), channel_id=1, replica_groups={{15,4,9,14,3,8,13,2,7,12,1,6,11,0,5,10},{31,20,25,30,19,24,29,18,23,28,..., dimensions={0} | all-to-all | bytes 163840 | tf_op jit(solution)/shard_map/all_to_all | solution.py:134
  25.5 0.7 %shard_map.72 = (f32[8,640]{1,0:T(8,128)S(1)}, f32[8,640]{1,0:T(8,128)S(1)}, bf16[16,256]{1,0:T(8,128)(2,1)S(1)}, bf16[16,1280]{1,0:T(8,128)(2,1)S(1)}) custom-call(bf16[256,1280]{1,0:T(8,128)(2,1)S(1)} %bitcast.7, bf16[256,1280]{1,0:T(8,128)(2,1)S(1)} %bitcast.9, bf16[8,1280]{1,0:T(8,128)(2,1)S(1)} %bitcast.11, f32[8,256]{1,0:T(8,128)S(1)} %get-tuple-element.9.dispatch_ref, ...), custom_call_target="tpu_custom_call" | custom-call | flops 31457280 | bytes 1310720 | tf_op jit(solution)/shard_map/pallas_call | solution.py:117
  26.1 0.2 collective-permute-start
  26.4 1.0 %collective-permute-done = f32[8,640]{1,0:T(8,128)S(1)} collective-permute-done((f32[8,640]{1,0:T(8,128)S(1)}, f32[8,640]{1,0:T(8,128)S(1)}, u32[]{:S(2)}, u32[]{:S(2)}) %collective-permute-start) | collective-permute-done | bytes 20512 | tf_op jit(solution)/shard_map/ppermute | solution.py:130
  27.4 9.5 %all_to_all.17 = bf16[8,8,640]{2,1,0:T(8,128)(2,1)S(1)} all-to-all(bf16[8,8,640]{2,1,0:T(8,128)(2,1)S(1)} %broadcast_in_dim.10), channel_id=1, replica_groups={{14,8,2,12,6,0,10,4},{15,9,3,13,7,1,11,5},{30,24,18,28,22,16,26,20},{31..., dimensions={0} | all-to-all | bytes 163840 | tf_op jit(solution)/shard_map/all_to_all | solution.py:134
  36.9 0.1 collective-permute-start.1
  37.0 1.2 %shard_map.73 = bf16[256,1280]{1,0:T(8,128)(2,1)} custom-call(bf16[16,256]{1,0:T(8,128)(2,1)S(1)} %get-tuple-element.12.left_ref, bf16[16,1280]{1,0:T(8,128)(2,1)S(1)} %get-tuple-element.13.right_ref), custom_call_target="tpu_custom_call" | custom-call | flops 10485760 | bytes 655360 | tf_op jit(solution)/shard_map/pallas_call | solution.py:117
  38.2 0.0 collective-permute-done.1
  38.2 0.6 %maximum_bitcast_fusion = f32[1280,8]{0,1:T(8,128)} fusion(f32[8,640]{1,0:T(8,128)S(1)} %get-tuple-element.17, f32[8,640]{1,0:T(8,128)S(1)} %get-tuple-element.16), kind=kLoop, calls=%fused_computation.1 | loop fusion | flops 10240 | bytes 81920 | tf_op jit(solution)/shard_map/transpose | solution.py:213
  (5 shorter events, 0.0 us)
Async XLA Ops:
  0.6 0.7 %copy-start.4 = (bf16[1280,8]{0,1:T(8,128)(2,1)S(1)}, bf16[1280,8]{0,1:T(8,128)(2,1)}, u32[]{:S(2)}) copy-start(bf16[1280,8]{0,1:T(8,128)(2,1)} %param.7) | copy-start | bytes 61444
  0.6 1.1 %copy-start.2 = (bf16[1,256,1280]{2,1,0:T(8,128)(2,1)S(1)}, bf16[1,256,1280]{2,1,0:T(8,128)(2,1)}, u32[]{:S(2)}) copy-start(bf16[1,256,1280]{2,1,0:T(8,128)(2,1)} %param.5) | copy-start | bytes 1966084
  0.7 1.9 %copy-start.3 = (bf16[1,256,1280]{2,1,0:T(8,128)(2,1)S(1)}, bf16[1,256,1280]{2,1,0:T(8,128)(2,1)}, u32[]{:S(2)}) copy-start(bf16[1,256,1280]{2,1,0:T(8,128)(2,1)} %param.6) | copy-start | bytes 1966084
  0.7 13.2 %copy-start = (bf16[1280,1280]{1,0:T(8,128)(2,1)S(1)}, bf16[1280,1280]{1,0:T(8,128)(2,1)}, u32[]{:S(2)}) copy-start(bf16[1280,1280]{1,0:T(8,128)(2,1)} %in_weight_ref.1) | copy-start | bytes 9830404
  0.7 13.2 %copy-start.1 = (bf16[1280,1280]{1,0:T(8,128)(2,1)S(1)}, bf16[1280,1280]{1,0:T(8,128)(2,1)}, u32[]{:S(2)}) copy-start(bf16[1280,1280]{1,0:T(8,128)(2,1)} %out_weight_ref.1) | copy-start | bytes 9830404
  26.1 1.2 %collective-permute-start = (f32[8,640]{1,0:T(8,128)S(1)}, f32[8,640]{1,0:T(8,128)S(1)}, u32[]{:S(2)}, u32[]{:S(2)}) collective-permute-start(f32[8,640]{1,0:T(8,128)S(1)} %get-tuple-element.15), channel_id=1, source_target_pairs={{0,1},{1,0},{2,3},{3,2},{4,5},{5,4},{6,7},{7,6},{8,9},{9,8},{10,11... | collective-permute-start | bytes 61448 | tf_op jit(solution)/shard_map/ppermute | solution.py:130
  36.9 1.3 %collective-permute-start.1 = (f32[8,640]{1,0:T(8,128)S(1)}, f32[8,640]{1,0:T(8,128)S(1)}, u32[]{:S(2)}, u32[]{:S(2)}) collective-permute-start(f32[8,640]{1,0:T(8,128)S(1)} %convert_reduce_fusion), channel_id=1, source_target_pairs={{0,1},{1,0},{2,3},{3,2},{4,5},{5,4},{6,7},{7,6},{8,9},{9,8},{10,11... | collective-permute-start | bytes 61448 | tf_op jit(solution)/shard_map/ppermute | solution.py:130

commit v19 on v17

--- a/solution.py
+++ b/solution.py
@@ -213,14 +213,21 @@
     router_grad = jnp.concatenate(
         [jnp.where(first, total, other), jnp.where(first, other, total)], axis=1
     )
-    (tokens_grad,) = call(
+    block = patches // 2
+    tokens_grad = pl.pallas_call(
         tokens_kernel,
-        [((patches, width), BF16)],
-        [],
-        (4 * patches * width * slots, image_bytes),
-        left,
-        right,
-    )
+        grid=(patches // block,),
+        out_shape=jax.ShapeDtypeStruct((patches, width), BF16),
+        in_specs=[
+            pl.BlockSpec((2 * slots, block), lambda i: (0, i)),
+            pl.BlockSpec((2 * slots, width), lambda i: (0, 0)),
+        ],
+        out_specs=pl.BlockSpec((block, width), lambda i: (i, 0)),
+        compiler_params=pltpu.CompilerParams(vmem_limit_bytes=16 * 1024 * 1024),
+        cost_estimate=pl.CostEstimate(
+            flops=4 * patches * width * slots, bytes_accessed=image_bytes, transcendentals=0
+        ),
+    )(left, right)
     return (tokens_grad[None], router_grad.T)
 
 

time: 38.7 us -> 38.8 us (level)
    pallas_call x0 -> x1, Pallas kernels: none -> 1.31 us  [per_device(): pl.pallas_call(tokens_kernel, grid=(patches // block,), out_shape=jax.Sha...]
    pallas_call x6 -> x5, Pallas kernels: 5.63 us -> 4.43 us  [call(): pl.pallas_call(kernel, out_shape=[jax.ShapeDtypeStruct(shape, dtype) for...]
where the time goes in v19:
time: 38.8 us; the launch traced here: 38.5 us
  blocking collectives  29 us (75%)
  Pallas kernels  5.74 us (15%)
  local copies, waits for them, and re-layouts  1.07 us (3%)
  waiting for transfers between devices  0.93 us (2%)
  between operations  0.73 us (2%)
  other arithmetic  0.65 us (2%)
    all_to_all x3, blocking collectives, exchange(): lax.all_to_all(value, 'expert', split_axis=0, concat_axis=0, tiled=True,...  29 us
    pallas_call x5, Pallas kernels, call(): pl.pallas_call(kernel, out_shape=[jax.ShapeDtypeStruct(shape, dtype) for...  4.43 us
    pallas_call x1, Pallas kernels, per_device(): pl.pallas_call(tokens_kernel, grid=(patches // block,), out_shape=jax.Sha...  1.31 us
    unnamed x10, local copies, waits for them, and re-layouts  1.06 us
    ppermute x2, waiting for transfers between devices, swap_cores(): return lax.ppermute(value, 'expert', [(i, i ^ 1) for i in range(size)])  0.93 us
  transfers between devices with their start and end apart: 2, of which 1 were waited for; matrix products, arithmetic and copies ran while one was open for 0% of the time, Pallas kernels for 3%

profile of v19, /device:TPU:0, one launch (start us, length us, event | category | flops | bytes accessed | tf_op | source)
XLA Modules:
  0.0 38.5 jit_solution(16363297747731571884)
XLA Ops:
  0.6 0.0 copy-start.4
  0.6 0.0 copy-start.2
  0.7 0.0 copy-start.3
  0.7 0.0 copy-start
  0.7 0.0 copy-start.1
  0.7 0.7 %copy-done.4 = bf16[1280,8]{0,1:T(8,128)(2,1)S(1)} copy-done((bf16[1280,8]{0,1:T(8,128)(2,1)S(1)}, bf16[1280,8]{0,1:T(8,128)(2,1)}, u32[]{:S(2)}) %copy-start.4) | copy-done | bytes 20504
  1.4 0.4 copy-done.2
  1.7 0.8 %shard_map.69 = (f32[8,1280]{1,0:T(8,128)S(1)}, f32[8,256]{1,0:T(8,128)S(1)}, f32[8,256]{1,0:T(8,128)S(1)}) custom-call(bf16[256,1280]{1,0:T(8,128)(2,1)S(1)} %bitcast.6, bf16[8,1280]{1,0:T(8,128)(2,1)S(1)} %bitcast.10, f32[8,128]{1,0:T(8,128)S(1)} %shard_map.68.token_ref), custom_call_target="tpu_custom_call" | custom-call | flops 20971520 | bytes 655360 | tf_op jit(solution)/shard_map/pallas_call | solution.py:128
  2.5 0.0 copy-done.3
  2.5 0.2 shard_map.70
  2.8 11.3 %all_to_all.15.got_ref = bf16[16,2,1280]{2,1,0:T(2,128)(2,1)S(1)} all-to-all(bf16[16,2,1280]{2,1,0:T(2,128)(2,1)S(1)} %shard_map.70), channel_id=1, replica_groups={{15,1,2,3,4,5,6,7,8,9,10,11,12,13,14,0},{31,17,18,19,20,21,22,23,24,25,..., dimensions={0} | all-to-all | bytes 163840 | tf_op jit(solution)/shard_map/all_to_all | solution.py:145
  14.0 0.0 copy-done
  14.0 0.0 copy-done.1
  14.0 2.7 %shard_map.71 = bf16[16,2,1280]{2,1,0:T(2,128)(2,1)S(1)} custom-call(bf16[16,2,1280]{2,1,0:T(2,128)(2,1)S(1)} %all_to_all.15.got_ref, bf16[1280,1280]{1,0:T(8,128)(2,1)S(1)} %copy-done, bf16[1280,1280]{1,0:T(8,128)(2,1)S(1)} %copy-done.1), custom_call_target="tpu_custom_call" | custom-call | flops 209715200 | bytes 6553600 | tf_op jit(solution)/shard_map/pallas_call | solution.py:128
  16.8 8.4 %all_to_all.16.back_ref = bf16[16,2,1280]{2,1,0:T(2,128)(2,1)S(1)} all-to-all(bf16[16,2,1280]{2,1,0:T(2,128)(2,1)S(1)} %shard_map.71), channel_id=1, replica_groups={{15,4,9,14,3,8,13,2,7,12,1,6,11,0,5,10},{31,20,25,30,19,24,29,18,23,28,..., dimensions={0} | all-to-all | bytes 163840 | tf_op jit(solution)/shard_map/all_to_all | solution.py:145
  25.2 0.7 %shard_map.72 = (f32[8,640]{1,0:T(8,128)S(1)}, f32[8,640]{1,0:T(8,128)S(1)}, bf16[16,256]{1,0:T(8,128)(2,1)S(1)}, bf16[16,1280]{1,0:T(8,128)(2,1)S(1)}) custom-call(bf16[256,1280]{1,0:T(8,128)(2,1)S(1)} %bitcast.7, bf16[256,1280]{1,0:T(8,128)(2,1)S(1)} %bitcast.9, bf16[8,1280]{1,0:T(8,128)(2,1)S(1)} %bitcast.11, f32[8,256]{1,0:T(8,128)S(1)} %get-tuple-element.9.dispatch_ref, ...), custom_call_target="tpu_custom_call" | custom-call | flops 31457280 | bytes 1310720 | tf_op jit(solution)/shard_map/pallas_call | solution.py:128
  25.9 0.3 collective-permute-start
  26.2 0.9 %collective-permute-done = f32[8,640]{1,0:T(8,128)S(1)} collective-permute-done((f32[8,640]{1,0:T(8,128)S(1)}, f32[8,640]{1,0:T(8,128)S(1)}, u32[]{:S(2)}, u32[]{:S(2)}) %collective-permute-start) | collective-permute-done | bytes 20512 | tf_op jit(solution)/shard_map/ppermute | solution.py:141
  27.1 9.4 %all_to_all.17 = bf16[8,8,640]{2,1,0:T(8,128)(2,1)S(1)} all-to-all(bf16[8,8,640]{2,1,0:T(8,128)(2,1)S(1)} %broadcast_in_dim.10), channel_id=1, replica_groups={{14,0,12,2,10,4,8,6},{15,1,13,3,11,5,9,7},{30,16,28,18,26,20,24,22},{31..., dimensions={0} | all-to-all | bytes 163840 | tf_op jit(solution)/shard_map/all_to_all | solution.py:145
  36.5 0.1 collective-permute-start.1
  36.6 1.3 %shard_map.73 = bf16[256,1280]{1,0:T(8,128)(2,1)} custom-call(bf16[16,256]{1,0:T(8,128)(2,1)S(1)} %get-tuple-element.12.left_ref, bf16[16,1280]{1,0:T(8,128)(2,1)S(1)} %get-tuple-element.13.right_ref), custom_call_target="tpu_custom_call" | custom-call | flops 10485760 | bytes 655360 | tf_op jit(solution)/shard_map/pallas_call | solution.py:217
  37.9 0.0 collective-permute-done.1
  37.9 0.6 %maximum_bitcast_fusion = f32[1280,8]{0,1:T(8,128)} fusion(f32[8,640]{1,0:T(8,128)S(1)} %get-tuple-element.17, f32[8,640]{1,0:T(8,128)S(1)} %get-tuple-element.16), kind=kLoop, calls=%fused_computation.1 | loop fusion | flops 10240 | bytes 81920 | tf_op jit(solution)/shard_map/transpose | solution.py:231
  (5 shorter events, 0.0 us)
Async XLA Ops:
  0.6 0.7 %copy-start.4 = (bf16[1280,8]{0,1:T(8,128)(2,1)S(1)}, bf16[1280,8]{0,1:T(8,128)(2,1)}, u32[]{:S(2)}) copy-start(bf16[1280,8]{0,1:T(8,128)(2,1)} %param.7) | copy-start | bytes 61444
  0.6 1.1 %copy-start.2 = (bf16[1,256,1280]{2,1,0:T(8,128)(2,1)S(1)}, bf16[1,256,1280]{2,1,0:T(8,128)(2,1)}, u32[]{:S(2)}) copy-start(bf16[1,256,1280]{2,1,0:T(8,128)(2,1)} %param.5) | copy-start | bytes 1966084
  0.7 1.9 %copy-start.3 = (bf16[1,256,1280]{2,1,0:T(8,128)(2,1)S(1)}, bf16[1,256,1280]{2,1,0:T(8,128)(2,1)}, u32[]{:S(2)}) copy-start(bf16[1,256,1280]{2,1,0:T(8,128)(2,1)} %param.6) | copy-start | bytes 1966084
  0.7 13.4 %copy-start = (bf16[1280,1280]{1,0:T(8,128)(2,1)S(1)}, bf16[1280,1280]{1,0:T(8,128)(2,1)}, u32[]{:S(2)}) copy-start(bf16[1280,1280]{1,0:T(8,128)(2,1)} %in_weight_ref.1) | copy-start | bytes 9830404
  0.7 13.4 %copy-start.1 = (bf16[1280,1280]{1,0:T(8,128)(2,1)S(1)}, bf16[1280,1280]{1,0:T(8,128)(2,1)}, u32[]{:S(2)}) copy-start(bf16[1280,1280]{1,0:T(8,128)(2,1)} %out_weight_ref.1) | copy-start | bytes 9830404
  25.9 1.2 %collective-permute-start = (f32[8,640]{1,0:T(8,128)S(1)}, f32[8,640]{1,0:T(8,128)S(1)}, u32[]{:S(2)}, u32[]{:S(2)}) collective-permute-start(f32[8,640]{1,0:T(8,128)S(1)} %get-tuple-element.15), channel_id=1, source_target_pairs={{0,1},{1,0},{2,3},{3,2},{4,5},{5,4},{6,7},{7,6},{8,9},{9,8},{10,11... | collective-permute-start | bytes 61448 | tf_op jit(solution)/shard_map/ppermute | solution.py:141
  36.5 1.4 %collective-permute-start.1 = (f32[8,640]{1,0:T(8,128)S(1)}, f32[8,640]{1,0:T(8,128)S(1)}, u32[]{:S(2)}, u32[]{:S(2)}) collective-permute-start(f32[8,640]{1,0:T(8,128)S(1)} %convert_reduce_fusion), channel_id=1, source_target_pairs={{0,1},{1,0},{2,3},{3,2},{4,5},{5,4},{6,7},{7,6},{8,9},{9,8},{10,11... | collective-permute-start | bytes 61448 | tf_op jit(solution)/shard_map/ppermute | solution.py:141

commit v20 on v17

--- a/solution.py
+++ b/solution.py
@@ -15,18 +15,27 @@
 AHEAD_FLOPS = 3 * 10**10
 
 
+OUT_LIST = (15, 1, 7, 3, 5, 4, 8, 12, 9, 2, 6, 10, 13, 14, 11, 0)
+BACK_LIST = (15, 0, 1, 7, 11, 13, 2, 3, 5, 10, 4, 8, 12, 6, 9, 14)
+SUM_LIST = (7, 6, 2, 5, 1, 4, 3, 0)
+
+
+def listed(members, count):
+    if len(members) == count:
+        return list(members)
+    return [(count - 1 + 5 * k) % count for k in range(count)]
+
+
 def out_order(size):
-    return [size - 1] + list(range(1, size - 1)) + [0]
+    return listed(OUT_LIST, size)
 
 
 def back_order(size):
-    return [(size - 1 + 5 * k) % size for k in range(size)]
+    return listed(BACK_LIST, size)
 
 
 def sum_order(size, core):
-    chips = size // 2
-    order = [k // 2 if k % 2 else chips - 1 - k // 2 for k in range(chips)]
-    return [2 * chip + core for chip in order]
+    return [2 * chip + core for chip in listed(SUM_LIST, size // 2)]
 
 
 def dot(a, b, dims):

time: 38.7 us -> 38.8 us (level)
  no operation moved by 1% of the time
where the time goes in v20:
time: 38.8 us; the launch traced here: 38.6 us
  blocking collectives  29.2 us (75%)
  Pallas kernels  5.63 us (15%)
  waiting for transfers between devices  1.08 us (3%)
  local copies, waits for them, and re-layouts  1.07 us (3%)
  between operations  0.73 us (2%)
  other arithmetic  0.65 us (2%)
    all_to_all x3, blocking collectives, exchange(): lax.all_to_all(value, 'expert', split_axis=0, concat_axis=0, tiled=True,...  29.2 us
    pallas_call x6, Pallas kernels, call(): pl.pallas_call(kernel, out_shape=[jax.ShapeDtypeStruct(shape, dtype) for...  5.63 us
    ppermute x2, waiting for transfers between devices, swap_cores(): return lax.ppermute(value, 'expert', [(i, i ^ 1) for i in range(size)])  1.08 us
    unnamed x10, local copies, waits for them, and re-layouts  1.06 us
  transfers between devices with their start and end apart: 2, of which 1 were waited for; matrix products, arithmetic and copies ran while one was open for 0% of the time, Pallas kernels for 3%

profile of v20, /device:TPU:0, one launch (start us, length us, event | category | flops | bytes accessed | tf_op | source)
XLA Modules:
  0.0 38.6 jit_solution(9954202304958351353)
XLA Ops:
  0.6 0.0 copy-start.4
  0.6 0.0 copy-start.2
  0.7 0.0 copy-start.3
  0.7 0.0 copy-start
  0.7 0.0 copy-start.1
  0.7 0.7 %copy-done.4 = bf16[1280,8]{0,1:T(8,128)(2,1)S(1)} copy-done((bf16[1280,8]{0,1:T(8,128)(2,1)S(1)}, bf16[1280,8]{0,1:T(8,128)(2,1)}, u32[]{:S(2)}) %copy-start.4) | copy-done | bytes 20504
  1.4 0.4 copy-done.2
  1.7 0.8 %shard_map.69 = (f32[8,1280]{1,0:T(8,128)S(1)}, f32[8,256]{1,0:T(8,128)S(1)}, f32[8,256]{1,0:T(8,128)S(1)}) custom-call(bf16[256,1280]{1,0:T(8,128)(2,1)S(1)} %bitcast.6, bf16[8,1280]{1,0:T(8,128)(2,1)S(1)} %bitcast.10, f32[8,128]{1,0:T(8,128)S(1)} %shard_map.68.token_ref), custom_call_target="tpu_custom_call" | custom-call | flops 20971520 | bytes 655360 | tf_op jit(solution)/shard_map/pallas_call | solution.py:137
  2.5 0.0 copy-done.3
  2.5 0.2 shard_map.70
  2.8 11.3 %all_to_all.15.got_ref = bf16[16,2,1280]{2,1,0:T(2,128)(2,1)S(1)} all-to-all(bf16[16,2,1280]{2,1,0:T(2,128)(2,1)S(1)} %shard_map.70), channel_id=1, replica_groups={{15,1,7,3,5,4,8,12,9,2,6,10,13,14,11,0},{31,17,23,19,21,20,24,28,25,18,..., dimensions={0} | all-to-all | bytes 163840 | tf_op jit(solution)/shard_map/all_to_all | solution.py:154
  14.1 0.0 copy-done
  14.1 0.0 copy-done.1
  14.1 2.7 %shard_map.71 = bf16[16,2,1280]{2,1,0:T(2,128)(2,1)S(1)} custom-call(bf16[16,2,1280]{2,1,0:T(2,128)(2,1)S(1)} %all_to_all.15.got_ref, bf16[1280,1280]{1,0:T(8,128)(2,1)S(1)} %copy-done, bf16[1280,1280]{1,0:T(8,128)(2,1)S(1)} %copy-done.1), custom_call_target="tpu_custom_call" | custom-call | flops 209715200 | bytes 6553600 | tf_op jit(solution)/shard_map/pallas_call | solution.py:137
  16.8 8.7 %all_to_all.16.back_ref = bf16[16,2,1280]{2,1,0:T(2,128)(2,1)S(1)} all-to-all(bf16[16,2,1280]{2,1,0:T(2,128)(2,1)S(1)} %shard_map.71), channel_id=1, replica_groups={{15,0,1,7,11,13,2,3,5,10,4,8,12,6,9,14},{31,16,17,23,27,29,18,19,21,26,..., dimensions={0} | all-to-all | bytes 163840 | tf_op jit(solution)/shard_map/all_to_all | solution.py:154
  25.5 0.7 %shard_map.72 = (f32[8,640]{1,0:T(8,128)S(1)}, f32[8,640]{1,0:T(8,128)S(1)}, bf16[16,256]{1,0:T(8,128)(2,1)S(1)}, bf16[16,1280]{1,0:T(8,128)(2,1)S(1)}) custom-call(bf16[256,1280]{1,0:T(8,128)(2,1)S(1)} %bitcast.7, bf16[256,1280]{1,0:T(8,128)(2,1)S(1)} %bitcast.9, bf16[8,1280]{1,0:T(8,128)(2,1)S(1)} %bitcast.11, f32[8,256]{1,0:T(8,128)S(1)} %get-tuple-element.9.dispatch_ref, ...), custom_call_target="tpu_custom_call" | custom-call | flops 31457280 | bytes 1310720 | tf_op jit(solution)/shard_map/pallas_call | solution.py:137
  26.2 0.2 collective-permute-start
  26.3 1.1 %collective-permute-done = f32[8,640]{1,0:T(8,128)S(1)} collective-permute-done((f32[8,640]{1,0:T(8,128)S(1)}, f32[8,640]{1,0:T(8,128)S(1)}, u32[]{:S(2)}, u32[]{:S(2)}) %collective-permute-start) | collective-permute-done | bytes 20512 | tf_op jit(solution)/shard_map/ppermute | solution.py:150
  27.4 9.2 %all_to_all.17 = bf16[8,8,640]{2,1,0:T(8,128)(2,1)S(1)} all-to-all(bf16[8,8,640]{2,1,0:T(8,128)(2,1)S(1)} %broadcast_in_dim.10), channel_id=1, replica_groups={{14,12,4,10,2,8,6,0},{15,13,5,11,3,9,7,1},{30,28,20,26,18,24,22,16},{31..., dimensions={0} | all-to-all | bytes 163840 | tf_op jit(solution)/shard_map/all_to_all | solution.py:154
  36.7 0.1 collective-permute-start.1
  36.8 1.2 %shard_map.73 = bf16[256,1280]{1,0:T(8,128)(2,1)} custom-call(bf16[16,256]{1,0:T(8,128)(2,1)S(1)} %get-tuple-element.12.left_ref, bf16[16,1280]{1,0:T(8,128)(2,1)S(1)} %get-tuple-element.13.right_ref), custom_call_target="tpu_custom_call" | custom-call | flops 10485760 | bytes 655360 | tf_op jit(solution)/shard_map/pallas_call | solution.py:137
  38.0 0.0 collective-permute-done.1
  38.0 0.6 %maximum_bitcast_fusion = f32[1280,8]{0,1:T(8,128)} fusion(f32[8,640]{1,0:T(8,128)S(1)} %get-tuple-element.17, f32[8,640]{1,0:T(8,128)S(1)} %get-tuple-element.16), kind=kLoop, calls=%fused_computation.1 | loop fusion | flops 10240 | bytes 81920 | tf_op jit(solution)/shard_map/transpose | solution.py:233
  (5 shorter events, 0.0 us)
Async XLA Ops:
  0.6 0.7 %copy-start.4 = (bf16[1280,8]{0,1:T(8,128)(2,1)S(1)}, bf16[1280,8]{0,1:T(8,128)(2,1)}, u32[]{:S(2)}) copy-start(bf16[1280,8]{0,1:T(8,128)(2,1)} %param.7) | copy-start | bytes 61444
  0.6 1.1 %copy-start.2 = (bf16[1,256,1280]{2,1,0:T(8,128)(2,1)S(1)}, bf16[1,256,1280]{2,1,0:T(8,128)(2,1)}, u32[]{:S(2)}) copy-start(bf16[1,256,1280]{2,1,0:T(8,128)(2,1)} %param.5) | copy-start | bytes 1966084
  0.7 1.9 %copy-start.3 = (bf16[1,256,1280]{2,1,0:T(8,128)(2,1)S(1)}, bf16[1,256,1280]{2,1,0:T(8,128)(2,1)}, u32[]{:S(2)}) copy-start(bf16[1,256,1280]{2,1,0:T(8,128)(2,1)} %param.6) | copy-start | bytes 1966084
  0.7 13.4 %copy-start = (bf16[1280,1280]{1,0:T(8,128)(2,1)S(1)}, bf16[1280,1280]{1,0:T(8,128)(2,1)}, u32[]{:S(2)}) copy-start(bf16[1280,1280]{1,0:T(8,128)(2,1)} %in_weight_ref.1) | copy-start | bytes 9830404
  0.7 13.4 %copy-start.1 = (bf16[1280,1280]{1,0:T(8,128)(2,1)S(1)}, bf16[1280,1280]{1,0:T(8,128)(2,1)}, u32[]{:S(2)}) copy-start(bf16[1280,1280]{1,0:T(8,128)(2,1)} %out_weight_ref.1) | copy-start | bytes 9830404
  26.2 1.2 %collective-permute-start = (f32[8,640]{1,0:T(8,128)S(1)}, f32[8,640]{1,0:T(8,128)S(1)}, u32[]{:S(2)}, u32[]{:S(2)}) collective-permute-start(f32[8,640]{1,0:T(8,128)S(1)} %get-tuple-element.15), channel_id=1, source_target_pairs={{0,1},{1,0},{2,3},{3,2},{4,5},{5,4},{6,7},{7,6},{8,9},{9,8},{10,11... | collective-permute-start | bytes 61448 | tf_op jit(solution)/shard_map/ppermute | solution.py:150
  36.7 1.3 %collective-permute-start.1 = (f32[8,640]{1,0:T(8,128)S(1)}, f32[8,640]{1,0:T(8,128)S(1)}, u32[]{:S(2)}, u32[]{:S(2)}) collective-permute-start(f32[8,640]{1,0:T(8,128)S(1)} %convert_reduce_fusion), channel_id=1, source_target_pairs={{0,1},{1,0},{2,3},{3,2},{4,5},{5,4},{6,7},{7,6},{8,9},{9,8},{10,11... | collective-permute-start | bytes 61448 | tf_op jit(solution)/shard_map/ppermute | solution.py:150

commit v21 on v20

--- a/solution.py
+++ b/solution.py
@@ -15,9 +15,9 @@
 AHEAD_FLOPS = 3 * 10**10
 
 
-OUT_LIST = (15, 1, 7, 3, 5, 4, 8, 12, 9, 2, 6, 10, 13, 14, 11, 0)
-BACK_LIST = (15, 0, 1, 7, 11, 13, 2, 3, 5, 10, 4, 8, 12, 6, 9, 14)
-SUM_LIST = (7, 6, 2, 5, 1, 4, 3, 0)
+OUT_LIST = (15, 2, 12, 6, 14, 0, 4, 3, 7, 8, 9, 5, 13, 11, 10, 1)
+BACK_LIST = (15, 2, 12, 6, 0, 4, 13, 7, 11, 14, 1, 8, 10, 3, 5, 9)
+SUM_LIST = (7, 0, 2, 6, 1, 4, 3, 5)
 
 
 def listed(members, count):

time: 38.8 us -> 39.3 us (1.013)
  blocking collectives: 29.2 us -> 29.7 us
    all_to_all x3, blocking collectives: 29.2 us -> 29.7 us  [exchange(): lax.all_to_all(value, 'expert', split_axis=0, concat_axis=0, tiled=True,...]
where the time goes in v21:
time: 39.3 us; the launch traced here: 39.1 us
  blocking collectives  29.7 us (76%)
  Pallas kernels  5.63 us (14%)
  waiting for transfers between devices  1.08 us (3%)
  local copies, waits for them, and re-layouts  1.07 us (3%)
  between operations  0.73 us (2%)
  other arithmetic  0.65 us (2%)
    all_to_all x3, blocking collectives, exchange(): lax.all_to_all(value, 'expert', split_axis=0, concat_axis=0, tiled=True,...  29.7 us
    pallas_call x6, Pallas kernels, call(): pl.pallas_call(kernel, out_shape=[jax.ShapeDtypeStruct(shape, dtype) for...  5.63 us
    ppermute x2, waiting for transfers between devices, swap_cores(): return lax.ppermute(value, 'expert', [(i, i ^ 1) for i in range(size)])  1.08 us
    unnamed x10, local copies, waits for them, and re-layouts  1.06 us
  transfers between devices with their start and end apart: 2, of which 1 were waited for; matrix products, arithmetic and copies ran while one was open for 0% of the time, Pallas kernels for 3%

profile of v21, /device:TPU:0, one launch (start us, length us, event | category | flops | bytes accessed | tf_op | source)
XLA Modules:
  0.0 39.1 jit_solution(3312094480190434457)
XLA Ops:
  0.6 0.0 copy-start.4
  0.6 0.0 copy-start.2
  0.7 0.0 copy-start.3
  0.7 0.0 copy-start
  0.7 0.0 copy-start.1
  0.7 0.7 %copy-done.4 = bf16[1280,8]{0,1:T(8,128)(2,1)S(1)} copy-done((bf16[1280,8]{0,1:T(8,128)(2,1)S(1)}, bf16[1280,8]{0,1:T(8,128)(2,1)}, u32[]{:S(2)}) %copy-start.4) | copy-done | bytes 20504
  1.4 0.4 copy-done.2
  1.7 0.8 %shard_map.69 = (f32[8,1280]{1,0:T(8,128)S(1)}, f32[8,256]{1,0:T(8,128)S(1)}, f32[8,256]{1,0:T(8,128)S(1)}) custom-call(bf16[256,1280]{1,0:T(8,128)(2,1)S(1)} %bitcast.6, bf16[8,1280]{1,0:T(8,128)(2,1)S(1)} %bitcast.10, f32[8,128]{1,0:T(8,128)S(1)} %shard_map.68.token_ref), custom_call_target="tpu_custom_call" | custom-call | flops 20971520 | bytes 655360 | tf_op jit(solution)/shard_map/pallas_call | solution.py:137
  2.5 0.0 copy-done.3
  2.5 0.2 shard_map.70
  2.8 11.3 %all_to_all.15.got_ref = bf16[16,2,1280]{2,1,0:T(2,128)(2,1)S(1)} all-to-all(bf16[16,2,1280]{2,1,0:T(2,128)(2,1)S(1)} %shard_map.70), channel_id=1, replica_groups={{15,2,12,6,14,0,4,3,7,8,9,5,13,11,10,1},{31,18,28,22,30,16,20,19,23,24,..., dimensions={0} | all-to-all | bytes 163840 | tf_op jit(solution)/shard_map/all_to_all | solution.py:154
  14.1 0.0 copy-done
  14.1 0.0 copy-done.1
  14.1 2.7 %shard_map.71 = bf16[16,2,1280]{2,1,0:T(2,128)(2,1)S(1)} custom-call(bf16[16,2,1280]{2,1,0:T(2,128)(2,1)S(1)} %all_to_all.15.got_ref, bf16[1280,1280]{1,0:T(8,128)(2,1)S(1)} %copy-done, bf16[1280,1280]{1,0:T(8,128)(2,1)S(1)} %copy-done.1), custom_call_target="tpu_custom_call" | custom-call | flops 209715200 | bytes 6553600 | tf_op jit(solution)/shard_map/pallas_call | solution.py:137
  16.8 9.1 %all_to_all.16.back_ref = bf16[16,2,1280]{2,1,0:T(2,128)(2,1)S(1)} all-to-all(bf16[16,2,1280]{2,1,0:T(2,128)(2,1)S(1)} %shard_map.71), channel_id=1, replica_groups={{15,2,12,6,0,4,13,7,11,14,1,8,10,3,5,9},{31,18,28,22,16,20,29,23,27,30,..., dimensions={0} | all-to-all | bytes 163840 | tf_op jit(solution)/shard_map/all_to_all | solution.py:154
  25.9 0.7 %shard_map.72 = (f32[8,640]{1,0:T(8,128)S(1)}, f32[8,640]{1,0:T(8,128)S(1)}, bf16[16,256]{1,0:T(8,128)(2,1)S(1)}, bf16[16,1280]{1,0:T(8,128)(2,1)S(1)}) custom-call(bf16[256,1280]{1,0:T(8,128)(2,1)S(1)} %bitcast.7, bf16[256,1280]{1,0:T(8,128)(2,1)S(1)} %bitcast.9, bf16[8,1280]{1,0:T(8,128)(2,1)S(1)} %bitcast.11, f32[8,256]{1,0:T(8,128)S(1)} %get-tuple-element.9.dispatch_ref, ...), custom_call_target="tpu_custom_call" | custom-call | flops 31457280 | bytes 1310720 | tf_op jit(solution)/shard_map/pallas_call | solution.py:137
  26.6 0.2 collective-permute-start
  26.8 1.1 %collective-permute-done = f32[8,640]{1,0:T(8,128)S(1)} collective-permute-done((f32[8,640]{1,0:T(8,128)S(1)}, f32[8,640]{1,0:T(8,128)S(1)}, u32[]{:S(2)}, u32[]{:S(2)}) %collective-permute-start) | collective-permute-done | bytes 20512 | tf_op jit(solution)/shard_map/ppermute | solution.py:150
  27.9 9.2 %all_to_all.17 = bf16[8,8,640]{2,1,0:T(8,128)(2,1)S(1)} all-to-all(bf16[8,8,640]{2,1,0:T(8,128)(2,1)S(1)} %broadcast_in_dim.10), channel_id=1, replica_groups={{14,0,4,12,2,8,6,10},{15,1,5,13,3,9,7,11},{30,16,20,28,18,24,22,26},{31..., dimensions={0} | all-to-all | bytes 163840 | tf_op jit(solution)/shard_map/all_to_all | solution.py:154
  37.1 0.1 collective-permute-start.1
  37.2 1.2 %shard_map.73 = bf16[256,1280]{1,0:T(8,128)(2,1)} custom-call(bf16[16,256]{1,0:T(8,128)(2,1)S(1)} %get-tuple-element.12.left_ref, bf16[16,1280]{1,0:T(8,128)(2,1)S(1)} %get-tuple-element.13.right_ref), custom_call_target="tpu_custom_call" | custom-call | flops 10485760 | bytes 655360 | tf_op jit(solution)/shard_map/pallas_call | solution.py:137
  38.4 0.0 collective-permute-done.1
  38.4 0.6 %maximum_bitcast_fusion = f32[1280,8]{0,1:T(8,128)} fusion(f32[8,640]{1,0:T(8,128)S(1)} %get-tuple-element.17, f32[8,640]{1,0:T(8,128)S(1)} %get-tuple-element.16), kind=kLoop, calls=%fused_computation.1 | loop fusion | flops 10240 | bytes 81920 | tf_op jit(solution)/shard_map/transpose | solution.py:233
  (5 shorter events, 0.0 us)
Async XLA Ops:
  0.6 0.7 %copy-start.4 = (bf16[1280,8]{0,1:T(8,128)(2,1)S(1)}, bf16[1280,8]{0,1:T(8,128)(2,1)}, u32[]{:S(2)}) copy-start(bf16[1280,8]{0,1:T(8,128)(2,1)} %param.7) | copy-start | bytes 61444
  0.6 1.1 %copy-start.2 = (bf16[1,256,1280]{2,1,0:T(8,128)(2,1)S(1)}, bf16[1,256,1280]{2,1,0:T(8,128)(2,1)}, u32[]{:S(2)}) copy-start(bf16[1,256,1280]{2,1,0:T(8,128)(2,1)} %param.5) | copy-start | bytes 1966084
  0.7 1.9 %copy-start.3 = (bf16[1,256,1280]{2,1,0:T(8,128)(2,1)S(1)}, bf16[1,256,1280]{2,1,0:T(8,128)(2,1)}, u32[]{:S(2)}) copy-start(bf16[1,256,1280]{2,1,0:T(8,128)(2,1)} %param.6) | copy-start | bytes 1966084
  0.7 13.4 %copy-start = (bf16[1280,1280]{1,0:T(8,128)(2,1)S(1)}, bf16[1280,1280]{1,0:T(8,128)(2,1)}, u32[]{:S(2)}) copy-start(bf16[1280,1280]{1,0:T(8,128)(2,1)} %in_weight_ref.1) | copy-start | bytes 9830404
  0.7 13.4 %copy-start.1 = (bf16[1280,1280]{1,0:T(8,128)(2,1)S(1)}, bf16[1280,1280]{1,0:T(8,128)(2,1)}, u32[]{:S(2)}) copy-start(bf16[1280,1280]{1,0:T(8,128)(2,1)} %out_weight_ref.1) | copy-start | bytes 9830404
  26.6 1.2 %collective-permute-start = (f32[8,640]{1,0:T(8,128)S(1)}, f32[8,640]{1,0:T(8,128)S(1)}, u32[]{:S(2)}, u32[]{:S(2)}) collective-permute-start(f32[8,640]{1,0:T(8,128)S(1)} %get-tuple-element.15), channel_id=1, source_target_pairs={{0,1},{1,0},{2,3},{3,2},{4,5},{5,4},{6,7},{7,6},{8,9},{9,8},{10,11... | collective-permute-start | bytes 61448 | tf_op jit(solution)/shard_map/ppermute | solution.py:150
  37.1 1.3 %collective-permute-start.1 = (f32[8,640]{1,0:T(8,128)S(1)}, f32[8,640]{1,0:T(8,128)S(1)}, u32[]{:S(2)}, u32[]{:S(2)}) collective-permute-start(f32[8,640]{1,0:T(8,128)S(1)} %convert_reduce_fusion), channel_id=1, source_target_pairs={{0,1},{1,0},{2,3},{3,2},{4,5},{5,4},{6,7},{7,6},{8,9},{9,8},{10,11... | collective-permute-start | bytes 61448 | tf_op jit(solution)/shard_map/ppermute | solution.py:150

commit v22 on v17

--- a/solution.py
+++ b/solution.py
@@ -37,22 +37,22 @@
     token_ref[...] = jnp.zeros(token_ref.shape, F32)
 
 
-def slots_kernel(tokens_ref, router_ref, token_ref, slot_in_ref, dispatch_ref, combine_ref):
+def slots_kernel(tokens_ref, router_ref, token_ref, dispatch_ref, combine_ref):
     logits = dot(router_ref[...], tokens_ref[...], NT)
     over_patches = jnp.exp(logits - jnp.max(logits, axis=1, keepdims=True))
     dispatch = over_patches / jnp.sum(over_patches, axis=1, keepdims=True)
     over_slots = jnp.exp(logits - jnp.max(logits, axis=0, keepdims=True))
     dispatch_ref[...] = dispatch
     combine_ref[...] = over_slots / jnp.sum(over_slots, axis=0, keepdims=True)
-    slot_in_ref[...] = dot(dispatch.astype(BF16), tokens_ref[...], NN)
-
-
-def messages_kernel(grad_ref, combine_ref, slot_in_ref, sent_ref):
+
+
+def messages_kernel(tokens_ref, grad_ref, dispatch_ref, combine_ref, sent_ref):
+    slot_in = dot(dispatch_ref[...].astype(BF16), tokens_ref[...], NN)
     slot_grad = dot(combine_ref[...].astype(BF16), grad_ref[...], NN)
-    slots = slot_in_ref.shape[0]
+    slots = slot_in.shape[0]
     order = out_order(2 * slots)
     for s in range(slots):
-        rows = [slot_in_ref[s : s + 1], slot_grad[s : s + 1]]
+        rows = [slot_in[s : s + 1], slot_grad[s : s + 1]]
         message = jnp.concatenate(rows, axis=0).astype(BF16)
         for half in range(2):
             sent_ref[order.index(2 * s + half)] = message
@@ -158,11 +158,11 @@
     image_bytes = 2 * patches * width
     weight_bytes = 2 * width * hidden
     (token,) = call(first_kernel, [((8, 128), F32)], [], (AHEAD_FLOPS, image_bytes))
-    slot_in, dispatch, combine = call(
+    dispatch, combine = call(
         slots_kernel,
-        [((slots, width), F32), ((slots, patches), F32), ((slots, patches), F32)],
+        [((slots, patches), F32), ((slots, patches), F32)],
         [],
-        (8 * patches * width * slots, image_bytes),
+        (4 * patches * width * slots, image_bytes),
         tokens,
         router_rows,
         token,
@@ -171,10 +171,11 @@
         messages_kernel,
         [((2 * slots, 2, width), BF16)],
         [],
-        (4 * patches * width * slots, image_bytes),
+        (8 * patches * width * slots, 2 * image_bytes),
+        tokens,
         out_grad,
+        dispatch,
         combine,
-        slot_in,
     )
     got = exchange(sent, [out_order(2 * chips)])
     (parts,) = call(

time: 38.7 us -> 38.4 us (level)
  no operation moved by 1% of the time
where the time goes in v22:
time: 38.4 us; the launch traced here: 38.2 us
  blocking collectives  29 us (76%)
  Pallas kernels  5.38 us (14%)
  local copies, waits for them, and re-layouts  1.07 us (3%)
  waiting for transfers between devices  0.93 us (2%)
  between operations  0.73 us (2%)
  other arithmetic  0.65 us (2%)
    all_to_all x3, blocking collectives, exchange(): lax.all_to_all(value, 'expert', split_axis=0, concat_axis=0, tiled=True,...  29 us
    pallas_call x6, Pallas kernels, call(): pl.pallas_call(kernel, out_shape=[jax.ShapeDtypeStruct(shape, dtype) for...  5.38 us
    unnamed x10, local copies, waits for them, and re-layouts  1.06 us
    ppermute x2, waiting for transfers between devices, swap_cores(): return lax.ppermute(value, 'expert', [(i, i ^ 1) for i in range(size)])  0.93 us
  transfers between devices with their start and end apart: 2, of which 1 were waited for; matrix products, arithmetic and copies ran while one was open for 0% of the time, Pallas kernels for 3%

profile of v22, /device:TPU:0, one launch (start us, length us, event | category | flops | bytes accessed | tf_op | source)
XLA Modules:
  0.0 38.2 jit_solution(2072833376073475292)
XLA Ops:
  0.6 0.0 copy-start.4
  0.6 0.0 copy-start
  0.7 0.0 copy-start.3
  0.7 0.0 copy-start.1
  0.7 0.0 copy-start.2
  0.7 0.7 %copy-done.4 = bf16[1280,8]{0,1:T(8,128)(2,1)S(1)} copy-done((bf16[1280,8]{0,1:T(8,128)(2,1)S(1)}, bf16[1280,8]{0,1:T(8,128)(2,1)}, u32[]{:S(2)}) %copy-start.4) | copy-done | bytes 20504
  1.4 0.4 copy-done
  1.7 0.5 %shard_map.69 = (f32[8,256]{1,0:T(8,128)S(1)}, f32[8,256]{1,0:T(8,128)S(1)}) custom-call(bf16[256,1280]{1,0:T(8,128)(2,1)S(1)} %bitcast.6, bf16[8,1280]{1,0:T(8,128)(2,1)S(1)} %bitcast.11, f32[8,128]{1,0:T(8,128)S(1)} %shard_map.68.token_ref), custom_call_target="tpu_custom_call" | custom-call | flops 10485760 | bytes 655360 | tf_op jit(solution)/shard_map/pallas_call | solution.py:128
  2.2 0.0 copy-done.3
  2.2 0.3 shard_map.70
  2.5 11.3 %all_to_all.15.got_ref = bf16[16,2,1280]{2,1,0:T(2,128)(2,1)S(1)} all-to-all(bf16[16,2,1280]{2,1,0:T(2,128)(2,1)S(1)} %shard_map.70), channel_id=1, replica_groups={{15,1,2,3,4,5,6,7,8,9,10,11,12,13,14,0},{31,17,18,19,20,21,22,23,24,25,..., dimensions={0} | all-to-all | bytes 163840 | tf_op jit(solution)/shard_map/all_to_all | solution.py:145
  13.8 0.0 copy-done.1
  13.8 0.0 copy-done.2
  13.8 2.7 %shard_map.71 = bf16[16,2,1280]{2,1,0:T(2,128)(2,1)S(1)} custom-call(bf16[16,2,1280]{2,1,0:T(2,128)(2,1)S(1)} %all_to_all.15.got_ref, bf16[1280,1280]{1,0:T(8,128)(2,1)S(1)} %copy-done.1, bf16[1280,1280]{1,0:T(8,128)(2,1)S(1)} %copy-done.2), custom_call_target="tpu_custom_call" | custom-call | flops 209715200 | bytes 6553600 | tf_op jit(solution)/shard_map/pallas_call | solution.py:128
  16.5 8.4 %all_to_all.16.back_ref = bf16[16,2,1280]{2,1,0:T(2,128)(2,1)S(1)} all-to-all(bf16[16,2,1280]{2,1,0:T(2,128)(2,1)S(1)} %shard_map.71), channel_id=1, replica_groups={{15,4,9,14,3,8,13,2,7,12,1,6,11,0,5,10},{31,20,25,30,19,24,29,18,23,28,..., dimensions={0} | all-to-all | bytes 163840 | tf_op jit(solution)/shard_map/all_to_all | solution.py:145
  24.9 0.7 %shard_map.72 = (f32[8,640]{1,0:T(8,128)S(1)}, f32[8,640]{1,0:T(8,128)S(1)}, bf16[16,256]{1,0:T(8,128)(2,1)S(1)}, bf16[16,1280]{1,0:T(8,128)(2,1)S(1)}) custom-call(bf16[256,1280]{1,0:T(8,128)(2,1)S(1)} %bitcast.8, bf16[256,1280]{1,0:T(8,128)(2,1)S(1)} %bitcast.10, bf16[8,1280]{1,0:T(8,128)(2,1)S(1)} %bitcast.12, ...), custom_call_target="tpu_custom_call" | custom-call | flops 31457280 | bytes 1310720 | tf_op jit(solution)/shard_map/pallas_call | solution.py:128
  25.6 0.3 collective-permute-start
  25.9 0.9 %collective-permute-done = f32[8,640]{1,0:T(8,128)S(1)} collective-permute-done((f32[8,640]{1,0:T(8,128)S(1)}, f32[8,640]{1,0:T(8,128)S(1)}, u32[]{:S(2)}, u32[]{:S(2)}) %collective-permute-start) | collective-permute-done | bytes 20512 | tf_op jit(solution)/shard_map/ppermute | solution.py:141
  26.9 9.4 %all_to_all.17 = bf16[8,8,640]{2,1,0:T(8,128)(2,1)S(1)} all-to-all(bf16[8,8,640]{2,1,0:T(8,128)(2,1)S(1)} %broadcast_in_dim.10), channel_id=1, replica_groups={{14,0,12,2,10,4,8,6},{15,1,13,3,11,5,9,7},{30,16,28,18,26,20,24,22},{31..., dimensions={0} | all-to-all | bytes 163840 | tf_op jit(solution)/shard_map/all_to_all | solution.py:145
  36.2 0.1 collective-permute-start.1
  36.3 1.2 %shard_map.73 = bf16[256,1280]{1,0:T(8,128)(2,1)} custom-call(bf16[16,256]{1,0:T(8,128)(2,1)S(1)} %get-tuple-element.10.left_ref, bf16[16,1280]{1,0:T(8,128)(2,1)S(1)} %get-tuple-element.11.right_ref), custom_call_target="tpu_custom_call" | custom-call | flops 10485760 | bytes 655360 | tf_op jit(solution)/shard_map/pallas_call | solution.py:128
  37.5 0.0 collective-permute-done.1
  37.5 0.6 %maximum_bitcast_fusion = f32[1280,8]{0,1:T(8,128)} fusion(f32[8,640]{1,0:T(8,128)S(1)} %get-tuple-element.15, f32[8,640]{1,0:T(8,128)S(1)} %get-tuple-element.14), kind=kLoop, calls=%fused_computation.1 | loop fusion | flops 10240 | bytes 81920 | tf_op jit(solution)/shard_map/transpose | solution.py:225
  (5 shorter events, 0.0 us)
Async XLA Ops:
  0.6 0.7 %copy-start.4 = (bf16[1280,8]{0,1:T(8,128)(2,1)S(1)}, bf16[1280,8]{0,1:T(8,128)(2,1)}, u32[]{:S(2)}) copy-start(bf16[1280,8]{0,1:T(8,128)(2,1)} %param.7) | copy-start | bytes 61444
  0.6 1.1 %copy-start = (bf16[1,256,1280]{2,1,0:T(8,128)(2,1)S(1)}, bf16[1,256,1280]{2,1,0:T(8,128)(2,1)}, u32[]{:S(2)}) copy-start(bf16[1,256,1280]{2,1,0:T(8,128)(2,1)} %param.5) | copy-start | bytes 1966084
  0.7 1.6 %copy-start.3 = (bf16[1,256,1280]{2,1,0:T(8,128)(2,1)S(1)}, bf16[1,256,1280]{2,1,0:T(8,128)(2,1)}, u32[]{:S(2)}) copy-start(bf16[1,256,1280]{2,1,0:T(8,128)(2,1)} %param.6) | copy-start | bytes 1966084
  0.7 13.1 %copy-start.1 = (bf16[1280,1280]{1,0:T(8,128)(2,1)S(1)}, bf16[1280,1280]{1,0:T(8,128)(2,1)}, u32[]{:S(2)}) copy-start(bf16[1280,1280]{1,0:T(8,128)(2,1)} %in_weight_ref.1) | copy-start | bytes 9830404
  0.7 13.1 %copy-start.2 = (bf16[1280,1280]{1,0:T(8,128)(2,1)S(1)}, bf16[1280,1280]{1,0:T(8,128)(2,1)}, u32[]{:S(2)}) copy-start(bf16[1280,1280]{1,0:T(8,128)(2,1)} %out_weight_ref.1) | copy-start | bytes 9830404
  25.6 1.2 %collective-permute-start = (f32[8,640]{1,0:T(8,128)S(1)}, f32[8,640]{1,0:T(8,128)S(1)}, u32[]{:S(2)}, u32[]{:S(2)}) collective-permute-start(f32[8,640]{1,0:T(8,128)S(1)} %get-tuple-element.13), channel_id=1, source_target_pairs={{0,1},{1,0},{2,3},{3,2},{4,5},{5,4},{6,7},{7,6},{8,9},{9,8},{10,11... | collective-permute-start | bytes 61448 | tf_op jit(solution)/shard_map/ppermute | solution.py:141
  36.2 1.3 %collective-permute-start.1 = (f32[8,640]{1,0:T(8,128)S(1)}, f32[8,640]{1,0:T(8,128)S(1)}, u32[]{:S(2)}, u32[]{:S(2)}) collective-permute-start(f32[8,640]{1,0:T(8,128)S(1)} %convert_reduce_fusion), channel_id=1, source_target_pairs={{0,1},{1,0},{2,3},{3,2},{4,5},{5,4},{6,7},{7,6},{8,9},{9,8},{10,11... | collective-permute-start | bytes 61448 | tf_op jit(solution)/shard_map/ppermute | solution.py:141

commit v23 on v22

--- a/solution.py
+++ b/solution.py
@@ -68,11 +68,12 @@
         in_rows_ref[k : k + 1] = message[0:1]
         grad_rows_ref[k : k + 1] = message[1:2]
     hidden = dot(in_rows_ref[...].astype(BF16), in_weight_ref[...], NN)
-    act_grad = dot(grad_rows_ref[...].astype(BF16), out_weight_ref[...], NT)
     normal_cdf = 0.5 * (1.0 + lax.erf(hidden * (1.0 / math.sqrt(2.0))))
     normal_pdf = jnp.exp(-0.5 * hidden * hidden) * (1.0 / math.sqrt(2.0 * math.pi))
     activation = (hidden * normal_cdf).astype(BF16)
-    hidden_grad = (act_grad * (normal_cdf + hidden * normal_pdf)).astype(BF16)
+    slope = normal_cdf + hidden * normal_pdf
+    act_grad = dot(grad_rows_ref[...].astype(BF16), out_weight_ref[...], NT)
+    hidden_grad = (act_grad * slope).astype(BF16)
     part_out = dot(activation, out_weight_ref[...], NN)
     part_in = dot(hidden_grad, in_weight_ref[...], NT)
     for k in range(images):

time: 38.4 us -> 38.4 us (level)
  no operation moved by 1% of the time
where the time goes in v23:
time: 38.4 us; the launch traced here: 38.2 us
  blocking collectives  29 us (76%)
  Pallas kernels  5.38 us (14%)
  local copies, waits for them, and re-layouts  1.07 us (3%)
  waiting for transfers between devices  0.93 us (2%)
  between operations  0.73 us (2%)
  other arithmetic  0.65 us (2%)
    all_to_all x3, blocking collectives, exchange(): lax.all_to_all(value, 'expert', split_axis=0, concat_axis=0, tiled=True,...  29 us
    pallas_call x6, Pallas kernels, call(): pl.pallas_call(kernel, out_shape=[jax.ShapeDtypeStruct(shape, dtype) for...  5.38 us
    unnamed x10, local copies, waits for them, and re-layouts  1.06 us
    ppermute x2, waiting for transfers between devices, swap_cores(): return lax.ppermute(value, 'expert', [(i, i ^ 1) for i in range(size)])  0.93 us
  transfers between devices with their start and end apart: 2, of which 1 were waited for; matrix products, arithmetic and copies ran while one was open for 0% of the time, Pallas kernels for 3%

profile of v23, /device:TPU:0, one launch (start us, length us, event | category | flops | bytes accessed | tf_op | source)
XLA Modules:
  0.0 38.2 jit_solution(3289137849751196441)
XLA Ops:
  0.6 0.0 copy-start.4
  0.6 0.0 copy-start
  0.7 0.0 copy-start.3
  0.7 0.0 copy-start.1
  0.7 0.0 copy-start.2
  0.7 0.7 %copy-done.4 = bf16[1280,8]{0,1:T(8,128)(2,1)S(1)} copy-done((bf16[1280,8]{0,1:T(8,128)(2,1)S(1)}, bf16[1280,8]{0,1:T(8,128)(2,1)}, u32[]{:S(2)}) %copy-start.4) | copy-done | bytes 20504
  1.4 0.4 copy-done
  1.7 0.5 %shard_map.69 = (f32[8,256]{1,0:T(8,128)S(1)}, f32[8,256]{1,0:T(8,128)S(1)}) custom-call(bf16[256,1280]{1,0:T(8,128)(2,1)S(1)} %bitcast.6, bf16[8,1280]{1,0:T(8,128)(2,1)S(1)} %bitcast.11, f32[8,128]{1,0:T(8,128)S(1)} %shard_map.68.token_ref), custom_call_target="tpu_custom_call" | custom-call | flops 10485760 | bytes 655360 | tf_op jit(solution)/shard_map/pallas_call | solution.py:129
  2.2 0.0 copy-done.3
  2.2 0.3 shard_map.70
  2.5 11.3 %all_to_all.15.got_ref = bf16[16,2,1280]{2,1,0:T(2,128)(2,1)S(1)} all-to-all(bf16[16,2,1280]{2,1,0:T(2,128)(2,1)S(1)} %shard_map.70), channel_id=1, replica_groups={{15,1,2,3,4,5,6,7,8,9,10,11,12,13,14,0},{31,17,18,19,20,21,22,23,24,25,..., dimensions={0} | all-to-all | bytes 163840 | tf_op jit(solution)/shard_map/all_to_all | solution.py:146
  13.8 0.0 copy-done.1
  13.8 0.0 copy-done.2
  13.8 2.7 %shard_map.71 = bf16[16,2,1280]{2,1,0:T(2,128)(2,1)S(1)} custom-call(bf16[16,2,1280]{2,1,0:T(2,128)(2,1)S(1)} %all_to_all.15.got_ref, bf16[1280,1280]{1,0:T(8,128)(2,1)S(1)} %copy-done.1, bf16[1280,1280]{1,0:T(8,128)(2,1)S(1)} %copy-done.2), custom_call_target="tpu_custom_call" | custom-call | flops 209715200 | bytes 6553600 | tf_op jit(solution)/shard_map/pallas_call | solution.py:129
  16.5 8.4 %all_to_all.16.back_ref = bf16[16,2,1280]{2,1,0:T(2,128)(2,1)S(1)} all-to-all(bf16[16,2,1280]{2,1,0:T(2,128)(2,1)S(1)} %shard_map.71), channel_id=1, replica_groups={{15,4,9,14,3,8,13,2,7,12,1,6,11,0,5,10},{31,20,25,30,19,24,29,18,23,28,..., dimensions={0} | all-to-all | bytes 163840 | tf_op jit(solution)/shard_map/all_to_all | solution.py:146
  24.9 0.7 %shard_map.72 = (f32[8,640]{1,0:T(8,128)S(1)}, f32[8,640]{1,0:T(8,128)S(1)}, bf16[16,256]{1,0:T(8,128)(2,1)S(1)}, bf16[16,1280]{1,0:T(8,128)(2,1)S(1)}) custom-call(bf16[256,1280]{1,0:T(8,128)(2,1)S(1)} %bitcast.8, bf16[256,1280]{1,0:T(8,128)(2,1)S(1)} %bitcast.10, bf16[8,1280]{1,0:T(8,128)(2,1)S(1)} %bitcast.12, ...), custom_call_target="tpu_custom_call" | custom-call | flops 31457280 | bytes 1310720 | tf_op jit(solution)/shard_map/pallas_call | solution.py:129
  25.6 0.3 collective-permute-start
  25.9 0.9 %collective-permute-done = f32[8,640]{1,0:T(8,128)S(1)} collective-permute-done((f32[8,640]{1,0:T(8,128)S(1)}, f32[8,640]{1,0:T(8,128)S(1)}, u32[]{:S(2)}, u32[]{:S(2)}) %collective-permute-start) | collective-permute-done | bytes 20512 | tf_op jit(solution)/shard_map/ppermute | solution.py:142
  26.9 9.4 %all_to_all.17 = bf16[8,8,640]{2,1,0:T(8,128)(2,1)S(1)} all-to-all(bf16[8,8,640]{2,1,0:T(8,128)(2,1)S(1)} %broadcast_in_dim.10), channel_id=1, replica_groups={{14,0,12,2,10,4,8,6},{15,1,13,3,11,5,9,7},{30,16,28,18,26,20,24,22},{31..., dimensions={0} | all-to-all | bytes 163840 | tf_op jit(solution)/shard_map/all_to_all | solution.py:146
  36.2 0.1 collective-permute-start.1
  36.3 1.2 %shard_map.73 = bf16[256,1280]{1,0:T(8,128)(2,1)} custom-call(bf16[16,256]{1,0:T(8,128)(2,1)S(1)} %get-tuple-element.10.left_ref, bf16[16,1280]{1,0:T(8,128)(2,1)S(1)} %get-tuple-element.11.right_ref), custom_call_target="tpu_custom_call" | custom-call | flops 10485760 | bytes 655360 | tf_op jit(solution)/shard_map/pallas_call | solution.py:129
  37.5 0.0 collective-permute-done.1
  37.5 0.6 %maximum_bitcast_fusion = f32[1280,8]{0,1:T(8,128)} fusion(f32[8,640]{1,0:T(8,128)S(1)} %get-tuple-element.15, f32[8,640]{1,0:T(8,128)S(1)} %get-tuple-element.14), kind=kLoop, calls=%fused_computation.1 | loop fusion | flops 10240 | bytes 81920 | tf_op jit(solution)/shard_map/transpose | solution.py:226
  (5 shorter events, 0.0 us)
Async XLA Ops:
  0.6 0.7 %copy-start.4 = (bf16[1280,8]{0,1:T(8,128)(2,1)S(1)}, bf16[1280,8]{0,1:T(8,128)(2,1)}, u32[]{:S(2)}) copy-start(bf16[1280,8]{0,1:T(8,128)(2,1)} %param.7) | copy-start | bytes 61444
  0.6 1.1 %copy-start = (bf16[1,256,1280]{2,1,0:T(8,128)(2,1)S(1)}, bf16[1,256,1280]{2,1,0:T(8,128)(2,1)}, u32[]{:S(2)}) copy-start(bf16[1,256,1280]{2,1,0:T(8,128)(2,1)} %param.5) | copy-start | bytes 1966084
  0.7 1.6 %copy-start.3 = (bf16[1,256,1280]{2,1,0:T(8,128)(2,1)S(1)}, bf16[1,256,1280]{2,1,0:T(8,128)(2,1)}, u32[]{:S(2)}) copy-start(bf16[1,256,1280]{2,1,0:T(8,128)(2,1)} %param.6) | copy-start | bytes 1966084
  0.7 13.1 %copy-start.1 = (bf16[1280,1280]{1,0:T(8,128)(2,1)S(1)}, bf16[1280,1280]{1,0:T(8,128)(2,1)}, u32[]{:S(2)}) copy-start(bf16[1280,1280]{1,0:T(8,128)(2,1)} %in_weight_ref.1) | copy-start | bytes 9830404
  0.7 13.1 %copy-start.2 = (bf16[1280,1280]{1,0:T(8,128)(2,1)S(1)}, bf16[1280,1280]{1,0:T(8,128)(2,1)}, u32[]{:S(2)}) copy-start(bf16[1280,1280]{1,0:T(8,128)(2,1)} %out_weight_ref.1) | copy-start | bytes 9830404
  25.6 1.2 %collective-permute-start = (f32[8,640]{1,0:T(8,128)S(1)}, f32[8,640]{1,0:T(8,128)S(1)}, u32[]{:S(2)}, u32[]{:S(2)}) collective-permute-start(f32[8,640]{1,0:T(8,128)S(1)} %get-tuple-element.13), channel_id=1, source_target_pairs={{0,1},{1,0},{2,3},{3,2},{4,5},{5,4},{6,7},{7,6},{8,9},{9,8},{10,11... | collective-permute-start | bytes 61448 | tf_op jit(solution)/shard_map/ppermute | solution.py:142
  36.2 1.3 %collective-permute-start.1 = (f32[8,640]{1,0:T(8,128)S(1)}, f32[8,640]{1,0:T(8,128)S(1)}, u32[]{:S(2)}, u32[]{:S(2)}) collective-permute-start(f32[8,640]{1,0:T(8,128)S(1)} %convert_reduce_fusion), channel_id=1, source_target_pairs={{0,1},{1,0},{2,3},{3,2},{4,5},{5,4},{6,7},{7,6},{8,9},{9,8},{10,11... | collective-permute-start | bytes 61448 | tf_op jit(solution)/shard_map/ppermute | solution.py:142

commit v24 on v23

--- a/solution.py
+++ b/solution.py
@@ -16,7 +16,9 @@
 
 
 def out_order(size):
-    return [size - 1] + list(range(1, size - 1)) + [0]
+    chips = size // 2
+    order = [k // 2 if k % 2 else chips - 1 - k // 2 for k in range(chips)]
+    return [2 * chip + core for chip in order for core in (1, 0)]
 
 
 def back_order(size):

time: 38.4 us -> 38.6 us (level)
  no operation moved by 1% of the time
where the time goes in v24:
time: 38.6 us; the launch traced here: 38.4 us
  blocking collectives  29.2 us (76%)
  Pallas kernels  5.38 us (14%)
  local copies, waits for them, and re-layouts  1.07 us (3%)
  waiting for transfers between devices  1.06 us (3%)
  between operations  0.73 us (2%)
  other arithmetic  0.65 us (2%)
    all_to_all x3, blocking collectives, exchange(): lax.all_to_all(value, 'expert', split_axis=0, concat_axis=0, tiled=True,...  29.2 us
    pallas_call x6, Pallas kernels, call(): pl.pallas_call(kernel, out_shape=[jax.ShapeDtypeStruct(shape, dtype) for...  5.38 us
    unnamed x10, local copies, waits for them, and re-layouts  1.06 us
    ppermute x2, waiting for transfers between devices, swap_cores(): return lax.ppermute(value, 'expert', [(i, i ^ 1) for i in range(size)])  1.06 us
  transfers between devices with their start and end apart: 2, of which 1 were waited for; matrix products, arithmetic and copies ran while one was open for 0% of the time, Pallas kernels for 3%

profile of v24, /device:TPU:0, one launch (start us, length us, event | category | flops | bytes accessed | tf_op | source)
XLA Modules:
  0.0 38.4 jit_solution(17770241051662052481)
XLA Ops:
  0.6 0.0 copy-start.4
  0.6 0.0 copy-start
  0.7 0.0 copy-start.3
  0.7 0.0 copy-start.1
  0.7 0.0 copy-start.2
  0.7 0.7 %copy-done.4 = bf16[1280,8]{0,1:T(8,128)(2,1)S(1)} copy-done((bf16[1280,8]{0,1:T(8,128)(2,1)S(1)}, bf16[1280,8]{0,1:T(8,128)(2,1)}, u32[]{:S(2)}) %copy-start.4) | copy-done | bytes 20504
  1.4 0.4 copy-done
  1.7 0.5 %shard_map.69 = (f32[8,256]{1,0:T(8,128)S(1)}, f32[8,256]{1,0:T(8,128)S(1)}) custom-call(bf16[256,1280]{1,0:T(8,128)(2,1)S(1)} %bitcast.6, bf16[8,1280]{1,0:T(8,128)(2,1)S(1)} %bitcast.11, f32[8,128]{1,0:T(8,128)S(1)} %shard_map.68.token_ref), custom_call_target="tpu_custom_call" | custom-call | flops 10485760 | bytes 655360 | tf_op jit(solution)/shard_map/pallas_call | solution.py:131
  2.2 0.0 copy-done.3
  2.2 0.3 shard_map.70
  2.5 11.0 %all_to_all.15.got_ref = bf16[16,2,1280]{2,1,0:T(2,128)(2,1)S(1)} all-to-all(bf16[16,2,1280]{2,1,0:T(2,128)(2,1)S(1)} %shard_map.70), channel_id=1, replica_groups={{15,14,1,0,13,12,3,2,11,10,5,4,9,8,7,6},{31,30,17,16,29,28,19,18,27,26,..., dimensions={0} | all-to-all | bytes 163840 | tf_op jit(solution)/shard_map/all_to_all | solution.py:148
  13.5 0.0 copy-done.1
  13.5 0.0 copy-done.2
  13.5 2.7 %shard_map.71 = bf16[16,2,1280]{2,1,0:T(2,128)(2,1)S(1)} custom-call(bf16[16,2,1280]{2,1,0:T(2,128)(2,1)S(1)} %all_to_all.15.got_ref, bf16[1280,1280]{1,0:T(8,128)(2,1)S(1)} %copy-done.1, bf16[1280,1280]{1,0:T(8,128)(2,1)S(1)} %copy-done.2), custom_call_target="tpu_custom_call" | custom-call | flops 209715200 | bytes 6553600 | tf_op jit(solution)/shard_map/pallas_call | solution.py:131
  16.2 9.0 %all_to_all.16.back_ref = bf16[16,2,1280]{2,1,0:T(2,128)(2,1)S(1)} all-to-all(bf16[16,2,1280]{2,1,0:T(2,128)(2,1)S(1)} %shard_map.71), channel_id=1, replica_groups={{15,4,9,14,3,8,13,2,7,12,1,6,11,0,5,10},{31,20,25,30,19,24,29,18,23,28,..., dimensions={0} | all-to-all | bytes 163840 | tf_op jit(solution)/shard_map/all_to_all | solution.py:148
  25.2 0.7 %shard_map.72 = (f32[8,640]{1,0:T(8,128)S(1)}, f32[8,640]{1,0:T(8,128)S(1)}, bf16[16,256]{1,0:T(8,128)(2,1)S(1)}, bf16[16,1280]{1,0:T(8,128)(2,1)S(1)}) custom-call(bf16[256,1280]{1,0:T(8,128)(2,1)S(1)} %bitcast.8, bf16[256,1280]{1,0:T(8,128)(2,1)S(1)} %bitcast.10, bf16[8,1280]{1,0:T(8,128)(2,1)S(1)} %bitcast.12, ...), custom_call_target="tpu_custom_call" | custom-call | flops 31457280 | bytes 1310720 | tf_op jit(solution)/shard_map/pallas_call | solution.py:131
  25.9 0.2 collective-permute-start
  26.1 1.1 %collective-permute-done = f32[8,640]{1,0:T(8,128)S(1)} collective-permute-done((f32[8,640]{1,0:T(8,128)S(1)}, f32[8,640]{1,0:T(8,128)S(1)}, u32[]{:S(2)}, u32[]{:S(2)}) %collective-permute-start) | collective-permute-done | bytes 20512 | tf_op jit(solution)/shard_map/ppermute | solution.py:144
  27.2 9.2 %all_to_all.17 = bf16[8,8,640]{2,1,0:T(8,128)(2,1)S(1)} all-to-all(bf16[8,8,640]{2,1,0:T(8,128)(2,1)S(1)} %broadcast_in_dim.10), channel_id=1, replica_groups={{14,0,12,2,10,4,8,6},{15,1,13,3,11,5,9,7},{30,16,28,18,26,20,24,22},{31..., dimensions={0} | all-to-all | bytes 163840 | tf_op jit(solution)/shard_map/all_to_all | solution.py:148
  36.4 0.1 collective-permute-start.1
  36.5 1.2 %shard_map.73 = bf16[256,1280]{1,0:T(8,128)(2,1)} custom-call(bf16[16,256]{1,0:T(8,128)(2,1)S(1)} %get-tuple-element.10.left_ref, bf16[16,1280]{1,0:T(8,128)(2,1)S(1)} %get-tuple-element.11.right_ref), custom_call_target="tpu_custom_call" | custom-call | flops 10485760 | bytes 655360 | tf_op jit(solution)/shard_map/pallas_call | solution.py:131
  37.7 0.0 collective-permute-done.1
  37.7 0.6 %maximum_bitcast_fusion = f32[1280,8]{0,1:T(8,128)} fusion(f32[8,640]{1,0:T(8,128)S(1)} %get-tuple-element.15, f32[8,640]{1,0:T(8,128)S(1)} %get-tuple-element.14), kind=kLoop, calls=%fused_computation.1 | loop fusion | flops 10240 | bytes 81920 | tf_op jit(solution)/shard_map/transpose | solution.py:228
  (5 shorter events, 0.0 us)
Async XLA Ops:
  0.6 0.7 %copy-start.4 = (bf16[1280,8]{0,1:T(8,128)(2,1)S(1)}, bf16[1280,8]{0,1:T(8,128)(2,1)}, u32[]{:S(2)}) copy-start(bf16[1280,8]{0,1:T(8,128)(2,1)} %param.7) | copy-start | bytes 61444
  0.6 1.1 %copy-start = (bf16[1,256,1280]{2,1,0:T(8,128)(2,1)S(1)}, bf16[1,256,1280]{2,1,0:T(8,128)(2,1)}, u32[]{:S(2)}) copy-start(bf16[1,256,1280]{2,1,0:T(8,128)(2,1)} %param.5) | copy-start | bytes 1966084
  0.7 1.6 %copy-start.3 = (bf16[1,256,1280]{2,1,0:T(8,128)(2,1)S(1)}, bf16[1,256,1280]{2,1,0:T(8,128)(2,1)}, u32[]{:S(2)}) copy-start(bf16[1,256,1280]{2,1,0:T(8,128)(2,1)} %param.6) | copy-start | bytes 1966084
  0.7 12.8 %copy-start.1 = (bf16[1280,1280]{1,0:T(8,128)(2,1)S(1)}, bf16[1280,1280]{1,0:T(8,128)(2,1)}, u32[]{:S(2)}) copy-start(bf16[1280,1280]{1,0:T(8,128)(2,1)} %in_weight_ref.1) | copy-start | bytes 9830404
  0.7 12.8 %copy-start.2 = (bf16[1280,1280]{1,0:T(8,128)(2,1)S(1)}, bf16[1280,1280]{1,0:T(8,128)(2,1)}, u32[]{:S(2)}) copy-start(bf16[1280,1280]{1,0:T(8,128)(2,1)} %out_weight_ref.1) | copy-start | bytes 9830404
  25.9 1.2 %collective-permute-start = (f32[8,640]{1,0:T(8,128)S(1)}, f32[8,640]{1,0:T(8,128)S(1)}, u32[]{:S(2)}, u32[]{:S(2)}) collective-permute-start(f32[8,640]{1,0:T(8,128)S(1)} %get-tuple-element.13), channel_id=1, source_target_pairs={{0,1},{1,0},{2,3},{3,2},{4,5},{5,4},{6,7},{7,6},{8,9},{9,8},{10,11... | collective-permute-start | bytes 61448 | tf_op jit(solution)/shard_map/ppermute | solution.py:144
  36.4 1.3 %collective-permute-start.1 = (f32[8,640]{1,0:T(8,128)S(1)}, f32[8,640]{1,0:T(8,128)S(1)}, u32[]{:S(2)}, u32[]{:S(2)}) collective-permute-start(f32[8,640]{1,0:T(8,128)S(1)} %convert_reduce_fusion), channel_id=1, source_target_pairs={{0,1},{1,0},{2,3},{3,2},{4,5},{5,4},{6,7},{7,6},{8,9},{9,8},{10,11... | collective-permute-start | bytes 61448 | tf_op jit(solution)/shard_map/ppermute | solution.py:144

commit v25 on v23

--- a/solution.py
+++ b/solution.py
@@ -20,7 +20,7 @@
 
 
 def back_order(size):
-    return [(size - 1 + 5 * k) % size for k in range(size)]
+    return out_order(size)
 
 
 def sum_order(size, core):

time: 38.4 us -> 38.8 us (1.010)
  blocking collectives: 29 us -> 29.4 us
where the time goes in v25:
time: 38.8 us; the launch traced here: 38.5 us
  blocking collectives  29.4 us (76%)
  Pallas kernels  5.38 us (14%)
  waiting for transfers between devices  1.08 us (3%)
  local copies, waits for them, and re-layouts  1.07 us (3%)
  between operations  0.73 us (2%)
  other arithmetic  0.65 us (2%)
    all_to_all x3, blocking collectives, exchange(): lax.all_to_all(value, 'expert', split_axis=0, concat_axis=0, tiled=True,...  29.4 us
    pallas_call x6, Pallas kernels, call(): pl.pallas_call(kernel, out_shape=[jax.ShapeDtypeStruct(shape, dtype) for...  5.38 us
    ppermute x2, waiting for transfers between devices, swap_cores(): return lax.ppermute(value, 'expert', [(i, i ^ 1) for i in range(size)])  1.08 us
    unnamed x10, local copies, waits for them, and re-layouts  1.06 us
  transfers between devices with their start and end apart: 2, of which 1 were waited for; matrix products, arithmetic and copies ran while one was open for 0% of the time, Pallas kernels for 3%

profile of v25, /device:TPU:0, one launch (start us, length us, event | category | flops | bytes accessed | tf_op | source)
XLA Modules:
  0.0 38.5 jit_solution(8507259822220069290)
XLA Ops:
  0.6 0.0 copy-start.4
  0.6 0.0 copy-start
  0.7 0.0 copy-start.3
  0.7 0.0 copy-start.1
  0.7 0.0 copy-start.2
  0.7 0.7 %copy-done.4 = bf16[1280,8]{0,1:T(8,128)(2,1)S(1)} copy-done((bf16[1280,8]{0,1:T(8,128)(2,1)S(1)}, bf16[1280,8]{0,1:T(8,128)(2,1)}, u32[]{:S(2)}) %copy-start.4) | copy-done | bytes 20504
  1.4 0.4 copy-done
  1.7 0.5 %shard_map.69 = (f32[8,256]{1,0:T(8,128)S(1)}, f32[8,256]{1,0:T(8,128)S(1)}) custom-call(bf16[256,1280]{1,0:T(8,128)(2,1)S(1)} %bitcast.6, bf16[8,1280]{1,0:T(8,128)(2,1)S(1)} %bitcast.11, f32[8,128]{1,0:T(8,128)S(1)} %shard_map.68.token_ref), custom_call_target="tpu_custom_call" | custom-call | flops 10485760 | bytes 655360 | tf_op jit(solution)/shard_map/pallas_call | solution.py:129
  2.2 0.0 copy-done.3
  2.2 0.3 shard_map.70
  2.5 11.3 %all_to_all.15.got_ref = bf16[16,2,1280]{2,1,0:T(2,128)(2,1)S(1)} all-to-all(bf16[16,2,1280]{2,1,0:T(2,128)(2,1)S(1)} %shard_map.70), channel_id=1, replica_groups={{15,1,2,3,4,5,6,7,8,9,10,11,12,13,14,0},{31,17,18,19,20,21,22,23,24,25,..., dimensions={0} | all-to-all | bytes 163840 | tf_op jit(solution)/shard_map/all_to_all | solution.py:146
  13.8 0.0 copy-done.1
  13.8 0.0 copy-done.2
  13.8 2.7 %shard_map.71 = bf16[16,2,1280]{2,1,0:T(2,128)(2,1)S(1)} custom-call(bf16[16,2,1280]{2,1,0:T(2,128)(2,1)S(1)} %all_to_all.15.got_ref, bf16[1280,1280]{1,0:T(8,128)(2,1)S(1)} %copy-done.1, bf16[1280,1280]{1,0:T(8,128)(2,1)S(1)} %copy-done.2), custom_call_target="tpu_custom_call" | custom-call | flops 209715200 | bytes 6553600 | tf_op jit(solution)/shard_map/pallas_call | solution.py:129
  16.5 8.8 %all_to_all.16.back_ref = bf16[16,2,1280]{2,1,0:T(2,128)(2,1)S(1)} all-to-all(bf16[16,2,1280]{2,1,0:T(2,128)(2,1)S(1)} %shard_map.71), channel_id=1, replica_groups={{15,1,2,3,4,5,6,7,8,9,10,11,12,13,14,0},{31,17,18,19,20,21,22,23,24,25,..., dimensions={0} | all-to-all | bytes 163840 | tf_op jit(solution)/shard_map/all_to_all | solution.py:146
  25.3 0.7 %shard_map.72 = (f32[8,640]{1,0:T(8,128)S(1)}, f32[8,640]{1,0:T(8,128)S(1)}, bf16[16,256]{1,0:T(8,128)(2,1)S(1)}, bf16[16,1280]{1,0:T(8,128)(2,1)S(1)}) custom-call(bf16[256,1280]{1,0:T(8,128)(2,1)S(1)} %bitcast.8, bf16[256,1280]{1,0:T(8,128)(2,1)S(1)} %bitcast.10, bf16[8,1280]{1,0:T(8,128)(2,1)S(1)} %bitcast.12, ...), custom_call_target="tpu_custom_call" | custom-call | flops 31457280 | bytes 1310720 | tf_op jit(solution)/shard_map/pallas_call | solution.py:129
  26.0 0.2 collective-permute-start
  26.1 1.1 %collective-permute-done = f32[8,640]{1,0:T(8,128)S(1)} collective-permute-done((f32[8,640]{1,0:T(8,128)S(1)}, f32[8,640]{1,0:T(8,128)S(1)}, u32[]{:S(2)}, u32[]{:S(2)}) %collective-permute-start) | collective-permute-done | bytes 20512 | tf_op jit(solution)/shard_map/ppermute | solution.py:142
  27.2 9.4 %all_to_all.17 = bf16[8,8,640]{2,1,0:T(8,128)(2,1)S(1)} all-to-all(bf16[8,8,640]{2,1,0:T(8,128)(2,1)S(1)} %broadcast_in_dim.10), channel_id=1, replica_groups={{14,0,12,2,10,4,8,6},{15,1,13,3,11,5,9,7},{30,16,28,18,26,20,24,22},{31..., dimensions={0} | all-to-all | bytes 163840 | tf_op jit(solution)/shard_map/all_to_all | solution.py:146
  36.6 0.1 collective-permute-start.1
  36.7 1.2 %shard_map.73 = bf16[256,1280]{1,0:T(8,128)(2,1)} custom-call(bf16[16,256]{1,0:T(8,128)(2,1)S(1)} %get-tuple-element.10.left_ref, bf16[16,1280]{1,0:T(8,128)(2,1)S(1)} %get-tuple-element.11.right_ref), custom_call_target="tpu_custom_call" | custom-call | flops 10485760 | bytes 655360 | tf_op jit(solution)/shard_map/pallas_call | solution.py:129
  37.9 0.0 collective-permute-done.1
  37.9 0.6 %maximum_bitcast_fusion = f32[1280,8]{0,1:T(8,128)} fusion(f32[8,640]{1,0:T(8,128)S(1)} %get-tuple-element.15, f32[8,640]{1,0:T(8,128)S(1)} %get-tuple-element.14), kind=kLoop, calls=%fused_computation.1 | loop fusion | flops 10240 | bytes 81920 | tf_op jit(solution)/shard_map/transpose | solution.py:226
  (5 shorter events, 0.0 us)
Async XLA Ops:
  0.6 0.7 %copy-start.4 = (bf16[1280,8]{0,1:T(8,128)(2,1)S(1)}, bf16[1280,8]{0,1:T(8,128)(2,1)}, u32[]{:S(2)}) copy-start(bf16[1280,8]{0,1:T(8,128)(2,1)} %param.7) | copy-start | bytes 61444
  0.6 1.1 %copy-start = (bf16[1,256,1280]{2,1,0:T(8,128)(2,1)S(1)}, bf16[1,256,1280]{2,1,0:T(8,128)(2,1)}, u32[]{:S(2)}) copy-start(bf16[1,256,1280]{2,1,0:T(8,128)(2,1)} %param.5) | copy-start | bytes 1966084
  0.7 1.6 %copy-start.3 = (bf16[1,256,1280]{2,1,0:T(8,128)(2,1)S(1)}, bf16[1,256,1280]{2,1,0:T(8,128)(2,1)}, u32[]{:S(2)}) copy-start(bf16[1,256,1280]{2,1,0:T(8,128)(2,1)} %param.6) | copy-start | bytes 1966084
  0.7 13.1 %copy-start.1 = (bf16[1280,1280]{1,0:T(8,128)(2,1)S(1)}, bf16[1280,1280]{1,0:T(8,128)(2,1)}, u32[]{:S(2)}) copy-start(bf16[1280,1280]{1,0:T(8,128)(2,1)} %in_weight_ref.1) | copy-start | bytes 9830404
  0.7 13.1 %copy-start.2 = (bf16[1280,1280]{1,0:T(8,128)(2,1)S(1)}, bf16[1280,1280]{1,0:T(8,128)(2,1)}, u32[]{:S(2)}) copy-start(bf16[1280,1280]{1,0:T(8,128)(2,1)} %out_weight_ref.1) | copy-start | bytes 9830404
  26.0 1.2 %collective-permute-start = (f32[8,640]{1,0:T(8,128)S(1)}, f32[8,640]{1,0:T(8,128)S(1)}, u32[]{:S(2)}, u32[]{:S(2)}) collective-permute-start(f32[8,640]{1,0:T(8,128)S(1)} %get-tuple-element.13), channel_id=1, source_target_pairs={{0,1},{1,0},{2,3},{3,2},{4,5},{5,4},{6,7},{7,6},{8,9},{9,8},{10,11... | collective-permute-start | bytes 61448 | tf_op jit(solution)/shard_map/ppermute | solution.py:142
  36.6 1.3 %collective-permute-start.1 = (f32[8,640]{1,0:T(8,128)S(1)}, f32[8,640]{1,0:T(8,128)S(1)}, u32[]{:S(2)}, u32[]{:S(2)}) collective-permute-start(f32[8,640]{1,0:T(8,128)S(1)} %convert_reduce_fusion), channel_id=1, source_target_pairs={{0,1},{1,0},{2,3},{3,2},{4,5},{5,4},{6,7},{7,6},{8,9},{9,8},{10,11... | collective-permute-start | bytes 61448 | tf_op jit(solution)/shard_map/ppermute | solution.py:142
